TPU v7x, 32 devices: a whole 2x2x4 slice. The times are simulated.
32 devices in a mesh: trow: 4 (over y, core), tcol: 8 (over z, x).
Axes of the slice: x: 2, y: 2, z: 4, core: 2. Of those that a mesh axis runs over, the one named last changes fastest.
Arguments:
- object_planes: float32 [2, 1024, 2048], P(None, 'trow', 'tcol'), may hold values from -5 to 5
- probe: float32 [2, 128, 128], replicated, may hold values from -5 to 5
- intensities: bfloat16 [4, 8, 48, 128, 128], P('trow', 'tcol'), may hold values from 0 to 2
- row_offsets: int32 [4, 8, 48], P('trow', 'tcol'), may hold values from -64 to 192
- col_offsets: int32 [4, 8, 48], P('trow', 'tcol'), may hold values from -64 to 192
- counts: int32 [32], P(('trow', 'tcol')), may hold values from 1 to 48, 960 in all
Outputs:
- object_grad: float32 [2, 1024, 2048], P(None, 'trow', 'tcol')
- probe_grad: float32 [2, 128, 128], replicated
All inputs are finite; a program needn't handle non-finite values. No bound on the sum of `counts` on one device may be relied on, other than what follows from the above.
Results may differ from a plain program's by a relative error of at most 0.0003.
Values sent between devices are 32-bit elements; how exact they have to be, the bound alone decides.
No kernel may reach another device: no remote copies, remote signals or barrier semaphores. Data moves between devices by JAX's collectives and lax.ppermute only.
A program may use at most 64 MiB of HBM per device.

v0:
```python
import math

import jax
import jax.numpy as jnp
from jax import lax
from jax.sharding import PartitionSpec as P

P_SIZE = 128
POS_DEV = 48


group_size = 8
highest = lax.Precision.HIGHEST


def with_halo(array, sides, width):
    for axis, dim in sides:
        size, length = (lax.axis_size(axis), array.shape[dim])
        up = [(i, (i + 1) % size) for i in range(size - 1)]
        down = [(j, i) for i, j in up]
        last = lax.slice_in_dim(array, length - width, length, axis=dim)
        initial = lax.slice_in_dim(array, 0, width, axis=dim)
        before = lax.ppermute(last, axis, up)
        after = lax.ppermute(initial, axis, down)
        array = jnp.concatenate([before, array, after], axis=dim)
    return array


def shifted(value, axis, steps):
    count = lax.axis_size(axis)
    initial, last = (max(0, -steps), min(count, count - steps))
    return lax.ppermute(value, axis, [(source, source + steps) for source in range(initial, last)])


def dft_tables(length):
    index = jnp.arange(length, dtype=jnp.int32)
    product = index[:, None] * index[None, :] % length
    angle = product.astype(jnp.float32) * (-2.0 * math.pi / length)
    factor = 1.0 / math.sqrt(length)
    return (jnp.cos(angle) * factor, jnp.sin(angle) * factor)


def left_apply(matrix, batch):
    return jnp.einsum("jk,gkl->gjl", matrix, batch, precision=highest)


def right_apply(batch, matrix):
    return jnp.einsum("gjk,kl->gjl", batch, matrix, precision=highest)


def body(object_planes, probe, intensities, row_offsets, col_offsets, counts):
    margin = P_SIZE // 2
    tile_rows = object_planes.shape[1]
    tile_cols = object_planes.shape[2]
    padded = with_halo(object_planes, (("trow", 1), ("tcol", 2)), margin)
    cosine, sine_part = dft_tables(P_SIZE)
    probe_real = probe[0]
    probe_imag = probe[1]
    live_count = counts[0]
    row_list = row_offsets.reshape(-1)
    col_list = col_offsets.reshape(-1)
    measured_all = intensities.reshape(-1, P_SIZE, P_SIZE)
    group_total = (live_count + group_size - 1) // group_size

    def take_patch(row_at, col_at):
        return lax.dynamic_slice(padded, (0, row_at + margin, col_at + margin), (2, P_SIZE, P_SIZE))

    def one_group(group, carry):
        grad_window, probe_sum = carry
        first = group * group_size
        rows_here = lax.dynamic_slice_in_dim(row_list, first, group_size)
        cols_here = lax.dynamic_slice_in_dim(col_list, first, group_size)
        measured = lax.dynamic_slice_in_dim(measured_all, first, group_size, 0).astype(jnp.float32)
        live = (first + jnp.arange(group_size, dtype=jnp.int32) < live_count).astype(jnp.float32)
        patches = jax.vmap(take_patch)(rows_here, cols_here)
        patch_real = patches[:, 0]
        patch_imag = patches[:, 1]
        wave_real = probe_real * patch_real - probe_imag * patch_imag
        wave_imag = probe_real * patch_imag + probe_imag * patch_real
        half_real = left_apply(cosine, wave_real) - left_apply(sine_part, wave_imag)
        half_imag = left_apply(cosine, wave_imag) + left_apply(sine_part, wave_real)
        psi_real = right_apply(half_real, cosine) - right_apply(half_imag, sine_part)
        psi_imag = right_apply(half_real, sine_part) + right_apply(half_imag, cosine)
        weight = 2.0 * (psi_real * psi_real + psi_imag * psi_imag - measured) * live[:, None, None]
        grad_real = weight * psi_real
        grad_imag = weight * psi_imag
        back_real = left_apply(cosine, grad_real) + left_apply(sine_part, grad_imag)
        back_imag = left_apply(cosine, grad_imag) - left_apply(sine_part, grad_real)
        exit_real = right_apply(back_real, cosine) + right_apply(back_imag, sine_part)
        exit_imag = right_apply(back_imag, cosine) - right_apply(back_real, sine_part)
        probe_real_sum = jnp.sum(patch_real * exit_real + patch_imag * exit_imag, axis=0)
        probe_imag_sum = jnp.sum(patch_real * exit_imag - patch_imag * exit_real, axis=0)
        probe_sum = probe_sum + jnp.stack([probe_real_sum, probe_imag_sum])
        contrib_real = probe_real * exit_real + probe_imag * exit_imag
        contrib_imag = probe_real * exit_imag - probe_imag * exit_real
        contrib = jnp.stack([contrib_real, contrib_imag], axis=1)
        for member in range(group_size):
            row_at = rows_here[member] + margin
            col_at = cols_here[member] + margin
            current = lax.dynamic_slice(grad_window, (0, row_at, col_at), (2, P_SIZE, P_SIZE))
            grad_window = lax.dynamic_update_slice(
                grad_window, current + contrib[member], (0, row_at, col_at)
            )
        return (grad_window, probe_sum)

    start = (
        jnp.zeros((2, tile_rows + P_SIZE, tile_cols + P_SIZE), jnp.float32),
        jnp.zeros((2, P_SIZE, P_SIZE), jnp.float32),
    )
    grad_window, probe_sum = lax.fori_loop(0, group_total, one_group, start)
    from_below = shifted(grad_window[:, :margin, :], "trow", -1)
    from_above = shifted(grad_window[:, tile_rows + margin :, :], "trow", 1)
    middle = grad_window[:, margin : tile_rows + margin, :]
    middle = middle.at[:, tile_rows - margin :, :].add(from_below)
    middle = middle.at[:, :margin, :].add(from_above)
    from_right = shifted(middle[:, :, :margin], "tcol", -1)
    from_left = shifted(middle[:, :, tile_cols + margin :], "tcol", 1)
    center = middle[:, :, margin : tile_cols + margin]
    center = center.at[:, :, tile_cols - margin :].add(from_right)
    center = center.at[:, :, :margin].add(from_left)
    probe_total = lax.psum(probe_sum, ("trow", "tcol"))
    devices = lax.axis_size("trow") * lax.axis_size("tcol")
    probe_grad = probe_total / jnp.sqrt(jnp.float32(POS_DEV * devices))
    return (center, probe_grad)


def solution(mesh):
    return jax.shard_map(
        body,
        mesh=mesh,
        in_specs=(
            P(None, "trow", "tcol"),
            P(),
            P("trow", "tcol", None, None, None),
            P("trow", "tcol", None),
            P("trow", "tcol", None),
            P(("trow", "tcol")),
        ),
        out_specs=(P(None, "trow", "tcol"), P()),
        check_vma=False,
    )
```

profile of v0, /device:TPU:0, one launch (start us, length us, event | category | flops | bytes accessed | tf_op | source)
XLA Modules:
  0.0 693.5 jit_solution(2118354488391517851)
XLA Ops:
  8.3 2.4 collective-permute-start
  12.7 3.3 collective-permute-done.1
  16.2 3.4 collective-permute-start.2
  20.9 13.9 %collective-permute-done.2 = f32[2,384,64]{2,1,0:T(8,128)S(1)} collective-permute-done((f32[2,384,64]{2,1,0:T(8,128)S(1)}, f32[2,384,64]{2,1,0:T(8,128)S(1)}, u32[]{:S(2)}, u32[]{:S(2)}) %collective-permute-start.2) | collective-permute-done | bytes 196640 | tf_op jit(solution)/shard_map/ppermute | solution.py:23
  37.1 417.4 %while.26 = (s32[]{:T(128)}, f32[2,384,384]{2,1,0:T(8,128)S(1)}, f32[2,128,128]{2,1,0:T(8,128)S(1)}, s32[]{:T(128)}, s32[48]{0:T(128)S(1)}, /*index=5*/s32[48]{0...) while((s32[]{:T(128)}, f32[2,384,384]{2,1,0:T(8,128)S(1)}, ...), condition=%wide.region_3.4_spmd.clone.clone, body=%wide.region_0.3_spmd.clone.clone.sunk | while | flops 3233841152 | bytes 48631536 | solution.py:110
  37.2 22.4 %while.27 = (s32[]{:T(128)}, f32[2,384,384]{2,1,0:T(8,128)}, s32[8,3]{0,1:T(4,128)S(1)}, f32[8,2,128,128]{3,2,0,1:T(8,128)S(1)}, s32[]{:T(128)}) while((s32[]{:T(128)}, f32[2,384,384]{2,1,0:T(8,128)}, s32[8,3]{0,1:T(4,128)S(1)}, f32[8,2,128,128]{3,2,0,1:T(8,128)S(1)}, s32[]{:T(128)}) %tuple.110), condition=%wide.while_cond.4, body=%wide.while_body.4.sunk | while | flops 2 | bytes 262261 | solution.py:66
  37.8 2.2 bitcast_dynamic-update-slice_fusion.2
  83.4 2.5 dynamic_update_slice.80
  93.3 2.5 dynamic_update_slice.82
  98.5 2.5 dynamic_update_slice.83
  103.6 2.2 dynamic_update_slice.84
  108.4 2.5 dynamic_update_slice.85
  113.5 2.2 dynamic_update_slice.86
  118.2 2.4 dynamic_update_slice.87
  120.7 22.4 %while.27 = (s32[]{:T(128)}, f32[2,384,384]{2,1,0:T(8,128)}, s32[8,3]{0,1:T(4,128)S(1)}, f32[8,2,128,128]{3,2,0,1:T(8,128)S(1)}, s32[]{:T(128)}) while((s32[]{:T(128)}, f32[2,384,384]{2,1,0:T(8,128)}, s32[8,3]{0,1:T(4,128)S(1)}, f32[8,2,128,128]{3,2,0,1:T(8,128)S(1)}, s32[]{:T(128)}) %tuple.110), condition=%wide.while_cond.4, body=%wide.while_body.4.sunk | while | flops 2 | bytes 262261 | solution.py:66
  171.6 2.5 dynamic_update_slice.81
  181.7 2.3 dynamic_update_slice.83
  186.5 2.5 dynamic_update_slice.84
  191.7 2.5 dynamic_update_slice.85
  196.8 2.4 dynamic_update_slice.86
  201.6 2.5 dynamic_update_slice.87
  204.2 22.4 %while.27 = (s32[]{:T(128)}, f32[2,384,384]{2,1,0:T(8,128)}, s32[8,3]{0,1:T(4,128)S(1)}, f32[8,2,128,128]{3,2,0,1:T(8,128)S(1)}, s32[]{:T(128)}) while((s32[]{:T(128)}, f32[2,384,384]{2,1,0:T(8,128)}, s32[8,3]{0,1:T(4,128)S(1)}, f32[8,2,128,128]{3,2,0,1:T(8,128)S(1)}, s32[]{:T(128)}) %tuple.110), condition=%wide.while_cond.4, body=%wide.while_body.4.sunk | while | flops 2 | bytes 262261 | solution.py:66
  250.4 2.4 dynamic_update_slice.80
  260.3 2.5 dynamic_update_slice.82
  265.4 2.4 dynamic_update_slice.83
  270.4 2.5 dynamic_update_slice.84
  275.6 2.4 dynamic_update_slice.85
  280.6 2.2 dynamic_update_slice.86
  287.6 22.4 %while.27 = (s32[]{:T(128)}, f32[2,384,384]{2,1,0:T(8,128)}, s32[8,3]{0,1:T(4,128)S(1)}, f32[8,2,128,128]{3,2,0,1:T(8,128)S(1)}, s32[]{:T(128)}) while((s32[]{:T(128)}, f32[2,384,384]{2,1,0:T(8,128)}, s32[8,3]{0,1:T(4,128)S(1)}, f32[8,2,128,128]{3,2,0,1:T(8,128)S(1)}, s32[]{:T(128)}) %tuple.110), condition=%wide.while_cond.4, body=%wide.while_body.4.sunk | while | flops 2 | bytes 262261 | solution.py:66
  333.8 2.5 dynamic_update_slice.80
  338.9 2.2 dynamic_update_slice.81
  343.8 2.5 dynamic_update_slice.82
  349.0 2.5 dynamic_update_slice.83
  358.9 2.4 dynamic_update_slice.85
  364.0 2.3 dynamic_update_slice.86
  368.6 2.4 dynamic_update_slice.87
  371.2 22.4 %while.27 = (s32[]{:T(128)}, f32[2,384,384]{2,1,0:T(8,128)}, s32[8,3]{0,1:T(4,128)S(1)}, f32[8,2,128,128]{3,2,0,1:T(8,128)S(1)}, s32[]{:T(128)}) while((s32[]{:T(128)}, f32[2,384,384]{2,1,0:T(8,128)}, s32[8,3]{0,1:T(4,128)S(1)}, f32[8,2,128,128]{3,2,0,1:T(8,128)S(1)}, s32[]{:T(128)}) %tuple.110), condition=%wide.while_cond.4, body=%wide.while_body.4.sunk | while | flops 2 | bytes 262261 | solution.py:66
  417.4 2.5 dynamic_update_slice.80
  422.5 2.5 dynamic_update_slice.81
  432.3 2.2 dynamic_update_slice.83
  437.1 2.5 dynamic_update_slice.84
  442.3 2.4 dynamic_update_slice.85
  447.3 2.3 dynamic_update_slice.86
  451.9 2.5 dynamic_update_slice.87
  457.9 90.7 %collective-permute-start.5 = (f32[2,64,384]{2,1,0:T(8,128)S(1)}, f32[2,64,384]{2,1,0:T(8,128)S(1)}, u32[]{:S(2)}, u32[]{:S(2)}) collective-permute-start(f32[2,64,384]{2,1,0:T(8,128)S(1)} %get-tuple-element.452), channel_id=1, source_target_pairs={{0,8},{8,16},{16,24},{1,9},{9,17},{17,25},{2,10},{10,18},{18,26},{... | collective-permute-start | bytes 589832 | tf_op jit(solution)/shard_map/ppermute | solution.py:32
  551.1 123.6 %all-reduce.2.cloned.1.call-done = f32[2,128,128]{2,1,0:T(8,128)} async-done(((f32[2,128,128]{2,1,0:T(8,128)}), f32[2,128,128]{2,1,0:T(8,128)}) %all-reduce.2.cloned.1.call-update) | async-done | bytes 131088 | tf_op jit(solution)/shard_map/psum | solution.py:121
  676.5 3.4 collective-permute-start.7
  681.1 3.6 collective-permute-done.7
  (339 shorter events, 251.7 us)
Async XLA Ops:
  7.2 5.5 copy-start.3
  7.2 667.6 %all-reduce.2.cloned.1.call-start = ((), (), s32[]{:S(2)}) async-start(), calls=%async_computation | async-start | bytes 262144 | tf_op jit(solution)/shard_map/psum | solution.py:121
  8.3 4.3 collective-permute-start
  10.6 5.4 collective-permute-start.1
  12.7 8.2 %copy-start.4 = (f32[2,128,128]{2,1,0:T(8,128)S(1)}, f32[2,128,128]{2,1,0:T(8,128)}, u32[]{:S(2)}) copy-start(f32[2,128,128]{2,1,0:T(8,128)} %param.17) | copy-start | bytes 393220
  16.2 18.7 %collective-permute-start.2 = (f32[2,384,64]{2,1,0:T(8,128)S(1)}, f32[2,384,64]{2,1,0:T(8,128)S(1)}, u32[]{:S(2)}, u32[]{:S(2)}) collective-permute-start(f32[2,384,64]{2,1,0:T(8,128)S(1)} %get-tuple-element.456), channel_id=1, source_target_pairs={{0,1},{1,2},{2,3},{3,4},{4,5},{5,6},{6,7},{8,9},{9,10},{10,11},{11... | collective-permute-start | bytes 589832 | tf_op jit(solution)/shard_map/ppermute | solution.py:23
  19.6 15.3 %collective-permute-start.3 = (f32[2,384,64]{2,1,0:T(8,128)S(1)}, f32[2,384,64]{2,1,0:T(8,128)S(1)}, u32[]{:S(2)}, u32[]{:S(2)}) collective-permute-start(f32[2,384,64]{2,1,0:T(8,128)S(1)} %get-tuple-element.457), channel_id=1, source_target_pairs={{1,0},{2,1},{3,2},{4,3},{5,4},{6,5},{7,6},{9,8},{10,9},{11,10},{12... | collective-permute-start | bytes 589832 | tf_op jit(solution)/shard_map/ppermute | solution.py:24
  36.4 0.7 copy-start.5
  36.4 0.7 copy-start.6
  66.7 3.0 copy-start
  150.2 3.0 copy-start
  233.7 3.0 copy-start
  317.1 3.0 copy-start
  400.7 3.0 copy-start
  454.4 3.4 copy-start.1
  454.5 3.3 collective-permute-start.4
  457.9 91.8 %collective-permute-start.5 = (f32[2,64,384]{2,1,0:T(8,128)S(1)}, f32[2,64,384]{2,1,0:T(8,128)S(1)}, u32[]{:S(2)}, u32[]{:S(2)}) collective-permute-start(f32[2,64,384]{2,1,0:T(8,128)S(1)} %get-tuple-element.452), channel_id=1, source_target_pairs={{0,8},{8,16},{16,24},{1,9},{9,17},{17,25},{2,10},{10,18},{18,26},{... | collective-permute-start | bytes 589832 | tf_op jit(solution)/shard_map/ppermute | solution.py:32
  549.8 130.1 %collective-permute-start.6 = (f32[2,256,64]{2,1,0:T(8,128)S(1)}, f32[2,256,64]{2,1,0:T(8,128)S(1)}, u32[]{:S(2)}, u32[]{:S(2)}) collective-permute-start(f32[2,256,64]{2,1,0:T(8,128)S(1)} %get-tuple-element.455), channel_id=1, source_target_pairs={{1,0},{2,1},{3,2},{4,3},{5,4},{6,5},{7,6},{9,8},{10,9},{11,10},{12... | collective-permute-start | bytes 393224 | tf_op jit(solution)/shard_map/ppermute | solution.py:32
  676.5 8.2 %collective-permute-start.7 = (f32[2,256,64]{2,1,0:T(8,128)S(1)}, f32[2,256,64]{2,1,0:T(8,128)S(1)}, u32[]{:S(2)}, u32[]{:S(2)}) collective-permute-start(f32[2,256,64]{2,1,0:T(8,128)S(1)} %get-tuple-element.454), channel_id=1, source_target_pairs={{0,1},{1,2},{2,3},{3,4},{4,5},{5,6},{6,7},{8,9},{9,10},{10,11},{11... | collective-permute-start | bytes 393224 | tf_op jit(solution)/shard_map/ppermute | solution.py:32
  685.9 0.8 copy-start.2
Sparse Core Ops, SparseCore 0:
  548.7 125.9 all-reduce.1
where the time goes:
time: 698 us; the launch traced here: 694 us
  local copies, waits for them, and re-layouts  218 us (31%)
  waiting for transfers between devices  147 us (21%)
  starting transfers between devices  105 us (15%)
  loops' own time  101 us (14%)
  matrix products  95.6 us (14%)
  between operations  14.9 us (2%)
  other arithmetic  11.9 us (2%)
    psum x1, waiting for transfers between devices, body(): probe_total = lax.psum(probe_sum, ('trow', 'tcol'))  124 us
    gather x120, local copies, waits for them, and re-layouts  111 us
    another operation x1, loops' own time, body(): grad_window, probe_sum = lax.fori_loop(0, group_total, one_group, start)  100 us
    ppermute x4, starting transfers between devices, shifted(): lax.ppermute(value, axis, [(source, source + steps) for source in range(i...  96.7 us
    dynamic_update_slice x40, local copies, waits for them, and re-layouts, one_group(): lax.dynamic_update_slice(grad_window, current + contrib[member], (0, row_...  94.4 us
    dot_general x40, matrix products, left_apply(): return jnp.einsum('jk,gkl->gjl', matrix, batch, precision=highest)  49.5 us
    dot_general x40, matrix products, right_apply(): return jnp.einsum('gjk,kl->gjl', batch, matrix, precision=highest)  46.1 us
  transfers between devices with their start and end apart: 9, of which 6 were waited for; matrix products, arithmetic and copies ran while one was open for 0% of the time, Pallas kernels for 0%

commit v1 on v0

v1 whole, which is shorter than its diff:
```python
import functools

import jax
import jax.numpy as jnp
import numpy as np
from jax import lax
from jax.experimental import pallas as pl
from jax.experimental.pallas import tpu as pltpu
from jax.sharding import PartitionSpec as P

LANES = 128
VMEM_BYTES = 48 * 1024 * 1024
GROUP = 4


def dft_tables(length):
    index = np.arange(length)
    angle = -2.0 * np.pi * (np.outer(index, index) % length) / length
    cosine, sine = np.cos(angle) / np.sqrt(length), np.sin(angle) / np.sqrt(length)
    right = np.block([[cosine, sine], [-sine, cosine]])
    tables = []
    for table in (right, right.T):
        high = table.astype(jnp.bfloat16)
        low = (table - high.astype(np.float64)).astype(jnp.bfloat16)
        tables += [high, low]
    return np.stack(tables)


def split(value):
    high = value.astype(jnp.bfloat16)
    low = (value - high.astype(jnp.float32)).astype(jnp.bfloat16)
    return high, low


def dot(a, b):
    return jnp.dot(a, b, preferred_element_type=jnp.float32)


def times_table(value, high, low):
    big, small = split(value)
    return dot(big, high) + (dot(small, high) + dot(big, low))


def table_times(high, low, value):
    big, small = split(value)
    return dot(high, big) + (dot(high, small) + dot(low, big))


def main_kernel(
    rows_ref, cols_ref, count_ref,
    centre_ref, top_ref, bottom_ref, left_ref, right_ref, probe_ref, measured_ref, table_ref,
    grad_centre_ref, grad_top_ref, grad_bottom_ref, probe_sum_ref,
    window, grad,
):
    size = probe_ref.shape[1]
    margin = size // 2
    height, width = centre_ref.shape[1:]
    tiles = width // LANES
    columns = tiles + 2
    slots = measured_ref.shape[0]
    half = (height + size) // 2

    for plane in range(2):
        base = plane * columns
        for tile in range(tiles):
            lanes = slice(tile * LANES, (tile + 1) * LANES)
            window[base + 1 + tile, :margin] = top_ref[plane, :, lanes]
            window[base + 1 + tile, margin : margin + height] = centre_ref[plane, :, lanes]
            window[base + 1 + tile, margin + height :] = bottom_ref[plane, :, lanes]
        window[base, :half] = left_ref[plane]
        window[base, half:] = pltpu.roll(left_ref[plane], margin, axis=1)
        window[base + tiles + 1, :half] = right_ref[plane]
        window[base + tiles + 1, half:] = pltpu.roll(right_ref[plane], margin, axis=1)
    grad[...] = jnp.zeros_like(grad)
    probe_sum_ref[...] = jnp.zeros_like(probe_sum_ref)

    lane = lax.broadcasted_iota(jnp.int32, (size, LANES), 1)
    count = count_ref[0]

    def place(slot):
        row = rows_ref[slot] + margin
        col = cols_ref[slot] + LANES
        tile = lax.shift_right_logical(col, 7)
        return row, tile, col & (LANES - 1)

    def one_pair(first):
        patches, waves = [], []
        for slot in (first, first + 1):
            row, tile, turn = place(slot)
            here = lane >= turn
            patch = [
                jnp.where(
                    here,
                    window[plane * columns + tile, pl.ds(row, size), :],
                    window[plane * columns + tile + 1, pl.ds(row, size), :],
                )
                for plane in range(2)
            ]
            probe = [pltpu.roll(probe_ref[plane], turn, axis=1) for plane in range(2)]
            wave = jnp.concatenate(
                [
                    probe[0] * patch[0] - probe[1] * patch[1],
                    probe[0] * patch[1] + probe[1] * patch[0],
                ],
                axis=1,
            )
            patches.append((patch, probe))
            waves.append(wave)
        rows = jnp.concatenate(waves, axis=0)
        middle = times_table(rows, table_ref[0], table_ref[1])
        beside = jnp.concatenate(
            [
                jnp.concatenate([middle[:size, :size], middle[size:, :size]], axis=1),
                jnp.concatenate([middle[:size, size:], middle[size:, size:]], axis=1),
            ],
            axis=0,
        )
        psi = table_times(table_ref[2], table_ref[3], beside)
        real, imag = psi[:size], psi[size:]
        weights = []
        for member, slot in enumerate((first, first + 1)):
            lanes = slice(member * size, (member + 1) * size)
            scale = jnp.where(slot < count, 2.0, 0.0).astype(jnp.float32)
            power = real[:, lanes] * real[:, lanes] + imag[:, lanes] * imag[:, lanes]
            weights.append((power - measured_ref[slot].astype(jnp.float32)) * scale)
        weight = jnp.concatenate(weights, axis=1)
        psi = jnp.concatenate([weight * real, weight * imag], axis=0)
        back = table_times(table_ref[0], table_ref[1], psi)
        rows = jnp.concatenate(
            [
                jnp.concatenate([back[:size, :size], back[size:, :size]], axis=1),
                jnp.concatenate([back[:size, size:], back[size:, size:]], axis=1),
            ],
            axis=0,
        )
        exits = times_table(rows, table_ref[2], table_ref[3])
        for member, slot in enumerate((first, first + 1)):
            patch, probe = patches[member]
            row, tile, turn = place(slot)
            here = lane >= turn
            exit_real = exits[member * size : (member + 1) * size, :size]
            exit_imag = exits[member * size : (member + 1) * size, size:]
            terms = (
                patch[0] * exit_real + patch[1] * exit_imag,
                patch[0] * exit_imag - patch[1] * exit_real,
            )
            adds = (
                probe[0] * exit_real + probe[1] * exit_imag,
                probe[0] * exit_imag - probe[1] * exit_real,
            )
            back_turn = (LANES - turn) & (LANES - 1)
            for plane in range(2):
                probe_sum_ref[plane] += pltpu.roll(terms[plane], back_turn, axis=1)
                at = plane * columns + tile
                grad[at, pl.ds(row, size), :] += jnp.where(here, adds[plane], 0.0)
                grad[at + 1, pl.ds(row, size), :] += jnp.where(here, 0.0, adds[plane])

    def step(index, carry):
        for member in range(0, GROUP, 2):
            one_pair(index * GROUP + member)
        return carry

    lax.fori_loop(0, (count + GROUP - 1) // GROUP, step, 0)

    for plane in range(2):
        base = plane * columns
        for tile in range(columns):
            lanes = slice(tile * LANES, (tile + 1) * LANES)
            grad_top_ref[plane, :, lanes] = grad[base + tile, :margin]
            grad_centre_ref[plane, :, lanes] = grad[base + tile, margin : margin + height]
            grad_bottom_ref[plane, :, lanes] = grad[base + tile, margin + height :]


def main_call(rows, cols, count, centre, top, bottom, left, right, probe, measured, tables):
    height, width = centre.shape[1:]
    size = probe.shape[1]
    margin = size // 2
    columns = width // LANES + 2
    wide = columns * LANES
    smem = pl.BlockSpec(memory_space=pltpu.SMEM)
    vmem = pl.BlockSpec(memory_space=pltpu.VMEM)
    f32 = jnp.float32
    return pl.pallas_call(
        main_kernel,
        out_shape=(
            jax.ShapeDtypeStruct((2, height, wide), f32),
            jax.ShapeDtypeStruct((2, margin, wide), f32),
            jax.ShapeDtypeStruct((2, margin, wide), f32),
            jax.ShapeDtypeStruct((2, size, size), f32),
        ),
        in_specs=[smem] * 3 + [vmem] * 8,
        out_specs=(vmem,) * 4,
        scratch_shapes=[
            pltpu.VMEM((2 * columns, height + size, LANES), f32),
            pltpu.VMEM((2 * columns, height + size, LANES), f32),
        ],
        compiler_params=pltpu.CompilerParams(vmem_limit_bytes=VMEM_BYTES),
        name="slots",
    )(rows, cols, count, centre, top, bottom, left, right, probe, measured, tables)


def shifted(value, axis, steps):
    count = lax.axis_size(axis)
    first, last = max(0, -steps), min(count, count - steps)
    return lax.ppermute(value, axis, [(source, source + steps) for source in range(first, last)])


def swapped(value, axis, bit):
    return lax.ppermute(value, axis, [(i, i ^ bit) for i in range(lax.axis_size(axis))])


def sum_over_all(value):
    n_row, n_col = lax.axis_size("trow"), lax.axis_size("tcol")
    odd = lax.axis_index("trow") % 2
    mine = lax.dynamic_index_in_dim(value, odd, 0, keepdims=False)
    other = lax.dynamic_index_in_dim(value, 1 - odd, 0, keepdims=False)
    mine = mine + swapped(other, "trow", 1)
    bit = 2
    while bit < n_row:
        mine = mine + swapped(mine, "trow", bit)
        bit *= 2
    bit = 1
    while bit < n_col:
        mine = mine + swapped(mine, "tcol", bit)
        bit *= 2
    other = swapped(mine, "trow", 1)
    return jnp.where(odd == 0, jnp.stack([mine, other]), jnp.stack([other, mine]))


def body(tables, object_planes, probe, intensities, row_offsets, col_offsets, counts):
    size = probe.shape[1]
    margin = size // 2
    height, width = object_planes.shape[1:]
    half = (height + size) // 2

    top = shifted(object_planes[:, height - margin :], "trow", 1)
    bottom = shifted(object_planes[:, :margin], "trow", -1)
    tall = jnp.concatenate([top, object_planes, bottom], axis=1)
    last, first = tall[:, :, width - margin :], tall[:, :, :margin]
    left = shifted(jnp.concatenate([last[:, half:], last[:, :half]], axis=2), "tcol", 1)
    right = shifted(jnp.concatenate([first[:, :half], first[:, half:]], axis=2), "tcol", -1)

    centre, upper, lower, probe_sum = main_call(
        row_offsets.reshape(-1), col_offsets.reshape(-1), counts,
        object_planes, top, bottom, left, right, probe,
        intensities.reshape(-1, size, size), tables,
    )
    probe_total = sum_over_all(probe_sum)
    devices = lax.axis_size("trow") * lax.axis_size("tcol")
    probe_grad = probe_total / jnp.sqrt(jnp.float32(intensities.shape[2] * devices))

    from_below = shifted(upper, "trow", -1)
    from_above = shifted(lower, "trow", 1)
    centre = centre.at[:, height - margin :].add(from_below)
    centre = centre.at[:, :margin].add(from_above)
    start = LANES
    from_right = shifted(centre[:, :, start - margin : start], "tcol", -1)
    from_left = shifted(centre[:, :, start + width : start + width + margin], "tcol", 1)
    result = centre[:, :, start : start + width]
    result = result.at[:, :, width - margin :].add(from_right)
    result = result.at[:, :, :margin].add(from_left)
    return (result, probe_grad)


def solution(mesh):
    tables = dft_tables(LANES)
    inner = jax.shard_map(
        body,
        mesh=mesh,
        in_specs=(
            P(),
            P(None, "trow", "tcol"),
            P(),
            P("trow", "tcol", None, None, None),
            P("trow", "tcol", None),
            P("trow", "tcol", None),
            P(("trow", "tcol")),
        ),
        out_specs=(P(None, "trow", "tcol"), P()),
        check_vma=False,
    )

    def run(*args):
        return inner(jnp.asarray(tables), *args)

    return run
```

time: 698 us -> 103 us (0.15)
  local copies, waits for them, and re-layouts: 218 us -> 12.2 us
  waiting for transfers between devices: 147 us -> 29 us
  loops' own time: 101 us -> 0 us
  matrix products: 95.6 us -> 0 us
  starting transfers between devices: 105 us -> 49.9 us
  between operations: 14.9 us -> 1.59 us
  other arithmetic: 11.9 us -> 1.95 us
  Pallas kernels: 0 us -> 8.31 us
    psum x1 -> x0, waiting for transfers between devices: 124 us -> none  [body(): probe_total = lax.psum(probe_sum, ('trow', 'tcol'))]
    gather x120 -> x0, local copies, waits for them, and re-layouts: 111 us -> none
    another operation x6 -> x0, loops' own time: 101 us -> none  [the longest x1 100 us: body(): grad_window, probe_sum = lax.fori_loop(0, group_total, one_group, start)]
    dot_general x80 -> x0, matrix products: 95.6 us -> none  [the longest x40 49.5 us: left_apply(): return jnp.einsum('jk,gkl->gjl', matrix, batch, precision=highest)]
    dynamic_update_slice x40 -> x0, local copies, waits for them, and re-layouts: 94.4 us -> none  [one_group(): lax.dynamic_update_slice(grad_window, current + contrib[member], (0, row_...]
    ppermute x8 -> x14, starting transfers between devices: 105 us -> 49.9 us  [the longest x6 32.9 us: swapped(): lax.ppermute(value, axis, [(i, i ^ bit) for i in range(lax.axis_size(axis...]
    pallas_call x0 -> x1, Pallas kernels: none -> 8.31 us  [main_call(): pl.pallas_call(main_kernel, out_shape=(jax.ShapeDtypeStruct((2, height, w...]
    unnamed x14 -> x28, local copies, waits for them, and re-layouts: 1.42 us -> 8.48 us
  transfers between devices with their start and end apart: 9 -> 14, of which waited for: 6 -> 9; matrix products, arithmetic and copies ran while one was open for 0% -> 4% of each run, Pallas kernels for 0% -> 0%
where the time goes in v1:
time: 103 us
  starting transfers between devices  49.9 us (48%)
  waiting for transfers between devices  29 us (28%)
  local copies, waits for them, and re-layouts  12.2 us (12%)
  Pallas kernels  8.31 us (8%)
  other arithmetic  1.95 us (2%)
  between operations  1.59 us (2%)
    ppermute x6, starting transfers between devices, swapped(): lax.ppermute(value, axis, [(i, i ^ bit) for i in range(lax.axis_size(axis...  32.9 us
    ppermute x8, starting transfers between devices, shifted(): lax.ppermute(value, axis, [(source, source + steps) for source in range(f...  16.9 us
    ppermute x8, waiting for transfers between devices, shifted(): lax.ppermute(value, axis, [(source, source + steps) for source in range(f...  16.7 us
    ppermute x6, waiting for transfers between devices, swapped(): lax.ppermute(value, axis, [(i, i ^ bit) for i in range(lax.axis_size(axis...  12.2 us
    unnamed x28, local copies, waits for them, and re-layouts  8.48 us
    pallas_call x1, Pallas kernels, main_call(): pl.pallas_call(main_kernel, out_shape=(jax.ShapeDtypeStruct((2, height, w...  8.31 us
  transfers between devices with their start and end apart: 14, of which 9 were waited for; matrix products, arithmetic and copies ran while one was open for 4% of the time, Pallas kernels for 0%

profile of v1, /device:TPU:0, one launch (start us, length us, event | category | flops | bytes accessed | tf_op | source)
XLA Modules:
  0.0 102.9 jit_solution(16480916311334255714)
XLA Ops:
  0.6 1.0 fusion.5
  1.6 2.4 %collective-permute-start = (f32[2,64,256]{2,1,0:T(8,128)S(1)}, f32[2,64,256]{2,1,0:T(8,128)S(1)}, u32[]{:S(2)}, u32[]{:S(2)}) collective-permute-start(f32[2,64,256]{2,1,0:T(8,128)S(1)} %get-tuple-element.67), channel_id=1, source_target_pairs={{0,8},{8,16},{16,24},{1,9},{9,17},{17,25},{2,10},{10,18},{18,26},{... | collective-permute-start | bytes 393224 | tf_op jit(solution)/shard_map/ppermute | solution.py:205
  4.0 1.3 %collective-permute-start.1 = (f32[2,64,256]{2,1,0:T(8,128)S(1)}, f32[2,64,256]{2,1,0:T(8,128)S(1)}, u32[]{:S(2)}, u32[]{:S(2)}) collective-permute-start(f32[2,64,256]{2,1,0:T(8,128)S(1)} %get-tuple-element.66), channel_id=1, source_target_pairs={{8,0},{16,8},{24,16},{9,1},{17,9},{25,17},{10,2},{18,10},{26,18},{... | collective-permute-start | bytes 393224 | tf_op jit(solution)/shard_map/ppermute | solution.py:205
  5.3 1.1 %constant_dynamic-update-slice_fusion.1 = (f32[2,320,256]{2,1,0:T(8,128)S(1)}, f32[2,320,256]{2,1,0:T(8,128)S(1)}) fusion(f32[2,256,256]{2,1,0:T(8,128)} %centre_ref.1, f32[2,320,256]{2,1,0:T(8,128)S(1)} %constant_dynamic-update-slice_fusion.3), kind=kLoop, calls=%fused_computation.12 | loop fusion | bytes 1572864
  6.4 0.0 copy-start
  6.5 2.9 %collective-permute-done.1.bottom_ref = f32[2,64,256]{2,1,0:T(8,128)S(1)} collective-permute-done((f32[2,64,256]{2,1,0:T(8,128)S(1)}, f32[2,64,256]{2,1,0:T(8,128)S(1)}, u32[]{:S(2)}, u32[]{:S(2)}) %collective-permute-start.1) | collective-permute-done | bytes 131104 | tf_op jit(solution)/shard_map/ppermute | solution.py:205
  9.4 0.1 fusion.4
  9.5 0.1 fusion.3
  9.6 0.1 pad_maximum_fusion
  9.7 3.4 %collective-permute-start.2 = (f32[2,192,128]{2,1,0:T(8,128)S(1)}, f32[2,192,128]{2,1,0:T(8,128)S(1)}, u32[]{:S(2)}, u32[]{:S(2)}) collective-permute-start(f32[2,192,128]{2,1,0:T(8,128)S(1)} %pad_maximum_fusion), channel_id=1, source_target_pairs={{0,1},{1,2},{2,3},{3,4},{4,5},{5,6},{6,7},{8,9},{9,10},{10,11},{11... | collective-permute-start | bytes 589832 | tf_op jit(solution)/shard_map/ppermute | solution.py:205
  13.2 0.8 pad_maximum_fusion.1
  14.0 1.3 %collective-permute-start.3 = (f32[2,192,128]{2,1,0:T(8,128)}, f32[2,192,128]{2,1,0:T(8,128)S(1)}, u32[]{:S(2)}, u32[]{:S(2)}) collective-permute-start(f32[2,192,128]{2,1,0:T(8,128)} %pad_maximum_fusion.1), channel_id=1, source_target_pairs={{1,0},{2,1},{3,2},{4,3},{5,4},{6,5},{7,6},{9,8},{10,9},{11,10},{12... | collective-permute-start | bytes 589832 | tf_op jit(solution)/shard_map/ppermute | solution.py:205
  15.9 0.4 collective-permute-done.2.left_ref
  16.3 0.7 copy-done.3
  17.0 4.7 %collective-permute-done.3.right_ref = f32[2,192,128]{2,1,0:T(8,128)S(1)} collective-permute-done((f32[2,192,128]{2,1,0:T(8,128)}, f32[2,192,128]{2,1,0:T(8,128)S(1)}, u32[]{:S(2)}, u32[]{:S(2)}) %collective-permute-start.3) | collective-permute-done | bytes 196640 | tf_op jit(solution)/shard_map/ppermute | solution.py:205
  21.7 0.7 copy-done.5
  22.4 0.0 copy-start.2
  22.4 1.0 %copy-done.2 = bf16[4,256,256]{2,1,0:T(8,128)(2,1)S(1)} copy-done((bf16[4,256,256]{2,1,0:T(8,128)(2,1)S(1)}, bf16[4,256,256]{2,1,0:T(8,128)(2,1)}, u32[]{:S(2)}) %copy-start.2) | copy-done | bytes 524312
  23.5 0.9 copy-done.4
  24.4 0.9 copy-done.6
  25.3 0.9 copy-done.7
  26.2 8.3 %slots.1 = (f32[2,256,512]{2,1,0:T(8,128)S(1)}, f32[2,64,512]{2,1,0:T(8,128)S(1)}, f32[2,64,512]{2,1,0:T(8,128)S(1)}, f32[2,128,128]{2,1,0:T(8,128)S(1)}) custom-call(s32[48]{0:T(128)S(1)} %bitcast.10, s32[48]{0:T(128)S(1)} %bitcast.11, s32[1]{0:T(128)S(6)} %copy.15.count_ref, f32[2,256,256]{2,1,0:T(8,128)S(1)} %copy-done, ...), custom_call_target="tpu_custom_call" | custom-call | tf_op jit(solution)/shard_map/slots/pallas_call | solution.py:183
  34.5 0.7 copy-done.10
  35.2 0.7 copy-done.11
  35.9 24.2 %collective-permute-start.8 = (f32[128,128]{1,0:T(8,128)S(1)}, f32[128,128]{1,0:T(8,128)S(1)}, u32[]{:S(2)}, u32[]{:S(2)}) collective-permute-start(f32[128,128]{1,0:T(8,128)S(1)} %dynamic-slice_bitcast_fusion), channel_id=1, source_target_pairs={{0,8},{8,0},{16,24},{24,16},{1,9},{9,1},{17,25},{25,17},{2,10},{10... | collective-permute-start | bytes 196616 | tf_op jit(solution)/shard_map/ppermute | solution.py:209
  60.1 1.3 %collective-permute-start.4 = (f32[2,64,512]{2,1,0:T(8,128)}, f32[2,64,512]{2,1,0:T(8,128)S(1)}, u32[]{:S(2)}, u32[]{:S(2)}) collective-permute-start(f32[2,64,512]{2,1,0:T(8,128)} %copy-done.11), channel_id=1, source_target_pairs={{8,0},{16,8},{24,16},{9,1},{17,9},{25,17},{10,2},{18,10},{26,18},{... | collective-permute-start | bytes 786440 | tf_op jit(solution)/shard_map/ppermute | solution.py:205
  61.4 2.3 %collective-permute-start.9 = (f32[128,128]{1,0:T(8,128)S(1)}, f32[128,128]{1,0:T(8,128)S(1)}, u32[]{:S(2)}, u32[]{:S(2)}) collective-permute-start(f32[128,128]{1,0:T(8,128)S(1)} %bitcast_add_fusion), channel_id=1, source_target_pairs={{0,16},{8,24},{16,0},{24,8},{1,17},{9,25},{17,1},{25,9},{2,18},{10... | collective-permute-start | bytes 196616 | tf_op jit(solution)/shard_map/ppermute | solution.py:209
  63.8 5.7 %collective-permute-done.9 = f32[128,128]{1,0:T(8,128)S(1)} collective-permute-done((f32[128,128]{1,0:T(8,128)S(1)}, f32[128,128]{1,0:T(8,128)S(1)}, u32[]{:S(2)}, u32[]{:S(2)}) %collective-permute-start.9) | collective-permute-done | bytes 65568 | tf_op jit(solution)/shard_map/ppermute | solution.py:209
  69.4 2.5 %collective-permute-start.10 = (f32[128,128]{1,0:T(8,128)S(1)}, f32[128,128]{1,0:T(8,128)S(1)}, u32[]{:S(2)}, u32[]{:S(2)}) collective-permute-start(f32[128,128]{1,0:T(8,128)S(1)} %add.63), channel_id=1, source_target_pairs={{0,1},{1,0},{2,3},{3,2},{4,5},{5,4},{6,7},{7,6},{8,9},{9,8},{10,11... | collective-permute-start | bytes 196616 | tf_op jit(solution)/shard_map/ppermute | solution.py:209
  72.0 2.2 %collective-permute-done.10 = f32[128,128]{1,0:T(8,128)S(1)} collective-permute-done((f32[128,128]{1,0:T(8,128)S(1)}, f32[128,128]{1,0:T(8,128)S(1)}, u32[]{:S(2)}, u32[]{:S(2)}) %collective-permute-start.10) | collective-permute-done | bytes 65568 | tf_op jit(solution)/shard_map/ppermute | solution.py:209
  74.2 2.1 %collective-permute-start.11 = (f32[128,128]{1,0:T(8,128)S(1)}, f32[128,128]{1,0:T(8,128)S(1)}, u32[]{:S(2)}, u32[]{:S(2)}) collective-permute-start(f32[128,128]{1,0:T(8,128)S(1)} %add.64), channel_id=1, source_target_pairs={{0,2},{1,3},{2,0},{3,1},{4,6},{5,7},{6,4},{7,5},{8,10},{9,11},{10,... | collective-permute-start | bytes 196616 | tf_op jit(solution)/shard_map/ppermute | solution.py:209
  76.4 1.3 %collective-permute-start.5 = (f32[2,64,512]{2,1,0:T(8,128)}, f32[2,64,512]{2,1,0:T(8,128)S(1)}, u32[]{:S(2)}, u32[]{:S(2)}) collective-permute-start(f32[2,64,512]{2,1,0:T(8,128)} %copy-done.10), channel_id=1, source_target_pairs={{0,8},{8,16},{16,24},{1,9},{9,17},{17,25},{2,10},{10,18},{18,26},{... | collective-permute-start | bytes 786440 | tf_op jit(solution)/shard_map/ppermute | solution.py:205
  77.7 0.9 collective-permute-done.11
  78.6 1.7 %collective-permute-start.12 = (f32[128,128]{1,0:T(8,128)S(1)}, f32[128,128]{1,0:T(8,128)S(1)}, u32[]{:S(2)}, u32[]{:S(2)}) collective-permute-start(f32[128,128]{1,0:T(8,128)S(1)} %add.65), channel_id=1, source_target_pairs={{0,4},{1,5},{2,6},{3,7},{4,0},{5,1},{6,2},{7,3},{8,12},{9,13},{10,... | collective-permute-start | bytes 196616 | tf_op jit(solution)/shard_map/ppermute | solution.py:209
  80.3 0.1 add_dynamic-update-slice_fusion
  80.4 0.1 fusion
  80.5 3.4 %collective-permute-done.12 = f32[128,128]{1,0:T(8,128)S(1)} collective-permute-done((f32[128,128]{1,0:T(8,128)S(1)}, f32[128,128]{1,0:T(8,128)S(1)}, u32[]{:S(2)}, u32[]{:S(2)}) %collective-permute-start.12) | collective-permute-done | bytes 65568 | tf_op jit(solution)/shard_map/ppermute | solution.py:209
  83.9 0.1 collective-permute-start.13
  83.9 0.1 fusion.2
  84.1 1.3 %collective-permute-start.6 = (f32[2,256,64]{2,1,0:T(8,128)S(1)}, f32[2,256,64]{2,1,0:T(8,128)S(1)}, u32[]{:S(2)}, u32[]{:S(2)}) collective-permute-start(f32[2,256,64]{2,1,0:T(8,128)S(1)} %get-tuple-element.59), channel_id=1, source_target_pairs={{1,0},{2,1},{3,2},{4,3},{5,4},{6,5},{7,6},{9,8},{10,9},{11,10},{12... | collective-permute-start | bytes 393224 | tf_op jit(solution)/shard_map/ppermute | solution.py:205
  85.4 4.7 %collective-permute-start.7 = (f32[2,256,64]{2,1,0:T(8,128)S(1)}, f32[2,256,64]{2,1,0:T(8,128)S(1)}, u32[]{:S(2)}, u32[]{:S(2)}) collective-permute-start(f32[2,256,64]{2,1,0:T(8,128)S(1)} %get-tuple-element.58), channel_id=1, source_target_pairs={{0,1},{1,2},{2,3},{3,4},{4,5},{5,6},{6,7},{8,9},{9,10},{10,11},{11... | collective-permute-start | bytes 393224 | tf_op jit(solution)/shard_map/ppermute | solution.py:205
  90.2 0.7 fusion.1
  90.8 4.3 %collective-permute-done.6 = f32[2,256,64]{2,1,0:T(8,128)S(1)} collective-permute-done((f32[2,256,64]{2,1,0:T(8,128)S(1)}, f32[2,256,64]{2,1,0:T(8,128)S(1)}, u32[]{:S(2)}, u32[]{:S(2)}) %collective-permute-start.6) | collective-permute-done | bytes 131104 | tf_op jit(solution)/shard_map/ppermute | solution.py:205
  95.1 0.1 slice_add_fusion.1
  95.3 1.2 %scatter-add.16 = f32[2,256,256]{2,1,0:T(8,128)S(1)} dynamic-update-slice(f32[2,256,256]{2,1,0:T(8,128)S(1)} %slice.152, f32[2,256,64]{2,1,0:T(8,128)S(1)} %slice_add_fusion.1, s32[]{:T(128)} %constant.131.clone.1, s32[]{:T(128)} %constant.131.clone.1, s32[]{:T(128)} %constant.132.clone.1) | dynamic-update-slice | bytes 262148 | tf_op jit(solution)/shard_map/scatter-add | solution.py:260
  96.5 4.5 %collective-permute-done.7 = f32[2,256,64]{2,1,0:T(8,128)S(1)} collective-permute-done((f32[2,256,64]{2,1,0:T(8,128)S(1)}, f32[2,256,64]{2,1,0:T(8,128)S(1)}, u32[]{:S(2)}, u32[]{:S(2)}) %collective-permute-start.7) | collective-permute-done | bytes 131104 | tf_op jit(solution)/shard_map/ppermute | solution.py:205
  100.9 1.1 %scatter-add.19 = f32[2,256,256]{2,1,0:T(8,128)S(1)} dynamic-update-slice(f32[2,256,256]{2,1,0:T(8,128)S(1)} %scatter-add.16, f32[2,256,64]{2,1,0:T(8,128)S(1)} %slice_add_fusion, s32[]{:T(128)} %constant.131.clone.1, s32[]{:T(128)} %constant.131.clone.1, s32[]{:T(128)} %constant.131.clone.1) | dynamic-update-slice | bytes 262148 | tf_op jit(solution)/shard_map/scatter-add | solution.py:261
  102.1 0.8 copy-done.12
  (30 shorter events, 0.2 us)
Async XLA Ops:
  1.6 3.7 %collective-permute-start = (f32[2,64,256]{2,1,0:T(8,128)S(1)}, f32[2,64,256]{2,1,0:T(8,128)S(1)}, u32[]{:S(2)}, u32[]{:S(2)}) collective-permute-start(f32[2,64,256]{2,1,0:T(8,128)S(1)} %get-tuple-element.67), channel_id=1, source_target_pairs={{0,8},{8,16},{16,24},{1,9},{9,17},{17,25},{2,10},{10,18},{18,26},{... | collective-permute-start | bytes 393224 | tf_op jit(solution)/shard_map/ppermute | solution.py:205
  4.0 5.4 %collective-permute-start.1 = (f32[2,64,256]{2,1,0:T(8,128)S(1)}, f32[2,64,256]{2,1,0:T(8,128)S(1)}, u32[]{:S(2)}, u32[]{:S(2)}) collective-permute-start(f32[2,64,256]{2,1,0:T(8,128)S(1)} %get-tuple-element.66), channel_id=1, source_target_pairs={{8,0},{16,8},{24,16},{9,1},{17,9},{25,17},{10,2},{18,10},{26,18},{... | collective-permute-start | bytes 393224 | tf_op jit(solution)/shard_map/ppermute | solution.py:205
  6.4 16.0 %copy-start = (f32[2,256,256]{2,1,0:T(8,128)S(1)}, f32[2,256,256]{2,1,0:T(8,128)}, u32[]{:S(2)}) copy-start(f32[2,256,256]{2,1,0:T(8,128)} %centre_ref.1) | copy-start | bytes 1572868
  6.5 16.0 %copy-start.1 = (bf16[1,1,48,128,128]{4,3,2,1,0:T(8,128)(2,1)S(1)}, bf16[1,1,48,128,128]{4,3,2,1,0:T(8,128)(2,1)}, u32[]{:S(2)}) copy-start(bf16[1,1,48,128,128]{4,3,2,1,0:T(8,128)(2,1)} %param.17) | copy-start | bytes 4718596
  6.5 15.9 %copy-start.8 = (s32[1,1,48]{2,1,0:T(1,128)S(1)}, s32[1,1,48]{2,1,0:T(1,128)}, u32[]{:S(2)}) copy-start(s32[1,1,48]{2,1,0:T(1,128)} %param.18) | copy-start | bytes 580
  6.5 15.9 %copy-start.9 = (s32[1,1,48]{2,1,0:T(1,128)S(1)}, s32[1,1,48]{2,1,0:T(1,128)}, u32[]{:S(2)}) copy-start(s32[1,1,48]{2,1,0:T(1,128)} %param.19) | copy-start | bytes 580
  9.7 6.6 %collective-permute-start.2 = (f32[2,192,128]{2,1,0:T(8,128)S(1)}, f32[2,192,128]{2,1,0:T(8,128)S(1)}, u32[]{:S(2)}, u32[]{:S(2)}) collective-permute-start(f32[2,192,128]{2,1,0:T(8,128)S(1)} %pad_maximum_fusion), channel_id=1, source_target_pairs={{0,1},{1,2},{2,3},{3,4},{4,5},{5,6},{6,7},{8,9},{9,10},{10,11},{11... | collective-permute-start | bytes 589832 | tf_op jit(solution)/shard_map/ppermute | solution.py:205
  14.0 7.8 %collective-permute-start.3 = (f32[2,192,128]{2,1,0:T(8,128)}, f32[2,192,128]{2,1,0:T(8,128)S(1)}, u32[]{:S(2)}, u32[]{:S(2)}) collective-permute-start(f32[2,192,128]{2,1,0:T(8,128)} %pad_maximum_fusion.1), channel_id=1, source_target_pairs={{1,0},{2,1},{3,2},{4,3},{5,4},{6,5},{7,6},{9,8},{10,9},{11,10},{12... | collective-permute-start | bytes 589832 | tf_op jit(solution)/shard_map/ppermute | solution.py:205
  16.3 0.7 copy-start.3
  21.7 0.7 copy-start.5
  22.4 1.0 %copy-start.2 = (bf16[4,256,256]{2,1,0:T(8,128)(2,1)S(1)}, bf16[4,256,256]{2,1,0:T(8,128)(2,1)}, u32[]{:S(2)}) copy-start(bf16[4,256,256]{2,1,0:T(8,128)(2,1)} %constant.138.clone.table_ref) | copy-start | bytes 1572868
  23.5 0.9 copy-start.4
  24.4 0.9 copy-start.6
  25.3 0.9 copy-start.7
  34.5 0.7 copy-start.10
  35.2 0.7 copy-start.11
  35.9 25.5 %collective-permute-start.8 = (f32[128,128]{1,0:T(8,128)S(1)}, f32[128,128]{1,0:T(8,128)S(1)}, u32[]{:S(2)}, u32[]{:S(2)}) collective-permute-start(f32[128,128]{1,0:T(8,128)S(1)} %dynamic-slice_bitcast_fusion), channel_id=1, source_target_pairs={{0,8},{8,0},{16,24},{24,16},{1,9},{9,1},{17,25},{25,17},{2,10},{10... | collective-permute-start | bytes 196616 | tf_op jit(solution)/shard_map/ppermute | solution.py:209
  60.1 20.2 %collective-permute-start.4 = (f32[2,64,512]{2,1,0:T(8,128)}, f32[2,64,512]{2,1,0:T(8,128)S(1)}, u32[]{:S(2)}, u32[]{:S(2)}) collective-permute-start(f32[2,64,512]{2,1,0:T(8,128)} %copy-done.11), channel_id=1, source_target_pairs={{8,0},{16,8},{24,16},{9,1},{17,9},{25,17},{10,2},{18,10},{26,18},{... | collective-permute-start | bytes 786440 | tf_op jit(solution)/shard_map/ppermute | solution.py:205
  61.4 8.0 %collective-permute-start.9 = (f32[128,128]{1,0:T(8,128)S(1)}, f32[128,128]{1,0:T(8,128)S(1)}, u32[]{:S(2)}, u32[]{:S(2)}) collective-permute-start(f32[128,128]{1,0:T(8,128)S(1)} %bitcast_add_fusion), channel_id=1, source_target_pairs={{0,16},{8,24},{16,0},{24,8},{1,17},{9,25},{17,1},{25,9},{2,18},{10... | collective-permute-start | bytes 196616 | tf_op jit(solution)/shard_map/ppermute | solution.py:209
  69.4 4.8 %collective-permute-start.10 = (f32[128,128]{1,0:T(8,128)S(1)}, f32[128,128]{1,0:T(8,128)S(1)}, u32[]{:S(2)}, u32[]{:S(2)}) collective-permute-start(f32[128,128]{1,0:T(8,128)S(1)} %add.63), channel_id=1, source_target_pairs={{0,1},{1,0},{2,3},{3,2},{4,5},{5,4},{6,7},{7,6},{8,9},{9,8},{10,11... | collective-permute-start | bytes 196616 | tf_op jit(solution)/shard_map/ppermute | solution.py:209
  74.2 4.4 %collective-permute-start.11 = (f32[128,128]{1,0:T(8,128)S(1)}, f32[128,128]{1,0:T(8,128)S(1)}, u32[]{:S(2)}, u32[]{:S(2)}) collective-permute-start(f32[128,128]{1,0:T(8,128)S(1)} %add.64), channel_id=1, source_target_pairs={{0,2},{1,3},{2,0},{3,1},{4,6},{5,7},{6,4},{7,5},{8,10},{9,11},{10,... | collective-permute-start | bytes 196616 | tf_op jit(solution)/shard_map/ppermute | solution.py:209
  76.4 4.0 %collective-permute-start.5 = (f32[2,64,512]{2,1,0:T(8,128)}, f32[2,64,512]{2,1,0:T(8,128)S(1)}, u32[]{:S(2)}, u32[]{:S(2)}) collective-permute-start(f32[2,64,512]{2,1,0:T(8,128)} %copy-done.10), channel_id=1, source_target_pairs={{0,8},{8,16},{16,24},{1,9},{9,17},{17,25},{2,10},{10,18},{18,26},{... | collective-permute-start | bytes 786440 | tf_op jit(solution)/shard_map/ppermute | solution.py:205
  78.6 5.2 %collective-permute-start.12 = (f32[128,128]{1,0:T(8,128)S(1)}, f32[128,128]{1,0:T(8,128)S(1)}, u32[]{:S(2)}, u32[]{:S(2)}) collective-permute-start(f32[128,128]{1,0:T(8,128)S(1)} %add.65), channel_id=1, source_target_pairs={{0,4},{1,5},{2,6},{3,7},{4,0},{5,1},{6,2},{7,3},{8,12},{9,13},{10,... | collective-permute-start | bytes 196616 | tf_op jit(solution)/shard_map/ppermute | solution.py:209
  83.9 6.3 %collective-permute-start.13 = (f32[128,128]{1,0:T(8,128)S(1)}, f32[128,128]{1,0:T(8,128)S(1)}, u32[]{:S(2)}, u32[]{:S(2)}) collective-permute-start(f32[128,128]{1,0:T(8,128)S(1)} %add.66), channel_id=1, source_target_pairs={{0,8},{8,0},{16,24},{24,16},{1,9},{9,1},{17,25},{25,17},{2,10},{10... | collective-permute-start | bytes 196616 | tf_op jit(solution)/shard_map/ppermute | solution.py:209
  84.1 11.0 %collective-permute-start.6 = (f32[2,256,64]{2,1,0:T(8,128)S(1)}, f32[2,256,64]{2,1,0:T(8,128)S(1)}, u32[]{:S(2)}, u32[]{:S(2)}) collective-permute-start(f32[2,256,64]{2,1,0:T(8,128)S(1)} %get-tuple-element.59), channel_id=1, source_target_pairs={{1,0},{2,1},{3,2},{4,3},{5,4},{6,5},{7,6},{9,8},{10,9},{11,10},{12... | collective-permute-start | bytes 393224 | tf_op jit(solution)/shard_map/ppermute | solution.py:205
  85.4 15.5 %collective-permute-start.7 = (f32[2,256,64]{2,1,0:T(8,128)S(1)}, f32[2,256,64]{2,1,0:T(8,128)S(1)}, u32[]{:S(2)}, u32[]{:S(2)}) collective-permute-start(f32[2,256,64]{2,1,0:T(8,128)S(1)} %get-tuple-element.58), channel_id=1, source_target_pairs={{0,1},{1,2},{2,3},{3,4},{4,5},{5,6},{6,7},{8,9},{9,10},{10,11},{11... | collective-permute-start | bytes 393224 | tf_op jit(solution)/shard_map/ppermute | solution.py:205
  102.1 0.8 copy-start.12

commit v2 on v1

v2 whole, which is shorter than its diff:
```python
import jax
import jax.numpy as jnp
import numpy as np
from jax import lax
from jax.experimental import pallas as pl
from jax.experimental.pallas import tpu as pltpu
from jax.sharding import PartitionSpec as P

LANES = 128
VMEM_BYTES = 56 * 1024 * 1024
GROUP = 8
F32 = jnp.float32
ANY = pl.BlockSpec(memory_space=pl.ANY)
VMEM = pl.BlockSpec(memory_space=pltpu.VMEM)
SMEM = pl.BlockSpec(memory_space=pltpu.SMEM)


def dft_tables(length):
    index = np.arange(length)
    angle = -2.0 * np.pi * (np.outer(index, index) % length) / length
    cosine, sine = np.cos(angle) / np.sqrt(length), np.sin(angle) / np.sqrt(length)
    right = np.block([[cosine, sine], [-sine, cosine]])
    tables = []
    for table in (right, right.T):
        high = table.astype(jnp.bfloat16)
        low = (table - high.astype(np.float64)).astype(jnp.bfloat16)
        tables += [high, low]
    return np.stack(tables)


def split(value):
    high = value.astype(jnp.bfloat16)
    low = (value - high.astype(F32)).astype(jnp.bfloat16)
    return high, low


def dot(a, b):
    return jnp.dot(a, b, preferred_element_type=F32)


def times_table(value, high, low):
    big, small = split(value)
    return dot(jnp.concatenate([big, small, big], axis=1), jnp.concatenate([high, high, low], axis=0))


def table_times(high, low, value):
    big, small = split(value)
    return dot(jnp.concatenate([high, high, low], axis=1), jnp.concatenate([big, small, big], axis=0))


def folded(tall, low_lanes):
    half = tall.shape[0] // 2
    lane = lax.broadcasted_iota(jnp.int32, (half, LANES), 1)
    here = (lane < LANES // 2) == low_lanes
    return jnp.where(here, tall[:half], pltpu.roll(tall[half:], LANES // 2, axis=1))


def side_kernel(centre_ref, near_ref, far_ref, near_out, far_out, tall, sem):
    height, width = centre_ref.shape[1:]
    margin = near_ref.shape[1]
    odd_row = lax.axis_index("trow") % 2
    odd_col = lax.axis_index("tcol") % 2
    copies = []
    for index in range(2):
        right = (odd_col == 0) if index == 0 else (odd_col == 1)
        lanes = pl.ds(pl.multiple_of(jnp.where(right, width - LANES, 0), LANES), LANES)
        near_at = pl.multiple_of(jnp.where(odd_row == 1, 0, margin + height), 8)
        far_at = pl.multiple_of(jnp.where(odd_row == 1, margin + height, 0), 8)
        for plane in range(2):
            copies += [
                (centre_ref.at[plane, :, lanes], tall.at[index, plane, pl.ds(margin, height)]),
                (near_ref.at[plane, :, lanes], tall.at[index, plane, pl.ds(near_at, margin)]),
                (far_ref.at[plane, :, lanes], tall.at[index, plane, pl.ds(far_at, margin)]),
            ]
    copies = [pltpu.make_async_copy(a, b, sem.at[i]) for i, (a, b) in enumerate(copies)]
    for copy in copies:
        copy.start()
    for copy in copies:
        copy.wait()
    for plane in range(2):
        near_out[plane] = folded(tall[0, plane], odd_col == 1)
        far_out[plane] = folded(tall[1, plane], odd_col == 0)


def side_call(centre, near, far):
    height = centre.shape[1] + 2 * near.shape[1]
    shape = jax.ShapeDtypeStruct((2, height // 2, LANES), F32)
    return pl.pallas_call(
        side_kernel,
        out_shape=(shape, shape),
        in_specs=[ANY] * 3,
        out_specs=(VMEM, VMEM),
        scratch_shapes=[pltpu.VMEM((2, 2, height, LANES), F32), pltpu.SemaphoreType.DMA((12,))],
        name="side_columns",
    )(centre, near, far)


def main_kernel(
    rows_ref, cols_ref, count_ref,
    centre_ref, near_row_ref, far_row_ref, near_col_ref, far_col_ref, probe_ref, measured_ref, table_ref,
    centre_out, near_row_out, far_row_out, side_out, mine_out, other_out,
    window, grad, sides, probe, measured, table, probe_sum, rows_out, side, centre_sem, edge_sem, small_sem, measured_sem, out_sem,
):
    size = probe.shape[1]
    margin = size // 2
    height, width = centre_ref.shape[1:]
    tiles = width // LANES
    columns = tiles + 2
    slots = measured_ref.shape[0]
    half = (height + size) // 2
    odd_row = lax.axis_index("trow") % 2
    odd_col = lax.axis_index("tcol") % 2
    near_at = pl.multiple_of(jnp.where(odd_row == 1, 0, margin + height), 8)
    far_at = pl.multiple_of(jnp.where(odd_row == 1, margin + height, 0), 8)
    count = count_ref[0]
    groups = (count + GROUP - 1) // GROUP

    small = [
        pltpu.make_async_copy(probe_ref, probe, small_sem.at[0]),
        pltpu.make_async_copy(table_ref, table, small_sem.at[1]),
        pltpu.make_async_copy(near_col_ref, sides.at[0], small_sem.at[2]),
        pltpu.make_async_copy(far_col_ref, sides.at[1], small_sem.at[3]),
    ]
    for plane in range(2):
        for tile in range(tiles):
            lanes = slice(tile * LANES, (tile + 1) * LANES)
            to = window.at[plane * columns + 1 + tile]
            index = plane * tiles + tile
            small += [
                pltpu.make_async_copy(centre_ref.at[plane, :, lanes], to.at[pl.ds(margin, height)], centre_sem.at[index]),
                pltpu.make_async_copy(near_row_ref.at[plane, :, lanes], to.at[pl.ds(near_at, margin)], edge_sem.at[2 * index]),
                pltpu.make_async_copy(far_row_ref.at[plane, :, lanes], to.at[pl.ds(far_at, margin)], edge_sem.at[2 * index + 1]),
            ]

    def measured_copy(group):
        some = pl.ds(group * GROUP, GROUP)
        return pltpu.make_async_copy(measured_ref.at[some], measured.at[some], measured_sem.at[group])

    for copy in small:
        copy.start()
    for group in range(slots // GROUP):
        @pl.when(group < groups)
        def _():
            measured_copy(group).start()
    grad[...] = jnp.zeros_like(grad)
    probe_sum[...] = jnp.zeros_like(probe_sum)
    for copy in small:
        copy.wait()
    near_tile = jnp.where(odd_col == 1, 0, tiles + 1)
    far_tile = jnp.where(odd_col == 1, tiles + 1, 0)
    for plane in range(2):
        for index, tile in enumerate((near_tile, far_tile)):
            window[plane * columns + tile, :half] = sides[index, plane]
            window[plane * columns + tile, half:] = pltpu.roll(sides[index, plane], margin, axis=1)

    lane = lax.broadcasted_iota(jnp.int32, (size, LANES), 1)

    def place(slot):
        row = rows_ref[slot] + margin
        col = cols_ref[slot] + LANES
        tile = lax.shift_right_logical(col, 7)
        return row, tile, col & (LANES - 1)

    def load(first):
        kept, waves = [], []
        for slot in (first, first + 1):
            row, tile, turn = place(slot)
            here = lane >= turn
            patch = [
                jnp.where(
                    here,
                    window[plane * columns + tile, pl.ds(row, size), :],
                    window[plane * columns + tile + 1, pl.ds(row, size), :],
                )
                for plane in range(2)
            ]
            turned = [pltpu.roll(probe[plane], turn, axis=1) for plane in range(2)]
            wave_real = turned[0] * patch[0] - turned[1] * patch[1]
            wave_imag = turned[0] * patch[1] + turned[1] * patch[0]
            kept.append((patch, turned))
            waves.append(jnp.concatenate([wave_real, wave_imag], axis=1))
        return kept, jnp.concatenate(waves, axis=0)

    def regroup(pair):
        return jnp.concatenate(
            [
                jnp.concatenate([pair[:size, :size], pair[size:, :size]], axis=1),
                jnp.concatenate([pair[:size, size:], pair[size:, size:]], axis=1),
            ],
            axis=0,
        )

    def weigh(first, psi):
        real, imag = psi[:size], psi[size:]
        weights = []
        for member, slot in enumerate((first, first + 1)):
            lanes = slice(member * size, (member + 1) * size)
            scale = jnp.where(slot < count, 2.0, 0.0).astype(F32)
            power = real[:, lanes] * real[:, lanes] + imag[:, lanes] * imag[:, lanes]
            weights.append((power - measured[slot].astype(F32)) * scale)
        weight = jnp.concatenate(weights, axis=1)
        return jnp.concatenate([weight * real, weight * imag], axis=0)

    def add_up(first, kept, exits):
        for member, slot in enumerate((first, first + 1)):
            patch, turned = kept[member]
            row, tile, turn = place(slot)
            here = lane >= turn
            exit_real = exits[member * size : (member + 1) * size, :size]
            exit_imag = exits[member * size : (member + 1) * size, size:]
            terms = (patch[0] * exit_real + patch[1] * exit_imag, patch[0] * exit_imag - patch[1] * exit_real)
            adds = (turned[0] * exit_real + turned[1] * exit_imag, turned[0] * exit_imag - turned[1] * exit_real)
            back = (LANES - turn) & (LANES - 1)
            for plane in range(2):
                probe_sum[plane] += pltpu.roll(terms[plane], back, axis=1)
                at = plane * columns + tile
                grad[at, pl.ds(row, size), :] += jnp.where(here, adds[plane], 0.0)
                grad[at + 1, pl.ds(row, size), :] += jnp.where(here, 0.0, adds[plane])

    def step(group, carry):
        measured_copy(group).wait()
        firsts = [group * GROUP + member for member in range(0, GROUP, 2)]
        loaded = [load(first) for first in firsts]
        pairs = [regroup(times_table(wave, table[0], table[1])) for _, wave in loaded]
        pairs = [weigh(first, table_times(table[2], table[3], pair)) for first, pair in zip(firsts, pairs)]
        pairs = [regroup(table_times(table[0], table[1], pair)) for pair in pairs]
        pairs = [times_table(pair, table[2], table[3]) for pair in pairs]
        for first, (kept, _), pair in zip(firsts, loaded, pairs):
            add_up(first, kept, pair)
        return carry

    lax.fori_loop(0, groups, step, 0)

    total = lax.axis_size("trow") * lax.axis_size("tcol") * slots
    probe_sum[...] *= 1.0 / np.sqrt(np.float32(total))
    narrow = lax.broadcasted_iota(jnp.int32, (height + size, LANES), 1) < margin
    for plane in range(2):
        side[plane] = jnp.where(narrow, grad[plane * columns + tiles + 1], grad[plane * columns])
    outs = [
        pltpu.make_async_copy(probe_sum.at[odd_row], mine_out, out_sem.at[0]),
        pltpu.make_async_copy(probe_sum.at[1 - odd_row], other_out, out_sem.at[1]),
        pltpu.make_async_copy(side.at[:, pl.ds(margin, height)], side_out, out_sem.at[2]),
    ]
    for plane in range(2):
        for tile in range(tiles):
            lanes = slice(tile * LANES, (tile + 1) * LANES)
            at = grad.at[plane * columns + 1 + tile]
            outs += [
                (at.at[pl.ds(near_at, margin)], near_row_out.at[plane, :, lanes]),
                (at.at[pl.ds(far_at, margin)], far_row_out.at[plane, :, lanes]),
                (at.at[pl.ds(margin, height)], centre_out.at[plane, :, lanes]),
            ]
        lanes = slice(width, width + LANES)
        outs += [
            (side.at[plane, pl.ds(near_at, margin)], near_row_out.at[plane, :, lanes]),
            (side.at[plane, pl.ds(far_at, margin)], far_row_out.at[plane, :, lanes]),
        ]
    outs = outs[:3] + [pltpu.make_async_copy(a, b, out_sem.at[3 + i]) for i, (a, b) in enumerate(outs[3:])]
    for copy in outs:
        copy.start()
    for copy in outs:
        copy.wait()


def main_call(rows, cols, count, centre, near_row, far_row, near_col, far_col, probe, measured, tables):
    height, width = centre.shape[1:]
    size = probe.shape[1]
    margin = size // 2
    tiles = width // LANES
    columns = tiles + 2
    slots = measured.shape[0]
    return pl.pallas_call(
        main_kernel,
        out_shape=(
            jax.ShapeDtypeStruct((2, height, width), F32),
            jax.ShapeDtypeStruct((2, margin, width + LANES), F32),
            jax.ShapeDtypeStruct((2, margin, width + LANES), F32),
            jax.ShapeDtypeStruct((2, height, LANES), F32),
            jax.ShapeDtypeStruct((size, size), F32),
            jax.ShapeDtypeStruct((size, size), F32),
        ),
        in_specs=[SMEM] * 3 + [ANY] * 8,
        out_specs=(ANY,) * 6,
        scratch_shapes=[
            pltpu.VMEM((2 * columns, height + size, LANES), F32),
            pltpu.VMEM((2 * columns, height + size, LANES), F32),
            pltpu.VMEM((2,) + near_col.shape, F32),
            pltpu.VMEM(probe.shape, F32),
            pltpu.VMEM(measured.shape, measured.dtype),
            pltpu.VMEM(tables.shape, tables.dtype),
            pltpu.VMEM(probe.shape, F32),
            pltpu.VMEM((2, margin, LANES), F32),
            pltpu.VMEM((2, height + size, LANES), F32),
            pltpu.SemaphoreType.DMA((2 * tiles,)),
            pltpu.SemaphoreType.DMA((4 * tiles,)),
            pltpu.SemaphoreType.DMA((4,)),
            pltpu.SemaphoreType.DMA((slots // GROUP,)),
            pltpu.SemaphoreType.DMA((3 + 2 * (3 * tiles + 2),)),
        ],
        compiler_params=pltpu.CompilerParams(vmem_limit_bytes=VMEM_BYTES),
        name="slots",
    )(rows, cols, count, centre, near_row, far_row, near_col, far_col, probe, measured, tables)


def side_sum_kernel(side_ref, near_ref, far_ref, near_out, far_out, side):
    margin = near_ref.shape[1]
    height = side_ref.shape[1]
    odd_row = lax.axis_index("trow") % 2
    odd_col = lax.axis_index("tcol") % 2
    near_at = pl.multiple_of(jnp.where(odd_row == 1, 0, height - margin), 8)
    far_at = pl.multiple_of(jnp.where(odd_row == 1, height - margin, 0), 8)
    wide = near_ref.shape[2]
    side[...] = side_ref[...]
    for plane in range(2):
        side[plane, pl.ds(near_at, margin), :] += near_ref[plane, :, wide - LANES :]
        side[plane, pl.ds(far_at, margin), :] += far_ref[plane, :, wide - LANES :]
    for plane in range(2):
        near_out[plane] = folded(side[plane], odd_col == 0)
        far_out[plane] = folded(side[plane], odd_col == 1)


def side_sum_call(side, near, far):
    shape = jax.ShapeDtypeStruct((2, side.shape[1] // 2, LANES), F32)
    return pl.pallas_call(
        side_sum_kernel,
        out_shape=(shape, shape),
        in_specs=[VMEM] * 3,
        out_specs=(VMEM, VMEM),
        scratch_shapes=[pltpu.VMEM(side.shape, F32)],
        name="side_sums",
    )(side, near, far)


def final_kernel(centre_ref, near_row_ref, far_row_ref, near_col_ref, far_col_ref, out_ref):
    height, width = centre_ref.shape[1:]
    margin = near_row_ref.shape[1]
    half = height // 2
    odd_row = lax.axis_index("trow") % 2
    odd_col = lax.axis_index("tcol") % 2
    near_at = pl.multiple_of(jnp.where(odd_row == 1, 0, height - margin), 8)
    far_at = pl.multiple_of(jnp.where(odd_row == 1, height - margin, 0), 8)
    narrow = lax.broadcasted_iota(jnp.int32, (half, LANES), 1) < LANES // 2
    out_ref[...] = centre_ref[...]
    for plane in range(2):
        near = jnp.where(odd_col == 1, near_col_ref[plane], far_col_ref[plane])
        far = jnp.where(odd_col == 1, far_col_ref[plane], near_col_ref[plane])
        for first, left, right in (
            (0, near, far),
            (half, pltpu.roll(near, LANES // 2, axis=1), pltpu.roll(far, LANES // 2, axis=1)),
        ):
            rows = slice(first, first + half)
            out_ref[plane, rows, :LANES] += jnp.where(narrow, left, 0.0)
            out_ref[plane, rows, width - LANES :] += jnp.where(narrow, 0.0, right)
        out_ref[plane, pl.ds(near_at, margin), :] += near_row_ref[plane, :, :width]
        out_ref[plane, pl.ds(far_at, margin), :] += far_row_ref[plane, :, :width]


def final_call(centre, near_row, far_row, near_col, far_col):
    return pl.pallas_call(
        final_kernel,
        out_shape=jax.ShapeDtypeStruct(centre.shape, F32),
        in_specs=[VMEM] * 5,
        out_specs=VMEM,
        name="final_sums",
    )(centre, near_row, far_row, near_col, far_col)


def near_swap(value, axis):
    return lax.ppermute(value, axis, [(i, i ^ 1) for i in range(lax.axis_size(axis))])


def far_swap(value, axis):
    pairs = [(i, i + 1) for i in range(1, lax.axis_size(axis) - 1, 2)]
    return lax.ppermute(value, axis, pairs + [(j, i) for i, j in pairs])


def sum_over_all(mine, other):
    n_row, n_col = lax.axis_size("trow"), lax.axis_size("tcol")
    steps = [(1 << k, 0) for k in range(1, n_row.bit_length() - 1)] + [(0, 1 << k) for k in range(n_col.bit_length() - 1)]
    mine = mine + near_swap(other, "trow")
    turned = list(steps)
    for k in range(0, len(steps) - 1, 2):
        turned[k], turned[k + 1] = steps[k + 1], steps[k]
    for even, odd in zip(steps, turned):
        pairs = []
        for r in range(n_row):
            for c in range(n_col):
                dr, dc = odd if r % 2 else even
                pairs.append((r * n_col + c, (r ^ dr) * n_col + (c ^ dc)))
        mine = mine + lax.ppermute(mine, ("trow", "tcol"), pairs)
    other = near_swap(mine, "trow")
    odd = lax.axis_index("trow") % 2
    return jnp.where(odd == 0, jnp.stack([mine, other]), jnp.stack([other, mine]))


def body(tables, object_planes, probe, intensities, row_offsets, col_offsets, counts):
    size = probe.shape[1]
    margin = size // 2
    height, width = object_planes.shape[1:]
    odd = lax.axis_index("trow") % 2
    last, first = object_planes[:, height - margin :], object_planes[:, :margin]
    near_row = near_swap(jnp.where(odd == 0, last, first), "trow")
    far_row = far_swap(jnp.where(odd == 0, first, last), "trow")
    near_side, far_side = side_call(object_planes, near_row, far_row)
    near_col = near_swap(near_side, "tcol")
    far_col = far_swap(far_side, "tcol")

    centre, near_row, far_row, side, mine, other = main_call(
        row_offsets.reshape(-1), col_offsets.reshape(-1), counts,
        object_planes, near_row, far_row, near_col, far_col, probe,
        intensities.reshape(-1, size, size), tables,
    )
    probe_grad = sum_over_all(mine, other)
    near_row = near_swap(near_row, "trow")
    far_row = far_swap(far_row, "trow")
    near_side, far_side = side_sum_call(side, near_row, far_row)
    near_col = near_swap(near_side, "tcol")
    far_col = far_swap(far_side, "tcol")
    return (final_call(centre, near_row, far_row, near_col, far_col), probe_grad)


def solution(mesh):
    tables = dft_tables(LANES)
    inner = jax.shard_map(
        body,
        mesh=mesh,
        in_specs=(
            P(),
            P(None, "trow", "tcol"),
            P(),
            P("trow", "tcol", None, None, None),
            P("trow", "tcol", None),
            P("trow", "tcol", None),
            P(("trow", "tcol")),
        ),
        out_specs=(P(None, "trow", "tcol"), P()),
        check_vma=False,
    )

    def run(*args):
        return inner(jnp.asarray(tables), *args)

    return run
```

time: 103 us -> 73 us (0.71)
  starting transfers between devices: 49.9 us -> 28.4 us
  Pallas kernels: 8.31 us -> 22.9 us
  waiting for transfers between devices: 29 us -> 14.9 us
  local copies, waits for them, and re-layouts: 12.2 us -> 2.85 us
    ppermute x14, starting transfers between devices: 49.9 us -> 28.4 us  [the longest x4 16.1 us: sum_over_all(): mine = mine + lax.ppermute(mine, ('trow', 'tcol'), pairs)]
    ppermute x14, waiting for transfers between devices: 29 us -> 14.9 us  [the longest x4 9.7 us: sum_over_all(): mine = mine + lax.ppermute(mine, ('trow', 'tcol'), pairs)]
    pallas_call x1, Pallas kernels: 8.31 us -> 16.6 us  [main_call(): pl.pallas_call(main_kernel, out_shape=(jax.ShapeDtypeStruct((2, height, w...]
    pallas_call x0 -> x3, Pallas kernels: none -> 6.37 us  [the longest x1 2.26 us: final_call(): pl.pallas_call(final_kernel, out_shape=jax.ShapeDtypeStruct(centre.shape,...]
    unnamed x28 -> x16, local copies, waits for them, and re-layouts: 8.48 us -> 2.85 us
    scatter-add x2 -> x0, local copies, waits for them, and re-layouts: 2.3 us -> none  [the longest x1 1.19 us: body(): result = result.at[:, :, width - margin:].add(from_right)]
    select_n x0 -> x2, other arithmetic: none -> 1.66 us  [the longest x1 1 us: body(): far_row = far_swap(jnp.where(odd == 0, first, last), 'trow')]
    slice x5 -> x0, local copies, waits for them, and re-layouts: 1.4 us -> none  [the longest x1 0.99 us: body(): bottom = shifted(object_planes[:, :margin], 'trow', -1)]
  transfers between devices with their start and end apart: 14 -> 14, of which waited for: 9 -> 6; matrix products, arithmetic and copies ran while one was open for 4% -> 1% of each run, Pallas kernels for 0% -> 6%
where the time goes in v2:
time: 73 us
  starting transfers between devices  28.4 us (39%)
  Pallas kernels  22.9 us (31%)
  waiting for transfers between devices  14.9 us (20%)
  local copies, waits for them, and re-layouts  2.85 us (4%)
  other arithmetic  2.55 us (3%)
  between operations  1.42 us (2%)
    pallas_call x1, Pallas kernels, main_call(): pl.pallas_call(main_kernel, out_shape=(jax.ShapeDtypeStruct((2, height, w...  16.6 us
    ppermute x4, starting transfers between devices, sum_over_all(): mine = mine + lax.ppermute(mine, ('trow', 'tcol'), pairs)  16.1 us
    ppermute x4, waiting for transfers between devices, sum_over_all(): mine = mine + lax.ppermute(mine, ('trow', 'tcol'), pairs)  9.7 us
    ppermute x6, starting transfers between devices, near_swap(): lax.ppermute(value, axis, [(i, i ^ 1) for i in range(lax.axis_size(axis))])  9.59 us
    ppermute x6, waiting for transfers between devices, near_swap(): lax.ppermute(value, axis, [(i, i ^ 1) for i in range(lax.axis_size(axis))])  5.15 us
    unnamed x16, local copies, waits for them, and re-layouts  2.85 us
    ppermute x4, starting transfers between devices, far_swap(): return lax.ppermute(value, axis, pairs + [(j, i) for i, j in pairs])  2.65 us
    pallas_call x1, Pallas kernels, final_call(): pl.pallas_call(final_kernel, out_shape=jax.ShapeDtypeStruct(centre.shape,...  2.26 us
  transfers between devices with their start and end apart: 14, of which 6 were waited for; matrix products, arithmetic and copies ran while one was open for 1% of the time, Pallas kernels for 6%

profile of v2, /device:TPU:0, one launch (start us, length us, event | category | flops | bytes accessed | tf_op | source)
XLA Modules:
  0.0 73.0 jit_solution(11004673609577090120)
XLA Ops:
  0.6 1.0 %slice_select_fusion = (f32[2,64,256]{2,1,0:T(8,128)S(1)}, f32[2,64,256]{2,1,0:T(8,128)S(1)}) fusion(f32[2,256,256]{2,1,0:T(8,128)} %centre_ref.3, pred[]{:T(512)S(6)} %eq.8), kind=kLoop, calls=%fused_computation.1 | loop fusion | flops 65536 | bytes 524289 | tf_op jit(solution)/shard_map/jit(_where)/select_n | solution.py:403
  1.6 0.7 collective-permute-start.1
  2.3 4.4 %collective-permute-start = (f32[2,64,256]{2,1,0:T(8,128)S(1)}, f32[2,64,256]{2,1,0:T(8,128)S(1)}, u32[]{:S(2)}, u32[]{:S(2)}) collective-permute-start(f32[2,64,256]{2,1,0:T(8,128)S(1)} %get-tuple-element.23), channel_id=1, source_target_pairs={{0,8},{8,0},{16,24},{24,16},{1,9},{9,1},{17,25},{25,17},{2,10},{10... | collective-permute-start | bytes 393224 | tf_op jit(solution)/shard_map/ppermute | solution.py:369
  6.7 0.0 collective-permute-done.1.far_ref.far_row_ref
  6.7 0.0 copy-start.2
  6.7 1.0 %collective-permute-done.near_ref.near_row_ref = f32[2,64,256]{2,1,0:T(8,128)S(1)} collective-permute-done((f32[2,64,256]{2,1,0:T(8,128)S(1)}, f32[2,64,256]{2,1,0:T(8,128)S(1)}, u32[]{:S(2)}, u32[]{:S(2)}) %collective-permute-start) | collective-permute-done | bytes 131104 | tf_op jit(solution)/shard_map/ppermute | solution.py:369
  7.7 0.0 copy-done.2
  7.7 0.0 copy-start.3
  7.7 0.7 copy-done.3
  8.4 2.2 %side_columns.1 = (f32[2,192,128]{2,1,0:T(8,128)}, f32[2,192,128]{2,1,0:T(8,128)}) custom-call(f32[2,256,256]{2,1,0:T(8,128)} %centre_ref.3, f32[2,64,256]{2,1,0:T(8,128)} %copy-done.3, f32[2,64,256]{2,1,0:T(8,128)} %copy-done.2), custom_call_target="tpu_custom_call" | custom-call | tf_op jit(solution)/shard_map/side_columns/pallas_call | solution.py:88
  10.5 1.6 %collective-permute-start.2 = (f32[2,192,128]{2,1,0:T(8,128)}, f32[2,192,128]{2,1,0:T(8,128)S(1)}, u32[]{:S(2)}, u32[]{:S(2)}) collective-permute-start(f32[2,192,128]{2,1,0:T(8,128)} %get-tuple-element.12), channel_id=1, source_target_pairs={{0,1},{1,0},{2,3},{3,2},{4,5},{5,4},{6,7},{7,6},{8,9},{9,8},{10,11... | collective-permute-start | bytes 589832 | tf_op jit(solution)/shard_map/ppermute | solution.py:369
  12.1 0.7 collective-permute-start.3
  13.4 3.9 %collective-permute-done.2.near_col_ref = f32[2,192,128]{2,1,0:T(8,128)S(1)} collective-permute-done((f32[2,192,128]{2,1,0:T(8,128)}, f32[2,192,128]{2,1,0:T(8,128)S(1)}, u32[]{:S(2)}, u32[]{:S(2)}) %collective-permute-start.2) | collective-permute-done | bytes 196640 | tf_op jit(solution)/shard_map/ppermute | solution.py:369
  17.3 0.0 copy-start.4
  17.3 0.0 collective-permute-done.3.far_col_ref
  17.3 0.7 copy-done.4
  18.0 0.1 copy-done.5
  18.1 16.6 %slots.1 = (f32[2,256,256]{2,1,0:T(8,128)}, f32[2,64,384]{2,1,0:T(8,128)}, f32[2,64,384]{2,1,0:T(8,128)}, f32[2,256,128]{2,1,0:T(8,128)}, f32[128,128]{1,0:T(8,128)}, /*index=5*/f32[128,128]{1,0:T(8,128)}) custom-call(s32[48]{0:T(128)} %bitcast.8, s32[48]{0:T(128)} %bitcast.9, s32[1]{0:T(128)S(6)} %copy.9.count_ref, f32[2,256,256]{2,1,0:T(8,128)} %centre_ref.3, ...), custom_call_target="tpu_custom_call" | custom-call | tf_op jit(solution)/shard_map/slots/pallas_call | solution.py:272
  34.6 0.1 collective-permute-start.8
  34.7 0.5 collective-permute-start.4
  35.2 0.7 collective-permute-start.5
  35.9 0.3 collective-permute-done.8
  36.2 0.9 %add.21 = f32[128,128]{1,0:T(8,128)S(1)} add(f32[128,128]{1,0:T(8,128)} %get-tuple-element.20, f32[128,128]{1,0:T(8,128)S(1)} %collective-permute-done.8) | non-fusion elementwise | flops 16384 | bytes 196608 | tf_op jit(solution)/shard_map/add | solution.py:380
  37.0 2.7 %collective-permute-start.9 = (f32[128,128]{1,0:T(8,128)S(1)}, f32[128,128]{1,0:T(8,128)S(1)}, u32[]{:S(2)}, u32[]{:S(2)}) collective-permute-start(f32[128,128]{1,0:T(8,128)S(1)} %add.21), channel_id=1, source_target_pairs={{0,16},{1,17},{2,18},{3,19},{4,20},{5,21},{6,22},{7,23},{8,9},{9,8... | collective-permute-start | bytes 196616 | tf_op jit(solution)/shard_map/ppermute | solution.py:390
  39.7 3.6 %collective-permute-done.9 = f32[128,128]{1,0:T(8,128)S(1)} collective-permute-done((f32[128,128]{1,0:T(8,128)S(1)}, f32[128,128]{1,0:T(8,128)S(1)}, u32[]{:S(2)}, u32[]{:S(2)}) %collective-permute-start.9) | collective-permute-done | bytes 65568 | tf_op jit(solution)/shard_map/ppermute | solution.py:390
  43.4 3.4 %collective-permute-start.10 = (f32[128,128]{1,0:T(8,128)S(1)}, f32[128,128]{1,0:T(8,128)S(1)}, u32[]{:S(2)}, u32[]{:S(2)}) collective-permute-start(f32[128,128]{1,0:T(8,128)S(1)} %add.22), channel_id=1, source_target_pairs={{0,1},{1,0},{2,3},{3,2},{4,5},{5,4},{6,7},{7,6},{8,24},{9,25},{10,... | collective-permute-start | bytes 196616 | tf_op jit(solution)/shard_map/ppermute | solution.py:390
  46.8 2.2 %collective-permute-done.10 = f32[128,128]{1,0:T(8,128)S(1)} collective-permute-done((f32[128,128]{1,0:T(8,128)S(1)}, f32[128,128]{1,0:T(8,128)S(1)}, u32[]{:S(2)}, u32[]{:S(2)}) %collective-permute-start.10) | collective-permute-done | bytes 65568 | tf_op jit(solution)/shard_map/ppermute | solution.py:390
  49.0 7.6 %collective-permute-start.11 = (f32[128,128]{1,0:T(8,128)S(1)}, f32[128,128]{1,0:T(8,128)S(1)}, u32[]{:S(2)}, u32[]{:S(2)}) collective-permute-start(f32[128,128]{1,0:T(8,128)S(1)} %add.23), channel_id=1, source_target_pairs={{0,2},{1,3},{2,0},{3,1},{4,6},{5,7},{6,4},{7,5},{8,12},{9,13},{10,... | collective-permute-start | bytes 196616 | tf_op jit(solution)/shard_map/ppermute | solution.py:390
  56.6 0.0 collective-permute-done.4.near_ref.near_row_ref
  56.6 0.0 collective-permute-done.5.far_ref.far_row_ref
  56.6 0.0 copy-start.1
  56.7 0.7 copy-done
  57.3 0.1 copy-done.1
  57.4 1.9 %side_sums.1 = (f32[2,128,128]{2,1,0:T(8,128)}, f32[2,128,128]{2,1,0:T(8,128)}) custom-call(f32[2,256,128]{2,1,0:T(8,128)} %get-tuple-element.17.side_ref, f32[2,64,384]{2,1,0:T(8,128)} %copy-done, f32[2,64,384]{2,1,0:T(8,128)} %copy-done.1), custom_call_target="tpu_custom_call" | custom-call | tf_op jit(solution)/shard_map/side_sums/pallas_call | solution.py:324
  59.3 2.0 %collective-permute-start.6 = (f32[2,128,128]{2,1,0:T(8,128)}, f32[2,128,128]{2,1,0:T(8,128)S(1)}, u32[]{:S(2)}, u32[]{:S(2)}) collective-permute-start(f32[2,128,128]{2,1,0:T(8,128)} %get-tuple-element.18), channel_id=1, source_target_pairs={{0,1},{1,0},{2,3},{3,2},{4,5},{5,4},{6,7},{7,6},{8,9},{9,8},{10,11... | collective-permute-start | bytes 393224 | tf_op jit(solution)/shard_map/ppermute | solution.py:369
  61.4 0.7 collective-permute-start.7
  62.0 0.0 collective-permute-done.11
  62.0 2.4 %collective-permute-start.12 = (f32[128,128]{1,0:T(8,128)S(1)}, f32[128,128]{1,0:T(8,128)S(1)}, u32[]{:S(2)}, u32[]{:S(2)}) collective-permute-start(f32[128,128]{1,0:T(8,128)S(1)} %add.24), channel_id=1, source_target_pairs={{0,4},{1,5},{2,6},{3,7},{4,0},{5,1},{6,2},{7,3},{8,10},{9,11},{10,... | collective-permute-start | bytes 196616 | tf_op jit(solution)/shard_map/ppermute | solution.py:390
  64.4 3.8 %collective-permute-done.12 = f32[128,128]{1,0:T(8,128)S(1)} collective-permute-done((f32[128,128]{1,0:T(8,128)S(1)}, f32[128,128]{1,0:T(8,128)S(1)}, u32[]{:S(2)}, u32[]{:S(2)}) %collective-permute-start.12) | collective-permute-done | bytes 65568 | tf_op jit(solution)/shard_map/ppermute | solution.py:390
  68.3 1.1 %collective-permute-start.13 = (f32[128,128]{1,0:T(8,128)S(1)}, f32[128,128]{1,0:T(8,128)S(1)}, u32[]{:S(2)}, u32[]{:S(2)}) collective-permute-start(f32[128,128]{1,0:T(8,128)S(1)} %add.25), channel_id=1, source_target_pairs={{0,8},{8,0},{16,24},{24,16},{1,9},{9,1},{17,25},{25,17},{2,10},{10... | collective-permute-start | bytes 196616 | tf_op jit(solution)/shard_map/ppermute | solution.py:369
  69.3 0.0 collective-permute-done.6.near_col_ref
  69.3 0.0 collective-permute-done.7.far_col_ref
  69.3 0.0 copy-start.7
  69.4 0.6 copy-done.6
  70.0 0.0 copy-done.7
  70.0 2.3 %final_sums.1 = f32[2,256,256]{2,1,0:T(8,128)} custom-call(f32[2,256,256]{2,1,0:T(8,128)} %get-tuple-element.14.centre_ref, f32[2,64,384]{2,1,0:T(8,128)} %copy-done, f32[2,64,384]{2,1,0:T(8,128)} %copy-done.1, f32[2,128,128]{2,1,0:T(8,128)} %copy-done.6, f32[2,128,128]{2,1,0:T(8,128)} %copy-done.7), custom_call_target="tpu_custom_call" | custom-call | tf_op jit(solution)/shard_map/final_sums/pallas_call | solution.py:359
  72.3 0.0 collective-permute-done.13
  72.3 0.7 maximum_select_fusion
  (7 shorter events, 0.0 us)
Async XLA Ops:
  1.6 5.1 %collective-permute-start.1 = (f32[2,64,256]{2,1,0:T(8,128)S(1)}, f32[2,64,256]{2,1,0:T(8,128)S(1)}, u32[]{:S(2)}, u32[]{:S(2)}) collective-permute-start(f32[2,64,256]{2,1,0:T(8,128)S(1)} %get-tuple-element.22), channel_id=1, source_target_pairs={{8,16},{16,8},{9,17},{17,9},{10,18},{18,10},{11,19},{19,11},{12,20... | collective-permute-start | bytes 393224 | tf_op jit(solution)/shard_map/ppermute | solution.py:374
  2.3 5.4 %collective-permute-start = (f32[2,64,256]{2,1,0:T(8,128)S(1)}, f32[2,64,256]{2,1,0:T(8,128)S(1)}, u32[]{:S(2)}, u32[]{:S(2)}) collective-permute-start(f32[2,64,256]{2,1,0:T(8,128)S(1)} %get-tuple-element.23), channel_id=1, source_target_pairs={{0,8},{8,0},{16,24},{24,16},{1,9},{9,1},{17,25},{25,17},{2,10},{10... | collective-permute-start | bytes 393224 | tf_op jit(solution)/shard_map/ppermute | solution.py:369
  6.7 1.0 %copy-start.2 = (f32[2,64,256]{2,1,0:T(8,128)}, f32[2,64,256]{2,1,0:T(8,128)S(1)}, u32[]{:S(2)}) copy-start(f32[2,64,256]{2,1,0:T(8,128)S(1)} %collective-permute-done.1.far_ref.far_row_ref) | copy-start | bytes 393220
  7.7 0.7 copy-start.3
  10.5 6.7 %collective-permute-start.2 = (f32[2,192,128]{2,1,0:T(8,128)}, f32[2,192,128]{2,1,0:T(8,128)S(1)}, u32[]{:S(2)}, u32[]{:S(2)}) collective-permute-start(f32[2,192,128]{2,1,0:T(8,128)} %get-tuple-element.12), channel_id=1, source_target_pairs={{0,1},{1,0},{2,3},{3,2},{4,5},{5,4},{6,7},{7,6},{8,9},{9,8},{10,11... | collective-permute-start | bytes 589832 | tf_op jit(solution)/shard_map/ppermute | solution.py:369
  12.1 5.2 %collective-permute-start.3 = (f32[2,192,128]{2,1,0:T(8,128)}, f32[2,192,128]{2,1,0:T(8,128)S(1)}, u32[]{:S(2)}, u32[]{:S(2)}) collective-permute-start(f32[2,192,128]{2,1,0:T(8,128)} %get-tuple-element.13), channel_id=1, source_target_pairs={{1,2},{3,4},{5,6},{2,1},{4,3},{6,5},{9,10},{11,12},{13,14},{10,9},... | collective-permute-start | bytes 589832 | tf_op jit(solution)/shard_map/ppermute | solution.py:374
  17.3 0.7 copy-start.4
  17.3 0.8 %copy-start.5 = (f32[2,192,128]{2,1,0:T(8,128)}, f32[2,192,128]{2,1,0:T(8,128)S(1)}, u32[]{:S(2)}) copy-start(f32[2,192,128]{2,1,0:T(8,128)S(1)} %collective-permute-done.3.far_col_ref) | copy-start | bytes 589828
  34.6 1.5 %collective-permute-start.8 = (f32[128,128]{1,0:T(8,128)}, f32[128,128]{1,0:T(8,128)S(1)}, u32[]{:S(2)}, u32[]{:S(2)}) collective-permute-start(f32[128,128]{1,0:T(8,128)} %get-tuple-element.21), channel_id=1, source_target_pairs={{0,8},{8,0},{16,24},{24,16},{1,9},{9,1},{17,25},{25,17},{2,10},{10... | collective-permute-start | bytes 196616 | tf_op jit(solution)/shard_map/ppermute | solution.py:369
  34.7 21.9 %collective-permute-start.4 = (f32[2,64,384]{2,1,0:T(8,128)}, f32[2,64,384]{2,1,0:T(8,128)S(1)}, u32[]{:S(2)}, u32[]{:S(2)}) collective-permute-start(f32[2,64,384]{2,1,0:T(8,128)} %get-tuple-element.15), channel_id=1, source_target_pairs={{0,8},{8,0},{16,24},{24,16},{1,9},{9,1},{17,25},{25,17},{2,10},{10... | collective-permute-start | bytes 589832 | tf_op jit(solution)/shard_map/ppermute | solution.py:369
  35.2 21.4 %collective-permute-start.5 = (f32[2,64,384]{2,1,0:T(8,128)}, f32[2,64,384]{2,1,0:T(8,128)S(1)}, u32[]{:S(2)}, u32[]{:S(2)}) collective-permute-start(f32[2,64,384]{2,1,0:T(8,128)} %get-tuple-element.16), channel_id=1, source_target_pairs={{8,16},{16,8},{9,17},{17,9},{10,18},{18,10},{11,19},{19,11},{12,20... | collective-permute-start | bytes 589832 | tf_op jit(solution)/shard_map/ppermute | solution.py:374
  37.0 6.3 %collective-permute-start.9 = (f32[128,128]{1,0:T(8,128)S(1)}, f32[128,128]{1,0:T(8,128)S(1)}, u32[]{:S(2)}, u32[]{:S(2)}) collective-permute-start(f32[128,128]{1,0:T(8,128)S(1)} %add.21), channel_id=1, source_target_pairs={{0,16},{1,17},{2,18},{3,19},{4,20},{5,21},{6,22},{7,23},{8,9},{9,8... | collective-permute-start | bytes 196616 | tf_op jit(solution)/shard_map/ppermute | solution.py:390
  43.4 5.6 %collective-permute-start.10 = (f32[128,128]{1,0:T(8,128)S(1)}, f32[128,128]{1,0:T(8,128)S(1)}, u32[]{:S(2)}, u32[]{:S(2)}) collective-permute-start(f32[128,128]{1,0:T(8,128)S(1)} %add.22), channel_id=1, source_target_pairs={{0,1},{1,0},{2,3},{3,2},{4,5},{5,4},{6,7},{7,6},{8,24},{9,25},{10,... | collective-permute-start | bytes 196616 | tf_op jit(solution)/shard_map/ppermute | solution.py:390
  49.0 13.0 %collective-permute-start.11 = (f32[128,128]{1,0:T(8,128)S(1)}, f32[128,128]{1,0:T(8,128)S(1)}, u32[]{:S(2)}, u32[]{:S(2)}) collective-permute-start(f32[128,128]{1,0:T(8,128)S(1)} %add.23), channel_id=1, source_target_pairs={{0,2},{1,3},{2,0},{3,1},{4,6},{5,7},{6,4},{7,5},{8,12},{9,13},{10,... | collective-permute-start | bytes 196616 | tf_op jit(solution)/shard_map/ppermute | solution.py:390
  56.6 0.7 copy-start
  56.6 0.8 %copy-start.1 = (f32[2,64,384]{2,1,0:T(8,128)}, f32[2,64,384]{2,1,0:T(8,128)S(1)}, u32[]{:S(2)}) copy-start(f32[2,64,384]{2,1,0:T(8,128)S(1)} %collective-permute-done.5.far_ref.far_row_ref) | copy-start | bytes 589828
  59.3 10.0 %collective-permute-start.6 = (f32[2,128,128]{2,1,0:T(8,128)}, f32[2,128,128]{2,1,0:T(8,128)S(1)}, u32[]{:S(2)}, u32[]{:S(2)}) collective-permute-start(f32[2,128,128]{2,1,0:T(8,128)} %get-tuple-element.18), channel_id=1, source_target_pairs={{0,1},{1,0},{2,3},{3,2},{4,5},{5,4},{6,7},{7,6},{8,9},{9,8},{10,11... | collective-permute-start | bytes 393224 | tf_op jit(solution)/shard_map/ppermute | solution.py:369
  61.4 8.0 %collective-permute-start.7 = (f32[2,128,128]{2,1,0:T(8,128)}, f32[2,128,128]{2,1,0:T(8,128)S(1)}, u32[]{:S(2)}, u32[]{:S(2)}) collective-permute-start(f32[2,128,128]{2,1,0:T(8,128)} %get-tuple-element.19), channel_id=1, source_target_pairs={{1,2},{3,4},{5,6},{2,1},{4,3},{6,5},{9,10},{11,12},{13,14},{10,9},... | collective-permute-start | bytes 393224 | tf_op jit(solution)/shard_map/ppermute | solution.py:374
  62.0 6.2 %collective-permute-start.12 = (f32[128,128]{1,0:T(8,128)S(1)}, f32[128,128]{1,0:T(8,128)S(1)}, u32[]{:S(2)}, u32[]{:S(2)}) collective-permute-start(f32[128,128]{1,0:T(8,128)S(1)} %add.24), channel_id=1, source_target_pairs={{0,4},{1,5},{2,6},{3,7},{4,0},{5,1},{6,2},{7,3},{8,10},{9,11},{10,... | collective-permute-start | bytes 196616 | tf_op jit(solution)/shard_map/ppermute | solution.py:390
  68.3 4.0 %collective-permute-start.13 = (f32[128,128]{1,0:T(8,128)S(1)}, f32[128,128]{1,0:T(8,128)S(1)}, u32[]{:S(2)}, u32[]{:S(2)}) collective-permute-start(f32[128,128]{1,0:T(8,128)S(1)} %add.25), channel_id=1, source_target_pairs={{0,8},{8,0},{16,24},{24,16},{1,9},{9,1},{17,25},{25,17},{2,10},{10... | collective-permute-start | bytes 196616 | tf_op jit(solution)/shard_map/ppermute | solution.py:369
  69.3 0.7 copy-start.6
  69.3 0.7 copy-start.7

commit v3 on v2

v3 whole, which is shorter than its diff:
```python
import jax
import jax.numpy as jnp
import numpy as np
from jax import lax
from jax.experimental import pallas as pl
from jax.experimental.pallas import tpu as pltpu
from jax.sharding import PartitionSpec as P

LANES = 128
VMEM_BYTES = 24 * 1024 * 1024
GROUP = 8
F32 = jnp.float32
HBM = pl.BlockSpec(memory_space=pltpu.HBM)
VMEM = pl.BlockSpec(memory_space=pltpu.VMEM)
SMEM = pl.BlockSpec(memory_space=pltpu.SMEM)
PARAMS = pltpu.CompilerParams(vmem_limit_bytes=VMEM_BYTES)


def in_hbm(*arrays):
    return [pltpu.with_memory_space_constraint(array, pltpu.HBM) for array in arrays]


def in_vmem(*arrays):
    return [pltpu.with_memory_space_constraint(array, pltpu.VMEM) for array in arrays]


def near(shape, dtype=F32):
    return pltpu.VMEM(tuple(shape), dtype)


def dft_tables(length):
    index = np.arange(length)
    angle = -2.0 * np.pi * (np.outer(index, index) % length) / length
    cosine, sine = np.cos(angle) / np.sqrt(length), np.sin(angle) / np.sqrt(length)
    right = np.block([[cosine, sine], [-sine, cosine]])
    return np.stack([right, right.T]).astype(np.float32)


def split(value):
    high = value.astype(jnp.bfloat16)
    low = (value - high.astype(F32)).astype(jnp.bfloat16)
    return high, low


def dot(a, b):
    return jnp.dot(a, b, preferred_element_type=F32)


def times_table(value, high, low):
    big, small = split(value)
    return dot(jnp.concatenate([big, small, big], axis=1), jnp.concatenate([high, high, low], axis=0))


def table_times(high, low, value):
    big, small = split(value)
    return dot(jnp.concatenate([high, high, low], axis=1), jnp.concatenate([big, small, big], axis=0))


def folded(tall, low_lanes):
    half = tall.shape[0] // 2
    lane = lax.broadcasted_iota(jnp.int32, (half, LANES), 1)
    here = (lane < LANES // 2) == low_lanes
    return jnp.where(here, tall[:half], pltpu.roll(tall[half:], LANES // 2, axis=1))


def parities():
    return lax.axis_index("trow") % 2, lax.axis_index("tcol") % 2


def place_of(odd, low, high):
    near = pl.multiple_of(jnp.where(odd == 1, low, high), 8)
    far = pl.multiple_of(jnp.where(odd == 1, high, low), 8)
    return near, far


def edge_kernel(centre_ref, window, near_out, far_out, sem):
    height, width = centre_ref.shape[1:]
    margin = near_out.shape[1]
    columns = window.shape[0] // 2
    odd_row, _ = parities()
    near, far = place_of(odd_row, 0, height - margin)
    copies = [
        (centre_ref.at[:, pl.ds(near, margin)], near_out),
        (centre_ref.at[:, pl.ds(far, margin)], far_out),
    ]
    for plane in range(2):
        for tile in range(width // LANES):
            lanes = slice(tile * LANES, (tile + 1) * LANES)
            copies.append((centre_ref.at[plane, :, lanes], window.at[plane * columns + 1 + tile, pl.ds(margin, height)]))
    copies = [pltpu.make_async_copy(a, b, sem.at[i]) for i, (a, b) in enumerate(copies)]
    for copy in copies:
        copy.start()
    for copy in copies:
        copy.wait()


def edge_call(centre, margin):
    height, width = centre.shape[1:]
    tiles = width // LANES
    edge = near((2, margin, width))
    return pl.pallas_call(
        edge_kernel,
        out_shape=(near((2 * (tiles + 2), height + 2 * margin, LANES)), edge, edge),
        in_specs=[HBM],
        out_specs=(VMEM,) * 3,
        scratch_shapes=[pltpu.SemaphoreType.DMA((2 + 2 * tiles,))],
        compiler_params=PARAMS,
        name="edge_rows",
    )(*in_hbm(centre))


def ready_kernel(probe_ref, measured_ref, table_ref, probe, measured, tables, table, sem):
    copies = [(table_ref, table), (probe_ref, probe), (measured_ref, measured)]
    copies = [pltpu.make_async_copy(a, b, sem.at[i]) for i, (a, b) in enumerate(copies)]
    for copy in copies:
        copy.start()
    copies[0].wait()
    for index in range(2):
        tables[2 * index], tables[2 * index + 1] = split(table[index])
    copies[1].wait()
    copies[2].wait()


def ready_call(probe, measured, table):
    return pl.pallas_call(
        ready_kernel,
        out_shape=(
            near(probe.shape),
            near(measured.shape, measured.dtype),
            near((4,) + table.shape[1:], jnp.bfloat16),
        ),
        in_specs=[HBM] * 3,
        out_specs=(VMEM,) * 3,
        scratch_shapes=[pltpu.VMEM(table.shape, F32), pltpu.SemaphoreType.DMA((3,))],
        compiler_params=PARAMS,
        name="ready",
    )(*in_hbm(probe, measured, table))


def side_kernel(tile_ref, near_ref, far_ref, window, near_out, far_out):
    margin = near_ref.shape[1]
    columns = window.shape[0] // 2
    odd_row, odd_col = parities()
    bottom = window.shape[1] - margin
    near, far = place_of(odd_row, 0, bottom)
    for plane in range(2):
        for tile in range(columns - 2):
            lanes = slice(tile * LANES, (tile + 1) * LANES)
            window[plane * columns + 1 + tile, margin:bottom] = tile_ref[plane * columns + 1 + tile, margin:bottom]
            window[plane * columns + 1 + tile, pl.ds(near, margin), :] = near_ref[plane, :, lanes]
            window[plane * columns + 1 + tile, pl.ds(far, margin), :] = far_ref[plane, :, lanes]
    for plane in range(2):
        near_tile = plane * columns + jnp.where(odd_col == 1, 1, columns - 2)
        far_tile = plane * columns + jnp.where(odd_col == 1, columns - 2, 1)
        near_out[plane] = folded(window[near_tile], odd_col == 1)
        far_out[plane] = folded(window[far_tile], odd_col == 0)


def side_call(window, near_row, far_row):
    shape = near((2, window.shape[1] // 2, LANES))
    return pl.pallas_call(
        side_kernel,
        out_shape=(near(window.shape), shape, shape),
        in_specs=[VMEM] * 3,
        out_specs=(VMEM,) * 3,
        compiler_params=PARAMS,
        name="side_columns",
    )(*in_vmem(window, near_row, far_row))


def sort_slots(cols_ref, count, inner_width, order):
    def visit(slot, inner):
        col = cols_ref[slot]
        is_inner = jnp.logical_and(col >= 0, col <= inner_width)
        order[jnp.where(is_inner, inner, order.shape[0] - 1 - (slot - inner))] = slot
        return inner + is_inner.astype(jnp.int32)

    return lax.fori_loop(0, count, visit, jnp.int32(0))


def run_slots(first_group, last_group, inner, count, order, rows_ref, cols_ref, window, probe, measured, table, grad, probe_sum):
    size = probe.shape[1]
    margin = size // 2
    columns = window.shape[0] // 2
    lane = lax.broadcasted_iota(jnp.int32, (size, LANES), 1)

    def find(index):
        at = jnp.where(index < inner, index, jnp.maximum(order.shape[0] - 1 - (index - inner), 0))
        live = index < count
        slot = jnp.where(live, order[at], 0)
        row = rows_ref[slot] + margin
        col = cols_ref[slot] + LANES
        scale = jnp.where(live, 2.0, 0.0).astype(F32)
        return slot, row, lax.shift_right_logical(col, 7), col & (LANES - 1), scale

    def load(pair):
        kept, waves = [], []
        for _, row, tile, turn, _ in pair:
            here = lane >= turn
            patch = [
                jnp.where(
                    here,
                    window[plane * columns + tile, pl.ds(row, size), :],
                    window[plane * columns + tile + 1, pl.ds(row, size), :],
                )
                for plane in range(2)
            ]
            turned = [pltpu.roll(probe[plane], turn, axis=1) for plane in range(2)]
            wave_real = turned[0] * patch[0] - turned[1] * patch[1]
            wave_imag = turned[0] * patch[1] + turned[1] * patch[0]
            kept.append((patch, turned))
            waves.append(jnp.concatenate([wave_real, wave_imag], axis=1))
        return kept, jnp.concatenate(waves, axis=0)

    def regroup(pair):
        return jnp.concatenate(
            [
                jnp.concatenate([pair[:size, :size], pair[size:, :size]], axis=1),
                jnp.concatenate([pair[:size, size:], pair[size:, size:]], axis=1),
            ],
            axis=0,
        )

    def weigh(pair, psi):
        real, imag = psi[:size], psi[size:]
        weights = []
        for member, (slot, _, _, _, scale) in enumerate(pair):
            lanes = slice(member * size, (member + 1) * size)
            power = real[:, lanes] * real[:, lanes] + imag[:, lanes] * imag[:, lanes]
            weights.append((power - measured[slot].astype(F32)) * scale)
        weight = jnp.concatenate(weights, axis=1)
        return jnp.concatenate([weight * real, weight * imag], axis=0)

    def add_up(pair, kept, exits):
        for member, (_, row, tile, turn, _) in enumerate(pair):
            patch, turned = kept[member]
            here = lane >= turn
            exit_real = exits[member * size : (member + 1) * size, :size]
            exit_imag = exits[member * size : (member + 1) * size, size:]
            terms = (patch[0] * exit_real + patch[1] * exit_imag, patch[0] * exit_imag - patch[1] * exit_real)
            adds = (turned[0] * exit_real + turned[1] * exit_imag, turned[0] * exit_imag - turned[1] * exit_real)
            back = (LANES - turn) & (LANES - 1)
            for plane in range(2):
                probe_sum[plane] += pltpu.roll(terms[plane], back, axis=1)
                at = plane * columns + tile
                grad[at, pl.ds(row, size), :] += jnp.where(here, adds[plane], 0.0)
                grad[at + 1, pl.ds(row, size), :] += jnp.where(here, 0.0, adds[plane])

    def step(group, carry):
        slots = [find(group * GROUP + member) for member in range(GROUP)]
        pairs = [slots[member : member + 2] for member in range(0, GROUP, 2)]
        loaded = [load(pair) for pair in pairs]
        waves = [regroup(times_table(wave, table[0], table[1])) for _, wave in loaded]
        waves = [weigh(pair, table_times(table[2], table[3], wave)) for pair, wave in zip(pairs, waves)]
        waves = [regroup(table_times(table[0], table[1], wave)) for wave in waves]
        waves = [times_table(wave, table[2], table[3]) for wave in waves]
        for pair, (kept, _), wave in zip(pairs, loaded, waves):
            add_up(pair, kept, wave)
        return carry

    lax.fori_loop(first_group, last_group, step, 0)


def inner_kernel(rows_ref, cols_ref, count_ref, window, probe, measured, table, grad, probe_sum, order):
    count = count_ref[0]
    grad[...] = jnp.zeros_like(grad)
    probe_sum[...] = jnp.zeros_like(probe_sum)
    inner_width = (window.shape[0] // 2 - 2) * LANES - probe.shape[1]
    inner = sort_slots(cols_ref, count, inner_width, order)
    run_slots(0, inner // GROUP, inner, count, order, rows_ref, cols_ref, window, probe, measured, table, grad, probe_sum)


def inner_call(rows, cols, count, window, probe, measured, tables):
    return pl.pallas_call(
        inner_kernel,
        out_shape=(near(window.shape), near(probe.shape)),
        in_specs=[SMEM] * 3 + [VMEM] * 4,
        out_specs=(VMEM,) * 2,
        scratch_shapes=[pltpu.SMEM((measured.shape[0],), jnp.int32)],
        compiler_params=PARAMS,
        cost_estimate=pl.CostEstimate(flops=10**10, bytes_accessed=2 * 10**7, transcendentals=0),
        name="slots_inside",
    )(rows, cols, count, *in_vmem(window, probe, measured, tables))


def outer_kernel(
    rows_ref, cols_ref, count_ref, window_ref, near_col_ref, far_col_ref, probe, measured, table, grad_ref, probe_ref,
    grad, near_row_out, far_row_out, side_out, mine_out, other_out, window, probe_sum, order,
):
    size = probe.shape[1]
    margin = size // 2
    columns = window.shape[0] // 2
    tall = window.shape[1]
    half = tall // 2
    odd_row, odd_col = parities()
    near, far = place_of(odd_row, 0, tall - margin)
    count = count_ref[0]
    inner_width = (columns - 2) * LANES - size
    inner = sort_slots(cols_ref, count, inner_width, order)
    probe_sum[...] = probe_ref[...]
    grad[...] = grad_ref[...]
    for plane in range(2):
        own = slice(plane * columns + 1, (plane + 1) * columns - 1)
        window[own] = window_ref[own]
        near_tile = plane * columns + jnp.where(odd_col == 1, 0, columns - 1)
        far_tile = plane * columns + jnp.where(odd_col == 1, columns - 1, 0)
        for tile, ref in ((near_tile, near_col_ref), (far_tile, far_col_ref)):
            window[tile, :half] = ref[plane]
            window[tile, half:] = pltpu.roll(ref[plane], margin, axis=1)
    groups = (count + GROUP - 1) // GROUP
    run_slots(
        inner // GROUP, groups, inner, count, order, rows_ref, cols_ref, window, probe, measured, table, grad, probe_sum
    )
    total = lax.axis_size("trow") * lax.axis_size("tcol") * measured.shape[0]
    factor = 1.0 / np.sqrt(np.float32(total))
    mine_out[...] = probe_sum[odd_row] * factor
    other_out[...] = probe_sum[1 - odd_row] * factor
    narrow = lax.broadcasted_iota(jnp.int32, (margin, LANES), 1) < margin
    for plane in range(2):
        base = plane * columns
        left, right = base, base + columns - 1
        for at, out in ((near, near_row_out), (far, far_row_out)):
            rows = pl.ds(at, margin)
            for tile in range(columns - 2):
                out[plane, :, tile * LANES : (tile + 1) * LANES] = grad[base + 1 + tile, rows, :]
            out[plane, :, (columns - 2) * LANES :] = jnp.where(narrow, grad[right, rows, :], grad[left, rows, :])
        for row in range(margin, tall - margin, margin):
            rows = slice(row, row + margin)
            side_out[plane, row - margin : row] = jnp.where(narrow, grad[right, rows, :], grad[left, rows, :])


def outer_call(rows, cols, count, window, near_col, far_col, probe, measured, tables, grad, probe_sum):
    size = probe.shape[1]
    margin = size // 2
    columns = window.shape[0] // 2
    height = window.shape[1] - size
    row = near((2, margin, (columns - 1) * LANES))
    part = near((size, size))
    return pl.pallas_call(
        outer_kernel,
        out_shape=(near(grad.shape), row, row, near((2, height, LANES)), part, part),
        in_specs=[SMEM] * 3 + [VMEM] * 8,
        out_specs=(VMEM,) * 6,
        scratch_shapes=[
            pltpu.VMEM(window.shape, F32),
            pltpu.VMEM(probe.shape, F32),
            pltpu.SMEM((measured.shape[0],), jnp.int32),
        ],
        compiler_params=PARAMS,
        name="slots_across",
    )(rows, cols, count, *in_vmem(window, near_col, far_col, probe, measured, tables, grad, probe_sum))


def side_sum_kernel(side_ref, near_ref, far_ref, near_out, far_out, side):
    margin = near_ref.shape[1]
    height = side_ref.shape[1]
    odd_row, odd_col = parities()
    near_at, far_at = place_of(odd_row, 0, height - margin)
    wide = near_ref.shape[2]
    side[...] = side_ref[...]
    for plane in range(2):
        side[plane, pl.ds(near_at, margin), :] += near_ref[plane, :, wide - LANES :]
        side[plane, pl.ds(far_at, margin), :] += far_ref[plane, :, wide - LANES :]
    for plane in range(2):
        near_out[plane] = folded(side[plane], odd_col == 0)
        far_out[plane] = folded(side[plane], odd_col == 1)


def side_sum_call(side, near_row, far_row):
    shape = near((2, side.shape[1] // 2, LANES))
    return pl.pallas_call(
        side_sum_kernel,
        out_shape=(shape, shape),
        in_specs=[VMEM] * 3,
        out_specs=(VMEM, VMEM),
        scratch_shapes=[pltpu.VMEM(side.shape, F32)],
        compiler_params=PARAMS,
        name="side_sums",
    )(*in_vmem(side, near_row, far_row))


def final_kernel(grad, near_row_ref, far_row_ref, near_col_ref, far_col_ref, out_ref):
    height, width = out_ref.shape[1:]
    columns = grad.shape[0] // 2
    margin = near_row_ref.shape[1]
    half = height // 2
    odd_row, odd_col = parities()
    near_at, far_at = place_of(odd_row, 0, height - margin)
    narrow = lax.broadcasted_iota(jnp.int32, (half, LANES), 1) < LANES // 2
    for plane in range(2):
        for tile in range(columns - 2):
            lanes = slice(tile * LANES, (tile + 1) * LANES)
            out_ref[plane, :, lanes] = grad[plane * columns + 1 + tile, margin : margin + height]
        near = jnp.where(odd_col == 1, near_col_ref[plane], far_col_ref[plane])
        far = jnp.where(odd_col == 1, far_col_ref[plane], near_col_ref[plane])
        for first, left, right in (
            (0, near, far),
            (half, pltpu.roll(near, LANES // 2, axis=1), pltpu.roll(far, LANES // 2, axis=1)),
        ):
            rows = slice(first, first + half)
            out_ref[plane, rows, :LANES] += jnp.where(narrow, left, 0.0)
            out_ref[plane, rows, width - LANES :] += jnp.where(narrow, 0.0, right)
        out_ref[plane, pl.ds(near_at, margin), :] += near_row_ref[plane, :, :width]
        out_ref[plane, pl.ds(far_at, margin), :] += far_row_ref[plane, :, :width]


def final_call(grad, near_row, far_row, near_col, far_col):
    margin = near_row.shape[1]
    shape = (2, grad.shape[1] - 2 * margin, near_row.shape[2] - LANES)
    return pl.pallas_call(
        final_kernel,
        out_shape=jax.ShapeDtypeStruct(shape, F32),
        in_specs=[VMEM] * 5,
        out_specs=VMEM,
        compiler_params=PARAMS,
        name="final_sums",
    )(*in_vmem(grad, near_row, far_row, near_col, far_col))


def near_swap(value, axis):
    return lax.ppermute(value, axis, [(i, i ^ 1) for i in range(lax.axis_size(axis))])


def far_swap(value, axis):
    pairs = [(i, i + 1) for i in range(1, lax.axis_size(axis) - 1, 2)]
    return lax.ppermute(value, axis, pairs + [(j, i) for i, j in pairs])


def doubling_steps(n_row, n_col):
    steps = [(0, 1)] + [(1 << k, 0) for k in range(1, n_row.bit_length() - 1)]
    rest = [(0, 1 << k) for k in range(1, n_col.bit_length() - 1)]
    turned = list(rest)
    for k in range(0, len(rest) - 1, 2):
        turned[k], turned[k + 1] = rest[k + 1], rest[k]
    return list(zip(steps, steps)) + list(zip(rest, turned))


def add_partner(mine, even, odd):
    n_row, n_col = lax.axis_size("trow"), lax.axis_size("tcol")
    pairs = []
    for r in range(n_row):
        for c in range(n_col):
            dr, dc = odd if r % 2 else even
            pairs.append((r * n_col + c, (r ^ dr) * n_col + (c ^ dc)))
    return mine + lax.ppermute(mine, ("trow", "tcol"), pairs)


def body(table, object_planes, probe, intensities, row_offsets, col_offsets, counts):
    size = probe.shape[1]
    rows, cols = row_offsets.reshape(-1), col_offsets.reshape(-1)
    window, near_row, far_row = edge_call(object_planes, size // 2)
    near_row = near_swap(near_row, "trow")
    far_row = far_swap(far_row, "trow")
    probe, measured, tables = ready_call(probe, intensities.reshape(-1, size, size), table)
    window, near_side, far_side = side_call(window, near_row, far_row)
    near_col = near_swap(near_side, "tcol")
    far_col = far_swap(far_side, "tcol")
    grad, probe_sum = inner_call(rows, cols, counts, window, probe, measured, tables)
    grad, near_row, far_row, side, mine, other = outer_call(
        rows, cols, counts, window, near_col, far_col, probe, measured, tables, grad, probe_sum
    )

    steps = doubling_steps(lax.axis_size("trow"), lax.axis_size("tcol"))
    mine = mine + near_swap(other, "trow")
    mine, near_row, far_row = lax.optimization_barrier((mine, near_row, far_row))
    near_row = near_swap(near_row, "trow")
    far_row = far_swap(far_row, "trow")
    mine = add_partner(mine, *steps[0])
    near_side, far_side = side_sum_call(side, near_row, far_row)
    mine, near_side, far_side = lax.optimization_barrier((mine, near_side, far_side))
    near_col = near_swap(near_side, "tcol")
    far_col = far_swap(far_side, "tcol")
    for even, odd in steps[1:]:
        mine = add_partner(mine, even, odd)
    object_grad = final_call(grad, near_row, far_row, near_col, far_col)
    mine, object_grad = lax.optimization_barrier((mine, object_grad))
    other = near_swap(mine, "trow")
    odd_row, _ = parities()
    probe_grad = jnp.where(odd_row == 0, jnp.stack([mine, other]), jnp.stack([other, mine]))
    return (object_grad, probe_grad)


def solution(mesh):
    table = dft_tables(LANES)
    inner = jax.shard_map(
        body,
        mesh=mesh,
        in_specs=(
            P(),
            P(None, "trow", "tcol"),
            P(),
            P("trow", "tcol", None, None, None),
            P("trow", "tcol", None),
            P("trow", "tcol", None),
            P(("trow", "tcol")),
        ),
        out_specs=(P(None, "trow", "tcol"), P()),
        check_vma=False,
    )

    def run(*args):
        return inner(jnp.asarray(table), *args)

    return run
```

time: 73 us -> 59.9 us (0.82)
  waiting for transfers between devices: 14.9 us -> 11.2 us
  Pallas kernels: 22.9 us -> 19.2 us
  local copies, waits for them, and re-layouts: 2.85 us -> 0.01 us
  other arithmetic: 2.55 us -> 0.71 us
  starting transfers between devices: 28.4 us -> 27.1 us
    ppermute x6, waiting for transfers between devices: 5.15 us -> 2.14 us  [near_swap(): lax.ppermute(value, axis, [(i, i ^ 1) for i in range(lax.axis_size(axis))])]
    unnamed x16 -> x4, local copies, waits for them, and re-layouts: 2.85 us -> 0.01 us
    pallas_call x3 -> x6, Pallas kernels: 21 us -> 19 us  [the longest x1 8.82 us: outer_call(): pl.pallas_call(outer_kernel, out_shape=(near(grad.shape), row, row, near(...]
    pallas_call x1, Pallas kernels: 1.93 us -> 0.15 us  [side_sum_call(): pl.pallas_call(side_sum_kernel, out_shape=(shape, shape), in_specs=[VMEM]...]
    select_n x2 -> x1, other arithmetic: 1.66 us -> 0.67 us  [body(): jnp.where(odd_row == 0, jnp.stack([mine, other]), jnp.stack([other, mine]))]
    add x5, other arithmetic: 0.89 us -> 0.05 us  [the longest x4 0.04 us: add_partner(): return mine + lax.ppermute(mine, ('trow', 'tcol'), pairs)]
  transfers between devices with their start and end apart: 14 -> 14, of which waited for: 6 -> 5; matrix products, arithmetic and copies ran while one was open for 1% -> 0% of each run, Pallas kernels for 6% -> 15%
where the time goes in v3:
time: 59.9 us; the launch traced here: 59.7 us
  starting transfers between devices  27.1 us (45%)
  Pallas kernels  19.2 us (32%)
  waiting for transfers between devices  11.2 us (19%)
  between operations  1.49 us (2%)
  other arithmetic  0.71 us (1%)
    ppermute x4, starting transfers between devices, add_partner(): return mine + lax.ppermute(mine, ('trow', 'tcol'), pairs)  15.4 us
    ppermute x4, waiting for transfers between devices, add_partner(): return mine + lax.ppermute(mine, ('trow', 'tcol'), pairs)  9.08 us
    ppermute x6, starting transfers between devices, near_swap(): lax.ppermute(value, axis, [(i, i ^ 1) for i in range(lax.axis_size(axis))])  9.02 us
    pallas_call x1, Pallas kernels, outer_call(): pl.pallas_call(outer_kernel, out_shape=(near(grad.shape), row, row, near(...  8.82 us
    pallas_call x1, Pallas kernels, inner_call(): pl.pallas_call(inner_kernel, out_shape=(near(window.shape), near(probe.sh...  6.09 us
    ppermute x4, starting transfers between devices, far_swap(): return lax.ppermute(value, axis, pairs + [(j, i) for i, j in pairs])  2.64 us
    ppermute x6, waiting for transfers between devices, near_swap(): lax.ppermute(value, axis, [(i, i ^ 1) for i in range(lax.axis_size(axis))])  2.14 us
    pallas_call x1, Pallas kernels, ready_call(): pl.pallas_call(ready_kernel, out_shape=(near(probe.shape), near(measured....  1.65 us
  transfers between devices with their start and end apart: 14, of which 5 were waited for; matrix products, arithmetic and copies ran while one was open for 0% of the time, Pallas kernels for 15%

profile of v3, /device:TPU:0, one launch (start us, length us, event | category | flops | bytes accessed | tf_op | source)
XLA Modules:
  0.0 59.7 jit_solution(9279657833060955125)
XLA Ops:
  0.6 1.3 %edge_rows.1 = (f32[8,384,128]{2,1,0:T(8,128)S(1)}, f32[2,64,256]{2,1,0:T(8,128)S(1)}, f32[2,64,256]{2,1,0:T(8,128)S(1)}) custom-call(f32[2,256,256]{2,1,0:T(8,128)} %centre_ref.1), custom_call_target="tpu_custom_call" | custom-call | tf_op jit(solution)/shard_map/edge_rows/pallas_call | solution.py:101
  1.9 0.5 collective-permute-start
  2.4 0.7 %collective-permute-start.1 = (f32[2,64,256]{2,1,0:T(8,128)S(1)}, f32[2,64,256]{2,1,0:T(8,128)S(1)}, u32[]{:S(2)}, u32[]{:S(2)}) collective-permute-start(f32[2,64,256]{2,1,0:T(8,128)S(1)} %get-tuple-element.31), channel_id=1, source_target_pairs={{8,16},{16,8},{9,17},{17,9},{10,18},{18,10},{11,19},{19,11},{12,20... | collective-permute-start | bytes 393224 | tf_op jit(solution)/shard_map/ppermute | solution.py:426
  3.7 0.0 copy-start
  3.8 0.0 copy-start.1
  3.8 1.7 %ready.1 = (f32[2,128,128]{2,1,0:T(8,128)S(1)}, bf16[48,128,128]{2,1,0:T(8,128)(2,1)S(1)}, bf16[4,256,256]{2,1,0:T(8,128)(2,1)S(1)}) custom-call(f32[2,128,128]{2,1,0:T(8,128)} %probe_ref.1, bf16[48,128,128]{2,1,0:T(8,128)(2,1)} %bitcast.9, f32[2,256,256]{2,1,0:T(8,128)} %constant.21.clone.table_ref), custom_call_target="tpu_custom_call" | custom-call | tf_op jit(solution)/shard_map/ready/pallas_call | solution.py:125
  5.4 0.0 collective-permute-done.near_ref
  5.4 0.0 collective-permute-done.1.far_ref
  5.4 0.2 side_columns.1
  5.7 2.6 %collective-permute-start.2 = (f32[2,192,128]{2,1,0:T(8,128)S(1)}, f32[2,192,128]{2,1,0:T(8,128)S(1)}, u32[]{:S(2)}, u32[]{:S(2)}) collective-permute-start(f32[2,192,128]{2,1,0:T(8,128)S(1)} %get-tuple-element.33), channel_id=1, source_target_pairs={{0,1},{1,0},{2,3},{3,2},{4,5},{5,4},{6,7},{7,6},{8,9},{9,8},{10,11... | collective-permute-start | bytes 589832 | tf_op jit(solution)/shard_map/ppermute | solution.py:421
  8.3 0.7 %collective-permute-start.3 = (f32[2,192,128]{2,1,0:T(8,128)S(1)}, f32[2,192,128]{2,1,0:T(8,128)S(1)}, u32[]{:S(2)}, u32[]{:S(2)}) collective-permute-start(f32[2,192,128]{2,1,0:T(8,128)S(1)} %get-tuple-element.34), channel_id=1, source_target_pairs={{1,2},{3,4},{5,6},{2,1},{4,3},{6,5},{9,10},{11,12},{13,14},{10,9},... | collective-permute-start | bytes 589832 | tf_op jit(solution)/shard_map/ppermute | solution.py:426
  8.9 0.0 copy-done
  8.9 0.0 copy-done.1
  8.9 6.1 %slots_inside.1 = (f32[8,384,128]{2,1,0:T(8,128)S(1)}, f32[2,128,128]{2,1,0:T(8,128)S(1)}) custom-call(s32[48]{0:T(128)S(1)} %bitcast.5, s32[48]{0:T(128)S(1)} %bitcast.7, s32[1]{0:T(128)S(6)} %copy.9.count_ref, f32[8,384,128]{2,1,0:T(8,128)S(1)} %get-tuple-element.32.window.window_ref, f32[2,128,128]{2,1,0:T(8,128)S(1)} %get-tuple-element.35.probe, ...), custom_call_target="tpu_custom_call" | custom-call | flops 10000000000 | bytes 20000000 | tf_op jit(solution)/shard_map/slots_inside/pallas_call | solution.py:274
  15.0 0.0 collective-permute-done.2.near_col_ref
  15.1 0.0 collective-permute-done.3.far_col_ref
  15.1 8.8 %slots_across.1 = (f32[8,384,128]{2,1,0:T(8,128)S(1)}, f32[2,64,384]{2,1,0:T(8,128)S(1)}, f32[2,64,384]{2,1,0:T(8,128)S(1)}, f32[2,256,128]{2,1,0:T(8,128)S(1)},...) custom-call(s32[48]{0:T(128)S(1)} %bitcast.6, s32[48]{0:T(128)S(1)} %bitcast.8, s32[1]{0:T(128)S(6)} %copy.9.count_ref, ...), custom_call_target="tpu_custom_call" | custom-call | tf_op jit(solution)/shard_map/slots_across/pallas_call | solution.py:339
  23.9 3.4 %collective-permute-start.4 = (f32[128,128]{1,0:T(8,128)S(1)}, f32[128,128]{1,0:T(8,128)S(1)}, u32[]{:S(2)}, u32[]{:S(2)}) collective-permute-start(f32[128,128]{1,0:T(8,128)S(1)} %get-tuple-element.41), channel_id=1, source_target_pairs={{0,8},{8,0},{16,24},{24,16},{1,9},{9,1},{17,25},{25,17},{2,10},{10... | collective-permute-start | bytes 196616 | tf_op jit(solution)/shard_map/ppermute | solution.py:421
  27.3 0.9 %collective-permute-done.4 = f32[128,128]{1,0:T(8,128)S(1)} collective-permute-done((f32[128,128]{1,0:T(8,128)S(1)}, f32[128,128]{1,0:T(8,128)S(1)}, u32[]{:S(2)}, u32[]{:S(2)}) %collective-permute-start.4) | collective-permute-done | bytes 65568 | tf_op jit(solution)/shard_map/ppermute | solution.py:421
  28.2 0.4 collective-permute-start.6
  28.6 0.7 %collective-permute-start.7 = (f32[2,64,384]{2,1,0:T(8,128)S(1)}, f32[2,64,384]{2,1,0:T(8,128)S(1)}, u32[]{:S(2)}, u32[]{:S(2)}) collective-permute-start(f32[2,64,384]{2,1,0:T(8,128)S(1)} %get-tuple-element.47), channel_id=1, source_target_pairs={{8,16},{16,8},{9,17},{17,9},{10,18},{18,10},{11,19},{19,11},{12,20... | collective-permute-start | bytes 589832 | tf_op jit(solution)/shard_map/ppermute | solution.py:426
  29.3 7.2 %collective-permute-start.5 = (f32[128,128]{1,0:T(8,128)S(1)}, f32[128,128]{1,0:T(8,128)S(1)}, u32[]{:S(2)}, u32[]{:S(2)}) collective-permute-start(f32[128,128]{1,0:T(8,128)S(1)} %add.19), channel_id=1, source_target_pairs={{0,1},{1,0},{2,3},{3,2},{4,5},{5,4},{6,7},{7,6},{8,9},{9,8},{10,11... | collective-permute-start | bytes 196616 | tf_op jit(solution)/shard_map/ppermute | solution.py:445
  36.5 2.2 %collective-permute-done.5 = f32[128,128]{1,0:T(8,128)S(1)} collective-permute-done((f32[128,128]{1,0:T(8,128)S(1)}, f32[128,128]{1,0:T(8,128)S(1)}, u32[]{:S(2)}, u32[]{:S(2)}) %collective-permute-start.5) | collective-permute-done | bytes 65568 | tf_op jit(solution)/shard_map/ppermute | solution.py:445
  38.8 0.0 collective-permute-done.6.near_ref.near_row_ref
  38.8 0.0 collective-permute-done.7.far_ref.far_row_ref
  38.8 0.1 side_sums.1
  39.0 3.1 %collective-permute-start.8 = (f32[128,128]{1,0:T(8,128)S(1)}, f32[128,128]{1,0:T(8,128)S(1)}, u32[]{:S(2)}, u32[]{:S(2)}) collective-permute-start(f32[128,128]{1,0:T(8,128)S(1)} %add.20), channel_id=1, source_target_pairs={{0,16},{1,17},{2,18},{3,19},{4,20},{5,21},{6,22},{7,23},{8,24},{9,... | collective-permute-start | bytes 196616 | tf_op jit(solution)/shard_map/ppermute | solution.py:445
  42.0 2.0 %collective-permute-start.11 = (f32[2,128,128]{2,1,0:T(8,128)S(1)}, f32[2,128,128]{2,1,0:T(8,128)S(1)}, u32[]{:S(2)}, u32[]{:S(2)}) collective-permute-start(f32[2,128,128]{2,1,0:T(8,128)S(1)} %get-tuple-element.52), channel_id=1, source_target_pairs={{0,1},{1,0},{2,3},{3,2},{4,5},{5,4},{6,7},{7,6},{8,9},{9,8},{10,11... | collective-permute-start | bytes 393224 | tf_op jit(solution)/shard_map/ppermute | solution.py:421
  44.1 0.7 %collective-permute-start.12 = (f32[2,128,128]{2,1,0:T(8,128)S(1)}, f32[2,128,128]{2,1,0:T(8,128)S(1)}, u32[]{:S(2)}, u32[]{:S(2)}) collective-permute-start(f32[2,128,128]{2,1,0:T(8,128)S(1)} %get-tuple-element.53), channel_id=1, source_target_pairs={{1,2},{3,4},{5,6},{2,1},{4,3},{6,5},{9,10},{11,12},{13,14},{10,9},... | collective-permute-start | bytes 393224 | tf_op jit(solution)/shard_map/ppermute | solution.py:426
  44.7 0.0 collective-permute-done.8
  44.8 3.3 %collective-permute-start.9 = (f32[128,128]{1,0:T(8,128)S(1)}, f32[128,128]{1,0:T(8,128)S(1)}, u32[]{:S(2)}, u32[]{:S(2)}) collective-permute-start(f32[128,128]{1,0:T(8,128)S(1)} %add.21), channel_id=1, source_target_pairs={{0,2},{1,3},{2,0},{3,1},{4,6},{5,7},{6,4},{7,5},{8,12},{9,13},{10,... | collective-permute-start | bytes 196616 | tf_op jit(solution)/shard_map/ppermute | solution.py:445
  48.1 4.2 %collective-permute-done.9 = f32[128,128]{1,0:T(8,128)S(1)} collective-permute-done((f32[128,128]{1,0:T(8,128)S(1)}, f32[128,128]{1,0:T(8,128)S(1)}, u32[]{:S(2)}, u32[]{:S(2)}) %collective-permute-start.9) | collective-permute-done | bytes 65568 | tf_op jit(solution)/shard_map/ppermute | solution.py:445
  52.3 1.8 %collective-permute-start.10 = (f32[128,128]{1,0:T(8,128)S(1)}, f32[128,128]{1,0:T(8,128)S(1)}, u32[]{:S(2)}, u32[]{:S(2)}) collective-permute-start(f32[128,128]{1,0:T(8,128)S(1)} %add.22), channel_id=1, source_target_pairs={{0,4},{1,5},{2,6},{3,7},{4,0},{5,1},{6,2},{7,3},{8,10},{9,11},{10,... | collective-permute-start | bytes 196616 | tf_op jit(solution)/shard_map/ppermute | solution.py:445
  54.1 0.0 collective-permute-done.11.near_col_ref
  54.1 0.0 collective-permute-done.12.far_col_ref
  54.1 1.0 %final_sums.1 = f32[2,256,256]{2,1,0:T(8,128)} custom-call(f32[8,384,128]{2,1,0:T(8,128)S(1)} %get-tuple-element.51.grad, f32[2,64,384]{2,1,0:T(8,128)S(1)} %collective-permute-done.6.near_ref.near_row_ref, f32[2,64,384]{2,1,0:T(8,128)S(1)} %collective-permute-done.7.far_ref.far_row_ref, f32[2,128,128]{2,1,0:T(8,128)S(1)} %collective-permute-done.11.near_col_ref, ...), custom_call_target="tpu_custom_call" | custom-call | tf_op jit(solution)/shard_map/final_sums/pallas_call | solution.py:410
  55.1 2.6 %collective-permute-done.10 = f32[128,128]{1,0:T(8,128)S(1)} collective-permute-done((f32[128,128]{1,0:T(8,128)S(1)}, f32[128,128]{1,0:T(8,128)S(1)}, u32[]{:S(2)}, u32[]{:S(2)}) %collective-permute-start.10) | collective-permute-done | bytes 65568 | tf_op jit(solution)/shard_map/ppermute | solution.py:445
  57.7 0.1 collective-permute-start.13
  57.8 1.2 %collective-permute-done.13 = f32[128,128]{1,0:T(8,128)S(1)} collective-permute-done((f32[128,128]{1,0:T(8,128)S(1)}, f32[128,128]{1,0:T(8,128)S(1)}, u32[]{:S(2)}, u32[]{:S(2)}) %collective-permute-start.13) | collective-permute-done | bytes 65568 | tf_op jit(solution)/shard_map/ppermute | solution.py:421
  59.0 0.7 %maximum_select_fusion = f32[2,128,128]{2,1,0:T(8,128)} fusion(f32[1,128,128]{2,1,0:T(8,128)S(1)} %bitcast.11, f32[1,128,128]{2,1,0:T(8,128)S(1)} %bitcast.10, pred[]{:T(512)S(6)} %eq.5), kind=kLoop, calls=%fused_computation | loop fusion | flops 98304 | bytes 262145 | tf_op jit(solution)/shard_map/jit(_where)/select_n | solution.py:479
  (5 shorter events, 0.0 us)
Async XLA Ops:
  1.9 3.5 %collective-permute-start = (f32[2,64,256]{2,1,0:T(8,128)S(1)}, f32[2,64,256]{2,1,0:T(8,128)S(1)}, u32[]{:S(2)}, u32[]{:S(2)}) collective-permute-start(f32[2,64,256]{2,1,0:T(8,128)S(1)} %get-tuple-element.30), channel_id=1, source_target_pairs={{0,8},{8,0},{16,24},{24,16},{1,9},{9,1},{17,25},{25,17},{2,10},{10... | collective-permute-start | bytes 393224 | tf_op jit(solution)/shard_map/ppermute | solution.py:421
  2.4 3.0 %collective-permute-start.1 = (f32[2,64,256]{2,1,0:T(8,128)S(1)}, f32[2,64,256]{2,1,0:T(8,128)S(1)}, u32[]{:S(2)}, u32[]{:S(2)}) collective-permute-start(f32[2,64,256]{2,1,0:T(8,128)S(1)} %get-tuple-element.31), channel_id=1, source_target_pairs={{8,16},{16,8},{9,17},{17,9},{10,18},{18,10},{11,19},{19,11},{12,20... | collective-permute-start | bytes 393224 | tf_op jit(solution)/shard_map/ppermute | solution.py:426
  3.7 5.2 %copy-start = (s32[1,1,48]{2,1,0:T(1,128)S(1)}, s32[1,1,48]{2,1,0:T(1,128)}, u32[]{:S(2)}) copy-start(s32[1,1,48]{2,1,0:T(1,128)} %param.10) | copy-start | bytes 580
  3.8 5.2 %copy-start.1 = (s32[1,1,48]{2,1,0:T(1,128)S(1)}, s32[1,1,48]{2,1,0:T(1,128)}, u32[]{:S(2)}) copy-start(s32[1,1,48]{2,1,0:T(1,128)} %param.11) | copy-start | bytes 580
  5.7 9.4 %collective-permute-start.2 = (f32[2,192,128]{2,1,0:T(8,128)S(1)}, f32[2,192,128]{2,1,0:T(8,128)S(1)}, u32[]{:S(2)}, u32[]{:S(2)}) collective-permute-start(f32[2,192,128]{2,1,0:T(8,128)S(1)} %get-tuple-element.33), channel_id=1, source_target_pairs={{0,1},{1,0},{2,3},{3,2},{4,5},{5,4},{6,7},{7,6},{8,9},{9,8},{10,11... | collective-permute-start | bytes 589832 | tf_op jit(solution)/shard_map/ppermute | solution.py:421
  8.3 6.8 %collective-permute-start.3 = (f32[2,192,128]{2,1,0:T(8,128)S(1)}, f32[2,192,128]{2,1,0:T(8,128)S(1)}, u32[]{:S(2)}, u32[]{:S(2)}) collective-permute-start(f32[2,192,128]{2,1,0:T(8,128)S(1)} %get-tuple-element.34), channel_id=1, source_target_pairs={{1,2},{3,4},{5,6},{2,1},{4,3},{6,5},{9,10},{11,12},{13,14},{10,9},... | collective-permute-start | bytes 589832 | tf_op jit(solution)/shard_map/ppermute | solution.py:426
  23.9 4.3 %collective-permute-start.4 = (f32[128,128]{1,0:T(8,128)S(1)}, f32[128,128]{1,0:T(8,128)S(1)}, u32[]{:S(2)}, u32[]{:S(2)}) collective-permute-start(f32[128,128]{1,0:T(8,128)S(1)} %get-tuple-element.41), channel_id=1, source_target_pairs={{0,8},{8,0},{16,24},{24,16},{1,9},{9,1},{17,25},{25,17},{2,10},{10... | collective-permute-start | bytes 196616 | tf_op jit(solution)/shard_map/ppermute | solution.py:421
  28.2 10.6 %collective-permute-start.6 = (f32[2,64,384]{2,1,0:T(8,128)S(1)}, f32[2,64,384]{2,1,0:T(8,128)S(1)}, u32[]{:S(2)}, u32[]{:S(2)}) collective-permute-start(f32[2,64,384]{2,1,0:T(8,128)S(1)} %get-tuple-element.46), channel_id=1, source_target_pairs={{0,8},{8,0},{16,24},{24,16},{1,9},{9,1},{17,25},{25,17},{2,10},{10... | collective-permute-start | bytes 589832 | tf_op jit(solution)/shard_map/ppermute | solution.py:421
  28.6 10.2 %collective-permute-start.7 = (f32[2,64,384]{2,1,0:T(8,128)S(1)}, f32[2,64,384]{2,1,0:T(8,128)S(1)}, u32[]{:S(2)}, u32[]{:S(2)}) collective-permute-start(f32[2,64,384]{2,1,0:T(8,128)S(1)} %get-tuple-element.47), channel_id=1, source_target_pairs={{8,16},{16,8},{9,17},{17,9},{10,18},{18,10},{11,19},{19,11},{12,20... | collective-permute-start | bytes 589832 | tf_op jit(solution)/shard_map/ppermute | solution.py:426
  29.3 9.5 %collective-permute-start.5 = (f32[128,128]{1,0:T(8,128)S(1)}, f32[128,128]{1,0:T(8,128)S(1)}, u32[]{:S(2)}, u32[]{:S(2)}) collective-permute-start(f32[128,128]{1,0:T(8,128)S(1)} %add.19), channel_id=1, source_target_pairs={{0,1},{1,0},{2,3},{3,2},{4,5},{5,4},{6,7},{7,6},{8,9},{9,8},{10,11... | collective-permute-start | bytes 196616 | tf_op jit(solution)/shard_map/ppermute | solution.py:445
  39.0 5.8 %collective-permute-start.8 = (f32[128,128]{1,0:T(8,128)S(1)}, f32[128,128]{1,0:T(8,128)S(1)}, u32[]{:S(2)}, u32[]{:S(2)}) collective-permute-start(f32[128,128]{1,0:T(8,128)S(1)} %add.20), channel_id=1, source_target_pairs={{0,16},{1,17},{2,18},{3,19},{4,20},{5,21},{6,22},{7,23},{8,24},{9,... | collective-permute-start | bytes 196616 | tf_op jit(solution)/shard_map/ppermute | solution.py:445
  42.0 12.1 %collective-permute-start.11 = (f32[2,128,128]{2,1,0:T(8,128)S(1)}, f32[2,128,128]{2,1,0:T(8,128)S(1)}, u32[]{:S(2)}, u32[]{:S(2)}) collective-permute-start(f32[2,128,128]{2,1,0:T(8,128)S(1)} %get-tuple-element.52), channel_id=1, source_target_pairs={{0,1},{1,0},{2,3},{3,2},{4,5},{5,4},{6,7},{7,6},{8,9},{9,8},{10,11... | collective-permute-start | bytes 393224 | tf_op jit(solution)/shard_map/ppermute | solution.py:421
  44.1 10.1 %collective-permute-start.12 = (f32[2,128,128]{2,1,0:T(8,128)S(1)}, f32[2,128,128]{2,1,0:T(8,128)S(1)}, u32[]{:S(2)}, u32[]{:S(2)}) collective-permute-start(f32[2,128,128]{2,1,0:T(8,128)S(1)} %get-tuple-element.53), channel_id=1, source_target_pairs={{1,2},{3,4},{5,6},{2,1},{4,3},{6,5},{9,10},{11,12},{13,14},{10,9},... | collective-permute-start | bytes 393224 | tf_op jit(solution)/shard_map/ppermute | solution.py:426
  44.8 7.5 %collective-permute-start.9 = (f32[128,128]{1,0:T(8,128)S(1)}, f32[128,128]{1,0:T(8,128)S(1)}, u32[]{:S(2)}, u32[]{:S(2)}) collective-permute-start(f32[128,128]{1,0:T(8,128)S(1)} %add.21), channel_id=1, source_target_pairs={{0,2},{1,3},{2,0},{3,1},{4,6},{5,7},{6,4},{7,5},{8,12},{9,13},{10,... | collective-permute-start | bytes 196616 | tf_op jit(solution)/shard_map/ppermute | solution.py:445
  52.3 5.4 %collective-permute-start.10 = (f32[128,128]{1,0:T(8,128)S(1)}, f32[128,128]{1,0:T(8,128)S(1)}, u32[]{:S(2)}, u32[]{:S(2)}) collective-permute-start(f32[128,128]{1,0:T(8,128)S(1)} %add.22), channel_id=1, source_target_pairs={{0,4},{1,5},{2,6},{3,7},{4,0},{5,1},{6,2},{7,3},{8,10},{9,11},{10,... | collective-permute-start | bytes 196616 | tf_op jit(solution)/shard_map/ppermute | solution.py:445
  57.7 1.3 %collective-permute-start.13 = (f32[128,128]{1,0:T(8,128)S(1)}, f32[128,128]{1,0:T(8,128)S(1)}, u32[]{:S(2)}, u32[]{:S(2)}) collective-permute-start(f32[128,128]{1,0:T(8,128)S(1)} %add.23), channel_id=1, source_target_pairs={{0,8},{8,0},{16,24},{24,16},{1,9},{9,1},{17,25},{25,17},{2,10},{10... | collective-permute-start | bytes 196616 | tf_op jit(solution)/shard_map/ppermute | solution.py:421

commit v4 on v3

--- a/solution.py
+++ b/solution.py
@@ -1,3 +1,5 @@
+import functools
+
 import jax
 import jax.numpy as jnp
 import numpy as np
@@ -22,6 +24,10 @@
 
 def in_vmem(*arrays):
     return [pltpu.with_memory_space_constraint(array, pltpu.VMEM) for array in arrays]
+
+
+def in_smem(*arrays):
+    return [pltpu.with_memory_space_constraint(array, pltpu.SMEM) for array in arrays]
 
 
 def near(shape, dtype=F32):
@@ -109,32 +115,65 @@
     )(*in_hbm(centre))
 
 
-def ready_kernel(probe_ref, measured_ref, table_ref, probe, measured, tables, table, sem):
-    copies = [(table_ref, table), (probe_ref, probe), (measured_ref, measured)]
-    copies = [pltpu.make_async_copy(a, b, sem.at[i]) for i, (a, b) in enumerate(copies)]
+def ready_kernel(
+    inner_columns, rows_ref, cols_ref, count_ref, probe_ref, measured_ref, table_ref, plan, turned, measured, tables,
+    row_list, col_list, probe, table, sem,
+):
+    slots = measured.shape[0]
+    margin = probe.shape[1] // 2
+    pairs = ((rows_ref, row_list), (cols_ref, col_list), (probe_ref, probe), (table_ref, table))
+    copies = [pltpu.make_async_copy(a, b, sem.at[i]) for i, (a, b) in enumerate(pairs + ((measured_ref, measured),))]
     for copy in copies:
         copy.start()
-    copies[0].wait()
+    for copy in copies[:3]:
+        copy.wait()
+    count = count_ref[0]
+    inner = jnp.int32(0)
+    for slot in range(slots):
+        first = col_list[slot]
+        live = slot < count
+        is_inner = jnp.logical_and(jnp.logical_and(first >= 0, first <= inner_columns), live)
+        at = jnp.where(is_inner, inner, slots - 1 - (slot - inner))
+        plan[jnp.where(live, at, 5 * slots + 1)] = slot
+        inner = inner + is_inner.astype(jnp.int32)
+        col = first + LANES
+        turn = col & (LANES - 1)
+        place = slots + 2 + 3 * slot
+        plan[place] = row_list[slot] + margin
+        plan[place + 1] = lax.shift_right_logical(col, 7)
+        plan[place + 2] = turn
+        for plane in range(2):
+            turned[slot, plane] = pltpu.roll(probe[plane], turn, axis=1)
+    plan[slots] = inner
+    plan[slots + 1] = count
+    copies[3].wait()
     for index in range(2):
         tables[2 * index], tables[2 * index + 1] = split(table[index])
-    copies[1].wait()
-    copies[2].wait()
-
-
-def ready_call(probe, measured, table):
-    return pl.pallas_call(
-        ready_kernel,
+    copies[4].wait()
+
+
+def ready_call(rows, cols, count, probe, measured, table, width):
+    slots = measured.shape[0]
+    return pl.pallas_call(
+        functools.partial(ready_kernel, width - probe.shape[1]),
         out_shape=(
-            near(probe.shape),
+            pltpu.SMEM((5 * slots + 2,), jnp.int32),
+            near((slots,) + probe.shape),
             near(measured.shape, measured.dtype),
             near((4,) + table.shape[1:], jnp.bfloat16),
         ),
-        in_specs=[HBM] * 3,
-        out_specs=(VMEM,) * 3,
-        scratch_shapes=[pltpu.VMEM(table.shape, F32), pltpu.SemaphoreType.DMA((3,))],
+        in_specs=[HBM] * 2 + [SMEM] + [HBM] * 3,
+        out_specs=(SMEM,) + (VMEM,) * 3,
+        scratch_shapes=[
+            pltpu.SMEM(rows.shape, jnp.int32),
+            pltpu.SMEM(cols.shape, jnp.int32),
+            pltpu.VMEM(probe.shape, F32),
+            pltpu.VMEM(table.shape, F32),
+            pltpu.SemaphoreType.DMA((5,)),
+        ],
         compiler_params=PARAMS,
         name="ready",
-    )(*in_hbm(probe, measured, table))
+    )(*in_hbm(rows, cols), count, *in_hbm(probe, measured, table))
 
 
 def side_kernel(tile_ref, near_ref, far_ref, window, near_out, far_out):
@@ -168,34 +207,23 @@
     )(*in_vmem(window, near_row, far_row))
 
 
-def sort_slots(cols_ref, count, inner_width, order):
-    def visit(slot, inner):
-        col = cols_ref[slot]
-        is_inner = jnp.logical_and(col >= 0, col <= inner_width)
-        order[jnp.where(is_inner, inner, order.shape[0] - 1 - (slot - inner))] = slot
-        return inner + is_inner.astype(jnp.int32)
-
-    return lax.fori_loop(0, count, visit, jnp.int32(0))
-
-
-def run_slots(first_group, last_group, inner, count, order, rows_ref, cols_ref, window, probe, measured, table, grad, probe_sum):
-    size = probe.shape[1]
-    margin = size // 2
+def run_slots(groups, start, inner, live, plan, window, turned, measured, table, grad, probe_sum):
+    slots = measured.shape[0]
+    size = turned.shape[2]
     columns = window.shape[0] // 2
     lane = lax.broadcasted_iota(jnp.int32, (size, LANES), 1)
 
     def find(index):
-        at = jnp.where(index < inner, index, jnp.maximum(order.shape[0] - 1 - (index - inner), 0))
-        live = index < count
-        slot = jnp.where(live, order[at], 0)
-        row = rows_ref[slot] + margin
-        col = cols_ref[slot] + LANES
-        scale = jnp.where(live, 2.0, 0.0).astype(F32)
-        return slot, row, lax.shift_right_logical(col, 7), col & (LANES - 1), scale
+        at = jnp.where(index < inner, start + index, jnp.maximum(slots - 1 - (index - inner), 0))
+        is_live = index < live
+        slot = plan[jnp.where(is_live, at, jnp.where(inner > 0, start, slots - 1))]
+        place = slots + 2 + 3 * slot
+        scale = jnp.where(is_live, 2.0, 0.0).astype(F32)
+        return slot, plan[place], plan[place + 1], plan[place + 2], scale
 
     def load(pair):
         kept, waves = [], []
-        for _, row, tile, turn, _ in pair:
+        for slot, row, tile, turn, _ in pair:
             here = lane >= turn
             patch = [
                 jnp.where(
@@ -205,10 +233,10 @@
                 )
                 for plane in range(2)
             ]
-            turned = [pltpu.roll(probe[plane], turn, axis=1) for plane in range(2)]
-            wave_real = turned[0] * patch[0] - turned[1] * patch[1]
-            wave_imag = turned[0] * patch[1] + turned[1] * patch[0]
-            kept.append((patch, turned))
+            probe = [turned[slot, plane] for plane in range(2)]
+            wave_real = probe[0] * patch[0] - probe[1] * patch[1]
+            wave_imag = probe[0] * patch[1] + probe[1] * patch[0]
+            kept.append(patch)
             waves.append(jnp.concatenate([wave_real, wave_imag], axis=1))
         return kept, jnp.concatenate(waves, axis=0)
 
@@ -232,13 +260,14 @@
         return jnp.concatenate([weight * real, weight * imag], axis=0)
 
     def add_up(pair, kept, exits):
-        for member, (_, row, tile, turn, _) in enumerate(pair):
-            patch, turned = kept[member]
+        for member, (slot, row, tile, turn, _) in enumerate(pair):
+            patch = kept[member]
+            probe = [turned[slot, plane] for plane in range(2)]
             here = lane >= turn
             exit_real = exits[member * size : (member + 1) * size, :size]
             exit_imag = exits[member * size : (member + 1) * size, size:]
             terms = (patch[0] * exit_real + patch[1] * exit_imag, patch[0] * exit_imag - patch[1] * exit_real)
-            adds = (turned[0] * exit_real + turned[1] * exit_imag, turned[0] * exit_imag - turned[1] * exit_real)
+            adds = (probe[0] * exit_real + probe[1] * exit_imag, probe[0] * exit_imag - probe[1] * exit_real)
             back = (LANES - turn) & (LANES - 1)
             for plane in range(2):
                 probe_sum[plane] += pltpu.roll(terms[plane], back, axis=1)
@@ -258,45 +287,40 @@
             add_up(pair, kept, wave)
         return carry
 
-    lax.fori_loop(first_group, last_group, step, 0)
-
-
-def inner_kernel(rows_ref, cols_ref, count_ref, window, probe, measured, table, grad, probe_sum, order):
-    count = count_ref[0]
+    lax.fori_loop(0, groups, step, 0)
+
+
+def inner_kernel(plan, window, turned, measured, table, grad, probe_sum):
     grad[...] = jnp.zeros_like(grad)
     probe_sum[...] = jnp.zeros_like(probe_sum)
-    inner_width = (window.shape[0] // 2 - 2) * LANES - probe.shape[1]
-    inner = sort_slots(cols_ref, count, inner_width, order)
-    run_slots(0, inner // GROUP, inner, count, order, rows_ref, cols_ref, window, probe, measured, table, grad, probe_sum)
-
-
-def inner_call(rows, cols, count, window, probe, measured, tables):
+    groups = plan[measured.shape[0]] // GROUP
+    here = groups * GROUP
+    run_slots(groups, 0, here, here, plan, window, turned, measured, table, grad, probe_sum)
+
+
+def inner_call(plan, window, turned, measured, tables):
     return pl.pallas_call(
         inner_kernel,
-        out_shape=(near(window.shape), near(probe.shape)),
-        in_specs=[SMEM] * 3 + [VMEM] * 4,
+        out_shape=(near(window.shape), near(turned.shape[1:])),
+        in_specs=[SMEM] + [VMEM] * 4,
         out_specs=(VMEM,) * 2,
-        scratch_shapes=[pltpu.SMEM((measured.shape[0],), jnp.int32)],
         compiler_params=PARAMS,
         cost_estimate=pl.CostEstimate(flops=10**10, bytes_accessed=2 * 10**7, transcendentals=0),
         name="slots_inside",
-    )(rows, cols, count, *in_vmem(window, probe, measured, tables))
+    )(*in_smem(plan), *in_vmem(window, turned, measured, tables))
 
 
 def outer_kernel(
-    rows_ref, cols_ref, count_ref, window_ref, near_col_ref, far_col_ref, probe, measured, table, grad_ref, probe_ref,
-    grad, near_row_out, far_row_out, side_out, mine_out, other_out, window, probe_sum, order,
+    plan, window_ref, near_col_ref, far_col_ref, turned, measured, table, grad_ref, probe_ref,
+    grad, near_row_out, far_row_out, side_out, mine_out, other_out, window, probe_sum,
 ):
-    size = probe.shape[1]
-    margin = size // 2
+    slots = measured.shape[0]
+    margin = turned.shape[2] // 2
     columns = window.shape[0] // 2
     tall = window.shape[1]
     half = tall // 2
     odd_row, odd_col = parities()
     near, far = place_of(odd_row, 0, tall - margin)
-    count = count_ref[0]
-    inner_width = (columns - 2) * LANES - size
-    inner = sort_slots(cols_ref, count, inner_width, order)
     probe_sum[...] = probe_ref[...]
     grad[...] = grad_ref[...]
     for plane in range(2):
@@ -307,12 +331,13 @@
         for tile, ref in ((near_tile, near_col_ref), (far_tile, far_col_ref)):
             window[tile, :half] = ref[plane]
             window[tile, half:] = pltpu.roll(ref[plane], margin, axis=1)
-    groups = (count + GROUP - 1) // GROUP
+    start = plan[slots] // GROUP * GROUP
+    inner = plan[slots] - start
+    live = plan[slots + 1] - start
     run_slots(
-        inner // GROUP, groups, inner, count, order, rows_ref, cols_ref, window, probe, measured, table, grad, probe_sum
+        (live + GROUP - 1) // GROUP, start, inner, live, plan, window, turned, measured, table, grad, probe_sum
     )
-    total = lax.axis_size("trow") * lax.axis_size("tcol") * measured.shape[0]
-    factor = 1.0 / np.sqrt(np.float32(total))
+    factor = 1.0 / np.sqrt(np.float32(lax.axis_size("trow") * lax.axis_size("tcol") * slots))
     mine_out[...] = probe_sum[odd_row] * factor
     other_out[...] = probe_sum[1 - odd_row] * factor
     narrow = lax.broadcasted_iota(jnp.int32, (margin, LANES), 1) < margin
@@ -329,26 +354,22 @@
             side_out[plane, row - margin : row] = jnp.where(narrow, grad[right, rows, :], grad[left, rows, :])
 
 
-def outer_call(rows, cols, count, window, near_col, far_col, probe, measured, tables, grad, probe_sum):
-    size = probe.shape[1]
+def outer_call(plan, window, near_col, far_col, turned, measured, tables, grad, probe_sum):
+    size = turned.shape[2]
     margin = size // 2
     columns = window.shape[0] // 2
-    height = window.shape[1] - size
     row = near((2, margin, (columns - 1) * LANES))
     part = near((size, size))
     return pl.pallas_call(
         outer_kernel,
-        out_shape=(near(grad.shape), row, row, near((2, height, LANES)), part, part),
-        in_specs=[SMEM] * 3 + [VMEM] * 8,
+        out_shape=(near(grad.shape), row, row, near((2, window.shape[1] - size, LANES)), part, part),
+        in_specs=[SMEM] + [VMEM] * 8,
         out_specs=(VMEM,) * 6,
-        scratch_shapes=[
-            pltpu.VMEM(window.shape, F32),
-            pltpu.VMEM(probe.shape, F32),
-            pltpu.SMEM((measured.shape[0],), jnp.int32),
-        ],
-        compiler_params=PARAMS,
+        scratch_shapes=[pltpu.VMEM(window.shape, F32), pltpu.VMEM(probe_sum.shape, F32)],
+        compiler_params=PARAMS,
+        cost_estimate=pl.CostEstimate(flops=10**10, bytes_accessed=2 * 10**7, transcendentals=0),
         name="slots_across",
-    )(rows, cols, count, *in_vmem(window, near_col, far_col, probe, measured, tables, grad, probe_sum))
+    )(*in_smem(plan), *in_vmem(window, near_col, far_col, turned, measured, tables, grad, probe_sum))
 
 
 def side_sum_kernel(side_ref, near_ref, far_ref, near_out, far_out, side):
@@ -448,16 +469,17 @@
 def body(table, object_planes, probe, intensities, row_offsets, col_offsets, counts):
     size = probe.shape[1]
     rows, cols = row_offsets.reshape(-1), col_offsets.reshape(-1)
+    measured = intensities.reshape(-1, size, size)
     window, near_row, far_row = edge_call(object_planes, size // 2)
     near_row = near_swap(near_row, "trow")
     far_row = far_swap(far_row, "trow")
-    probe, measured, tables = ready_call(probe, intensities.reshape(-1, size, size), table)
+    plan, turned, measured, tables = ready_call(rows, cols, counts, probe, measured, table, object_planes.shape[2])
     window, near_side, far_side = side_call(window, near_row, far_row)
     near_col = near_swap(near_side, "tcol")
     far_col = far_swap(far_side, "tcol")
-    grad, probe_sum = inner_call(rows, cols, counts, window, probe, measured, tables)
+    grad, probe_sum = inner_call(plan, window, turned, measured, tables)
     grad, near_row, far_row, side, mine, other = outer_call(
-        rows, cols, counts, window, near_col, far_col, probe, measured, tables, grad, probe_sum
+        plan, window, near_col, far_col, turned, measured, tables, grad, probe_sum
     )
 
     steps = doubling_steps(lax.axis_size("trow"), lax.axis_size("tcol"))

time: 59.9 us -> 57.4 us (0.958)
  starting transfers between devices: 27.1 us -> 24.8 us
  Pallas kernels: 19.2 us -> 18.2 us
  waiting for transfers between devices: 11.2 us -> 12 us
    ppermute x4, starting transfers between devices: 15.4 us -> 11.5 us  [add_partner(): return mine + lax.ppermute(mine, ('trow', 'tcol'), pairs)]
    ppermute x6, starting transfers between devices: 9.02 us -> 10.7 us  [near_swap(): lax.ppermute(value, axis, [(i, i ^ 1) for i in range(lax.axis_size(axis))])]
    pallas_call x1, Pallas kernels: 8.82 us -> 7.73 us  [outer_call(): pl.pallas_call(outer_kernel, out_shape=(near(grad.shape), row, row, near(...]
    ppermute x4, waiting for transfers between devices: 9.08 us -> 9.81 us  [add_partner(): return mine + lax.ppermute(mine, ('trow', 'tcol'), pairs)]
where the time goes in v4:
time: 57.4 us; the launch traced here: 57.2 us
  starting transfers between devices  24.8 us (43%)
  Pallas kernels  18.2 us (32%)
  waiting for transfers between devices  12 us (21%)
  between operations  1.46 us (3%)
  other arithmetic  0.71 us (1%)
    ppermute x4, starting transfers between devices, add_partner(): return mine + lax.ppermute(mine, ('trow', 'tcol'), pairs)  11.5 us
    ppermute x6, starting transfers between devices, near_swap(): lax.ppermute(value, axis, [(i, i ^ 1) for i in range(lax.axis_size(axis))])  10.7 us
    ppermute x4, waiting for transfers between devices, add_partner(): return mine + lax.ppermute(mine, ('trow', 'tcol'), pairs)  9.81 us
    pallas_call x1, Pallas kernels, outer_call(): pl.pallas_call(outer_kernel, out_shape=(near(grad.shape), row, row, near(...  7.73 us
    pallas_call x1, Pallas kernels, inner_call(): pl.pallas_call(inner_kernel, out_shape=(near(window.shape), near(turned.s...  5.07 us
    pallas_call x1, Pallas kernels, ready_call(): pl.pallas_call(functools.partial(ready_kernel, width - probe.shape[1]), o...  2.8 us
    ppermute x4, starting transfers between devices, far_swap(): return lax.ppermute(value, axis, pairs + [(j, i) for i, j in pairs])  2.64 us
    ppermute x6, waiting for transfers between devices, near_swap(): lax.ppermute(value, axis, [(i, i ^ 1) for i in range(lax.axis_size(axis))])  2.14 us
  transfers between devices with their start and end apart: 14, of which 5 were waited for; matrix products, arithmetic and copies ran while one was open for 0% of the time, Pallas kernels for 15%

profile of v4, /device:TPU:0, one launch (start us, length us, event | category | flops | bytes accessed | tf_op | source)
XLA Modules:
  0.0 57.2 jit_solution(16899953840597966421)
XLA Ops:
  0.6 1.3 %edge_rows.1 = (f32[8,384,128]{2,1,0:T(8,128)S(1)}, f32[2,64,256]{2,1,0:T(8,128)S(1)}, f32[2,64,256]{2,1,0:T(8,128)S(1)}) custom-call(f32[2,256,256]{2,1,0:T(8,128)} %centre_ref.1), custom_call_target="tpu_custom_call" | custom-call | tf_op jit(solution)/shard_map/edge_rows/pallas_call | solution.py:107
  1.9 0.5 collective-permute-start
  2.4 0.7 %collective-permute-start.1 = (f32[2,64,256]{2,1,0:T(8,128)S(1)}, f32[2,64,256]{2,1,0:T(8,128)S(1)}, u32[]{:S(2)}, u32[]{:S(2)}) collective-permute-start(f32[2,64,256]{2,1,0:T(8,128)S(1)} %get-tuple-element.33), channel_id=1, source_target_pairs={{8,16},{16,8},{9,17},{17,9},{10,18},{18,10},{11,19},{19,11},{12,20... | collective-permute-start | bytes 393224 | tf_op jit(solution)/shard_map/ppermute | solution.py:447
  3.7 2.8 %ready.1 = (s32[242]{0:T(256)S(4)}, f32[48,2,128,128]{3,2,1,0:T(8,128)S(1)}, bf16[48,128,128]{2,1,0:T(8,128)(2,1)S(1)}, bf16[4,256,256]{2,1,0:T(8,128)(2,1)S(1)}) custom-call(s32[48]{0:T(128)} %bitcast.8, s32[48]{0:T(128)} %bitcast.9, s32[1]{0:T(128)S(6)} %copy.9.count_ref, f32[2,128,128]{2,1,0:T(8,128)} %probe_ref.1, bf16[48,128,128]{2,1,0:T(8,128)(2,1)} %bitcast.5, ...), custom_call_target="tpu_custom_call" | custom-call | tf_op jit(solution)/shard_map/ready/pallas_call | solution.py:157
  6.5 0.0 collective-permute-done.near_ref
  6.6 0.0 collective-permute-done.1.far_ref
  6.6 0.2 side_columns.1
  6.8 2.6 %collective-permute-start.2 = (f32[2,192,128]{2,1,0:T(8,128)S(1)}, f32[2,192,128]{2,1,0:T(8,128)S(1)}, u32[]{:S(2)}, u32[]{:S(2)}) collective-permute-start(f32[2,192,128]{2,1,0:T(8,128)S(1)} %get-tuple-element.35), channel_id=1, source_target_pairs={{0,1},{1,0},{2,3},{3,2},{4,5},{5,4},{6,7},{7,6},{8,9},{9,8},{10,11... | collective-permute-start | bytes 589832 | tf_op jit(solution)/shard_map/ppermute | solution.py:442
  9.4 0.7 %collective-permute-start.3 = (f32[2,192,128]{2,1,0:T(8,128)S(1)}, f32[2,192,128]{2,1,0:T(8,128)S(1)}, u32[]{:S(2)}, u32[]{:S(2)}) collective-permute-start(f32[2,192,128]{2,1,0:T(8,128)S(1)} %get-tuple-element.36), channel_id=1, source_target_pairs={{1,2},{3,4},{5,6},{2,1},{4,3},{6,5},{9,10},{11,12},{13,14},{10,9},... | collective-permute-start | bytes 589832 | tf_op jit(solution)/shard_map/ppermute | solution.py:447
  10.0 5.1 %slots_inside.1 = (f32[8,384,128]{2,1,0:T(8,128)S(1)}, f32[2,128,128]{2,1,0:T(8,128)S(1)}) custom-call(s32[242]{0:T(256)S(4)} %get-tuple-element.30.plan, f32[8,384,128]{2,1,0:T(8,128)S(1)} %get-tuple-element.34.window.window_ref, f32[48,2,128,128]{3,2,1,0:T(8,128)S(1)} %get-tuple-element.37.turned, bf16[48,128,128]{2,1,0:T(8,128)(2,1)S(1)} %get-tuple-element.38.measured, ...), custom_call_target="tpu_custom_call" | custom-call | flops 10000000000 | bytes 20000000 | tf_op jit(solution)/shard_map/slots_inside/pallas_call | solution.py:302
  15.1 0.0 collective-permute-done.2.near_col_ref
  15.1 0.0 collective-permute-done.3.far_col_ref
  15.1 7.7 %slots_across.1 = (f32[8,384,128]{2,1,0:T(8,128)S(1)}, f32[2,64,384]{2,1,0:T(8,128)S(1)}, f32[2,64,384]{2,1,0:T(8,128)S(1)}, f32[2,256,128]{2,1,0:T(8,128)S(1)},...) custom-call(s32[242]{0:T(256)S(4)} %get-tuple-element.30.plan, f32[8,384,128]{2,1,0:T(8,128)S(1)} %get-tuple-element.34.window.window_ref, ...), custom_call_target="tpu_custom_call" | custom-call | flops 10000000000 | bytes 20000000 | tf_op jit(solution)/shard_map/slots_across/pallas_call | solution.py:363
  22.9 5.1 %collective-permute-start.4 = (f32[128,128]{1,0:T(8,128)S(1)}, f32[128,128]{1,0:T(8,128)S(1)}, u32[]{:S(2)}, u32[]{:S(2)}) collective-permute-start(f32[128,128]{1,0:T(8,128)S(1)} %get-tuple-element.43), channel_id=1, source_target_pairs={{0,8},{8,0},{16,24},{24,16},{1,9},{9,1},{17,25},{25,17},{2,10},{10... | collective-permute-start | bytes 196616 | tf_op jit(solution)/shard_map/ppermute | solution.py:442
  28.0 0.9 %collective-permute-done.4 = f32[128,128]{1,0:T(8,128)S(1)} collective-permute-done((f32[128,128]{1,0:T(8,128)S(1)}, f32[128,128]{1,0:T(8,128)S(1)}, u32[]{:S(2)}, u32[]{:S(2)}) %collective-permute-start.4) | collective-permute-done | bytes 65568 | tf_op jit(solution)/shard_map/ppermute | solution.py:442
  28.9 0.4 collective-permute-start.6
  29.3 0.7 %collective-permute-start.7 = (f32[2,64,384]{2,1,0:T(8,128)S(1)}, f32[2,64,384]{2,1,0:T(8,128)S(1)}, u32[]{:S(2)}, u32[]{:S(2)}) collective-permute-start(f32[2,64,384]{2,1,0:T(8,128)S(1)} %get-tuple-element.49), channel_id=1, source_target_pairs={{8,16},{16,8},{9,17},{17,9},{10,18},{18,10},{11,19},{19,11},{12,20... | collective-permute-start | bytes 589832 | tf_op jit(solution)/shard_map/ppermute | solution.py:447
  30.0 4.1 %collective-permute-start.5 = (f32[128,128]{1,0:T(8,128)S(1)}, f32[128,128]{1,0:T(8,128)S(1)}, u32[]{:S(2)}, u32[]{:S(2)}) collective-permute-start(f32[128,128]{1,0:T(8,128)S(1)} %add.19), channel_id=1, source_target_pairs={{0,1},{1,0},{2,3},{3,2},{4,5},{5,4},{6,7},{7,6},{8,9},{9,8},{10,11... | collective-permute-start | bytes 196616 | tf_op jit(solution)/shard_map/ppermute | solution.py:466
  34.0 2.2 %collective-permute-done.5 = f32[128,128]{1,0:T(8,128)S(1)} collective-permute-done((f32[128,128]{1,0:T(8,128)S(1)}, f32[128,128]{1,0:T(8,128)S(1)}, u32[]{:S(2)}, u32[]{:S(2)}) %collective-permute-start.5) | collective-permute-done | bytes 65568 | tf_op jit(solution)/shard_map/ppermute | solution.py:466
  36.3 0.0 collective-permute-done.6.near_ref.near_row_ref
  36.3 0.0 collective-permute-done.7.far_ref.far_row_ref
  36.3 0.1 side_sums.1
  36.4 3.1 %collective-permute-start.8 = (f32[128,128]{1,0:T(8,128)S(1)}, f32[128,128]{1,0:T(8,128)S(1)}, u32[]{:S(2)}, u32[]{:S(2)}) collective-permute-start(f32[128,128]{1,0:T(8,128)S(1)} %add.20), channel_id=1, source_target_pairs={{0,16},{1,17},{2,18},{3,19},{4,20},{5,21},{6,22},{7,23},{8,24},{9,... | collective-permute-start | bytes 196616 | tf_op jit(solution)/shard_map/ppermute | solution.py:466
  39.5 2.0 %collective-permute-start.11 = (f32[2,128,128]{2,1,0:T(8,128)S(1)}, f32[2,128,128]{2,1,0:T(8,128)S(1)}, u32[]{:S(2)}, u32[]{:S(2)}) collective-permute-start(f32[2,128,128]{2,1,0:T(8,128)S(1)} %get-tuple-element.54), channel_id=1, source_target_pairs={{0,1},{1,0},{2,3},{3,2},{4,5},{5,4},{6,7},{7,6},{8,9},{9,8},{10,11... | collective-permute-start | bytes 393224 | tf_op jit(solution)/shard_map/ppermute | solution.py:442
  41.5 0.7 %collective-permute-start.12 = (f32[2,128,128]{2,1,0:T(8,128)S(1)}, f32[2,128,128]{2,1,0:T(8,128)S(1)}, u32[]{:S(2)}, u32[]{:S(2)}) collective-permute-start(f32[2,128,128]{2,1,0:T(8,128)S(1)} %get-tuple-element.55), channel_id=1, source_target_pairs={{1,2},{3,4},{5,6},{2,1},{4,3},{6,5},{9,10},{11,12},{13,14},{10,9},... | collective-permute-start | bytes 393224 | tf_op jit(solution)/shard_map/ppermute | solution.py:447
  42.2 0.0 collective-permute-done.8
  42.2 3.3 %collective-permute-start.9 = (f32[128,128]{1,0:T(8,128)S(1)}, f32[128,128]{1,0:T(8,128)S(1)}, u32[]{:S(2)}, u32[]{:S(2)}) collective-permute-start(f32[128,128]{1,0:T(8,128)S(1)} %add.21), channel_id=1, source_target_pairs={{0,2},{1,3},{2,0},{3,1},{4,6},{5,7},{6,4},{7,5},{8,12},{9,13},{10,... | collective-permute-start | bytes 196616 | tf_op jit(solution)/shard_map/ppermute | solution.py:466
  45.6 4.1 %collective-permute-done.9 = f32[128,128]{1,0:T(8,128)S(1)} collective-permute-done((f32[128,128]{1,0:T(8,128)S(1)}, f32[128,128]{1,0:T(8,128)S(1)}, u32[]{:S(2)}, u32[]{:S(2)}) %collective-permute-start.9) | collective-permute-done | bytes 65568 | tf_op jit(solution)/shard_map/ppermute | solution.py:466
  49.7 1.1 %collective-permute-start.10 = (f32[128,128]{1,0:T(8,128)S(1)}, f32[128,128]{1,0:T(8,128)S(1)}, u32[]{:S(2)}, u32[]{:S(2)}) collective-permute-start(f32[128,128]{1,0:T(8,128)S(1)} %add.22), channel_id=1, source_target_pairs={{0,4},{1,5},{2,6},{3,7},{4,0},{5,1},{6,2},{7,3},{8,10},{9,11},{10,... | collective-permute-start | bytes 196616 | tf_op jit(solution)/shard_map/ppermute | solution.py:466
  50.8 0.0 collective-permute-done.11.near_col_ref
  50.8 0.0 collective-permute-done.12.far_col_ref
  50.8 1.0 %final_sums.1 = f32[2,256,256]{2,1,0:T(8,128)} custom-call(f32[8,384,128]{2,1,0:T(8,128)S(1)} %get-tuple-element.53.grad, f32[2,64,384]{2,1,0:T(8,128)S(1)} %collective-permute-done.6.near_ref.near_row_ref, f32[2,64,384]{2,1,0:T(8,128)S(1)} %collective-permute-done.7.far_ref.far_row_ref, f32[2,128,128]{2,1,0:T(8,128)S(1)} %collective-permute-done.11.near_col_ref, ...), custom_call_target="tpu_custom_call" | custom-call | tf_op jit(solution)/shard_map/final_sums/pallas_call | solution.py:431
  51.8 3.4 %collective-permute-done.10 = f32[128,128]{1,0:T(8,128)S(1)} collective-permute-done((f32[128,128]{1,0:T(8,128)S(1)}, f32[128,128]{1,0:T(8,128)S(1)}, u32[]{:S(2)}, u32[]{:S(2)}) %collective-permute-start.10) | collective-permute-done | bytes 65568 | tf_op jit(solution)/shard_map/ppermute | solution.py:466
  55.2 0.1 collective-permute-start.13
  55.3 1.2 %collective-permute-done.13 = f32[128,128]{1,0:T(8,128)S(1)} collective-permute-done((f32[128,128]{1,0:T(8,128)S(1)}, f32[128,128]{1,0:T(8,128)S(1)}, u32[]{:S(2)}, u32[]{:S(2)}) %collective-permute-start.13) | collective-permute-done | bytes 65568 | tf_op jit(solution)/shard_map/ppermute | solution.py:442
  56.5 0.7 %maximum_select_fusion = f32[2,128,128]{2,1,0:T(8,128)} fusion(f32[1,128,128]{2,1,0:T(8,128)S(1)} %bitcast.7, f32[1,128,128]{2,1,0:T(8,128)S(1)} %bitcast.6, pred[]{:T(512)S(6)} %eq.5), kind=kLoop, calls=%fused_computation | loop fusion | flops 98304 | bytes 262145 | tf_op jit(solution)/shard_map/jit(_where)/select_n | solution.py:501
  (5 shorter events, 0.0 us)
Async XLA Ops:
  1.9 4.6 %collective-permute-start = (f32[2,64,256]{2,1,0:T(8,128)S(1)}, f32[2,64,256]{2,1,0:T(8,128)S(1)}, u32[]{:S(2)}, u32[]{:S(2)}) collective-permute-start(f32[2,64,256]{2,1,0:T(8,128)S(1)} %get-tuple-element.32), channel_id=1, source_target_pairs={{0,8},{8,0},{16,24},{24,16},{1,9},{9,1},{17,25},{25,17},{2,10},{10... | collective-permute-start | bytes 393224 | tf_op jit(solution)/shard_map/ppermute | solution.py:442
  2.4 4.1 %collective-permute-start.1 = (f32[2,64,256]{2,1,0:T(8,128)S(1)}, f32[2,64,256]{2,1,0:T(8,128)S(1)}, u32[]{:S(2)}, u32[]{:S(2)}) collective-permute-start(f32[2,64,256]{2,1,0:T(8,128)S(1)} %get-tuple-element.33), channel_id=1, source_target_pairs={{8,16},{16,8},{9,17},{17,9},{10,18},{18,10},{11,19},{19,11},{12,20... | collective-permute-start | bytes 393224 | tf_op jit(solution)/shard_map/ppermute | solution.py:447
  6.8 8.3 %collective-permute-start.2 = (f32[2,192,128]{2,1,0:T(8,128)S(1)}, f32[2,192,128]{2,1,0:T(8,128)S(1)}, u32[]{:S(2)}, u32[]{:S(2)}) collective-permute-start(f32[2,192,128]{2,1,0:T(8,128)S(1)} %get-tuple-element.35), channel_id=1, source_target_pairs={{0,1},{1,0},{2,3},{3,2},{4,5},{5,4},{6,7},{7,6},{8,9},{9,8},{10,11... | collective-permute-start | bytes 589832 | tf_op jit(solution)/shard_map/ppermute | solution.py:442
  9.4 5.8 %collective-permute-start.3 = (f32[2,192,128]{2,1,0:T(8,128)S(1)}, f32[2,192,128]{2,1,0:T(8,128)S(1)}, u32[]{:S(2)}, u32[]{:S(2)}) collective-permute-start(f32[2,192,128]{2,1,0:T(8,128)S(1)} %get-tuple-element.36), channel_id=1, source_target_pairs={{1,2},{3,4},{5,6},{2,1},{4,3},{6,5},{9,10},{11,12},{13,14},{10,9},... | collective-permute-start | bytes 589832 | tf_op jit(solution)/shard_map/ppermute | solution.py:447
  22.9 6.0 %collective-permute-start.4 = (f32[128,128]{1,0:T(8,128)S(1)}, f32[128,128]{1,0:T(8,128)S(1)}, u32[]{:S(2)}, u32[]{:S(2)}) collective-permute-start(f32[128,128]{1,0:T(8,128)S(1)} %get-tuple-element.43), channel_id=1, source_target_pairs={{0,8},{8,0},{16,24},{24,16},{1,9},{9,1},{17,25},{25,17},{2,10},{10... | collective-permute-start | bytes 196616 | tf_op jit(solution)/shard_map/ppermute | solution.py:442
  28.9 7.4 %collective-permute-start.6 = (f32[2,64,384]{2,1,0:T(8,128)S(1)}, f32[2,64,384]{2,1,0:T(8,128)S(1)}, u32[]{:S(2)}, u32[]{:S(2)}) collective-permute-start(f32[2,64,384]{2,1,0:T(8,128)S(1)} %get-tuple-element.48), channel_id=1, source_target_pairs={{0,8},{8,0},{16,24},{24,16},{1,9},{9,1},{17,25},{25,17},{2,10},{10... | collective-permute-start | bytes 589832 | tf_op jit(solution)/shard_map/ppermute | solution.py:442
  29.3 7.0 %collective-permute-start.7 = (f32[2,64,384]{2,1,0:T(8,128)S(1)}, f32[2,64,384]{2,1,0:T(8,128)S(1)}, u32[]{:S(2)}, u32[]{:S(2)}) collective-permute-start(f32[2,64,384]{2,1,0:T(8,128)S(1)} %get-tuple-element.49), channel_id=1, source_target_pairs={{8,16},{16,8},{9,17},{17,9},{10,18},{18,10},{11,19},{19,11},{12,20... | collective-permute-start | bytes 589832 | tf_op jit(solution)/shard_map/ppermute | solution.py:447
  30.0 6.3 %collective-permute-start.5 = (f32[128,128]{1,0:T(8,128)S(1)}, f32[128,128]{1,0:T(8,128)S(1)}, u32[]{:S(2)}, u32[]{:S(2)}) collective-permute-start(f32[128,128]{1,0:T(8,128)S(1)} %add.19), channel_id=1, source_target_pairs={{0,1},{1,0},{2,3},{3,2},{4,5},{5,4},{6,7},{7,6},{8,9},{9,8},{10,11... | collective-permute-start | bytes 196616 | tf_op jit(solution)/shard_map/ppermute | solution.py:466
  36.4 5.8 %collective-permute-start.8 = (f32[128,128]{1,0:T(8,128)S(1)}, f32[128,128]{1,0:T(8,128)S(1)}, u32[]{:S(2)}, u32[]{:S(2)}) collective-permute-start(f32[128,128]{1,0:T(8,128)S(1)} %add.20), channel_id=1, source_target_pairs={{0,16},{1,17},{2,18},{3,19},{4,20},{5,21},{6,22},{7,23},{8,24},{9,... | collective-permute-start | bytes 196616 | tf_op jit(solution)/shard_map/ppermute | solution.py:466
  39.5 11.3 %collective-permute-start.11 = (f32[2,128,128]{2,1,0:T(8,128)S(1)}, f32[2,128,128]{2,1,0:T(8,128)S(1)}, u32[]{:S(2)}, u32[]{:S(2)}) collective-permute-start(f32[2,128,128]{2,1,0:T(8,128)S(1)} %get-tuple-element.54), channel_id=1, source_target_pairs={{0,1},{1,0},{2,3},{3,2},{4,5},{5,4},{6,7},{7,6},{8,9},{9,8},{10,11... | collective-permute-start | bytes 393224 | tf_op jit(solution)/shard_map/ppermute | solution.py:442
  41.5 9.2 %collective-permute-start.12 = (f32[2,128,128]{2,1,0:T(8,128)S(1)}, f32[2,128,128]{2,1,0:T(8,128)S(1)}, u32[]{:S(2)}, u32[]{:S(2)}) collective-permute-start(f32[2,128,128]{2,1,0:T(8,128)S(1)} %get-tuple-element.55), channel_id=1, source_target_pairs={{1,2},{3,4},{5,6},{2,1},{4,3},{6,5},{9,10},{11,12},{13,14},{10,9},... | collective-permute-start | bytes 393224 | tf_op jit(solution)/shard_map/ppermute | solution.py:447
  42.2 7.4 %collective-permute-start.9 = (f32[128,128]{1,0:T(8,128)S(1)}, f32[128,128]{1,0:T(8,128)S(1)}, u32[]{:S(2)}, u32[]{:S(2)}) collective-permute-start(f32[128,128]{1,0:T(8,128)S(1)} %add.21), channel_id=1, source_target_pairs={{0,2},{1,3},{2,0},{3,1},{4,6},{5,7},{6,4},{7,5},{8,12},{9,13},{10,... | collective-permute-start | bytes 196616 | tf_op jit(solution)/shard_map/ppermute | solution.py:466
  49.7 5.5 %collective-permute-start.10 = (f32[128,128]{1,0:T(8,128)S(1)}, f32[128,128]{1,0:T(8,128)S(1)}, u32[]{:S(2)}, u32[]{:S(2)}) collective-permute-start(f32[128,128]{1,0:T(8,128)S(1)} %add.22), channel_id=1, source_target_pairs={{0,4},{1,5},{2,6},{3,7},{4,0},{5,1},{6,2},{7,3},{8,10},{9,11},{10,... | collective-permute-start | bytes 196616 | tf_op jit(solution)/shard_map/ppermute | solution.py:466
  55.2 1.3 %collective-permute-start.13 = (f32[128,128]{1,0:T(8,128)S(1)}, f32[128,128]{1,0:T(8,128)S(1)}, u32[]{:S(2)}, u32[]{:S(2)}) collective-permute-start(f32[128,128]{1,0:T(8,128)S(1)} %add.23), channel_id=1, source_target_pairs={{0,8},{8,0},{16,24},{24,16},{1,9},{9,1},{17,25},{25,17},{2,10},{10... | collective-permute-start | bytes 196616 | tf_op jit(solution)/shard_map/ppermute | solution.py:442

commit v5 on v4

--- a/solution.py
+++ b/solution.py
@@ -1,5 +1,3 @@
-import functools
-
 import jax
 import jax.numpy as jnp
 import numpy as np
@@ -79,21 +77,14 @@
     return near, far
 
 
-def edge_kernel(centre_ref, window, near_out, far_out, sem):
-    height, width = centre_ref.shape[1:]
+def edge_kernel(centre_ref, near_out, far_out, sem):
     margin = near_out.shape[1]
-    columns = window.shape[0] // 2
     odd_row, _ = parities()
-    near, far = place_of(odd_row, 0, height - margin)
+    near, far = place_of(odd_row, 0, centre_ref.shape[1] - margin)
     copies = [
-        (centre_ref.at[:, pl.ds(near, margin)], near_out),
-        (centre_ref.at[:, pl.ds(far, margin)], far_out),
+        pltpu.make_async_copy(centre_ref.at[:, pl.ds(far, margin)], far_out, sem.at[0]),
+        pltpu.make_async_copy(centre_ref.at[:, pl.ds(near, margin)], near_out, sem.at[1]),
     ]
-    for plane in range(2):
-        for tile in range(width // LANES):
-            lanes = slice(tile * LANES, (tile + 1) * LANES)
-            copies.append((centre_ref.at[plane, :, lanes], window.at[plane * columns + 1 + tile, pl.ds(margin, height)]))
-    copies = [pltpu.make_async_copy(a, b, sem.at[i]) for i, (a, b) in enumerate(copies)]
     for copy in copies:
         copy.start()
     for copy in copies:
@@ -101,33 +92,39 @@
 
 
 def edge_call(centre, margin):
-    height, width = centre.shape[1:]
-    tiles = width // LANES
-    edge = near((2, margin, width))
+    edge = near((2, margin, centre.shape[2]))
     return pl.pallas_call(
         edge_kernel,
-        out_shape=(near((2 * (tiles + 2), height + 2 * margin, LANES)), edge, edge),
+        out_shape=(edge, edge),
         in_specs=[HBM],
-        out_specs=(VMEM,) * 3,
-        scratch_shapes=[pltpu.SemaphoreType.DMA((2 + 2 * tiles,))],
+        out_specs=(VMEM,) * 2,
+        scratch_shapes=[pltpu.SemaphoreType.DMA((2,))],
         compiler_params=PARAMS,
         name="edge_rows",
     )(*in_hbm(centre))
 
 
 def ready_kernel(
-    inner_columns, rows_ref, cols_ref, count_ref, probe_ref, measured_ref, table_ref, plan, turned, measured, tables,
+    rows_ref, cols_ref, count_ref, probe_ref, measured_ref, table_ref, centre_ref, plan, turned, measured, tables, window,
     row_list, col_list, probe, table, sem,
 ):
     slots = measured.shape[0]
     margin = probe.shape[1] // 2
-    pairs = ((rows_ref, row_list), (cols_ref, col_list), (probe_ref, probe), (table_ref, table))
-    copies = [pltpu.make_async_copy(a, b, sem.at[i]) for i, (a, b) in enumerate(pairs + ((measured_ref, measured),))]
+    height, width = centre_ref.shape[1:]
+    columns = window.shape[0] // 2
+    inner_columns = width - probe.shape[2]
+    copies = [(rows_ref, row_list), (cols_ref, col_list), (probe_ref, probe), (table_ref, table)]
+    for plane in range(2):
+        for tile in range(columns - 2):
+            lanes = slice(tile * LANES, (tile + 1) * LANES)
+            copies.append((centre_ref.at[plane, :, lanes], window.at[plane * columns + 1 + tile, pl.ds(margin, height)]))
+    copies.append((measured_ref, measured))
+    copies = [pltpu.make_async_copy(a, b, sem.at[i]) for i, (a, b) in enumerate(copies)]
     for copy in copies:
         copy.start()
     for copy in copies[:3]:
         copy.wait()
-    count = count_ref[0]
+    count = count_ref[0, 0]
     inner = jnp.int32(0)
     for slot in range(slots):
         first = col_list[slot]
@@ -149,31 +146,35 @@
     copies[3].wait()
     for index in range(2):
         tables[2 * index], tables[2 * index + 1] = split(table[index])
-    copies[4].wait()
-
-
-def ready_call(rows, cols, count, probe, measured, table, width):
+    for copy in copies[4:]:
+        copy.wait()
+
+
+def ready_call(rows, cols, count, probe, measured, table, centre):
     slots = measured.shape[0]
-    return pl.pallas_call(
-        functools.partial(ready_kernel, width - probe.shape[1]),
+    height, width = centre.shape[1:]
+    tiles = width // LANES
+    return pl.pallas_call(
+        ready_kernel,
         out_shape=(
             pltpu.SMEM((5 * slots + 2,), jnp.int32),
             near((slots,) + probe.shape),
             near(measured.shape, measured.dtype),
             near((4,) + table.shape[1:], jnp.bfloat16),
+            near((2 * (tiles + 2), height + probe.shape[1], LANES)),
         ),
-        in_specs=[HBM] * 2 + [SMEM] + [HBM] * 3,
-        out_specs=(SMEM,) + (VMEM,) * 3,
+        in_specs=[HBM] * 2 + [VMEM] + [HBM] * 4,
+        out_specs=(SMEM,) + (VMEM,) * 4,
         scratch_shapes=[
             pltpu.SMEM(rows.shape, jnp.int32),
             pltpu.SMEM(cols.shape, jnp.int32),
             pltpu.VMEM(probe.shape, F32),
             pltpu.VMEM(table.shape, F32),
-            pltpu.SemaphoreType.DMA((5,)),
+            pltpu.SemaphoreType.DMA((5 + 2 * tiles,)),
         ],
         compiler_params=PARAMS,
         name="ready",
-    )(*in_hbm(rows, cols), count, *in_hbm(probe, measured, table))
+    )(*in_hbm(rows, cols), *in_vmem(jnp.broadcast_to(count, (8, LANES))), *in_hbm(probe, measured, table, centre))
 
 
 def side_kernel(tile_ref, near_ref, far_ref, window, near_out, far_out):
@@ -448,54 +449,70 @@
 
 
 def doubling_steps(n_row, n_col):
-    steps = [(0, 1)] + [(1 << k, 0) for k in range(1, n_row.bit_length() - 1)]
     rest = [(0, 1 << k) for k in range(1, n_col.bit_length() - 1)]
     turned = list(rest)
     for k in range(0, len(rest) - 1, 2):
         turned[k], turned[k + 1] = rest[k + 1], rest[k]
-    return list(zip(steps, steps)) + list(zip(rest, turned))
-
-
-def add_partner(mine, even, odd):
+    rows = [(1 << k, 0) for k in range(1, n_row.bit_length() - 1)]
+    return list(zip(rows, rows)), list(zip(rest, turned)) + [((0, 1), (0, 1))]
+
+
+def add_kernel(a_ref, b_ref, out_ref):
+    out_ref[...] = a_ref[...] + b_ref[...]
+
+
+def add_call(a, b):
+    return pl.pallas_call(
+        add_kernel,
+        out_shape=near(a.shape),
+        in_specs=[VMEM] * 2,
+        out_specs=VMEM,
+        compiler_params=PARAMS,
+        cost_estimate=pl.CostEstimate(flops=2 * 10**9, bytes_accessed=10**5, transcendentals=0),
+        name="add",
+    )(*in_vmem(a, b))
+
+
+def add_partner(mine, even, odd, add=jnp.add):
     n_row, n_col = lax.axis_size("trow"), lax.axis_size("tcol")
     pairs = []
     for r in range(n_row):
         for c in range(n_col):
             dr, dc = odd if r % 2 else even
             pairs.append((r * n_col + c, (r ^ dr) * n_col + (c ^ dc)))
-    return mine + lax.ppermute(mine, ("trow", "tcol"), pairs)
+    return add(mine, lax.ppermute(mine, ("trow", "tcol"), pairs))
 
 
 def body(table, object_planes, probe, intensities, row_offsets, col_offsets, counts):
     size = probe.shape[1]
     rows, cols = row_offsets.reshape(-1), col_offsets.reshape(-1)
     measured = intensities.reshape(-1, size, size)
-    window, near_row, far_row = edge_call(object_planes, size // 2)
+    near_row, far_row = edge_call(object_planes, size // 2)
+    far_row = far_swap(far_row, "trow")
     near_row = near_swap(near_row, "trow")
-    far_row = far_swap(far_row, "trow")
-    plan, turned, measured, tables = ready_call(rows, cols, counts, probe, measured, table, object_planes.shape[2])
+    plan, turned, measured, tables, window = ready_call(rows, cols, counts, probe, measured, table, object_planes)
     window, near_side, far_side = side_call(window, near_row, far_row)
+    far_col = far_swap(far_side, "tcol")
     near_col = near_swap(near_side, "tcol")
-    far_col = far_swap(far_side, "tcol")
     grad, probe_sum = inner_call(plan, window, turned, measured, tables)
     grad, near_row, far_row, side, mine, other = outer_call(
         plan, window, near_col, far_col, turned, measured, tables, grad, probe_sum
     )
 
-    steps = doubling_steps(lax.axis_size("trow"), lax.axis_size("tcol"))
+    along_rows, along_cols = doubling_steps(lax.axis_size("trow"), lax.axis_size("tcol"))
     mine = mine + near_swap(other, "trow")
     mine, near_row, far_row = lax.optimization_barrier((mine, near_row, far_row))
     near_row = near_swap(near_row, "trow")
     far_row = far_swap(far_row, "trow")
-    mine = add_partner(mine, *steps[0])
+    for step in along_rows:
+        mine = add_partner(mine, *step, add=add_call)
     near_side, far_side = side_sum_call(side, near_row, far_row)
     mine, near_side, far_side = lax.optimization_barrier((mine, near_side, far_side))
     near_col = near_swap(near_side, "tcol")
     far_col = far_swap(far_side, "tcol")
-    for even, odd in steps[1:]:
-        mine = add_partner(mine, even, odd)
+    for step in along_cols:
+        mine = add_partner(mine, *step)
     object_grad = final_call(grad, near_row, far_row, near_col, far_col)
-    mine, object_grad = lax.optimization_barrier((mine, object_grad))
     other = near_swap(mine, "trow")
     odd_row, _ = parities()
     probe_grad = jnp.where(odd_row == 0, jnp.stack([mine, other]), jnp.stack([other, mine]))

time: 57.4 us -> 56.2 us (0.979)
  starting transfers between devices: 24.8 us -> 21.6 us
  Pallas kernels: 18.2 us -> 20.4 us
    ppermute x6, starting transfers between devices: 10.7 us -> 7.28 us  [near_swap(): lax.ppermute(value, axis, [(i, i ^ 1) for i in range(lax.axis_size(axis))])]
    pallas_call x1, Pallas kernels: 5.07 us -> 7.45 us  [inner_call(): pl.pallas_call(inner_kernel, out_shape=(near(window.shape), near(turned.s...]
    ppermute x6, waiting for transfers between devices: 2.14 us -> 1.25 us  [near_swap(): lax.ppermute(value, axis, [(i, i ^ 1) for i in range(lax.axis_size(axis))])]
    ppermute x4, waiting for transfers between devices: 9.81 us -> 10.5 us  [add_partner(): return add(mine, lax.ppermute(mine, ('trow', 'tcol'), pairs))]
    pallas_call x2 -> x3, Pallas kernels: 4.07 us -> 3.93 us  [the longest x1 2.92 us: ready_call(): pl.pallas_call(ready_kernel, out_shape=(pltpu.SMEM((5 * slots + 2,), jnp....]
  transfers between devices with their start and end apart: 14 -> 14, of which waited for: 5 -> 5; matrix products, arithmetic and copies ran while one was open for 0% -> 0% of each run, Pallas kernels for 15% -> 20%
where the time goes in v5:
time: 56.2 us; the launch traced here: 56 us
  starting transfers between devices  21.6 us (38%)
  Pallas kernels  20.4 us (36%)
  waiting for transfers between devices  11.8 us (21%)
  between operations  1.44 us (3%)
  other arithmetic  0.7 us (1%)
    ppermute x4, starting transfers between devices, add_partner(): return add(mine, lax.ppermute(mine, ('trow', 'tcol'), pairs))  11.7 us
    ppermute x4, waiting for transfers between devices, add_partner(): return add(mine, lax.ppermute(mine, ('trow', 'tcol'), pairs))  10.5 us
    pallas_call x1, Pallas kernels, outer_call(): pl.pallas_call(outer_kernel, out_shape=(near(grad.shape), row, row, near(...  7.7 us
    pallas_call x1, Pallas kernels, inner_call(): pl.pallas_call(inner_kernel, out_shape=(near(window.shape), near(turned.s...  7.45 us
    ppermute x6, starting transfers between devices, near_swap(): lax.ppermute(value, axis, [(i, i ^ 1) for i in range(lax.axis_size(axis))])  7.28 us
    pallas_call x1, Pallas kernels, ready_call(): pl.pallas_call(ready_kernel, out_shape=(pltpu.SMEM((5 * slots + 2,), jnp....  2.92 us
    ppermute x4, starting transfers between devices, far_swap(): return lax.ppermute(value, axis, pairs + [(j, i) for i, j in pairs])  2.64 us
    ppermute x6, waiting for transfers between devices, near_swap(): lax.ppermute(value, axis, [(i, i ^ 1) for i in range(lax.axis_size(axis))])  1.25 us
  transfers between devices with their start and end apart: 14, of which 5 were waited for; matrix products, arithmetic and copies ran while one was open for 0% of the time, Pallas kernels for 20%

profile of v5, /device:TPU:0, one launch (start us, length us, event | category | flops | bytes accessed | tf_op | source)
XLA Modules:
  0.0 56.0 jit_solution(9333623604816694190)
XLA Ops:
  0.6 1.0 %edge_rows.1 = (f32[2,64,256]{2,1,0:T(8,128)S(1)}, f32[2,64,256]{2,1,0:T(8,128)S(1)}) custom-call(f32[2,256,256]{2,1,0:T(8,128)} %centre_ref.3), custom_call_target="tpu_custom_call" | custom-call | tf_op jit(solution)/shard_map/edge_rows/pallas_call | solution.py:96
  1.6 0.5 collective-permute-start
  2.2 0.7 %collective-permute-start.1 = (f32[2,64,256]{2,1,0:T(8,128)S(1)}, f32[2,64,256]{2,1,0:T(8,128)S(1)}, u32[]{:S(2)}, u32[]{:S(2)}) collective-permute-start(f32[2,64,256]{2,1,0:T(8,128)S(1)} %get-tuple-element.31), channel_id=1, source_target_pairs={{8,16},{16,8},{9,17},{17,9},{10,18},{18,10},{11,19},{19,11},{12,20... | collective-permute-start | bytes 393224 | tf_op jit(solution)/shard_map/ppermute | solution.py:448
  3.5 2.9 %ready.1 = (s32[242]{0:T(256)S(4)}, f32[48,2,128,128]{3,2,1,0:T(8,128)S(1)}, bf16[48,128,128]{2,1,0:T(8,128)(2,1)S(1)}, bf16[4,256,256]{2,1,0:T(8,128)(2,1)S(1)}, f32[8,384,128]{2,1,0:T(8,128)S(1)}) custom-call(s32[48]{0:T(128)} %bitcast.10, s32[48]{0:T(128)} %bitcast.11, s32[8,128]{1,0:T(8,128)S(1)} %broadcast_in_dim.2.count_ref, f32[2,128,128]{2,1,0:T(8,128)} %probe_ref.1, ...), custom_call_target="tpu_custom_call" | custom-call | tf_op jit(solution)/shard_map/ready/pallas_call | solution.py:157
  6.4 0.0 collective-permute-done.near_ref
  6.4 0.0 collective-permute-done.1.far_ref
  6.4 0.2 side_columns.1
  6.7 2.6 %collective-permute-start.2 = (f32[2,192,128]{2,1,0:T(8,128)S(1)}, f32[2,192,128]{2,1,0:T(8,128)S(1)}, u32[]{:S(2)}, u32[]{:S(2)}) collective-permute-start(f32[2,192,128]{2,1,0:T(8,128)S(1)} %get-tuple-element.33), channel_id=1, source_target_pairs={{0,1},{1,0},{2,3},{3,2},{4,5},{5,4},{6,7},{7,6},{8,9},{9,8},{10,11... | collective-permute-start | bytes 589832 | tf_op jit(solution)/shard_map/ppermute | solution.py:443
  9.2 0.7 %collective-permute-start.3 = (f32[2,192,128]{2,1,0:T(8,128)S(1)}, f32[2,192,128]{2,1,0:T(8,128)S(1)}, u32[]{:S(2)}, u32[]{:S(2)}) collective-permute-start(f32[2,192,128]{2,1,0:T(8,128)S(1)} %get-tuple-element.34), channel_id=1, source_target_pairs={{1,2},{3,4},{5,6},{2,1},{4,3},{6,5},{9,10},{11,12},{13,14},{10,9},... | collective-permute-start | bytes 589832 | tf_op jit(solution)/shard_map/ppermute | solution.py:448
  9.9 7.4 %slots_inside.1 = (f32[8,384,128]{2,1,0:T(8,128)S(1)}, f32[2,128,128]{2,1,0:T(8,128)S(1)}) custom-call(s32[242]{0:T(256)S(4)} %get-tuple-element.28.plan, f32[8,384,128]{2,1,0:T(8,128)S(1)} %get-tuple-element.32.window.window_ref, f32[48,2,128,128]{3,2,1,0:T(8,128)S(1)} %get-tuple-element.35.turned, bf16[48,128,128]{2,1,0:T(8,128)(2,1)S(1)} %get-tuple-element.36.measured, ...), custom_call_target="tpu_custom_call" | custom-call | flops 10000000000 | bytes 20000000 | tf_op jit(solution)/shard_map/slots_inside/pallas_call | solution.py:303
  17.4 0.0 collective-permute-done.2.near_col_ref
  17.4 0.0 collective-permute-done.3.far_col_ref
  17.4 7.7 %slots_across.1 = (f32[8,384,128]{2,1,0:T(8,128)S(1)}, f32[2,64,384]{2,1,0:T(8,128)S(1)}, f32[2,64,384]{2,1,0:T(8,128)S(1)}, f32[2,256,128]{2,1,0:T(8,128)S(1)},...) custom-call(s32[242]{0:T(256)S(4)} %get-tuple-element.28.plan, f32[8,384,128]{2,1,0:T(8,128)S(1)} %get-tuple-element.32.window.window_ref, ...), custom_call_target="tpu_custom_call" | custom-call | flops 10000000000 | bytes 20000000 | tf_op jit(solution)/shard_map/slots_across/pallas_call | solution.py:364
  25.1 0.1 collective-permute-start.4
  25.2 1.2 %collective-permute-done.4 = f32[128,128]{1,0:T(8,128)S(1)} collective-permute-done((f32[128,128]{1,0:T(8,128)S(1)}, f32[128,128]{1,0:T(8,128)S(1)}, u32[]{:S(2)}, u32[]{:S(2)}) %collective-permute-start.4) | collective-permute-done | bytes 65568 | tf_op jit(solution)/shard_map/ppermute | solution.py:443
  26.4 3.6 %collective-permute-start.7 = (f32[128,128]{1,0:T(8,128)S(1)}, f32[128,128]{1,0:T(8,128)S(1)}, u32[]{:S(2)}, u32[]{:S(2)}) collective-permute-start(f32[128,128]{1,0:T(8,128)S(1)} %add.17.a_ref), channel_id=1, source_target_pairs={{0,16},{1,17},{2,18},{3,19},{4,20},{5,21},{6,22},{7,23},{8,24},{9,... | collective-permute-start | bytes 196616 | tf_op jit(solution)/shard_map/ppermute | solution.py:483
  30.1 0.0 collective-permute-start.5
  30.1 0.7 %collective-permute-start.6 = (f32[2,64,384]{2,1,0:T(8,128)S(1)}, f32[2,64,384]{2,1,0:T(8,128)S(1)}, u32[]{:S(2)}, u32[]{:S(2)}) collective-permute-start(f32[2,64,384]{2,1,0:T(8,128)S(1)} %get-tuple-element.46), channel_id=1, source_target_pairs={{8,16},{16,8},{9,17},{17,9},{10,18},{18,10},{11,19},{19,11},{12,20... | collective-permute-start | bytes 589832 | tf_op jit(solution)/shard_map/ppermute | solution.py:448
  30.7 1.7 %collective-permute-done.7.b_ref = f32[128,128]{1,0:T(8,128)S(1)} collective-permute-done((f32[128,128]{1,0:T(8,128)S(1)}, f32[128,128]{1,0:T(8,128)S(1)}, u32[]{:S(2)}, u32[]{:S(2)}) %collective-permute-start.7) | collective-permute-done | bytes 65568 | tf_op jit(solution)/shard_map/ppermute | solution.py:483
  32.5 0.0 collective-permute-done.5.near_ref.near_row_ref
  32.5 0.0 collective-permute-done.6.far_ref.far_row_ref
  32.5 0.1 side_sums.1
  32.7 4.3 %collective-permute-start.10 = (f32[128,128]{1,0:T(8,128)S(1)}, f32[128,128]{1,0:T(8,128)S(1)}, u32[]{:S(2)}, u32[]{:S(2)}) collective-permute-start(f32[128,128]{1,0:T(8,128)S(1)} %add.22), channel_id=1, source_target_pairs={{0,2},{1,3},{2,0},{3,1},{4,6},{5,7},{6,4},{7,5},{8,12},{9,13},{10,... | collective-permute-start | bytes 196616 | tf_op jit(solution)/shard_map/ppermute | solution.py:483
  37.0 2.2 %collective-permute-done.10 = f32[128,128]{1,0:T(8,128)S(1)} collective-permute-done((f32[128,128]{1,0:T(8,128)S(1)}, f32[128,128]{1,0:T(8,128)S(1)}, u32[]{:S(2)}, u32[]{:S(2)}) %collective-permute-start.10) | collective-permute-done | bytes 65568 | tf_op jit(solution)/shard_map/ppermute | solution.py:483
  39.2 3.1 %collective-permute-start.11 = (f32[128,128]{1,0:T(8,128)S(1)}, f32[128,128]{1,0:T(8,128)S(1)}, u32[]{:S(2)}, u32[]{:S(2)}) collective-permute-start(f32[128,128]{1,0:T(8,128)S(1)} %add.19), channel_id=1, source_target_pairs={{0,4},{1,5},{2,6},{3,7},{4,0},{5,1},{6,2},{7,3},{8,10},{9,11},{10,... | collective-permute-start | bytes 196616 | tf_op jit(solution)/shard_map/ppermute | solution.py:483
  42.4 1.5 %collective-permute-start.8 = (f32[2,128,128]{2,1,0:T(8,128)S(1)}, f32[2,128,128]{2,1,0:T(8,128)S(1)}, u32[]{:S(2)}, u32[]{:S(2)}) collective-permute-start(f32[2,128,128]{2,1,0:T(8,128)S(1)} %get-tuple-element.51), channel_id=1, source_target_pairs={{0,1},{1,0},{2,3},{3,2},{4,5},{5,4},{6,7},{7,6},{8,9},{9,8},{10,11... | collective-permute-start | bytes 393224 | tf_op jit(solution)/shard_map/ppermute | solution.py:443
  43.9 0.7 %collective-permute-start.9 = (f32[2,128,128]{2,1,0:T(8,128)S(1)}, f32[2,128,128]{2,1,0:T(8,128)S(1)}, u32[]{:S(2)}, u32[]{:S(2)}) collective-permute-start(f32[2,128,128]{2,1,0:T(8,128)S(1)} %get-tuple-element.52), channel_id=1, source_target_pairs={{1,2},{3,4},{5,6},{2,1},{4,3},{6,5},{9,10},{11,12},{13,14},{10,9},... | collective-permute-start | bytes 393224 | tf_op jit(solution)/shard_map/ppermute | solution.py:448
  44.6 2.2 %collective-permute-done.11 = f32[128,128]{1,0:T(8,128)S(1)} collective-permute-done((f32[128,128]{1,0:T(8,128)S(1)}, f32[128,128]{1,0:T(8,128)S(1)}, u32[]{:S(2)}, u32[]{:S(2)}) %collective-permute-start.11) | collective-permute-done | bytes 65568 | tf_op jit(solution)/shard_map/ppermute | solution.py:483
  46.7 0.6 %collective-permute-start.12 = (f32[128,128]{1,0:T(8,128)S(1)}, f32[128,128]{1,0:T(8,128)S(1)}, u32[]{:S(2)}, u32[]{:S(2)}) collective-permute-start(f32[128,128]{1,0:T(8,128)S(1)} %add.20), channel_id=1, source_target_pairs={{0,1},{1,0},{2,3},{3,2},{4,5},{5,4},{6,7},{7,6},{8,9},{9,8},{10,11... | collective-permute-start | bytes 196616 | tf_op jit(solution)/shard_map/ppermute | solution.py:483
  47.4 4.3 %collective-permute-done.12 = f32[128,128]{1,0:T(8,128)S(1)} collective-permute-done((f32[128,128]{1,0:T(8,128)S(1)}, f32[128,128]{1,0:T(8,128)S(1)}, u32[]{:S(2)}, u32[]{:S(2)}) %collective-permute-start.12) | collective-permute-done | bytes 65568 | tf_op jit(solution)/shard_map/ppermute | solution.py:483
  51.7 2.6 %collective-permute-start.13 = (f32[128,128]{1,0:T(8,128)S(1)}, f32[128,128]{1,0:T(8,128)S(1)}, u32[]{:S(2)}, u32[]{:S(2)}) collective-permute-start(f32[128,128]{1,0:T(8,128)S(1)} %add.21), channel_id=1, source_target_pairs={{0,8},{8,0},{16,24},{24,16},{1,9},{9,1},{17,25},{25,17},{2,10},{10... | collective-permute-start | bytes 196616 | tf_op jit(solution)/shard_map/ppermute | solution.py:443
  54.3 0.0 collective-permute-done.8.near_col_ref
  54.3 0.0 collective-permute-done.9.far_col_ref
  54.3 1.0 %final_sums.1 = f32[2,256,256]{2,1,0:T(8,128)} custom-call(f32[8,384,128]{2,1,0:T(8,128)S(1)} %get-tuple-element.40.grad, f32[2,64,384]{2,1,0:T(8,128)S(1)} %collective-permute-done.5.near_ref.near_row_ref, f32[2,64,384]{2,1,0:T(8,128)S(1)} %collective-permute-done.6.far_ref.far_row_ref, f32[2,128,128]{2,1,0:T(8,128)S(1)} %collective-permute-done.8.near_col_ref, ...), custom_call_target="tpu_custom_call" | custom-call | tf_op jit(solution)/shard_map/final_sums/pallas_call | solution.py:432
  55.3 0.0 collective-permute-done.13
  55.3 0.7 %maximum_select_fusion = f32[2,128,128]{2,1,0:T(8,128)} fusion(f32[1,128,128]{2,1,0:T(8,128)S(1)} %bitcast.9, f32[1,128,128]{2,1,0:T(8,128)S(1)} %bitcast.8, pred[]{:T(512)S(6)} %eq.5), kind=kLoop, calls=%fused_computation | loop fusion | flops 98304 | bytes 262145 | tf_op jit(solution)/shard_map/jit(_where)/select_n | solution.py:518
  (6 shorter events, 0.0 us)
Async XLA Ops:
  1.6 4.8 %collective-permute-start = (f32[2,64,256]{2,1,0:T(8,128)S(1)}, f32[2,64,256]{2,1,0:T(8,128)S(1)}, u32[]{:S(2)}, u32[]{:S(2)}) collective-permute-start(f32[2,64,256]{2,1,0:T(8,128)S(1)} %get-tuple-element.30), channel_id=1, source_target_pairs={{0,8},{8,0},{16,24},{24,16},{1,9},{9,1},{17,25},{25,17},{2,10},{10... | collective-permute-start | bytes 393224 | tf_op jit(solution)/shard_map/ppermute | solution.py:443
  2.2 4.3 %collective-permute-start.1 = (f32[2,64,256]{2,1,0:T(8,128)S(1)}, f32[2,64,256]{2,1,0:T(8,128)S(1)}, u32[]{:S(2)}, u32[]{:S(2)}) collective-permute-start(f32[2,64,256]{2,1,0:T(8,128)S(1)} %get-tuple-element.31), channel_id=1, source_target_pairs={{8,16},{16,8},{9,17},{17,9},{10,18},{18,10},{11,19},{19,11},{12,20... | collective-permute-start | bytes 393224 | tf_op jit(solution)/shard_map/ppermute | solution.py:448
  6.7 10.7 %collective-permute-start.2 = (f32[2,192,128]{2,1,0:T(8,128)S(1)}, f32[2,192,128]{2,1,0:T(8,128)S(1)}, u32[]{:S(2)}, u32[]{:S(2)}) collective-permute-start(f32[2,192,128]{2,1,0:T(8,128)S(1)} %get-tuple-element.33), channel_id=1, source_target_pairs={{0,1},{1,0},{2,3},{3,2},{4,5},{5,4},{6,7},{7,6},{8,9},{9,8},{10,11... | collective-permute-start | bytes 589832 | tf_op jit(solution)/shard_map/ppermute | solution.py:443
  9.2 8.1 %collective-permute-start.3 = (f32[2,192,128]{2,1,0:T(8,128)S(1)}, f32[2,192,128]{2,1,0:T(8,128)S(1)}, u32[]{:S(2)}, u32[]{:S(2)}) collective-permute-start(f32[2,192,128]{2,1,0:T(8,128)S(1)} %get-tuple-element.34), channel_id=1, source_target_pairs={{1,2},{3,4},{5,6},{2,1},{4,3},{6,5},{9,10},{11,12},{13,14},{10,9},... | collective-permute-start | bytes 589832 | tf_op jit(solution)/shard_map/ppermute | solution.py:448
  25.1 1.3 %collective-permute-start.4 = (f32[128,128]{1,0:T(8,128)S(1)}, f32[128,128]{1,0:T(8,128)S(1)}, u32[]{:S(2)}, u32[]{:S(2)}) collective-permute-start(f32[128,128]{1,0:T(8,128)S(1)} %get-tuple-element.42), channel_id=1, source_target_pairs={{0,8},{8,0},{16,24},{24,16},{1,9},{9,1},{17,25},{25,17},{2,10},{10... | collective-permute-start | bytes 196616 | tf_op jit(solution)/shard_map/ppermute | solution.py:443
  26.4 6.0 %collective-permute-start.7 = (f32[128,128]{1,0:T(8,128)S(1)}, f32[128,128]{1,0:T(8,128)S(1)}, u32[]{:S(2)}, u32[]{:S(2)}) collective-permute-start(f32[128,128]{1,0:T(8,128)S(1)} %add.17.a_ref), channel_id=1, source_target_pairs={{0,16},{1,17},{2,18},{3,19},{4,20},{5,21},{6,22},{7,23},{8,24},{9,... | collective-permute-start | bytes 196616 | tf_op jit(solution)/shard_map/ppermute | solution.py:483
  30.1 2.4 %collective-permute-start.5 = (f32[2,64,384]{2,1,0:T(8,128)S(1)}, f32[2,64,384]{2,1,0:T(8,128)S(1)}, u32[]{:S(2)}, u32[]{:S(2)}) collective-permute-start(f32[2,64,384]{2,1,0:T(8,128)S(1)} %get-tuple-element.45), channel_id=1, source_target_pairs={{0,8},{8,0},{16,24},{24,16},{1,9},{9,1},{17,25},{25,17},{2,10},{10... | collective-permute-start | bytes 589832 | tf_op jit(solution)/shard_map/ppermute | solution.py:443
  30.1 2.4 %collective-permute-start.6 = (f32[2,64,384]{2,1,0:T(8,128)S(1)}, f32[2,64,384]{2,1,0:T(8,128)S(1)}, u32[]{:S(2)}, u32[]{:S(2)}) collective-permute-start(f32[2,64,384]{2,1,0:T(8,128)S(1)} %get-tuple-element.46), channel_id=1, source_target_pairs={{8,16},{16,8},{9,17},{17,9},{10,18},{18,10},{11,19},{19,11},{12,20... | collective-permute-start | bytes 589832 | tf_op jit(solution)/shard_map/ppermute | solution.py:448
  32.7 6.6 %collective-permute-start.10 = (f32[128,128]{1,0:T(8,128)S(1)}, f32[128,128]{1,0:T(8,128)S(1)}, u32[]{:S(2)}, u32[]{:S(2)}) collective-permute-start(f32[128,128]{1,0:T(8,128)S(1)} %add.22), channel_id=1, source_target_pairs={{0,2},{1,3},{2,0},{3,1},{4,6},{5,7},{6,4},{7,5},{8,12},{9,13},{10,... | collective-permute-start | bytes 196616 | tf_op jit(solution)/shard_map/ppermute | solution.py:483
  39.2 7.5 %collective-permute-start.11 = (f32[128,128]{1,0:T(8,128)S(1)}, f32[128,128]{1,0:T(8,128)S(1)}, u32[]{:S(2)}, u32[]{:S(2)}) collective-permute-start(f32[128,128]{1,0:T(8,128)S(1)} %add.19), channel_id=1, source_target_pairs={{0,4},{1,5},{2,6},{3,7},{4,0},{5,1},{6,2},{7,3},{8,10},{9,11},{10,... | collective-permute-start | bytes 196616 | tf_op jit(solution)/shard_map/ppermute | solution.py:483
  42.4 11.9 %collective-permute-start.8 = (f32[2,128,128]{2,1,0:T(8,128)S(1)}, f32[2,128,128]{2,1,0:T(8,128)S(1)}, u32[]{:S(2)}, u32[]{:S(2)}) collective-permute-start(f32[2,128,128]{2,1,0:T(8,128)S(1)} %get-tuple-element.51), channel_id=1, source_target_pairs={{0,1},{1,0},{2,3},{3,2},{4,5},{5,4},{6,7},{7,6},{8,9},{9,8},{10,11... | collective-permute-start | bytes 393224 | tf_op jit(solution)/shard_map/ppermute | solution.py:443
  43.9 10.4 %collective-permute-start.9 = (f32[2,128,128]{2,1,0:T(8,128)S(1)}, f32[2,128,128]{2,1,0:T(8,128)S(1)}, u32[]{:S(2)}, u32[]{:S(2)}) collective-permute-start(f32[2,128,128]{2,1,0:T(8,128)S(1)} %get-tuple-element.52), channel_id=1, source_target_pairs={{1,2},{3,4},{5,6},{2,1},{4,3},{6,5},{9,10},{11,12},{13,14},{10,9},... | collective-permute-start | bytes 393224 | tf_op jit(solution)/shard_map/ppermute | solution.py:448
  46.7 5.0 %collective-permute-start.12 = (f32[128,128]{1,0:T(8,128)S(1)}, f32[128,128]{1,0:T(8,128)S(1)}, u32[]{:S(2)}, u32[]{:S(2)}) collective-permute-start(f32[128,128]{1,0:T(8,128)S(1)} %add.20), channel_id=1, source_target_pairs={{0,1},{1,0},{2,3},{3,2},{4,5},{5,4},{6,7},{7,6},{8,9},{9,8},{10,11... | collective-permute-start | bytes 196616 | tf_op jit(solution)/shard_map/ppermute | solution.py:483
  51.7 3.6 %collective-permute-start.13 = (f32[128,128]{1,0:T(8,128)S(1)}, f32[128,128]{1,0:T(8,128)S(1)}, u32[]{:S(2)}, u32[]{:S(2)}) collective-permute-start(f32[128,128]{1,0:T(8,128)S(1)} %add.21), channel_id=1, source_target_pairs={{0,8},{8,0},{16,24},{24,16},{1,9},{9,1},{17,25},{25,17},{2,10},{10... | collective-permute-start | bytes 196616 | tf_op jit(solution)/shard_map/ppermute | solution.py:443

commit v6 on v5

--- a/solution.py
+++ b/solution.py
@@ -468,7 +468,7 @@
         in_specs=[VMEM] * 2,
         out_specs=VMEM,
         compiler_params=PARAMS,
-        cost_estimate=pl.CostEstimate(flops=2 * 10**9, bytes_accessed=10**5, transcendentals=0),
+        cost_estimate=pl.CostEstimate(flops=10**9, bytes_accessed=10**5, transcendentals=0),
         name="add",
     )(*in_vmem(a, b))
 
@@ -504,13 +504,13 @@
     mine, near_row, far_row = lax.optimization_barrier((mine, near_row, far_row))
     near_row = near_swap(near_row, "trow")
     far_row = far_swap(far_row, "trow")
-    for step in along_rows:
-        mine = add_partner(mine, *step, add=add_call)
+    mine = add_partner(mine, *along_cols[-1])
+    mine = add_partner(mine, *along_cols[0], add=add_call)
     near_side, far_side = side_sum_call(side, near_row, far_row)
     mine, near_side, far_side = lax.optimization_barrier((mine, near_side, far_side))
     near_col = near_swap(near_side, "tcol")
     far_col = far_swap(far_side, "tcol")
-    for step in along_cols:
+    for step in along_cols[1:-1] + along_rows:
         mine = add_partner(mine, *step)
     object_grad = final_call(grad, near_row, far_row, near_col, far_col)
     other = near_swap(mine, "trow")

time: 56.2 us -> 55.5 us (0.988); the launches traced: 56 us -> 56.3 us
  starting transfers between devices: 21.6 us -> 23.3 us
  waiting for transfers between devices: 11.8 us -> 10.4 us
    ppermute x4, waiting for transfers between devices: 10.5 us -> 8.93 us  [add_partner(): return add(mine, lax.ppermute(mine, ('trow', 'tcol'), pairs))]
    ppermute x6, starting transfers between devices: 7.28 us -> 8.28 us  [near_swap(): lax.ppermute(value, axis, [(i, i ^ 1) for i in range(lax.axis_size(axis))])]
    ppermute x4, starting transfers between devices: 11.7 us -> 12.4 us  [add_partner(): return add(mine, lax.ppermute(mine, ('trow', 'tcol'), pairs))]
where the time goes in v6:
time: 55.5 us; the launch traced here: 56.3 us
  starting transfers between devices  23.3 us (42%)
  Pallas kernels  20.4 us (37%)
  waiting for transfers between devices  10.4 us (19%)
  between operations  1.48 us (3%)
  other arithmetic  0.7 us (1%)
    ppermute x4, starting transfers between devices, add_partner(): return add(mine, lax.ppermute(mine, ('trow', 'tcol'), pairs))  12.4 us
    ppermute x4, waiting for transfers between devices, add_partner(): return add(mine, lax.ppermute(mine, ('trow', 'tcol'), pairs))  8.93 us
    ppermute x6, starting transfers between devices, near_swap(): lax.ppermute(value, axis, [(i, i ^ 1) for i in range(lax.axis_size(axis))])  8.28 us
    pallas_call x1, Pallas kernels, outer_call(): pl.pallas_call(outer_kernel, out_shape=(near(grad.shape), row, row, near(...  7.64 us
    pallas_call x1, Pallas kernels, inner_call(): pl.pallas_call(inner_kernel, out_shape=(near(window.shape), near(turned.s...  7.44 us
    pallas_call x1, Pallas kernels, ready_call(): pl.pallas_call(ready_kernel, out_shape=(pltpu.SMEM((5 * slots + 2,), jnp....  2.92 us
    ppermute x4, starting transfers between devices, far_swap(): return lax.ppermute(value, axis, pairs + [(j, i) for i, j in pairs])  2.64 us
    ppermute x6, waiting for transfers between devices, near_swap(): lax.ppermute(value, axis, [(i, i ^ 1) for i in range(lax.axis_size(axis))])  1.48 us
  transfers between devices with their start and end apart: 14, of which 5 were waited for; matrix products, arithmetic and copies ran while one was open for 0% of the time, Pallas kernels for 20%

profile of v6, /device:TPU:0, one launch (start us, length us, event | category | flops | bytes accessed | tf_op | source)
XLA Modules:
  0.0 56.3 jit_solution(14808918088357341522)
XLA Ops:
  0.6 1.0 %edge_rows.1 = (f32[2,64,256]{2,1,0:T(8,128)S(1)}, f32[2,64,256]{2,1,0:T(8,128)S(1)}) custom-call(f32[2,256,256]{2,1,0:T(8,128)} %centre_ref.3), custom_call_target="tpu_custom_call" | custom-call | tf_op jit(solution)/shard_map/edge_rows/pallas_call | solution.py:96
  1.6 0.5 collective-permute-start
  2.2 0.7 %collective-permute-start.1 = (f32[2,64,256]{2,1,0:T(8,128)S(1)}, f32[2,64,256]{2,1,0:T(8,128)S(1)}, u32[]{:S(2)}, u32[]{:S(2)}) collective-permute-start(f32[2,64,256]{2,1,0:T(8,128)S(1)} %get-tuple-element.31), channel_id=1, source_target_pairs={{8,16},{16,8},{9,17},{17,9},{10,18},{18,10},{11,19},{19,11},{12,20... | collective-permute-start | bytes 393224 | tf_op jit(solution)/shard_map/ppermute | solution.py:448
  3.5 2.9 %ready.1 = (s32[242]{0:T(256)S(4)}, f32[48,2,128,128]{3,2,1,0:T(8,128)S(1)}, bf16[48,128,128]{2,1,0:T(8,128)(2,1)S(1)}, bf16[4,256,256]{2,1,0:T(8,128)(2,1)S(1)}, f32[8,384,128]{2,1,0:T(8,128)S(1)}) custom-call(s32[48]{0:T(128)} %bitcast.10, s32[48]{0:T(128)} %bitcast.11, s32[8,128]{1,0:T(8,128)S(1)} %broadcast_in_dim.2.count_ref, f32[2,128,128]{2,1,0:T(8,128)} %probe_ref.1, ...), custom_call_target="tpu_custom_call" | custom-call | tf_op jit(solution)/shard_map/ready/pallas_call | solution.py:157
  6.4 0.0 collective-permute-done.near_ref
  6.4 0.0 collective-permute-done.1.far_ref
  6.4 0.2 side_columns.1
  6.7 2.6 %collective-permute-start.2 = (f32[2,192,128]{2,1,0:T(8,128)S(1)}, f32[2,192,128]{2,1,0:T(8,128)S(1)}, u32[]{:S(2)}, u32[]{:S(2)}) collective-permute-start(f32[2,192,128]{2,1,0:T(8,128)S(1)} %get-tuple-element.33), channel_id=1, source_target_pairs={{0,1},{1,0},{2,3},{3,2},{4,5},{5,4},{6,7},{7,6},{8,9},{9,8},{10,11... | collective-permute-start | bytes 589832 | tf_op jit(solution)/shard_map/ppermute | solution.py:443
  9.2 0.7 %collective-permute-start.3 = (f32[2,192,128]{2,1,0:T(8,128)S(1)}, f32[2,192,128]{2,1,0:T(8,128)S(1)}, u32[]{:S(2)}, u32[]{:S(2)}) collective-permute-start(f32[2,192,128]{2,1,0:T(8,128)S(1)} %get-tuple-element.34), channel_id=1, source_target_pairs={{1,2},{3,4},{5,6},{2,1},{4,3},{6,5},{9,10},{11,12},{13,14},{10,9},... | collective-permute-start | bytes 589832 | tf_op jit(solution)/shard_map/ppermute | solution.py:448
  9.9 7.4 %slots_inside.1 = (f32[8,384,128]{2,1,0:T(8,128)S(1)}, f32[2,128,128]{2,1,0:T(8,128)S(1)}) custom-call(s32[242]{0:T(256)S(4)} %get-tuple-element.28.plan, f32[8,384,128]{2,1,0:T(8,128)S(1)} %get-tuple-element.32.window.window_ref, f32[48,2,128,128]{3,2,1,0:T(8,128)S(1)} %get-tuple-element.35.turned, bf16[48,128,128]{2,1,0:T(8,128)(2,1)S(1)} %get-tuple-element.36.measured, ...), custom_call_target="tpu_custom_call" | custom-call | flops 10000000000 | bytes 20000000 | tf_op jit(solution)/shard_map/slots_inside/pallas_call | solution.py:303
  17.4 0.0 collective-permute-done.2.near_col_ref
  17.4 0.0 collective-permute-done.3.far_col_ref
  17.4 7.6 %slots_across.1 = (f32[8,384,128]{2,1,0:T(8,128)S(1)}, f32[2,64,384]{2,1,0:T(8,128)S(1)}, f32[2,64,384]{2,1,0:T(8,128)S(1)}, f32[2,256,128]{2,1,0:T(8,128)S(1)},...) custom-call(s32[242]{0:T(256)S(4)} %get-tuple-element.28.plan, f32[8,384,128]{2,1,0:T(8,128)S(1)} %get-tuple-element.32.window.window_ref, ...), custom_call_target="tpu_custom_call" | custom-call | flops 10000000000 | bytes 20000000 | tf_op jit(solution)/shard_map/slots_across/pallas_call | solution.py:364
  25.0 0.1 collective-permute-start.4
  25.1 1.2 %collective-permute-done.4 = f32[128,128]{1,0:T(8,128)S(1)} collective-permute-done((f32[128,128]{1,0:T(8,128)S(1)}, f32[128,128]{1,0:T(8,128)S(1)}, u32[]{:S(2)}, u32[]{:S(2)}) %collective-permute-start.4) | collective-permute-done | bytes 65568 | tf_op jit(solution)/shard_map/ppermute | solution.py:443
  26.4 6.3 %collective-permute-start.7 = (f32[128,128]{1,0:T(8,128)S(1)}, f32[128,128]{1,0:T(8,128)S(1)}, u32[]{:S(2)}, u32[]{:S(2)}) collective-permute-start(f32[128,128]{1,0:T(8,128)S(1)} %add.17), channel_id=1, source_target_pairs={{0,1},{1,0},{2,3},{3,2},{4,5},{5,4},{6,7},{7,6},{8,9},{9,8},{10,11... | collective-permute-start | bytes 196616 | tf_op jit(solution)/shard_map/ppermute | solution.py:483
  32.7 0.1 collective-permute-start.5
  32.8 0.7 %collective-permute-start.6 = (f32[2,64,384]{2,1,0:T(8,128)S(1)}, f32[2,64,384]{2,1,0:T(8,128)S(1)}, u32[]{:S(2)}, u32[]{:S(2)}) collective-permute-start(f32[2,64,384]{2,1,0:T(8,128)S(1)} %get-tuple-element.46), channel_id=1, source_target_pairs={{8,16},{16,8},{9,17},{17,9},{10,18},{18,10},{11,19},{19,11},{12,20... | collective-permute-start | bytes 589832 | tf_op jit(solution)/shard_map/ppermute | solution.py:448
  33.4 1.9 %collective-permute-done.7 = f32[128,128]{1,0:T(8,128)S(1)} collective-permute-done((f32[128,128]{1,0:T(8,128)S(1)}, f32[128,128]{1,0:T(8,128)S(1)}, u32[]{:S(2)}, u32[]{:S(2)}) %collective-permute-start.7) | collective-permute-done | bytes 65568 | tf_op jit(solution)/shard_map/ppermute | solution.py:483
  35.3 1.5 %collective-permute-start.8 = (f32[128,128]{1,0:T(8,128)S(1)}, f32[128,128]{1,0:T(8,128)S(1)}, u32[]{:S(2)}, u32[]{:S(2)}) collective-permute-start(f32[128,128]{1,0:T(8,128)S(1)} %add.18.a_ref), channel_id=1, source_target_pairs={{0,2},{1,3},{2,0},{3,1},{4,6},{5,7},{6,4},{7,5},{8,12},{9,13},{10,... | collective-permute-start | bytes 196616 | tf_op jit(solution)/shard_map/ppermute | solution.py:483
  36.8 2.8 %collective-permute-done.8.b_ref = f32[128,128]{1,0:T(8,128)S(1)} collective-permute-done((f32[128,128]{1,0:T(8,128)S(1)}, f32[128,128]{1,0:T(8,128)S(1)}, u32[]{:S(2)}, u32[]{:S(2)}) %collective-permute-start.8) | collective-permute-done | bytes 65568 | tf_op jit(solution)/shard_map/ppermute | solution.py:483
  39.6 0.0 collective-permute-done.5.near_ref.near_row_ref
  39.7 0.0 collective-permute-done.6.far_ref.far_row_ref
  39.7 0.1 side_sums.1
  39.8 4.5 %collective-permute-start.11 = (f32[128,128]{1,0:T(8,128)S(1)}, f32[128,128]{1,0:T(8,128)S(1)}, u32[]{:S(2)}, u32[]{:S(2)}) collective-permute-start(f32[128,128]{1,0:T(8,128)S(1)} %add.22), channel_id=1, source_target_pairs={{0,4},{1,5},{2,6},{3,7},{4,0},{5,1},{6,2},{7,3},{8,10},{9,11},{10,... | collective-permute-start | bytes 196616 | tf_op jit(solution)/shard_map/ppermute | solution.py:483
  44.3 0.7 %collective-permute-start.10 = (f32[2,128,128]{2,1,0:T(8,128)S(1)}, f32[2,128,128]{2,1,0:T(8,128)S(1)}, u32[]{:S(2)}, u32[]{:S(2)}) collective-permute-start(f32[2,128,128]{2,1,0:T(8,128)S(1)} %get-tuple-element.52), channel_id=1, source_target_pairs={{1,2},{3,4},{5,6},{2,1},{4,3},{6,5},{9,10},{11,12},{13,14},{10,9},... | collective-permute-start | bytes 393224 | tf_op jit(solution)/shard_map/ppermute | solution.py:448
  45.0 5.0 %collective-permute-start.9 = (f32[2,128,128]{2,1,0:T(8,128)S(1)}, f32[2,128,128]{2,1,0:T(8,128)S(1)}, u32[]{:S(2)}, u32[]{:S(2)}) collective-permute-start(f32[2,128,128]{2,1,0:T(8,128)S(1)} %get-tuple-element.51), channel_id=1, source_target_pairs={{0,1},{1,0},{2,3},{3,2},{4,5},{5,4},{6,7},{7,6},{8,9},{9,8},{10,11... | collective-permute-start | bytes 393224 | tf_op jit(solution)/shard_map/ppermute | solution.py:443
  49.9 0.0 collective-permute-done.11
  50.0 0.1 collective-permute-start.12
  50.0 4.3 %collective-permute-done.12 = f32[128,128]{1,0:T(8,128)S(1)} collective-permute-done((f32[128,128]{1,0:T(8,128)S(1)}, f32[128,128]{1,0:T(8,128)S(1)}, u32[]{:S(2)}, u32[]{:S(2)}) %collective-permute-start.12) | collective-permute-done | bytes 65568 | tf_op jit(solution)/shard_map/ppermute | solution.py:483
  54.3 0.1 collective-permute-start.13
  54.4 0.0 collective-permute-done.10.far_col_ref
  54.4 0.0 collective-permute-done.9.near_col_ref
  54.4 1.0 %final_sums.1 = f32[2,256,256]{2,1,0:T(8,128)} custom-call(f32[8,384,128]{2,1,0:T(8,128)S(1)} %get-tuple-element.40.grad, f32[2,64,384]{2,1,0:T(8,128)S(1)} %collective-permute-done.5.near_ref.near_row_ref, f32[2,64,384]{2,1,0:T(8,128)S(1)} %collective-permute-done.6.far_ref.far_row_ref, f32[2,128,128]{2,1,0:T(8,128)S(1)} %collective-permute-done.9.near_col_ref, ...), custom_call_target="tpu_custom_call" | custom-call | tf_op jit(solution)/shard_map/final_sums/pallas_call | solution.py:432
  55.4 0.2 collective-permute-done.13
  55.6 0.7 %maximum_select_fusion = f32[2,128,128]{2,1,0:T(8,128)} fusion(f32[1,128,128]{2,1,0:T(8,128)S(1)} %bitcast.9, f32[1,128,128]{2,1,0:T(8,128)S(1)} %bitcast.8, pred[]{:T(512)S(6)} %eq.5), kind=kLoop, calls=%fused_computation | loop fusion | flops 98304 | bytes 262145 | tf_op jit(solution)/shard_map/jit(_where)/select_n | solution.py:518
  (6 shorter events, 0.0 us)
Async XLA Ops:
  1.6 4.8 %collective-permute-start = (f32[2,64,256]{2,1,0:T(8,128)S(1)}, f32[2,64,256]{2,1,0:T(8,128)S(1)}, u32[]{:S(2)}, u32[]{:S(2)}) collective-permute-start(f32[2,64,256]{2,1,0:T(8,128)S(1)} %get-tuple-element.30), channel_id=1, source_target_pairs={{0,8},{8,0},{16,24},{24,16},{1,9},{9,1},{17,25},{25,17},{2,10},{10... | collective-permute-start | bytes 393224 | tf_op jit(solution)/shard_map/ppermute | solution.py:443
  2.2 4.3 %collective-permute-start.1 = (f32[2,64,256]{2,1,0:T(8,128)S(1)}, f32[2,64,256]{2,1,0:T(8,128)S(1)}, u32[]{:S(2)}, u32[]{:S(2)}) collective-permute-start(f32[2,64,256]{2,1,0:T(8,128)S(1)} %get-tuple-element.31), channel_id=1, source_target_pairs={{8,16},{16,8},{9,17},{17,9},{10,18},{18,10},{11,19},{19,11},{12,20... | collective-permute-start | bytes 393224 | tf_op jit(solution)/shard_map/ppermute | solution.py:448
  6.7 10.7 %collective-permute-start.2 = (f32[2,192,128]{2,1,0:T(8,128)S(1)}, f32[2,192,128]{2,1,0:T(8,128)S(1)}, u32[]{:S(2)}, u32[]{:S(2)}) collective-permute-start(f32[2,192,128]{2,1,0:T(8,128)S(1)} %get-tuple-element.33), channel_id=1, source_target_pairs={{0,1},{1,0},{2,3},{3,2},{4,5},{5,4},{6,7},{7,6},{8,9},{9,8},{10,11... | collective-permute-start | bytes 589832 | tf_op jit(solution)/shard_map/ppermute | solution.py:443
  9.2 8.1 %collective-permute-start.3 = (f32[2,192,128]{2,1,0:T(8,128)S(1)}, f32[2,192,128]{2,1,0:T(8,128)S(1)}, u32[]{:S(2)}, u32[]{:S(2)}) collective-permute-start(f32[2,192,128]{2,1,0:T(8,128)S(1)} %get-tuple-element.34), channel_id=1, source_target_pairs={{1,2},{3,4},{5,6},{2,1},{4,3},{6,5},{9,10},{11,12},{13,14},{10,9},... | collective-permute-start | bytes 589832 | tf_op jit(solution)/shard_map/ppermute | solution.py:448
  25.0 1.3 %collective-permute-start.4 = (f32[128,128]{1,0:T(8,128)S(1)}, f32[128,128]{1,0:T(8,128)S(1)}, u32[]{:S(2)}, u32[]{:S(2)}) collective-permute-start(f32[128,128]{1,0:T(8,128)S(1)} %get-tuple-element.42), channel_id=1, source_target_pairs={{0,8},{8,0},{16,24},{24,16},{1,9},{9,1},{17,25},{25,17},{2,10},{10... | collective-permute-start | bytes 196616 | tf_op jit(solution)/shard_map/ppermute | solution.py:443
  26.4 8.9 %collective-permute-start.7 = (f32[128,128]{1,0:T(8,128)S(1)}, f32[128,128]{1,0:T(8,128)S(1)}, u32[]{:S(2)}, u32[]{:S(2)}) collective-permute-start(f32[128,128]{1,0:T(8,128)S(1)} %add.17), channel_id=1, source_target_pairs={{0,1},{1,0},{2,3},{3,2},{4,5},{5,4},{6,7},{7,6},{8,9},{9,8},{10,11... | collective-permute-start | bytes 196616 | tf_op jit(solution)/shard_map/ppermute | solution.py:483
  32.7 7.0 %collective-permute-start.5 = (f32[2,64,384]{2,1,0:T(8,128)S(1)}, f32[2,64,384]{2,1,0:T(8,128)S(1)}, u32[]{:S(2)}, u32[]{:S(2)}) collective-permute-start(f32[2,64,384]{2,1,0:T(8,128)S(1)} %get-tuple-element.45), channel_id=1, source_target_pairs={{0,8},{8,0},{16,24},{24,16},{1,9},{9,1},{17,25},{25,17},{2,10},{10... | collective-permute-start | bytes 589832 | tf_op jit(solution)/shard_map/ppermute | solution.py:443
  32.8 6.9 %collective-permute-start.6 = (f32[2,64,384]{2,1,0:T(8,128)S(1)}, f32[2,64,384]{2,1,0:T(8,128)S(1)}, u32[]{:S(2)}, u32[]{:S(2)}) collective-permute-start(f32[2,64,384]{2,1,0:T(8,128)S(1)} %get-tuple-element.46), channel_id=1, source_target_pairs={{8,16},{16,8},{9,17},{17,9},{10,18},{18,10},{11,19},{19,11},{12,20... | collective-permute-start | bytes 589832 | tf_op jit(solution)/shard_map/ppermute | solution.py:448
  35.3 4.3 %collective-permute-start.8 = (f32[128,128]{1,0:T(8,128)S(1)}, f32[128,128]{1,0:T(8,128)S(1)}, u32[]{:S(2)}, u32[]{:S(2)}) collective-permute-start(f32[128,128]{1,0:T(8,128)S(1)} %add.18.a_ref), channel_id=1, source_target_pairs={{0,2},{1,3},{2,0},{3,1},{4,6},{5,7},{6,4},{7,5},{8,12},{9,13},{10,... | collective-permute-start | bytes 196616 | tf_op jit(solution)/shard_map/ppermute | solution.py:483
  39.8 10.1 %collective-permute-start.11 = (f32[128,128]{1,0:T(8,128)S(1)}, f32[128,128]{1,0:T(8,128)S(1)}, u32[]{:S(2)}, u32[]{:S(2)}) collective-permute-start(f32[128,128]{1,0:T(8,128)S(1)} %add.22), channel_id=1, source_target_pairs={{0,4},{1,5},{2,6},{3,7},{4,0},{5,1},{6,2},{7,3},{8,10},{9,11},{10,... | collective-permute-start | bytes 196616 | tf_op jit(solution)/shard_map/ppermute | solution.py:483
  44.3 10.1 %collective-permute-start.10 = (f32[2,128,128]{2,1,0:T(8,128)S(1)}, f32[2,128,128]{2,1,0:T(8,128)S(1)}, u32[]{:S(2)}, u32[]{:S(2)}) collective-permute-start(f32[2,128,128]{2,1,0:T(8,128)S(1)} %get-tuple-element.52), channel_id=1, source_target_pairs={{1,2},{3,4},{5,6},{2,1},{4,3},{6,5},{9,10},{11,12},{13,14},{10,9},... | collective-permute-start | bytes 393224 | tf_op jit(solution)/shard_map/ppermute | solution.py:448
  45.0 9.4 %collective-permute-start.9 = (f32[2,128,128]{2,1,0:T(8,128)S(1)}, f32[2,128,128]{2,1,0:T(8,128)S(1)}, u32[]{:S(2)}, u32[]{:S(2)}) collective-permute-start(f32[2,128,128]{2,1,0:T(8,128)S(1)} %get-tuple-element.51), channel_id=1, source_target_pairs={{0,1},{1,0},{2,3},{3,2},{4,5},{5,4},{6,7},{7,6},{8,9},{9,8},{10,11... | collective-permute-start | bytes 393224 | tf_op jit(solution)/shard_map/ppermute | solution.py:443
  50.0 4.3 %collective-permute-start.12 = (f32[128,128]{1,0:T(8,128)S(1)}, f32[128,128]{1,0:T(8,128)S(1)}, u32[]{:S(2)}, u32[]{:S(2)}) collective-permute-start(f32[128,128]{1,0:T(8,128)S(1)} %add.20), channel_id=1, source_target_pairs={{0,16},{1,17},{2,18},{3,19},{4,20},{5,21},{6,22},{7,23},{8,24},{9,... | collective-permute-start | bytes 196616 | tf_op jit(solution)/shard_map/ppermute | solution.py:483
  54.3 1.3 %collective-permute-start.13 = (f32[128,128]{1,0:T(8,128)S(1)}, f32[128,128]{1,0:T(8,128)S(1)}, u32[]{:S(2)}, u32[]{:S(2)}) collective-permute-start(f32[128,128]{1,0:T(8,128)S(1)} %add.21), channel_id=1, source_target_pairs={{0,8},{8,0},{16,24},{24,16},{1,9},{9,1},{17,25},{25,17},{2,10},{10... | collective-permute-start | bytes 196616 | tf_op jit(solution)/shard_map/ppermute | solution.py:443

commit v7 on v6

--- a/solution.py
+++ b/solution.py
@@ -449,12 +449,9 @@
 
 
 def doubling_steps(n_row, n_col):
-    rest = [(0, 1 << k) for k in range(1, n_col.bit_length() - 1)]
-    turned = list(rest)
-    for k in range(0, len(rest) - 1, 2):
-        turned[k], turned[k + 1] = rest[k + 1], rest[k]
-    rows = [(1 << k, 0) for k in range(1, n_row.bit_length() - 1)]
-    return list(zip(rows, rows)), list(zip(rest, turned)) + [((0, 1), (0, 1))]
+    along_cols = [(0, 1)] + [(0, 1 << k) for k in range(1, n_col.bit_length() - 1)][::-1]
+    along_rows = [(1 << k, 0) for k in range(1, n_row.bit_length() - 1)]
+    return along_rows, along_cols
 
 
 def add_kernel(a_ref, b_ref, out_ref):
@@ -473,13 +470,9 @@
     )(*in_vmem(a, b))
 
 
-def add_partner(mine, even, odd, add=jnp.add):
+def add_partner(mine, step, add=jnp.add):
     n_row, n_col = lax.axis_size("trow"), lax.axis_size("tcol")
-    pairs = []
-    for r in range(n_row):
-        for c in range(n_col):
-            dr, dc = odd if r % 2 else even
-            pairs.append((r * n_col + c, (r ^ dr) * n_col + (c ^ dc)))
+    pairs = [(r * n_col + c, (r ^ step[0]) * n_col + (c ^ step[1])) for r in range(n_row) for c in range(n_col)]
     return add(mine, lax.ppermute(mine, ("trow", "tcol"), pairs))
 
 
@@ -504,14 +497,15 @@
     mine, near_row, far_row = lax.optimization_barrier((mine, near_row, far_row))
     near_row = near_swap(near_row, "trow")
     far_row = far_swap(far_row, "trow")
-    mine = add_partner(mine, *along_cols[-1])
-    mine = add_partner(mine, *along_cols[0], add=add_call)
+    mine = add_partner(mine, along_cols[0])
+    mine = add_partner(mine, along_cols[1], add=add_call)
     near_side, far_side = side_sum_call(side, near_row, far_row)
     mine, near_side, far_side = lax.optimization_barrier((mine, near_side, far_side))
     near_col = near_swap(near_side, "tcol")
     far_col = far_swap(far_side, "tcol")
-    for step in along_cols[1:-1] + along_rows:
-        mine = add_partner(mine, *step)
+    for step in along_cols[2:] + along_rows:
+        mine = add_partner(mine, step)
+    mine, near_col, far_col = lax.optimization_barrier((mine, near_col, far_col))
     object_grad = final_call(grad, near_row, far_row, near_col, far_col)
     other = near_swap(mine, "trow")
     odd_row, _ = parities()

time: 55.5 us -> 53.7 us (0.968); the launches traced: 56.3 us -> 53.4 us
  Pallas kernels: 20.4 us -> 13.2 us
  waiting for transfers between devices: 10.4 us -> 15.4 us
  starting transfers between devices: 23.3 us -> 22.7 us
    ppermute x4, starting transfers between devices: 12.4 us -> 5.3 us  [add_partner(): return add(mine, lax.ppermute(mine, ('trow', 'tcol'), pairs))]
    ppermute x6, starting transfers between devices: 8.28 us -> 14.8 us  [near_swap(): lax.ppermute(value, axis, [(i, i ^ 1) for i in range(lax.axis_size(axis))])]
    ppermute x4, waiting for transfers between devices: 8.93 us -> 13.8 us  [add_partner(): return add(mine, lax.ppermute(mine, ('trow', 'tcol'), pairs))]
    pallas_call x1, Pallas kernels: 7.44 us -> 2.59 us  [inner_call(): pl.pallas_call(inner_kernel, out_shape=(near(window.shape), near(turned.s...]
    pallas_call x1, Pallas kernels: 7.64 us -> 5.28 us  [outer_call(): pl.pallas_call(outer_kernel, out_shape=(near(grad.shape), row, row, near(...]
  transfers between devices with their start and end apart: 14 -> 14, of which waited for: 5 -> 7; matrix products, arithmetic and copies ran while one was open for 0% -> 0% of each run, Pallas kernels for 20% -> 12%
where the time goes in v7:
time: 53.7 us; the launch traced here: 53.4 us
  starting transfers between devices  22.7 us (42%)
  waiting for transfers between devices  15.4 us (29%)
  Pallas kernels  13.2 us (25%)
  between operations  1.47 us (3%)
  other arithmetic  0.7 us (1%)
    ppermute x6, starting transfers between devices, near_swap(): lax.ppermute(value, axis, [(i, i ^ 1) for i in range(lax.axis_size(axis))])  14.8 us
    ppermute x4, waiting for transfers between devices, add_partner(): return add(mine, lax.ppermute(mine, ('trow', 'tcol'), pairs))  13.8 us
    ppermute x4, starting transfers between devices, add_partner(): return add(mine, lax.ppermute(mine, ('trow', 'tcol'), pairs))  5.3 us
    pallas_call x1, Pallas kernels, outer_call(): pl.pallas_call(outer_kernel, out_shape=(near(grad.shape), row, row, near(...  5.28 us
    pallas_call x1, Pallas kernels, ready_call(): pl.pallas_call(ready_kernel, out_shape=(pltpu.SMEM((5 * slots + 2,), jnp....  2.92 us
    ppermute x4, starting transfers between devices, far_swap(): return lax.ppermute(value, axis, pairs + [(j, i) for i, j in pairs])  2.64 us
    pallas_call x1, Pallas kernels, inner_call(): pl.pallas_call(inner_kernel, out_shape=(near(window.shape), near(turned.s...  2.59 us
    ppermute x6, waiting for transfers between devices, near_swap(): lax.ppermute(value, axis, [(i, i ^ 1) for i in range(lax.axis_size(axis))])  1.54 us
  transfers between devices with their start and end apart: 14, of which 7 were waited for; matrix products, arithmetic and copies ran while one was open for 0% of the time, Pallas kernels for 12%

profile of v7, /device:TPU:0, one launch (start us, length us, event | category | flops | bytes accessed | tf_op | source)
XLA Modules:
  0.0 53.4 jit_solution(8169531717974300013)
XLA Ops:
  0.6 1.0 %edge_rows.1 = (f32[2,64,256]{2,1,0:T(8,128)S(1)}, f32[2,64,256]{2,1,0:T(8,128)S(1)}) custom-call(f32[2,256,256]{2,1,0:T(8,128)} %centre_ref.3), custom_call_target="tpu_custom_call" | custom-call | tf_op jit(solution)/shard_map/edge_rows/pallas_call | solution.py:96
  1.6 0.5 collective-permute-start
  2.2 0.7 %collective-permute-start.1 = (f32[2,64,256]{2,1,0:T(8,128)S(1)}, f32[2,64,256]{2,1,0:T(8,128)S(1)}, u32[]{:S(2)}, u32[]{:S(2)}) collective-permute-start(f32[2,64,256]{2,1,0:T(8,128)S(1)} %get-tuple-element.34), channel_id=1, source_target_pairs={{8,16},{16,8},{9,17},{17,9},{10,18},{18,10},{11,19},{19,11},{12,20... | collective-permute-start | bytes 393224 | tf_op jit(solution)/shard_map/ppermute | solution.py:448
  3.5 2.9 %ready.1 = (s32[242]{0:T(256)S(4)}, f32[48,2,128,128]{3,2,1,0:T(8,128)S(1)}, bf16[48,128,128]{2,1,0:T(8,128)(2,1)S(1)}, bf16[4,256,256]{2,1,0:T(8,128)(2,1)S(1)}, f32[8,384,128]{2,1,0:T(8,128)S(1)}) custom-call(s32[48]{0:T(128)} %bitcast.10, s32[48]{0:T(128)} %bitcast.11, s32[8,128]{1,0:T(8,128)S(1)} %broadcast_in_dim.2.count_ref, f32[2,128,128]{2,1,0:T(8,128)} %probe_ref.1, ...), custom_call_target="tpu_custom_call" | custom-call | tf_op jit(solution)/shard_map/ready/pallas_call | solution.py:157
  6.4 0.0 collective-permute-done.near_ref
  6.4 0.0 collective-permute-done.1.far_ref
  6.4 0.2 side_columns.1
  6.7 2.6 %collective-permute-start.2 = (f32[2,192,128]{2,1,0:T(8,128)S(1)}, f32[2,192,128]{2,1,0:T(8,128)S(1)}, u32[]{:S(2)}, u32[]{:S(2)}) collective-permute-start(f32[2,192,128]{2,1,0:T(8,128)S(1)} %get-tuple-element.36), channel_id=1, source_target_pairs={{0,1},{1,0},{2,3},{3,2},{4,5},{5,4},{6,7},{7,6},{8,9},{9,8},{10,11... | collective-permute-start | bytes 589832 | tf_op jit(solution)/shard_map/ppermute | solution.py:443
  9.2 0.7 %collective-permute-start.3 = (f32[2,192,128]{2,1,0:T(8,128)S(1)}, f32[2,192,128]{2,1,0:T(8,128)S(1)}, u32[]{:S(2)}, u32[]{:S(2)}) collective-permute-start(f32[2,192,128]{2,1,0:T(8,128)S(1)} %get-tuple-element.37), channel_id=1, source_target_pairs={{1,2},{3,4},{5,6},{2,1},{4,3},{6,5},{9,10},{11,12},{13,14},{10,9},... | collective-permute-start | bytes 589832 | tf_op jit(solution)/shard_map/ppermute | solution.py:448
  9.9 2.6 %slots_inside.1 = (f32[8,384,128]{2,1,0:T(8,128)S(1)}, f32[2,128,128]{2,1,0:T(8,128)S(1)}) custom-call(s32[242]{0:T(256)S(4)} %get-tuple-element.31.plan, f32[8,384,128]{2,1,0:T(8,128)S(1)} %get-tuple-element.35.window.window_ref, f32[48,2,128,128]{3,2,1,0:T(8,128)S(1)} %get-tuple-element.38.turned, bf16[48,128,128]{2,1,0:T(8,128)(2,1)S(1)} %get-tuple-element.39.measured, ...), custom_call_target="tpu_custom_call" | custom-call | flops 10000000000 | bytes 20000000 | tf_op jit(solution)/shard_map/slots_inside/pallas_call | solution.py:303
  12.5 0.4 collective-permute-done.2.near_col_ref
  12.9 0.0 collective-permute-done.3.far_col_ref
  12.9 5.3 %slots_across.1 = (f32[8,384,128]{2,1,0:T(8,128)S(1)}, f32[2,64,384]{2,1,0:T(8,128)S(1)}, f32[2,64,384]{2,1,0:T(8,128)S(1)}, f32[2,256,128]{2,1,0:T(8,128)S(1)},...) custom-call(s32[242]{0:T(256)S(4)} %get-tuple-element.31.plan, f32[8,384,128]{2,1,0:T(8,128)S(1)} %get-tuple-element.35.window.window_ref, ...), custom_call_target="tpu_custom_call" | custom-call | flops 10000000000 | bytes 20000000 | tf_op jit(solution)/shard_map/slots_across/pallas_call | solution.py:364
  18.2 10.9 %collective-permute-start.4 = (f32[128,128]{1,0:T(8,128)S(1)}, f32[128,128]{1,0:T(8,128)S(1)}, u32[]{:S(2)}, u32[]{:S(2)}) collective-permute-start(f32[128,128]{1,0:T(8,128)S(1)} %get-tuple-element.45), channel_id=1, source_target_pairs={{0,8},{8,0},{16,24},{24,16},{1,9},{9,1},{17,25},{25,17},{2,10},{10... | collective-permute-start | bytes 196616 | tf_op jit(solution)/shard_map/ppermute | solution.py:443
  29.1 0.9 %collective-permute-done.4 = f32[128,128]{1,0:T(8,128)S(1)} collective-permute-done((f32[128,128]{1,0:T(8,128)S(1)}, f32[128,128]{1,0:T(8,128)S(1)}, u32[]{:S(2)}, u32[]{:S(2)}) %collective-permute-start.4) | collective-permute-done | bytes 65568 | tf_op jit(solution)/shard_map/ppermute | solution.py:443
  30.0 2.8 %collective-permute-start.7 = (f32[128,128]{1,0:T(8,128)S(1)}, f32[128,128]{1,0:T(8,128)S(1)}, u32[]{:S(2)}, u32[]{:S(2)}) collective-permute-start(f32[128,128]{1,0:T(8,128)S(1)} %add.17), channel_id=1, source_target_pairs={{0,1},{1,0},{2,3},{3,2},{4,5},{5,4},{6,7},{7,6},{8,9},{9,8},{10,11... | collective-permute-start | bytes 196616 | tf_op jit(solution)/shard_map/ppermute | solution.py:476
  32.8 0.1 collective-permute-start.5
  32.9 0.7 %collective-permute-start.6 = (f32[2,64,384]{2,1,0:T(8,128)S(1)}, f32[2,64,384]{2,1,0:T(8,128)S(1)}, u32[]{:S(2)}, u32[]{:S(2)}) collective-permute-start(f32[2,64,384]{2,1,0:T(8,128)S(1)} %get-tuple-element.49), channel_id=1, source_target_pairs={{8,16},{16,8},{9,17},{17,9},{10,18},{18,10},{11,19},{19,11},{12,20... | collective-permute-start | bytes 589832 | tf_op jit(solution)/shard_map/ppermute | solution.py:448
  33.6 1.9 %collective-permute-done.7 = f32[128,128]{1,0:T(8,128)S(1)} collective-permute-done((f32[128,128]{1,0:T(8,128)S(1)}, f32[128,128]{1,0:T(8,128)S(1)}, u32[]{:S(2)}, u32[]{:S(2)}) %collective-permute-start.7) | collective-permute-done | bytes 65568 | tf_op jit(solution)/shard_map/ppermute | solution.py:476
  35.5 2.4 %collective-permute-start.8 = (f32[128,128]{1,0:T(8,128)S(1)}, f32[128,128]{1,0:T(8,128)S(1)}, u32[]{:S(2)}, u32[]{:S(2)}) collective-permute-start(f32[128,128]{1,0:T(8,128)S(1)} %add.18.a_ref), channel_id=1, source_target_pairs={{0,4},{1,5},{2,6},{3,7},{4,0},{5,1},{6,2},{7,3},{8,12},{9,13},{10,... | collective-permute-start | bytes 196616 | tf_op jit(solution)/shard_map/ppermute | solution.py:476
  37.8 4.7 %collective-permute-done.8.b_ref = f32[128,128]{1,0:T(8,128)S(1)} collective-permute-done((f32[128,128]{1,0:T(8,128)S(1)}, f32[128,128]{1,0:T(8,128)S(1)}, u32[]{:S(2)}, u32[]{:S(2)}) %collective-permute-start.8) | collective-permute-done | bytes 65568 | tf_op jit(solution)/shard_map/ppermute | solution.py:476
  42.6 0.0 collective-permute-done.5.near_ref.near_row_ref
  42.6 0.0 collective-permute-done.6.far_ref.far_row_ref
  42.6 0.1 side_sums.1
  42.8 0.1 collective-permute-start.9
  42.8 0.6 %collective-permute-start.11 = (f32[2,128,128]{2,1,0:T(8,128)S(1)}, f32[2,128,128]{2,1,0:T(8,128)S(1)}, u32[]{:S(2)}, u32[]{:S(2)}) collective-permute-start(f32[2,128,128]{2,1,0:T(8,128)S(1)} %get-tuple-element.55), channel_id=1, source_target_pairs={{0,1},{1,0},{2,3},{3,2},{4,5},{5,4},{6,7},{7,6},{8,9},{9,8},{10,11... | collective-permute-start | bytes 393224 | tf_op jit(solution)/shard_map/ppermute | solution.py:443
  43.5 0.7 %collective-permute-start.12 = (f32[2,128,128]{2,1,0:T(8,128)S(1)}, f32[2,128,128]{2,1,0:T(8,128)S(1)}, u32[]{:S(2)}, u32[]{:S(2)}) collective-permute-start(f32[2,128,128]{2,1,0:T(8,128)S(1)} %get-tuple-element.56), channel_id=1, source_target_pairs={{1,2},{3,4},{5,6},{2,1},{4,3},{6,5},{9,10},{11,12},{13,14},{10,9},... | collective-permute-start | bytes 393224 | tf_op jit(solution)/shard_map/ppermute | solution.py:448
  44.1 3.0 %collective-permute-done.9 = f32[128,128]{1,0:T(8,128)S(1)} collective-permute-done((f32[128,128]{1,0:T(8,128)S(1)}, f32[128,128]{1,0:T(8,128)S(1)}, u32[]{:S(2)}, u32[]{:S(2)}) %collective-permute-start.9) | collective-permute-done | bytes 65568 | tf_op jit(solution)/shard_map/ppermute | solution.py:476
  47.1 0.1 collective-permute-start.10
  47.2 4.3 %collective-permute-done.10 = f32[128,128]{1,0:T(8,128)S(1)} collective-permute-done((f32[128,128]{1,0:T(8,128)S(1)}, f32[128,128]{1,0:T(8,128)S(1)}, u32[]{:S(2)}, u32[]{:S(2)}) %collective-permute-start.10) | collective-permute-done | bytes 65568 | tf_op jit(solution)/shard_map/ppermute | solution.py:476
  51.4 0.0 collective-permute-done.11.near_col_ref
  51.5 0.0 collective-permute-done.12.far_col_ref
  51.5 0.1 collective-permute-start.13
  51.6 1.0 %final_sums.1 = f32[2,256,256]{2,1,0:T(8,128)} custom-call(f32[8,384,128]{2,1,0:T(8,128)S(1)} %get-tuple-element.43.grad, f32[2,64,384]{2,1,0:T(8,128)S(1)} %collective-permute-done.5.near_ref.near_row_ref, f32[2,64,384]{2,1,0:T(8,128)S(1)} %collective-permute-done.6.far_ref.far_row_ref, f32[2,128,128]{2,1,0:T(8,128)S(1)} %collective-permute-done.11.near_col_ref, ...), custom_call_target="tpu_custom_call" | custom-call | tf_op jit(solution)/shard_map/final_sums/pallas_call | solution.py:432
  52.5 0.2 collective-permute-done.13
  52.8 0.7 %maximum_select_fusion = f32[2,128,128]{2,1,0:T(8,128)} fusion(f32[1,128,128]{2,1,0:T(8,128)S(1)} %bitcast.9, f32[1,128,128]{2,1,0:T(8,128)S(1)} %bitcast.8, pred[]{:T(512)S(6)} %eq.5), kind=kLoop, calls=%fused_computation | loop fusion | flops 98304 | bytes 262145 | tf_op jit(solution)/shard_map/jit(_where)/select_n | solution.py:512
  (6 shorter events, 0.0 us)
Async XLA Ops:
  1.6 4.8 %collective-permute-start = (f32[2,64,256]{2,1,0:T(8,128)S(1)}, f32[2,64,256]{2,1,0:T(8,128)S(1)}, u32[]{:S(2)}, u32[]{:S(2)}) collective-permute-start(f32[2,64,256]{2,1,0:T(8,128)S(1)} %get-tuple-element.33), channel_id=1, source_target_pairs={{0,8},{8,0},{16,24},{24,16},{1,9},{9,1},{17,25},{25,17},{2,10},{10... | collective-permute-start | bytes 393224 | tf_op jit(solution)/shard_map/ppermute | solution.py:443
  2.2 4.3 %collective-permute-start.1 = (f32[2,64,256]{2,1,0:T(8,128)S(1)}, f32[2,64,256]{2,1,0:T(8,128)S(1)}, u32[]{:S(2)}, u32[]{:S(2)}) collective-permute-start(f32[2,64,256]{2,1,0:T(8,128)S(1)} %get-tuple-element.34), channel_id=1, source_target_pairs={{8,16},{16,8},{9,17},{17,9},{10,18},{18,10},{11,19},{19,11},{12,20... | collective-permute-start | bytes 393224 | tf_op jit(solution)/shard_map/ppermute | solution.py:448
  6.7 6.2 %collective-permute-start.2 = (f32[2,192,128]{2,1,0:T(8,128)S(1)}, f32[2,192,128]{2,1,0:T(8,128)S(1)}, u32[]{:S(2)}, u32[]{:S(2)}) collective-permute-start(f32[2,192,128]{2,1,0:T(8,128)S(1)} %get-tuple-element.36), channel_id=1, source_target_pairs={{0,1},{1,0},{2,3},{3,2},{4,5},{5,4},{6,7},{7,6},{8,9},{9,8},{10,11... | collective-permute-start | bytes 589832 | tf_op jit(solution)/shard_map/ppermute | solution.py:443
  9.2 3.7 %collective-permute-start.3 = (f32[2,192,128]{2,1,0:T(8,128)S(1)}, f32[2,192,128]{2,1,0:T(8,128)S(1)}, u32[]{:S(2)}, u32[]{:S(2)}) collective-permute-start(f32[2,192,128]{2,1,0:T(8,128)S(1)} %get-tuple-element.37), channel_id=1, source_target_pairs={{1,2},{3,4},{5,6},{2,1},{4,3},{6,5},{9,10},{11,12},{13,14},{10,9},... | collective-permute-start | bytes 589832 | tf_op jit(solution)/shard_map/ppermute | solution.py:448
  18.2 11.8 %collective-permute-start.4 = (f32[128,128]{1,0:T(8,128)S(1)}, f32[128,128]{1,0:T(8,128)S(1)}, u32[]{:S(2)}, u32[]{:S(2)}) collective-permute-start(f32[128,128]{1,0:T(8,128)S(1)} %get-tuple-element.45), channel_id=1, source_target_pairs={{0,8},{8,0},{16,24},{24,16},{1,9},{9,1},{17,25},{25,17},{2,10},{10... | collective-permute-start | bytes 196616 | tf_op jit(solution)/shard_map/ppermute | solution.py:443
  30.0 5.4 %collective-permute-start.7 = (f32[128,128]{1,0:T(8,128)S(1)}, f32[128,128]{1,0:T(8,128)S(1)}, u32[]{:S(2)}, u32[]{:S(2)}) collective-permute-start(f32[128,128]{1,0:T(8,128)S(1)} %add.17), channel_id=1, source_target_pairs={{0,1},{1,0},{2,3},{3,2},{4,5},{5,4},{6,7},{7,6},{8,9},{9,8},{10,11... | collective-permute-start | bytes 196616 | tf_op jit(solution)/shard_map/ppermute | solution.py:476
  32.8 9.7 %collective-permute-start.5 = (f32[2,64,384]{2,1,0:T(8,128)S(1)}, f32[2,64,384]{2,1,0:T(8,128)S(1)}, u32[]{:S(2)}, u32[]{:S(2)}) collective-permute-start(f32[2,64,384]{2,1,0:T(8,128)S(1)} %get-tuple-element.48), channel_id=1, source_target_pairs={{0,8},{8,0},{16,24},{24,16},{1,9},{9,1},{17,25},{25,17},{2,10},{10... | collective-permute-start | bytes 589832 | tf_op jit(solution)/shard_map/ppermute | solution.py:443
  32.9 9.7 %collective-permute-start.6 = (f32[2,64,384]{2,1,0:T(8,128)S(1)}, f32[2,64,384]{2,1,0:T(8,128)S(1)}, u32[]{:S(2)}, u32[]{:S(2)}) collective-permute-start(f32[2,64,384]{2,1,0:T(8,128)S(1)} %get-tuple-element.49), channel_id=1, source_target_pairs={{8,16},{16,8},{9,17},{17,9},{10,18},{18,10},{11,19},{19,11},{12,20... | collective-permute-start | bytes 589832 | tf_op jit(solution)/shard_map/ppermute | solution.py:448
  35.5 7.1 %collective-permute-start.8 = (f32[128,128]{1,0:T(8,128)S(1)}, f32[128,128]{1,0:T(8,128)S(1)}, u32[]{:S(2)}, u32[]{:S(2)}) collective-permute-start(f32[128,128]{1,0:T(8,128)S(1)} %add.18.a_ref), channel_id=1, source_target_pairs={{0,4},{1,5},{2,6},{3,7},{4,0},{5,1},{6,2},{7,3},{8,12},{9,13},{10,... | collective-permute-start | bytes 196616 | tf_op jit(solution)/shard_map/ppermute | solution.py:476
  42.8 4.3 %collective-permute-start.9 = (f32[128,128]{1,0:T(8,128)S(1)}, f32[128,128]{1,0:T(8,128)S(1)}, u32[]{:S(2)}, u32[]{:S(2)}) collective-permute-start(f32[128,128]{1,0:T(8,128)S(1)} %add.22), channel_id=1, source_target_pairs={{0,2},{1,3},{2,0},{3,1},{4,6},{5,7},{6,4},{7,5},{8,10},{9,11},{10,... | collective-permute-start | bytes 196616 | tf_op jit(solution)/shard_map/ppermute | solution.py:476
  42.8 8.6 %collective-permute-start.11 = (f32[2,128,128]{2,1,0:T(8,128)S(1)}, f32[2,128,128]{2,1,0:T(8,128)S(1)}, u32[]{:S(2)}, u32[]{:S(2)}) collective-permute-start(f32[2,128,128]{2,1,0:T(8,128)S(1)} %get-tuple-element.55), channel_id=1, source_target_pairs={{0,1},{1,0},{2,3},{3,2},{4,5},{5,4},{6,7},{7,6},{8,9},{9,8},{10,11... | collective-permute-start | bytes 393224 | tf_op jit(solution)/shard_map/ppermute | solution.py:443
  43.5 8.0 %collective-permute-start.12 = (f32[2,128,128]{2,1,0:T(8,128)S(1)}, f32[2,128,128]{2,1,0:T(8,128)S(1)}, u32[]{:S(2)}, u32[]{:S(2)}) collective-permute-start(f32[2,128,128]{2,1,0:T(8,128)S(1)} %get-tuple-element.56), channel_id=1, source_target_pairs={{1,2},{3,4},{5,6},{2,1},{4,3},{6,5},{9,10},{11,12},{13,14},{10,9},... | collective-permute-start | bytes 393224 | tf_op jit(solution)/shard_map/ppermute | solution.py:448
  47.1 4.3 %collective-permute-start.10 = (f32[128,128]{1,0:T(8,128)S(1)}, f32[128,128]{1,0:T(8,128)S(1)}, u32[]{:S(2)}, u32[]{:S(2)}) collective-permute-start(f32[128,128]{1,0:T(8,128)S(1)} %add.19), channel_id=1, source_target_pairs={{0,16},{1,17},{2,18},{3,19},{4,20},{5,21},{6,22},{7,23},{8,24},{9,... | collective-permute-start | bytes 196616 | tf_op jit(solution)/shard_map/ppermute | solution.py:476
  51.5 1.3 %collective-permute-start.13 = (f32[128,128]{1,0:T(8,128)S(1)}, f32[128,128]{1,0:T(8,128)S(1)}, u32[]{:S(2)}, u32[]{:S(2)}) collective-permute-start(f32[128,128]{1,0:T(8,128)S(1)} %add.20), channel_id=1, source_target_pairs={{0,8},{8,0},{16,24},{24,16},{1,9},{9,1},{17,25},{25,17},{2,10},{10... | collective-permute-start | bytes 196616 | tf_op jit(solution)/shard_map/ppermute | solution.py:443

commit v8 on v7

--- a/solution.py
+++ b/solution.py
@@ -9,6 +9,7 @@
 LANES = 128
 VMEM_BYTES = 24 * 1024 * 1024
 GROUP = 8
+ADDED = 4
 F32 = jnp.float32
 HBM = pl.BlockSpec(memory_space=pltpu.HBM)
 VMEM = pl.BlockSpec(memory_space=pltpu.VMEM)
@@ -208,23 +209,27 @@
     )(*in_vmem(window, near_row, far_row))
 
 
-def run_slots(groups, start, inner, live, plan, window, turned, measured, table, grad, probe_sum):
-    slots = measured.shape[0]
-    size = turned.shape[2]
-    columns = window.shape[0] // 2
-    lane = lax.broadcasted_iota(jnp.int32, (size, LANES), 1)
-
+def finder(plan, slots, start, inner, live):
     def find(index):
         at = jnp.where(index < inner, start + index, jnp.maximum(slots - 1 - (index - inner), 0))
         is_live = index < live
         slot = plan[jnp.where(is_live, at, jnp.where(inner > 0, start, slots - 1))]
         place = slots + 2 + 3 * slot
         scale = jnp.where(is_live, 2.0, 0.0).astype(F32)
-        return slot, plan[place], plan[place + 1], plan[place + 2], scale
+        return slot, plan[place], plan[place + 1], plan[place + 2], scale, jnp.where(is_live, slot, slots)
+
+    return find
+
+
+def run_slots(groups, find, window, turned, measured, table, exits, probe_sum):
+    size = turned.shape[2]
+    columns = window.shape[0] // 2
+    lane = lax.broadcasted_iota(jnp.int32, (size, LANES), 1)
+    exits[exits.shape[0] - 1] = jnp.zeros(exits.shape[1:], F32)
 
     def load(pair):
         kept, waves = [], []
-        for slot, row, tile, turn, _ in pair:
+        for slot, row, tile, turn, _, _ in pair:
             here = lane >= turn
             patch = [
                 jnp.where(
@@ -253,28 +258,24 @@
     def weigh(pair, psi):
         real, imag = psi[:size], psi[size:]
         weights = []
-        for member, (slot, _, _, _, scale) in enumerate(pair):
+        for member, (slot, _, _, _, scale, _) in enumerate(pair):
             lanes = slice(member * size, (member + 1) * size)
             power = real[:, lanes] * real[:, lanes] + imag[:, lanes] * imag[:, lanes]
             weights.append((power - measured[slot].astype(F32)) * scale)
         weight = jnp.concatenate(weights, axis=1)
         return jnp.concatenate([weight * real, weight * imag], axis=0)
 
-    def add_up(pair, kept, exits):
-        for member, (slot, row, tile, turn, _) in enumerate(pair):
+    def add_up(pair, kept, pair_exits):
+        for member, (_, _, _, turn, _, kept_at) in enumerate(pair):
             patch = kept[member]
-            probe = [turned[slot, plane] for plane in range(2)]
-            here = lane >= turn
-            exit_real = exits[member * size : (member + 1) * size, :size]
-            exit_imag = exits[member * size : (member + 1) * size, size:]
+            exit_real = pair_exits[member * size : (member + 1) * size, :size]
+            exit_imag = pair_exits[member * size : (member + 1) * size, size:]
+            exits[kept_at, 0] = exit_real
+            exits[kept_at, 1] = exit_imag
             terms = (patch[0] * exit_real + patch[1] * exit_imag, patch[0] * exit_imag - patch[1] * exit_real)
-            adds = (probe[0] * exit_real + probe[1] * exit_imag, probe[0] * exit_imag - probe[1] * exit_real)
             back = (LANES - turn) & (LANES - 1)
             for plane in range(2):
                 probe_sum[plane] += pltpu.roll(terms[plane], back, axis=1)
-                at = plane * columns + tile
-                grad[at, pl.ds(row, size), :] += jnp.where(here, adds[plane], 0.0)
-                grad[at + 1, pl.ds(row, size), :] += jnp.where(here, 0.0, adds[plane])
 
     def step(group, carry):
         slots = [find(group * GROUP + member) for member in range(GROUP)]
@@ -291,18 +292,19 @@
     lax.fori_loop(0, groups, step, 0)
 
 
-def inner_kernel(plan, window, turned, measured, table, grad, probe_sum):
-    grad[...] = jnp.zeros_like(grad)
+def inner_kernel(plan, window, turned, measured, table, exits, probe_sum):
+    slots = measured.shape[0]
     probe_sum[...] = jnp.zeros_like(probe_sum)
-    groups = plan[measured.shape[0]] // GROUP
-    here = groups * GROUP
-    run_slots(groups, 0, here, here, plan, window, turned, measured, table, grad, probe_sum)
+    groups = plan[slots] // GROUP
+    find = finder(plan, slots, 0, groups * GROUP, groups * GROUP)
+    run_slots(groups, find, window, turned, measured, table, exits, probe_sum)
 
 
 def inner_call(plan, window, turned, measured, tables):
+    slots = measured.shape[0]
     return pl.pallas_call(
         inner_kernel,
-        out_shape=(near(window.shape), near(turned.shape[1:])),
+        out_shape=(near((slots + 1,) + turned.shape[1:]), near(turned.shape[1:])),
         in_specs=[SMEM] + [VMEM] * 4,
         out_specs=(VMEM,) * 2,
         compiler_params=PARAMS,
@@ -312,18 +314,15 @@
 
 
 def outer_kernel(
-    plan, window_ref, near_col_ref, far_col_ref, turned, measured, table, grad_ref, probe_ref,
-    grad, near_row_out, far_row_out, side_out, mine_out, other_out, window, probe_sum,
+    plan, window_ref, near_col_ref, far_col_ref, turned, measured, table, probe_ref,
+    exits, mine_out, other_out, window, probe_sum,
 ):
     slots = measured.shape[0]
     margin = turned.shape[2] // 2
     columns = window.shape[0] // 2
-    tall = window.shape[1]
-    half = tall // 2
+    half = window.shape[1] // 2
     odd_row, odd_col = parities()
-    near, far = place_of(odd_row, 0, tall - margin)
     probe_sum[...] = probe_ref[...]
-    grad[...] = grad_ref[...]
     for plane in range(2):
         own = slice(plane * columns + 1, (plane + 1) * columns - 1)
         window[own] = window_ref[own]
@@ -333,14 +332,62 @@
             window[tile, :half] = ref[plane]
             window[tile, half:] = pltpu.roll(ref[plane], margin, axis=1)
     start = plan[slots] // GROUP * GROUP
-    inner = plan[slots] - start
     live = plan[slots + 1] - start
-    run_slots(
-        (live + GROUP - 1) // GROUP, start, inner, live, plan, window, turned, measured, table, grad, probe_sum
-    )
+    find = finder(plan, slots, start, plan[slots] - start, live)
+    run_slots((live + GROUP - 1) // GROUP, find, window, turned, measured, table, exits, probe_sum)
     factor = 1.0 / np.sqrt(np.float32(lax.axis_size("trow") * lax.axis_size("tcol") * slots))
     mine_out[...] = probe_sum[odd_row] * factor
     other_out[...] = probe_sum[1 - odd_row] * factor
+
+
+def outer_call(plan, window, near_col, far_col, turned, measured, tables, probe_sum):
+    slots = measured.shape[0]
+    part = near(probe_sum.shape[1:])
+    return pl.pallas_call(
+        outer_kernel,
+        out_shape=(near((slots + 1,) + turned.shape[1:]), part, part),
+        in_specs=[SMEM] + [VMEM] * 7,
+        out_specs=(VMEM,) * 3,
+        scratch_shapes=[pltpu.VMEM(window.shape, F32), pltpu.VMEM(probe_sum.shape, F32)],
+        compiler_params=PARAMS,
+        cost_estimate=pl.CostEstimate(flops=10**10, bytes_accessed=2 * 10**7, transcendentals=0),
+        name="slots_across",
+    )(*in_smem(plan), *in_vmem(window, near_col, far_col, turned, measured, tables, probe_sum))
+
+
+def object_kernel(plan, turned, inner_exits, outer_exits, grad, near_row_out, far_row_out, side_out):
+    slots = turned.shape[0]
+    size = turned.shape[2]
+    margin = size // 2
+    columns = grad.shape[0] // 2
+    tall = grad.shape[1]
+    odd_row, _ = parities()
+    near, far = place_of(odd_row, 0, tall - margin)
+    lane = lax.broadcasted_iota(jnp.int32, (size, LANES), 1)
+    grad[...] = jnp.zeros_like(grad)
+
+    def add_some(find, exits):
+        def step(index, carry):
+            for member in range(ADDED):
+                slot, row, tile, turn, _, kept_at = find(index * ADDED + member)
+                here = lane >= turn
+                probe = [turned[slot, plane] for plane in range(2)]
+                exit_real, exit_imag = exits[kept_at, 0], exits[kept_at, 1]
+                adds = (probe[0] * exit_real + probe[1] * exit_imag, probe[0] * exit_imag - probe[1] * exit_real)
+                for plane in range(2):
+                    at = plane * columns + tile
+                    grad[at, pl.ds(row, size), :] += jnp.where(here, adds[plane], 0.0)
+                    grad[at + 1, pl.ds(row, size), :] += jnp.where(here, 0.0, adds[plane])
+            return carry
+
+        return step
+
+    start = plan[slots] // GROUP * GROUP
+    live = plan[slots + 1] - start
+    lax.fori_loop(0, start // ADDED, add_some(finder(plan, slots, 0, start, start), inner_exits), 0)
+    lax.fori_loop(
+        0, (live + ADDED - 1) // ADDED, add_some(finder(plan, slots, start, plan[slots] - start, live), outer_exits), 0
+    )
     narrow = lax.broadcasted_iota(jnp.int32, (margin, LANES), 1) < margin
     for plane in range(2):
         base = plane * columns
@@ -355,22 +402,18 @@
             side_out[plane, row - margin : row] = jnp.where(narrow, grad[right, rows, :], grad[left, rows, :])
 
 
-def outer_call(plan, window, near_col, far_col, turned, measured, tables, grad, probe_sum):
+def object_call(plan, window, turned, inner_exits, outer_exits):
     size = turned.shape[2]
-    margin = size // 2
-    columns = window.shape[0] // 2
-    row = near((2, margin, (columns - 1) * LANES))
-    part = near((size, size))
-    return pl.pallas_call(
-        outer_kernel,
-        out_shape=(near(grad.shape), row, row, near((2, window.shape[1] - size, LANES)), part, part),
-        in_specs=[SMEM] + [VMEM] * 8,
-        out_specs=(VMEM,) * 6,
-        scratch_shapes=[pltpu.VMEM(window.shape, F32), pltpu.VMEM(probe_sum.shape, F32)],
-        compiler_params=PARAMS,
-        cost_estimate=pl.CostEstimate(flops=10**10, bytes_accessed=2 * 10**7, transcendentals=0),
-        name="slots_across",
-    )(*in_smem(plan), *in_vmem(window, near_col, far_col, turned, measured, tables, grad, probe_sum))
+    row = near((2, size // 2, (window.shape[0] // 2 - 1) * LANES))
+    return pl.pallas_call(
+        object_kernel,
+        out_shape=(near(window.shape), row, row, near((2, window.shape[1] - size, LANES))),
+        in_specs=[SMEM] + [VMEM] * 3,
+        out_specs=(VMEM,) * 4,
+        compiler_params=PARAMS,
+        cost_estimate=pl.CostEstimate(flops=2 * 10**9, bytes_accessed=10**6, transcendentals=0),
+        name="object_sums",
+    )(*in_smem(plan), *in_vmem(turned, inner_exits, outer_exits))
 
 
 def side_sum_kernel(side_ref, near_ref, far_ref, near_out, far_out, side):
@@ -487,14 +530,13 @@
     window, near_side, far_side = side_call(window, near_row, far_row)
     far_col = far_swap(far_side, "tcol")
     near_col = near_swap(near_side, "tcol")
-    grad, probe_sum = inner_call(plan, window, turned, measured, tables)
-    grad, near_row, far_row, side, mine, other = outer_call(
-        plan, window, near_col, far_col, turned, measured, tables, grad, probe_sum
-    )
+    inner_exits, probe_sum = inner_call(plan, window, turned, measured, tables)
+    outer_exits, mine, other = outer_call(plan, window, near_col, far_col, turned, measured, tables, probe_sum)
 
     along_rows, along_cols = doubling_steps(lax.axis_size("trow"), lax.axis_size("tcol"))
     mine = mine + near_swap(other, "trow")
-    mine, near_row, far_row = lax.optimization_barrier((mine, near_row, far_row))
+    mine, outer_exits = lax.optimization_barrier((mine, outer_exits))
+    grad, near_row, far_row, side = object_call(plan, window, turned, inner_exits, outer_exits)
     near_row = near_swap(near_row, "trow")
     far_row = far_swap(far_row, "trow")
     mine = add_partner(mine, along_cols[0])

time: 53.7 us -> 52.6 us (0.980)
  the two profiles are of different devices: /device:TPU:0 before, /device:TPU:7 now
where the time goes in v8:
time: 52.6 us; the launch traced here: 52.5 us
  starting transfers between devices  30.5 us (58%)
  Pallas kernels  13.4 us (25%)
  waiting for transfers between devices  6.43 us (12%)
  between operations  1.47 us (3%)
  other arithmetic  0.71 us (1%)
    ppermute x6, starting transfers between devices, near_swap(): lax.ppermute(value, axis, [(i, i ^ 1) for i in range(lax.axis_size(axis))])  13.7 us
    ppermute x4, starting transfers between devices, add_partner(): return add(mine, lax.ppermute(mine, ('trow', 'tcol'), pairs))  9.35 us
    ppermute x4, starting transfers between devices, far_swap(): return lax.ppermute(value, axis, pairs + [(j, i) for i, j in pairs])  7.47 us
    pallas_call x1, Pallas kernels, outer_call(): pl.pallas_call(outer_kernel, out_shape=(near((slots + 1,) + turned.shape[...  4.6 us
    ppermute x4, waiting for transfers between devices, add_partner(): return add(mine, lax.ppermute(mine, ('trow', 'tcol'), pairs))  4.46 us
    pallas_call x1, Pallas kernels, ready_call(): pl.pallas_call(ready_kernel, out_shape=(pltpu.SMEM((5 * slots + 2,), jnp....  2.92 us
    pallas_call x1, Pallas kernels, inner_call(): pl.pallas_call(inner_kernel, out_shape=(near((slots + 1,) + turned.shape[...  2.21 us
    pallas_call x1, Pallas kernels, object_call(): pl.pallas_call(object_kernel, out_shape=(near(window.shape), row, row, ne...  1.32 us
  transfers between devices with their start and end apart: 14, of which 5 were waited for; matrix products, arithmetic and copies ran while one was open for 0% of the time, Pallas kernels for 14%

profile of v8, /device:TPU:7, one launch (start us, length us, event | category | flops | bytes accessed | tf_op | source)
XLA Modules:
  0.0 52.5 jit_solution(1321715137372665618)
XLA Ops:
  0.6 1.0 %edge_rows.1 = (f32[2,64,256]{2,1,0:T(8,128)S(1)}, f32[2,64,256]{2,1,0:T(8,128)S(1)}) custom-call(f32[2,256,256]{2,1,0:T(8,128)} %centre_ref.3), custom_call_target="tpu_custom_call" | custom-call | tf_op jit(solution)/shard_map/edge_rows/pallas_call | solution.py:97
  1.6 0.7 %collective-permute-start = (f32[2,64,256]{2,1,0:T(8,128)S(1)}, f32[2,64,256]{2,1,0:T(8,128)S(1)}, u32[]{:S(2)}, u32[]{:S(2)}) collective-permute-start(f32[2,64,256]{2,1,0:T(8,128)S(1)} %get-tuple-element.34), channel_id=1, source_target_pairs={{0,8},{8,0},{16,24},{24,16},{1,9},{9,1},{17,25},{25,17},{2,10},{10... | collective-permute-start | bytes 393224 | tf_op jit(solution)/shard_map/ppermute | solution.py:486
  2.4 0.7 %collective-permute-start.1 = (f32[2,64,256]{2,1,0:T(8,128)S(1)}, f32[2,64,256]{2,1,0:T(8,128)S(1)}, u32[]{:S(2)}, u32[]{:S(2)}) collective-permute-start(f32[2,64,256]{2,1,0:T(8,128)S(1)} %get-tuple-element.35), channel_id=1, source_target_pairs={{8,16},{16,8},{9,17},{17,9},{10,18},{18,10},{11,19},{19,11},{12,20... | collective-permute-start | bytes 393224 | tf_op jit(solution)/shard_map/ppermute | solution.py:491
  3.7 2.9 %ready.1 = (s32[242]{0:T(256)S(4)}, f32[48,2,128,128]{3,2,1,0:T(8,128)S(1)}, bf16[48,128,128]{2,1,0:T(8,128)(2,1)S(1)}, bf16[4,256,256]{2,1,0:T(8,128)(2,1)S(1)}, f32[8,384,128]{2,1,0:T(8,128)S(1)}) custom-call(s32[48]{0:T(128)} %bitcast.10, s32[48]{0:T(128)} %bitcast.11, s32[8,128]{1,0:T(8,128)S(1)} %broadcast_in_dim.2.count_ref, f32[2,128,128]{2,1,0:T(8,128)} %probe_ref.1, ...), custom_call_target="tpu_custom_call" | custom-call | tf_op jit(solution)/shard_map/ready/pallas_call | solution.py:158
  6.6 0.0 collective-permute-done.near_ref
  6.6 0.0 collective-permute-done.1.far_ref
  6.7 0.2 side_columns.1
  6.9 0.3 collective-permute-start.2
  7.2 4.1 %collective-permute-start.3 = (f32[2,192,128]{2,1,0:T(8,128)S(1)}, f32[2,192,128]{2,1,0:T(8,128)S(1)}, u32[]{:S(2)}, u32[]{:S(2)}) collective-permute-start(f32[2,192,128]{2,1,0:T(8,128)S(1)} %get-tuple-element.41), channel_id=1, source_target_pairs={{1,2},{3,4},{5,6},{2,1},{4,3},{6,5},{9,10},{11,12},{13,14},{10,9},... | collective-permute-start | bytes 589832 | tf_op jit(solution)/shard_map/ppermute | solution.py:491
  11.3 2.2 %slots_inside.1 = (f32[49,2,128,128]{3,2,1,0:T(8,128)S(1)}, f32[2,128,128]{2,1,0:T(8,128)S(1)}) custom-call(s32[242]{0:T(256)S(4)} %get-tuple-element.31.plan, f32[8,384,128]{2,1,0:T(8,128)S(1)} %get-tuple-element.36.window.window_ref, f32[48,2,128,128]{3,2,1,0:T(8,128)S(1)} %get-tuple-element.32.turned, ...), custom_call_target="tpu_custom_call" | custom-call | flops 10000000000 | bytes 20000000 | tf_op jit(solution)/shard_map/slots_inside/pallas_call | solution.py:305
  13.6 0.0 collective-permute-done.2.near_col_ref
  13.6 1.1 %collective-permute-done.3.far_col_ref = f32[2,192,128]{2,1,0:T(8,128)S(1)} collective-permute-done((f32[2,192,128]{2,1,0:T(8,128)S(1)}, f32[2,192,128]{2,1,0:T(8,128)S(1)}, u32[]{:S(2)}, u32[]{:S(2)}) %collective-permute-start.3) | collective-permute-done | bytes 196640 | tf_op jit(solution)/shard_map/ppermute | solution.py:491
  14.6 4.6 %slots_across.1 = (f32[49,2,128,128]{3,2,1,0:T(8,128)S(1)}, f32[128,128]{1,0:T(8,128)S(1)}, f32[128,128]{1,0:T(8,128)S(1)}) custom-call(s32[242]{0:T(256)S(4)} %get-tuple-element.31.plan, f32[8,384,128]{2,1,0:T(8,128)S(1)} %get-tuple-element.36.window.window_ref, f32[2,192,128]{2,1,0:T(8,128)S(1)} %collective-permute-done.2.near_col_ref, ...), custom_call_target="tpu_custom_call" | custom-call | flops 10000000000 | bytes 20000000 | tf_op jit(solution)/shard_map/slots_across/pallas_call | solution.py:346
  19.2 6.5 %collective-permute-start.4 = (f32[128,128]{1,0:T(8,128)S(1)}, f32[128,128]{1,0:T(8,128)S(1)}, u32[]{:S(2)}, u32[]{:S(2)}) collective-permute-start(f32[128,128]{1,0:T(8,128)S(1)} %get-tuple-element.44), channel_id=1, source_target_pairs={{0,8},{8,0},{16,24},{24,16},{1,9},{9,1},{17,25},{25,17},{2,10},{10... | collective-permute-start | bytes 196616 | tf_op jit(solution)/shard_map/ppermute | solution.py:486
  25.7 0.9 %collective-permute-done.4 = f32[128,128]{1,0:T(8,128)S(1)} collective-permute-done((f32[128,128]{1,0:T(8,128)S(1)}, f32[128,128]{1,0:T(8,128)S(1)}, u32[]{:S(2)}, u32[]{:S(2)}) %collective-permute-start.4) | collective-permute-done | bytes 65568 | tf_op jit(solution)/shard_map/ppermute | solution.py:486
  26.6 0.1 collective-permute-start.7
  26.7 1.3 %object_sums.1 = (f32[8,384,128]{2,1,0:T(8,128)S(1)}, f32[2,64,384]{2,1,0:T(8,128)S(1)}, f32[2,64,384]{2,1,0:T(8,128)S(1)}, f32[2,256,128]{2,1,0:T(8,128)S(1)}) custom-call(s32[242]{0:T(256)S(4)} %get-tuple-element.31.plan, f32[48,2,128,128]{3,2,1,0:T(8,128)S(1)} %get-tuple-element.32.turned, f32[49,2,128,128]{3,2,1,0:T(8,128)S(1)} %get-tuple-element.39.inner_exits, ...), custom_call_target="tpu_custom_call" | custom-call | flops 2000000000 | bytes 1000000 | tf_op jit(solution)/shard_map/object_sums/pallas_call | solution.py:408
  28.0 0.4 collective-permute-start.5
  28.5 0.7 %collective-permute-start.6 = (f32[2,64,384]{2,1,0:T(8,128)S(1)}, f32[2,64,384]{2,1,0:T(8,128)S(1)}, u32[]{:S(2)}, u32[]{:S(2)}) collective-permute-start(f32[2,64,384]{2,1,0:T(8,128)S(1)} %get-tuple-element.49), channel_id=1, source_target_pairs={{8,16},{16,8},{9,17},{17,9},{10,18},{18,10},{11,19},{19,11},{12,20... | collective-permute-start | bytes 589832 | tf_op jit(solution)/shard_map/ppermute | solution.py:491
  29.1 0.7 %collective-permute-done.7 = f32[128,128]{1,0:T(8,128)S(1)} collective-permute-done((f32[128,128]{1,0:T(8,128)S(1)}, f32[128,128]{1,0:T(8,128)S(1)}, u32[]{:S(2)}, u32[]{:S(2)}) %collective-permute-start.7) | collective-permute-done | bytes 65568 | tf_op jit(solution)/shard_map/ppermute | solution.py:519
  29.8 2.3 %collective-permute-start.8 = (f32[128,128]{1,0:T(8,128)S(1)}, f32[128,128]{1,0:T(8,128)S(1)}, u32[]{:S(2)}, u32[]{:S(2)}) collective-permute-start(f32[128,128]{1,0:T(8,128)S(1)} %add.18.a_ref), channel_id=1, source_target_pairs={{0,4},{1,5},{2,6},{3,7},{4,0},{5,1},{6,2},{7,3},{8,12},{9,13},{10,... | collective-permute-start | bytes 196616 | tf_op jit(solution)/shard_map/ppermute | solution.py:519
  32.1 1.8 %collective-permute-done.8.b_ref = f32[128,128]{1,0:T(8,128)S(1)} collective-permute-done((f32[128,128]{1,0:T(8,128)S(1)}, f32[128,128]{1,0:T(8,128)S(1)}, u32[]{:S(2)}, u32[]{:S(2)}) %collective-permute-start.8) | collective-permute-done | bytes 65568 | tf_op jit(solution)/shard_map/ppermute | solution.py:519
  33.9 0.0 collective-permute-done.5.near_ref.near_row_ref
  33.9 0.0 collective-permute-done.6.far_ref.far_row_ref
  34.0 0.1 side_sums.1
  34.1 4.0 %collective-permute-start.9 = (f32[128,128]{1,0:T(8,128)S(1)}, f32[128,128]{1,0:T(8,128)S(1)}, u32[]{:S(2)}, u32[]{:S(2)}) collective-permute-start(f32[128,128]{1,0:T(8,128)S(1)} %add.22), channel_id=1, source_target_pairs={{0,2},{1,3},{2,0},{3,1},{4,6},{5,7},{6,4},{7,5},{8,10},{9,11},{10,... | collective-permute-start | bytes 196616 | tf_op jit(solution)/shard_map/ppermute | solution.py:519
  38.1 1.1 %collective-permute-start.11 = (f32[2,128,128]{2,1,0:T(8,128)S(1)}, f32[2,128,128]{2,1,0:T(8,128)S(1)}, u32[]{:S(2)}, u32[]{:S(2)}) collective-permute-start(f32[2,128,128]{2,1,0:T(8,128)S(1)} %get-tuple-element.55), channel_id=1, source_target_pairs={{0,1},{1,0},{2,3},{3,2},{4,5},{5,4},{6,7},{7,6},{8,9},{9,8},{10,11... | collective-permute-start | bytes 393224 | tf_op jit(solution)/shard_map/ppermute | solution.py:486
  39.3 2.0 %collective-permute-start.12 = (f32[2,128,128]{2,1,0:T(8,128)S(1)}, f32[2,128,128]{2,1,0:T(8,128)S(1)}, u32[]{:S(2)}, u32[]{:S(2)}) collective-permute-start(f32[2,128,128]{2,1,0:T(8,128)S(1)} %get-tuple-element.56), channel_id=1, source_target_pairs={{1,2},{3,4},{5,6},{2,1},{4,3},{6,5},{9,10},{11,12},{13,14},{10,9},... | collective-permute-start | bytes 393224 | tf_op jit(solution)/shard_map/ppermute | solution.py:491
  41.3 0.0 collective-permute-done.9
  41.3 3.0 %collective-permute-start.10 = (f32[128,128]{1,0:T(8,128)S(1)}, f32[128,128]{1,0:T(8,128)S(1)}, u32[]{:S(2)}, u32[]{:S(2)}) collective-permute-start(f32[128,128]{1,0:T(8,128)S(1)} %add.19), channel_id=1, source_target_pairs={{0,16},{1,17},{2,18},{3,19},{4,20},{5,21},{6,22},{7,23},{8,24},{9,... | collective-permute-start | bytes 196616 | tf_op jit(solution)/shard_map/ppermute | solution.py:519
  44.3 2.0 %collective-permute-done.10 = f32[128,128]{1,0:T(8,128)S(1)} collective-permute-done((f32[128,128]{1,0:T(8,128)S(1)}, f32[128,128]{1,0:T(8,128)S(1)}, u32[]{:S(2)}, u32[]{:S(2)}) %collective-permute-start.10) | collective-permute-done | bytes 65568 | tf_op jit(solution)/shard_map/ppermute | solution.py:519
  46.3 0.0 collective-permute-done.11.near_col_ref
  46.3 0.0 collective-permute-done.12.far_col_ref
  46.3 4.6 %collective-permute-start.13 = (f32[128,128]{1,0:T(8,128)S(1)}, f32[128,128]{1,0:T(8,128)S(1)}, u32[]{:S(2)}, u32[]{:S(2)}) collective-permute-start(f32[128,128]{1,0:T(8,128)S(1)} %add.20), channel_id=1, source_target_pairs={{0,8},{8,0},{16,24},{24,16},{1,9},{9,1},{17,25},{25,17},{2,10},{10... | collective-permute-start | bytes 196616 | tf_op jit(solution)/shard_map/ppermute | solution.py:486
  50.9 1.0 %final_sums.1 = f32[2,256,256]{2,1,0:T(8,128)} custom-call(f32[8,384,128]{2,1,0:T(8,128)S(1)} %get-tuple-element.47.grad, f32[2,64,384]{2,1,0:T(8,128)S(1)} %collective-permute-done.5.near_ref.near_row_ref, f32[2,64,384]{2,1,0:T(8,128)S(1)} %collective-permute-done.6.far_ref.far_row_ref, f32[2,128,128]{2,1,0:T(8,128)S(1)} %collective-permute-done.11.near_col_ref, ...), custom_call_target="tpu_custom_call" | custom-call | tf_op jit(solution)/shard_map/final_sums/pallas_call | solution.py:475
  51.8 0.0 collective-permute-done.13
  51.8 0.7 %maximum_select_fusion = f32[2,128,128]{2,1,0:T(8,128)} fusion(f32[1,128,128]{2,1,0:T(8,128)S(1)} %bitcast.9, f32[1,128,128]{2,1,0:T(8,128)S(1)} %bitcast.8, pred[]{:T(512)S(6)} %eq.5), kind=kLoop, calls=%fused_computation | loop fusion | flops 98304 | bytes 262145 | tf_op jit(solution)/shard_map/jit(_where)/select_n | solution.py:554
  (6 shorter events, 0.1 us)
Async XLA Ops:
  1.6 5.0 %collective-permute-start = (f32[2,64,256]{2,1,0:T(8,128)S(1)}, f32[2,64,256]{2,1,0:T(8,128)S(1)}, u32[]{:S(2)}, u32[]{:S(2)}) collective-permute-start(f32[2,64,256]{2,1,0:T(8,128)S(1)} %get-tuple-element.34), channel_id=1, source_target_pairs={{0,8},{8,0},{16,24},{24,16},{1,9},{9,1},{17,25},{25,17},{2,10},{10... | collective-permute-start | bytes 393224 | tf_op jit(solution)/shard_map/ppermute | solution.py:486
  2.4 4.3 %collective-permute-start.1 = (f32[2,64,256]{2,1,0:T(8,128)S(1)}, f32[2,64,256]{2,1,0:T(8,128)S(1)}, u32[]{:S(2)}, u32[]{:S(2)}) collective-permute-start(f32[2,64,256]{2,1,0:T(8,128)S(1)} %get-tuple-element.35), channel_id=1, source_target_pairs={{8,16},{16,8},{9,17},{17,9},{10,18},{18,10},{11,19},{19,11},{12,20... | collective-permute-start | bytes 393224 | tf_op jit(solution)/shard_map/ppermute | solution.py:491
  6.9 6.7 %collective-permute-start.2 = (f32[2,192,128]{2,1,0:T(8,128)S(1)}, f32[2,192,128]{2,1,0:T(8,128)S(1)}, u32[]{:S(2)}, u32[]{:S(2)}) collective-permute-start(f32[2,192,128]{2,1,0:T(8,128)S(1)} %get-tuple-element.40), channel_id=1, source_target_pairs={{0,1},{1,0},{2,3},{3,2},{4,5},{5,4},{6,7},{7,6},{8,9},{9,8},{10,11... | collective-permute-start | bytes 589832 | tf_op jit(solution)/shard_map/ppermute | solution.py:486
  7.2 7.4 %collective-permute-start.3 = (f32[2,192,128]{2,1,0:T(8,128)S(1)}, f32[2,192,128]{2,1,0:T(8,128)S(1)}, u32[]{:S(2)}, u32[]{:S(2)}) collective-permute-start(f32[2,192,128]{2,1,0:T(8,128)S(1)} %get-tuple-element.41), channel_id=1, source_target_pairs={{1,2},{3,4},{5,6},{2,1},{4,3},{6,5},{9,10},{11,12},{13,14},{10,9},... | collective-permute-start | bytes 589832 | tf_op jit(solution)/shard_map/ppermute | solution.py:491
  19.2 7.4 %collective-permute-start.4 = (f32[128,128]{1,0:T(8,128)S(1)}, f32[128,128]{1,0:T(8,128)S(1)}, u32[]{:S(2)}, u32[]{:S(2)}) collective-permute-start(f32[128,128]{1,0:T(8,128)S(1)} %get-tuple-element.44), channel_id=1, source_target_pairs={{0,8},{8,0},{16,24},{24,16},{1,9},{9,1},{17,25},{25,17},{2,10},{10... | collective-permute-start | bytes 196616 | tf_op jit(solution)/shard_map/ppermute | solution.py:486
  26.6 3.2 %collective-permute-start.7 = (f32[128,128]{1,0:T(8,128)S(1)}, f32[128,128]{1,0:T(8,128)S(1)}, u32[]{:S(2)}, u32[]{:S(2)}) collective-permute-start(f32[128,128]{1,0:T(8,128)S(1)} %add.17), channel_id=1, source_target_pairs={{0,1},{1,0},{2,3},{3,2},{4,5},{5,4},{6,7},{7,6},{8,9},{9,8},{10,11... | collective-permute-start | bytes 196616 | tf_op jit(solution)/shard_map/ppermute | solution.py:519
  28.0 5.9 %collective-permute-start.5 = (f32[2,64,384]{2,1,0:T(8,128)S(1)}, f32[2,64,384]{2,1,0:T(8,128)S(1)}, u32[]{:S(2)}, u32[]{:S(2)}) collective-permute-start(f32[2,64,384]{2,1,0:T(8,128)S(1)} %get-tuple-element.48), channel_id=1, source_target_pairs={{0,8},{8,0},{16,24},{24,16},{1,9},{9,1},{17,25},{25,17},{2,10},{10... | collective-permute-start | bytes 589832 | tf_op jit(solution)/shard_map/ppermute | solution.py:486
  28.5 5.5 %collective-permute-start.6 = (f32[2,64,384]{2,1,0:T(8,128)S(1)}, f32[2,64,384]{2,1,0:T(8,128)S(1)}, u32[]{:S(2)}, u32[]{:S(2)}) collective-permute-start(f32[2,64,384]{2,1,0:T(8,128)S(1)} %get-tuple-element.49), channel_id=1, source_target_pairs={{8,16},{16,8},{9,17},{17,9},{10,18},{18,10},{11,19},{19,11},{12,20... | collective-permute-start | bytes 589832 | tf_op jit(solution)/shard_map/ppermute | solution.py:491
  29.8 4.1 %collective-permute-start.8 = (f32[128,128]{1,0:T(8,128)S(1)}, f32[128,128]{1,0:T(8,128)S(1)}, u32[]{:S(2)}, u32[]{:S(2)}) collective-permute-start(f32[128,128]{1,0:T(8,128)S(1)} %add.18.a_ref), channel_id=1, source_target_pairs={{0,4},{1,5},{2,6},{3,7},{4,0},{5,1},{6,2},{7,3},{8,12},{9,13},{10,... | collective-permute-start | bytes 196616 | tf_op jit(solution)/shard_map/ppermute | solution.py:519
  34.1 7.2 %collective-permute-start.9 = (f32[128,128]{1,0:T(8,128)S(1)}, f32[128,128]{1,0:T(8,128)S(1)}, u32[]{:S(2)}, u32[]{:S(2)}) collective-permute-start(f32[128,128]{1,0:T(8,128)S(1)} %add.22), channel_id=1, source_target_pairs={{0,2},{1,3},{2,0},{3,1},{4,6},{5,7},{6,4},{7,5},{8,10},{9,11},{10,... | collective-permute-start | bytes 196616 | tf_op jit(solution)/shard_map/ppermute | solution.py:519
  38.1 8.2 %collective-permute-start.11 = (f32[2,128,128]{2,1,0:T(8,128)S(1)}, f32[2,128,128]{2,1,0:T(8,128)S(1)}, u32[]{:S(2)}, u32[]{:S(2)}) collective-permute-start(f32[2,128,128]{2,1,0:T(8,128)S(1)} %get-tuple-element.55), channel_id=1, source_target_pairs={{0,1},{1,0},{2,3},{3,2},{4,5},{5,4},{6,7},{7,6},{8,9},{9,8},{10,11... | collective-permute-start | bytes 393224 | tf_op jit(solution)/shard_map/ppermute | solution.py:486
  39.3 7.0 %collective-permute-start.12 = (f32[2,128,128]{2,1,0:T(8,128)S(1)}, f32[2,128,128]{2,1,0:T(8,128)S(1)}, u32[]{:S(2)}, u32[]{:S(2)}) collective-permute-start(f32[2,128,128]{2,1,0:T(8,128)S(1)} %get-tuple-element.56), channel_id=1, source_target_pairs={{1,2},{3,4},{5,6},{2,1},{4,3},{6,5},{9,10},{11,12},{13,14},{10,9},... | collective-permute-start | bytes 393224 | tf_op jit(solution)/shard_map/ppermute | solution.py:491
  41.3 5.0 %collective-permute-start.10 = (f32[128,128]{1,0:T(8,128)S(1)}, f32[128,128]{1,0:T(8,128)S(1)}, u32[]{:S(2)}, u32[]{:S(2)}) collective-permute-start(f32[128,128]{1,0:T(8,128)S(1)} %add.19), channel_id=1, source_target_pairs={{0,16},{1,17},{2,18},{3,19},{4,20},{5,21},{6,22},{7,23},{8,24},{9,... | collective-permute-start | bytes 196616 | tf_op jit(solution)/shard_map/ppermute | solution.py:519
  46.3 5.5 %collective-permute-start.13 = (f32[128,128]{1,0:T(8,128)S(1)}, f32[128,128]{1,0:T(8,128)S(1)}, u32[]{:S(2)}, u32[]{:S(2)}) collective-permute-start(f32[128,128]{1,0:T(8,128)S(1)} %add.20), channel_id=1, source_target_pairs={{0,8},{8,0},{16,24},{24,16},{1,9},{9,1},{17,25},{25,17},{2,10},{10... | collective-permute-start | bytes 196616 | tf_op jit(solution)/shard_map/ppermute | solution.py:486

commit v9 on v8

--- a/solution.py
+++ b/solution.py
@@ -221,7 +221,7 @@
     return find
 
 
-def run_slots(groups, find, window, turned, measured, table, exits, probe_sum):
+def run_slots(groups, size_of, first, find, window, turned, measured, table, exits, probe_sum):
     size = turned.shape[2]
     columns = window.shape[0] // 2
     lane = lax.broadcasted_iota(jnp.int32, (size, LANES), 1)
@@ -278,8 +278,8 @@
                 probe_sum[plane] += pltpu.roll(terms[plane], back, axis=1)
 
     def step(group, carry):
-        slots = [find(group * GROUP + member) for member in range(GROUP)]
-        pairs = [slots[member : member + 2] for member in range(0, GROUP, 2)]
+        slots = [find(first + group * size_of + member) for member in range(size_of)]
+        pairs = [slots[member : member + 2] for member in range(0, size_of, 2)]
         loaded = [load(pair) for pair in pairs]
         waves = [regroup(times_table(wave, table[0], table[1])) for _, wave in loaded]
         waves = [weigh(pair, table_times(table[2], table[3], wave)) for pair, wave in zip(pairs, waves)]
@@ -297,7 +297,7 @@
     probe_sum[...] = jnp.zeros_like(probe_sum)
     groups = plan[slots] // GROUP
     find = finder(plan, slots, 0, groups * GROUP, groups * GROUP)
-    run_slots(groups, find, window, turned, measured, table, exits, probe_sum)
+    run_slots(groups, GROUP, 0, find, window, turned, measured, table, exits, probe_sum)
 
 
 def inner_call(plan, window, turned, measured, tables):
@@ -334,7 +334,10 @@
     start = plan[slots] // GROUP * GROUP
     live = plan[slots + 1] - start
     find = finder(plan, slots, start, plan[slots] - start, live)
-    run_slots((live + GROUP - 1) // GROUP, find, window, turned, measured, table, exits, probe_sum)
+    large = live // (2 * GROUP)
+    run_slots(large, 2 * GROUP, 0, find, window, turned, measured, table, exits, probe_sum)
+    first = large * 2 * GROUP
+    run_slots((live - first + GROUP - 1) // GROUP, GROUP, first, find, window, turned, measured, table, exits, probe_sum)
     factor = 1.0 / np.sqrt(np.float32(lax.axis_size("trow") * lax.axis_size("tcol") * slots))
     mine_out[...] = probe_sum[odd_row] * factor
     other_out[...] = probe_sum[1 - odd_row] * factor

time: 52.6 us -> 52.3 us (level)
  the two profiles are of different devices: /device:TPU:7 before, /device:TPU:0 now
where the time goes in v9:
time: 52.3 us; the launch traced here: 52.2 us
  starting transfers between devices  24.7 us (47%)
  Pallas kernels  15.7 us (30%)
  waiting for transfers between devices  9.62 us (18%)
  between operations  1.49 us (3%)
  other arithmetic  0.7 us (1%)
    ppermute x6, starting transfers between devices, near_swap(): lax.ppermute(value, axis, [(i, i ^ 1) for i in range(lax.axis_size(axis))])  13.6 us
    ppermute x4, starting transfers between devices, add_partner(): return add(mine, lax.ppermute(mine, ('trow', 'tcol'), pairs))  8.48 us
    ppermute x4, waiting for transfers between devices, add_partner(): return add(mine, lax.ppermute(mine, ('trow', 'tcol'), pairs))  8.45 us
    pallas_call x1, Pallas kernels, inner_call(): pl.pallas_call(inner_kernel, out_shape=(near((slots + 1,) + turned.shape[...  4.41 us
    pallas_call x1, Pallas kernels, outer_call(): pl.pallas_call(outer_kernel, out_shape=(near((slots + 1,) + turned.shape[...  4.33 us
    pallas_call x1, Pallas kernels, ready_call(): pl.pallas_call(ready_kernel, out_shape=(pltpu.SMEM((5 * slots + 2,), jnp....  2.92 us
    ppermute x4, starting transfers between devices, far_swap(): return lax.ppermute(value, axis, pairs + [(j, i) for i, j in pairs])  2.64 us
    pallas_call x1, Pallas kernels, object_call(): pl.pallas_call(object_kernel, out_shape=(near(window.shape), row, row, ne...  1.67 us
  transfers between devices with their start and end apart: 14, of which 5 were waited for; matrix products, arithmetic and copies ran while one was open for 0% of the time, Pallas kernels for 19%

profile of v9, /device:TPU:0, one launch (start us, length us, event | category | flops | bytes accessed | tf_op | source)
XLA Modules:
  0.0 52.2 jit_solution(5757991103358198090)
XLA Ops:
  0.6 1.0 %edge_rows.1 = (f32[2,64,256]{2,1,0:T(8,128)S(1)}, f32[2,64,256]{2,1,0:T(8,128)S(1)}) custom-call(f32[2,256,256]{2,1,0:T(8,128)} %centre_ref.3), custom_call_target="tpu_custom_call" | custom-call | tf_op jit(solution)/shard_map/edge_rows/pallas_call | solution.py:97
  1.6 0.5 collective-permute-start
  2.2 0.7 %collective-permute-start.1 = (f32[2,64,256]{2,1,0:T(8,128)S(1)}, f32[2,64,256]{2,1,0:T(8,128)S(1)}, u32[]{:S(2)}, u32[]{:S(2)}) collective-permute-start(f32[2,64,256]{2,1,0:T(8,128)S(1)} %get-tuple-element.35), channel_id=1, source_target_pairs={{8,16},{16,8},{9,17},{17,9},{10,18},{18,10},{11,19},{19,11},{12,20... | collective-permute-start | bytes 393224 | tf_op jit(solution)/shard_map/ppermute | solution.py:494
  3.5 2.9 %ready.1 = (s32[242]{0:T(256)S(4)}, f32[48,2,128,128]{3,2,1,0:T(8,128)S(1)}, bf16[48,128,128]{2,1,0:T(8,128)(2,1)S(1)}, bf16[4,256,256]{2,1,0:T(8,128)(2,1)S(1)}, f32[8,384,128]{2,1,0:T(8,128)S(1)}) custom-call(s32[48]{0:T(128)} %bitcast.10, s32[48]{0:T(128)} %bitcast.11, s32[8,128]{1,0:T(8,128)S(1)} %broadcast_in_dim.2.count_ref, f32[2,128,128]{2,1,0:T(8,128)} %probe_ref.1, ...), custom_call_target="tpu_custom_call" | custom-call | tf_op jit(solution)/shard_map/ready/pallas_call | solution.py:158
  6.4 0.0 collective-permute-done.near_ref
  6.4 0.0 collective-permute-done.1.far_ref
  6.4 0.2 side_columns.1
  6.7 2.6 %collective-permute-start.2 = (f32[2,192,128]{2,1,0:T(8,128)S(1)}, f32[2,192,128]{2,1,0:T(8,128)S(1)}, u32[]{:S(2)}, u32[]{:S(2)}) collective-permute-start(f32[2,192,128]{2,1,0:T(8,128)S(1)} %get-tuple-element.40), channel_id=1, source_target_pairs={{0,1},{1,0},{2,3},{3,2},{4,5},{5,4},{6,7},{7,6},{8,9},{9,8},{10,11... | collective-permute-start | bytes 589832 | tf_op jit(solution)/shard_map/ppermute | solution.py:489
  9.2 0.7 %collective-permute-start.3 = (f32[2,192,128]{2,1,0:T(8,128)S(1)}, f32[2,192,128]{2,1,0:T(8,128)S(1)}, u32[]{:S(2)}, u32[]{:S(2)}) collective-permute-start(f32[2,192,128]{2,1,0:T(8,128)S(1)} %get-tuple-element.41), channel_id=1, source_target_pairs={{1,2},{3,4},{5,6},{2,1},{4,3},{6,5},{9,10},{11,12},{13,14},{10,9},... | collective-permute-start | bytes 589832 | tf_op jit(solution)/shard_map/ppermute | solution.py:494
  9.9 4.4 %slots_inside.1 = (f32[49,2,128,128]{3,2,1,0:T(8,128)S(1)}, f32[2,128,128]{2,1,0:T(8,128)S(1)}) custom-call(s32[242]{0:T(256)S(4)} %get-tuple-element.31.plan, f32[8,384,128]{2,1,0:T(8,128)S(1)} %get-tuple-element.36.window.window_ref, f32[48,2,128,128]{3,2,1,0:T(8,128)S(1)} %get-tuple-element.32.turned, ...), custom_call_target="tpu_custom_call" | custom-call | flops 10000000000 | bytes 20000000 | tf_op jit(solution)/shard_map/slots_inside/pallas_call | solution.py:305
  14.3 0.0 collective-permute-done.2.near_col_ref
  14.3 0.0 collective-permute-done.3.far_col_ref
  14.4 4.3 %slots_across.1 = (f32[49,2,128,128]{3,2,1,0:T(8,128)S(1)}, f32[128,128]{1,0:T(8,128)S(1)}, f32[128,128]{1,0:T(8,128)S(1)}) custom-call(s32[242]{0:T(256)S(4)} %get-tuple-element.31.plan, f32[8,384,128]{2,1,0:T(8,128)S(1)} %get-tuple-element.36.window.window_ref, f32[2,192,128]{2,1,0:T(8,128)S(1)} %collective-permute-done.2.near_col_ref, ...), custom_call_target="tpu_custom_call" | custom-call | flops 10000000000 | bytes 20000000 | tf_op jit(solution)/shard_map/slots_across/pallas_call | solution.py:349
  18.7 8.7 %collective-permute-start.4 = (f32[128,128]{1,0:T(8,128)S(1)}, f32[128,128]{1,0:T(8,128)S(1)}, u32[]{:S(2)}, u32[]{:S(2)}) collective-permute-start(f32[128,128]{1,0:T(8,128)S(1)} %get-tuple-element.44), channel_id=1, source_target_pairs={{0,8},{8,0},{16,24},{24,16},{1,9},{9,1},{17,25},{25,17},{2,10},{10... | collective-permute-start | bytes 196616 | tf_op jit(solution)/shard_map/ppermute | solution.py:489
  27.4 0.9 %collective-permute-done.4 = f32[128,128]{1,0:T(8,128)S(1)} collective-permute-done((f32[128,128]{1,0:T(8,128)S(1)}, f32[128,128]{1,0:T(8,128)S(1)}, u32[]{:S(2)}, u32[]{:S(2)}) %collective-permute-start.4) | collective-permute-done | bytes 65568 | tf_op jit(solution)/shard_map/ppermute | solution.py:489
  28.3 2.2 %collective-permute-start.7 = (f32[128,128]{1,0:T(8,128)S(1)}, f32[128,128]{1,0:T(8,128)S(1)}, u32[]{:S(2)}, u32[]{:S(2)}) collective-permute-start(f32[128,128]{1,0:T(8,128)S(1)} %add.17), channel_id=1, source_target_pairs={{0,1},{1,0},{2,3},{3,2},{4,5},{5,4},{6,7},{7,6},{8,9},{9,8},{10,11... | collective-permute-start | bytes 196616 | tf_op jit(solution)/shard_map/ppermute | solution.py:522
  30.5 1.7 %object_sums.1 = (f32[8,384,128]{2,1,0:T(8,128)S(1)}, f32[2,64,384]{2,1,0:T(8,128)S(1)}, f32[2,64,384]{2,1,0:T(8,128)S(1)}, f32[2,256,128]{2,1,0:T(8,128)S(1)}) custom-call(s32[242]{0:T(256)S(4)} %get-tuple-element.31.plan, f32[48,2,128,128]{3,2,1,0:T(8,128)S(1)} %get-tuple-element.32.turned, f32[49,2,128,128]{3,2,1,0:T(8,128)S(1)} %get-tuple-element.39.inner_exits, ...), custom_call_target="tpu_custom_call" | custom-call | flops 2000000000 | bytes 1000000 | tf_op jit(solution)/shard_map/object_sums/pallas_call | solution.py:411
  32.2 0.9 %collective-permute-start.5 = (f32[2,64,384]{2,1,0:T(8,128)S(1)}, f32[2,64,384]{2,1,0:T(8,128)S(1)}, u32[]{:S(2)}, u32[]{:S(2)}) collective-permute-start(f32[2,64,384]{2,1,0:T(8,128)S(1)} %get-tuple-element.48), channel_id=1, source_target_pairs={{0,8},{8,0},{16,24},{24,16},{1,9},{9,1},{17,25},{25,17},{2,10},{10... | collective-permute-start | bytes 589832 | tf_op jit(solution)/shard_map/ppermute | solution.py:489
  33.1 0.7 %collective-permute-start.6 = (f32[2,64,384]{2,1,0:T(8,128)S(1)}, f32[2,64,384]{2,1,0:T(8,128)S(1)}, u32[]{:S(2)}, u32[]{:S(2)}) collective-permute-start(f32[2,64,384]{2,1,0:T(8,128)S(1)} %get-tuple-element.49), channel_id=1, source_target_pairs={{8,16},{16,8},{9,17},{17,9},{10,18},{18,10},{11,19},{19,11},{12,20... | collective-permute-start | bytes 589832 | tf_op jit(solution)/shard_map/ppermute | solution.py:494
  33.8 0.0 collective-permute-done.7
  33.8 2.6 %collective-permute-start.8 = (f32[128,128]{1,0:T(8,128)S(1)}, f32[128,128]{1,0:T(8,128)S(1)}, u32[]{:S(2)}, u32[]{:S(2)}) collective-permute-start(f32[128,128]{1,0:T(8,128)S(1)} %add.18.a_ref), channel_id=1, source_target_pairs={{0,4},{1,5},{2,6},{3,7},{4,0},{5,1},{6,2},{7,3},{8,12},{9,13},{10,... | collective-permute-start | bytes 196616 | tf_op jit(solution)/shard_map/ppermute | solution.py:522
  36.4 3.3 %collective-permute-done.8.b_ref = f32[128,128]{1,0:T(8,128)S(1)} collective-permute-done((f32[128,128]{1,0:T(8,128)S(1)}, f32[128,128]{1,0:T(8,128)S(1)}, u32[]{:S(2)}, u32[]{:S(2)}) %collective-permute-start.8) | collective-permute-done | bytes 65568 | tf_op jit(solution)/shard_map/ppermute | solution.py:522
  39.7 0.0 collective-permute-done.5.near_ref.near_row_ref
  39.7 0.0 collective-permute-done.6.far_ref.far_row_ref
  39.7 0.1 side_sums.1
  39.9 0.1 collective-permute-start.9
  39.9 0.8 %collective-permute-start.11 = (f32[2,128,128]{2,1,0:T(8,128)S(1)}, f32[2,128,128]{2,1,0:T(8,128)S(1)}, u32[]{:S(2)}, u32[]{:S(2)}) collective-permute-start(f32[2,128,128]{2,1,0:T(8,128)S(1)} %get-tuple-element.55), channel_id=1, source_target_pairs={{0,1},{1,0},{2,3},{3,2},{4,5},{5,4},{6,7},{7,6},{8,9},{9,8},{10,11... | collective-permute-start | bytes 393224 | tf_op jit(solution)/shard_map/ppermute | solution.py:489
  40.8 0.7 %collective-permute-start.12 = (f32[2,128,128]{2,1,0:T(8,128)S(1)}, f32[2,128,128]{2,1,0:T(8,128)S(1)}, u32[]{:S(2)}, u32[]{:S(2)}) collective-permute-start(f32[2,128,128]{2,1,0:T(8,128)S(1)} %get-tuple-element.56), channel_id=1, source_target_pairs={{1,2},{3,4},{5,6},{2,1},{4,3},{6,5},{9,10},{11,12},{13,14},{10,9},... | collective-permute-start | bytes 393224 | tf_op jit(solution)/shard_map/ppermute | solution.py:494
  41.4 2.9 %collective-permute-done.9 = f32[128,128]{1,0:T(8,128)S(1)} collective-permute-done((f32[128,128]{1,0:T(8,128)S(1)}, f32[128,128]{1,0:T(8,128)S(1)}, u32[]{:S(2)}, u32[]{:S(2)}) %collective-permute-start.9) | collective-permute-done | bytes 65568 | tf_op jit(solution)/shard_map/ppermute | solution.py:522
  44.4 3.6 %collective-permute-start.10 = (f32[128,128]{1,0:T(8,128)S(1)}, f32[128,128]{1,0:T(8,128)S(1)}, u32[]{:S(2)}, u32[]{:S(2)}) collective-permute-start(f32[128,128]{1,0:T(8,128)S(1)} %add.19), channel_id=1, source_target_pairs={{0,16},{1,17},{2,18},{3,19},{4,20},{5,21},{6,22},{7,23},{8,24},{9,... | collective-permute-start | bytes 196616 | tf_op jit(solution)/shard_map/ppermute | solution.py:522
  48.0 2.2 %collective-permute-done.10 = f32[128,128]{1,0:T(8,128)S(1)} collective-permute-done((f32[128,128]{1,0:T(8,128)S(1)}, f32[128,128]{1,0:T(8,128)S(1)}, u32[]{:S(2)}, u32[]{:S(2)}) %collective-permute-start.10) | collective-permute-done | bytes 65568 | tf_op jit(solution)/shard_map/ppermute | solution.py:522
  50.2 0.0 collective-permute-done.11.near_col_ref
  50.2 0.0 collective-permute-done.12.far_col_ref
  50.3 0.1 collective-permute-start.13
  50.4 1.0 %final_sums.1 = f32[2,256,256]{2,1,0:T(8,128)} custom-call(f32[8,384,128]{2,1,0:T(8,128)S(1)} %get-tuple-element.47.grad, f32[2,64,384]{2,1,0:T(8,128)S(1)} %collective-permute-done.5.near_ref.near_row_ref, f32[2,64,384]{2,1,0:T(8,128)S(1)} %collective-permute-done.6.far_ref.far_row_ref, f32[2,128,128]{2,1,0:T(8,128)S(1)} %collective-permute-done.11.near_col_ref, ...), custom_call_target="tpu_custom_call" | custom-call | tf_op jit(solution)/shard_map/final_sums/pallas_call | solution.py:478
  51.3 0.2 collective-permute-done.13
  51.6 0.7 %maximum_select_fusion = f32[2,128,128]{2,1,0:T(8,128)} fusion(f32[1,128,128]{2,1,0:T(8,128)S(1)} %bitcast.9, f32[1,128,128]{2,1,0:T(8,128)S(1)} %bitcast.8, pred[]{:T(512)S(6)} %eq.5), kind=kLoop, calls=%fused_computation | loop fusion | flops 98304 | bytes 262145 | tf_op jit(solution)/shard_map/jit(_where)/select_n | solution.py:557
  (6 shorter events, 0.1 us)
Async XLA Ops:
  1.6 4.8 %collective-permute-start = (f32[2,64,256]{2,1,0:T(8,128)S(1)}, f32[2,64,256]{2,1,0:T(8,128)S(1)}, u32[]{:S(2)}, u32[]{:S(2)}) collective-permute-start(f32[2,64,256]{2,1,0:T(8,128)S(1)} %get-tuple-element.34), channel_id=1, source_target_pairs={{0,8},{8,0},{16,24},{24,16},{1,9},{9,1},{17,25},{25,17},{2,10},{10... | collective-permute-start | bytes 393224 | tf_op jit(solution)/shard_map/ppermute | solution.py:489
  2.2 4.3 %collective-permute-start.1 = (f32[2,64,256]{2,1,0:T(8,128)S(1)}, f32[2,64,256]{2,1,0:T(8,128)S(1)}, u32[]{:S(2)}, u32[]{:S(2)}) collective-permute-start(f32[2,64,256]{2,1,0:T(8,128)S(1)} %get-tuple-element.35), channel_id=1, source_target_pairs={{8,16},{16,8},{9,17},{17,9},{10,18},{18,10},{11,19},{19,11},{12,20... | collective-permute-start | bytes 393224 | tf_op jit(solution)/shard_map/ppermute | solution.py:494
  6.7 7.7 %collective-permute-start.2 = (f32[2,192,128]{2,1,0:T(8,128)S(1)}, f32[2,192,128]{2,1,0:T(8,128)S(1)}, u32[]{:S(2)}, u32[]{:S(2)}) collective-permute-start(f32[2,192,128]{2,1,0:T(8,128)S(1)} %get-tuple-element.40), channel_id=1, source_target_pairs={{0,1},{1,0},{2,3},{3,2},{4,5},{5,4},{6,7},{7,6},{8,9},{9,8},{10,11... | collective-permute-start | bytes 589832 | tf_op jit(solution)/shard_map/ppermute | solution.py:489
  9.2 5.1 %collective-permute-start.3 = (f32[2,192,128]{2,1,0:T(8,128)S(1)}, f32[2,192,128]{2,1,0:T(8,128)S(1)}, u32[]{:S(2)}, u32[]{:S(2)}) collective-permute-start(f32[2,192,128]{2,1,0:T(8,128)S(1)} %get-tuple-element.41), channel_id=1, source_target_pairs={{1,2},{3,4},{5,6},{2,1},{4,3},{6,5},{9,10},{11,12},{13,14},{10,9},... | collective-permute-start | bytes 589832 | tf_op jit(solution)/shard_map/ppermute | solution.py:494
  18.7 9.6 %collective-permute-start.4 = (f32[128,128]{1,0:T(8,128)S(1)}, f32[128,128]{1,0:T(8,128)S(1)}, u32[]{:S(2)}, u32[]{:S(2)}) collective-permute-start(f32[128,128]{1,0:T(8,128)S(1)} %get-tuple-element.44), channel_id=1, source_target_pairs={{0,8},{8,0},{16,24},{24,16},{1,9},{9,1},{17,25},{25,17},{2,10},{10... | collective-permute-start | bytes 196616 | tf_op jit(solution)/shard_map/ppermute | solution.py:489
  28.3 5.5 %collective-permute-start.7 = (f32[128,128]{1,0:T(8,128)S(1)}, f32[128,128]{1,0:T(8,128)S(1)}, u32[]{:S(2)}, u32[]{:S(2)}) collective-permute-start(f32[128,128]{1,0:T(8,128)S(1)} %add.17), channel_id=1, source_target_pairs={{0,1},{1,0},{2,3},{3,2},{4,5},{5,4},{6,7},{7,6},{8,9},{9,8},{10,11... | collective-permute-start | bytes 196616 | tf_op jit(solution)/shard_map/ppermute | solution.py:522
  32.2 7.5 %collective-permute-start.5 = (f32[2,64,384]{2,1,0:T(8,128)S(1)}, f32[2,64,384]{2,1,0:T(8,128)S(1)}, u32[]{:S(2)}, u32[]{:S(2)}) collective-permute-start(f32[2,64,384]{2,1,0:T(8,128)S(1)} %get-tuple-element.48), channel_id=1, source_target_pairs={{0,8},{8,0},{16,24},{24,16},{1,9},{9,1},{17,25},{25,17},{2,10},{10... | collective-permute-start | bytes 589832 | tf_op jit(solution)/shard_map/ppermute | solution.py:489
  33.1 6.6 %collective-permute-start.6 = (f32[2,64,384]{2,1,0:T(8,128)S(1)}, f32[2,64,384]{2,1,0:T(8,128)S(1)}, u32[]{:S(2)}, u32[]{:S(2)}) collective-permute-start(f32[2,64,384]{2,1,0:T(8,128)S(1)} %get-tuple-element.49), channel_id=1, source_target_pairs={{8,16},{16,8},{9,17},{17,9},{10,18},{18,10},{11,19},{19,11},{12,20... | collective-permute-start | bytes 589832 | tf_op jit(solution)/shard_map/ppermute | solution.py:494
  33.8 5.9 %collective-permute-start.8 = (f32[128,128]{1,0:T(8,128)S(1)}, f32[128,128]{1,0:T(8,128)S(1)}, u32[]{:S(2)}, u32[]{:S(2)}) collective-permute-start(f32[128,128]{1,0:T(8,128)S(1)} %add.18.a_ref), channel_id=1, source_target_pairs={{0,4},{1,5},{2,6},{3,7},{4,0},{5,1},{6,2},{7,3},{8,12},{9,13},{10,... | collective-permute-start | bytes 196616 | tf_op jit(solution)/shard_map/ppermute | solution.py:522
  39.9 4.5 %collective-permute-start.9 = (f32[128,128]{1,0:T(8,128)S(1)}, f32[128,128]{1,0:T(8,128)S(1)}, u32[]{:S(2)}, u32[]{:S(2)}) collective-permute-start(f32[128,128]{1,0:T(8,128)S(1)} %add.22), channel_id=1, source_target_pairs={{0,2},{1,3},{2,0},{3,1},{4,6},{5,7},{6,4},{7,5},{8,10},{9,11},{10,... | collective-permute-start | bytes 196616 | tf_op jit(solution)/shard_map/ppermute | solution.py:522
  39.9 10.3 %collective-permute-start.11 = (f32[2,128,128]{2,1,0:T(8,128)S(1)}, f32[2,128,128]{2,1,0:T(8,128)S(1)}, u32[]{:S(2)}, u32[]{:S(2)}) collective-permute-start(f32[2,128,128]{2,1,0:T(8,128)S(1)} %get-tuple-element.55), channel_id=1, source_target_pairs={{0,1},{1,0},{2,3},{3,2},{4,5},{5,4},{6,7},{7,6},{8,9},{9,8},{10,11... | collective-permute-start | bytes 393224 | tf_op jit(solution)/shard_map/ppermute | solution.py:489
  40.8 9.5 %collective-permute-start.12 = (f32[2,128,128]{2,1,0:T(8,128)S(1)}, f32[2,128,128]{2,1,0:T(8,128)S(1)}, u32[]{:S(2)}, u32[]{:S(2)}) collective-permute-start(f32[2,128,128]{2,1,0:T(8,128)S(1)} %get-tuple-element.56), channel_id=1, source_target_pairs={{1,2},{3,4},{5,6},{2,1},{4,3},{6,5},{9,10},{11,12},{13,14},{10,9},... | collective-permute-start | bytes 393224 | tf_op jit(solution)/shard_map/ppermute | solution.py:494
  44.4 5.9 %collective-permute-start.10 = (f32[128,128]{1,0:T(8,128)S(1)}, f32[128,128]{1,0:T(8,128)S(1)}, u32[]{:S(2)}, u32[]{:S(2)}) collective-permute-start(f32[128,128]{1,0:T(8,128)S(1)} %add.19), channel_id=1, source_target_pairs={{0,16},{1,17},{2,18},{3,19},{4,20},{5,21},{6,22},{7,23},{8,24},{9,... | collective-permute-start | bytes 196616 | tf_op jit(solution)/shard_map/ppermute | solution.py:522
  50.3 1.3 %collective-permute-start.13 = (f32[128,128]{1,0:T(8,128)S(1)}, f32[128,128]{1,0:T(8,128)S(1)}, u32[]{:S(2)}, u32[]{:S(2)}) collective-permute-start(f32[128,128]{1,0:T(8,128)S(1)} %add.20), channel_id=1, source_target_pairs={{0,8},{8,0},{16,24},{24,16},{1,9},{9,1},{17,25},{25,17},{2,10},{10... | collective-permute-start | bytes 196616 | tf_op jit(solution)/shard_map/ppermute | solution.py:489

commit v10 on v9

--- a/solution.py
+++ b/solution.py
@@ -358,39 +358,58 @@
     )(*in_smem(plan), *in_vmem(window, near_col, far_col, turned, measured, tables, probe_sum))
 
 
-def object_kernel(plan, turned, inner_exits, outer_exits, grad, near_row_out, far_row_out, side_out):
+def add_objects(groups, find, turned, exits, grad):
+    size = turned.shape[2]
+    columns = grad.shape[0] // 2
+    lane = lax.broadcasted_iota(jnp.int32, (size, LANES), 1)
+
+    def step(index, carry):
+        for member in range(ADDED):
+            slot, row, tile, turn, _, kept_at = find(index * ADDED + member)
+            here = lane >= turn
+            probe = [turned[slot, plane] for plane in range(2)]
+            exit_real, exit_imag = exits[kept_at, 0], exits[kept_at, 1]
+            adds = (probe[0] * exit_real + probe[1] * exit_imag, probe[0] * exit_imag - probe[1] * exit_real)
+            for plane in range(2):
+                at = plane * columns + tile
+                grad[at, pl.ds(row, size), :] += jnp.where(here, adds[plane], 0.0)
+                grad[at + 1, pl.ds(row, size), :] += jnp.where(here, 0.0, adds[plane])
+        return carry
+
+    lax.fori_loop(0, groups, step, 0)
+
+
+def first_object_kernel(plan, turned, exits, grad):
     slots = turned.shape[0]
-    size = turned.shape[2]
-    margin = size // 2
+    grad[...] = jnp.zeros_like(grad)
+    start = plan[slots] // GROUP * GROUP
+    add_objects(start // ADDED, finder(plan, slots, 0, start, start), turned, exits, grad)
+
+
+def first_object_call(plan, window, turned, exits):
+    return pl.pallas_call(
+        first_object_kernel,
+        out_shape=near(window.shape),
+        in_specs=[SMEM] + [VMEM] * 2,
+        out_specs=VMEM,
+        compiler_params=PARAMS,
+        cost_estimate=pl.CostEstimate(flops=10**9, bytes_accessed=10**5, transcendentals=0),
+        name="object_inside",
+    )(*in_smem(plan), *in_vmem(turned, exits))
+
+
+def object_kernel(plan, turned, exits, grad_ref, grad, near_row_out, far_row_out, side_out):
+    slots = turned.shape[0]
+    margin = turned.shape[2] // 2
     columns = grad.shape[0] // 2
     tall = grad.shape[1]
     odd_row, _ = parities()
     near, far = place_of(odd_row, 0, tall - margin)
-    lane = lax.broadcasted_iota(jnp.int32, (size, LANES), 1)
-    grad[...] = jnp.zeros_like(grad)
-
-    def add_some(find, exits):
-        def step(index, carry):
-            for member in range(ADDED):
-                slot, row, tile, turn, _, kept_at = find(index * ADDED + member)
-                here = lane >= turn
-                probe = [turned[slot, plane] for plane in range(2)]
-                exit_real, exit_imag = exits[kept_at, 0], exits[kept_at, 1]
-                adds = (probe[0] * exit_real + probe[1] * exit_imag, probe[0] * exit_imag - probe[1] * exit_real)
-                for plane in range(2):
-                    at = plane * columns + tile
-                    grad[at, pl.ds(row, size), :] += jnp.where(here, adds[plane], 0.0)
-                    grad[at + 1, pl.ds(row, size), :] += jnp.where(here, 0.0, adds[plane])
-            return carry
-
-        return step
-
+    grad[...] = grad_ref[...]
     start = plan[slots] // GROUP * GROUP
     live = plan[slots + 1] - start
-    lax.fori_loop(0, start // ADDED, add_some(finder(plan, slots, 0, start, start), inner_exits), 0)
-    lax.fori_loop(
-        0, (live + ADDED - 1) // ADDED, add_some(finder(plan, slots, start, plan[slots] - start, live), outer_exits), 0
-    )
+    find = finder(plan, slots, start, plan[slots] - start, live)
+    add_objects((live + ADDED - 1) // ADDED, find, turned, exits, grad)
     narrow = lax.broadcasted_iota(jnp.int32, (margin, LANES), 1) < margin
     for plane in range(2):
         base = plane * columns
@@ -405,18 +424,18 @@
             side_out[plane, row - margin : row] = jnp.where(narrow, grad[right, rows, :], grad[left, rows, :])
 
 
-def object_call(plan, window, turned, inner_exits, outer_exits):
+def object_call(plan, turned, exits, grad):
     size = turned.shape[2]
-    row = near((2, size // 2, (window.shape[0] // 2 - 1) * LANES))
+    row = near((2, size // 2, (grad.shape[0] // 2 - 1) * LANES))
     return pl.pallas_call(
         object_kernel,
-        out_shape=(near(window.shape), row, row, near((2, window.shape[1] - size, LANES))),
+        out_shape=(near(grad.shape), row, row, near((2, grad.shape[1] - size, LANES))),
         in_specs=[SMEM] + [VMEM] * 3,
         out_specs=(VMEM,) * 4,
         compiler_params=PARAMS,
-        cost_estimate=pl.CostEstimate(flops=2 * 10**9, bytes_accessed=10**6, transcendentals=0),
-        name="object_sums",
-    )(*in_smem(plan), *in_vmem(turned, inner_exits, outer_exits))
+        cost_estimate=pl.CostEstimate(flops=10**9, bytes_accessed=10**5, transcendentals=0),
+        name="object_across",
+    )(*in_smem(plan), *in_vmem(turned, exits, grad))
 
 
 def side_sum_kernel(side_ref, near_ref, far_ref, near_out, far_out, side):
@@ -537,9 +556,11 @@
     outer_exits, mine, other = outer_call(plan, window, near_col, far_col, turned, measured, tables, probe_sum)
 
     along_rows, along_cols = doubling_steps(lax.axis_size("trow"), lax.axis_size("tcol"))
+    other, inner_exits = lax.optimization_barrier((other, inner_exits))
+    grad = first_object_call(plan, window, turned, inner_exits)
     mine = mine + near_swap(other, "trow")
     mine, outer_exits = lax.optimization_barrier((mine, outer_exits))
-    grad, near_row, far_row, side = object_call(plan, window, turned, inner_exits, outer_exits)
+    grad, near_row, far_row, side = object_call(plan, turned, outer_exits, grad)
     near_row = near_swap(near_row, "trow")
     far_row = far_swap(far_row, "trow")
     mine = add_partner(mine, along_cols[0])

time: 52.3 us -> 50.9 us (0.973); the launches traced: 52.2 us -> 50.1 us
  Pallas kernels: 15.7 us -> 20.6 us
  starting transfers between devices: 24.7 us -> 20.4 us
  waiting for transfers between devices: 9.62 us -> 6.8 us
    ppermute x6, starting transfers between devices: 13.6 us -> 6.68 us  [near_swap(): lax.ppermute(value, axis, [(i, i ^ 1) for i in range(lax.axis_size(axis))])]
    pallas_call x1, Pallas kernels: 4.33 us -> 8.44 us  [outer_call(): pl.pallas_call(outer_kernel, out_shape=(near((slots + 1,) + turned.shape[...]
    ppermute x4, starting transfers between devices: 8.48 us -> 11.1 us  [add_partner(): return add(mine, lax.ppermute(mine, ('trow', 'tcol'), pairs))]
    ppermute x4, waiting for transfers between devices: 8.45 us -> 6.47 us  [add_partner(): return add(mine, lax.ppermute(mine, ('trow', 'tcol'), pairs))]
    ppermute x6, waiting for transfers between devices: 1.16 us -> 0.32 us  [near_swap(): lax.ppermute(value, axis, [(i, i ^ 1) for i in range(lax.axis_size(axis))])]
    pallas_call x1 -> x2, Pallas kernels: 1.67 us -> 2.51 us  [the longest x1 1.67 us: object_call(): pl.pallas_call(object_kernel, out_shape=(near(grad.shape), row, row, near...]
  transfers between devices with their start and end apart: 14 -> 14, of which waited for: 5 -> 5; matrix products, arithmetic and copies ran while one was open for 0% -> 0% of each run, Pallas kernels for 19% -> 22%
where the time goes in v10:
time: 50.9 us; the launch traced here: 50.1 us
  Pallas kernels  20.6 us (40%)
  starting transfers between devices  20.4 us (40%)
  waiting for transfers between devices  6.8 us (13%)
  between operations  1.5 us (3%)
  other arithmetic  0.7 us (1%)
    ppermute x4, starting transfers between devices, add_partner(): return add(mine, lax.ppermute(mine, ('trow', 'tcol'), pairs))  11.1 us
    pallas_call x1, Pallas kernels, outer_call(): pl.pallas_call(outer_kernel, out_shape=(near((slots + 1,) + turned.shape[...  8.44 us
    ppermute x6, starting transfers between devices, near_swap(): lax.ppermute(value, axis, [(i, i ^ 1) for i in range(lax.axis_size(axis))])  6.68 us
    ppermute x4, waiting for transfers between devices, add_partner(): return add(mine, lax.ppermute(mine, ('trow', 'tcol'), pairs))  6.47 us
    pallas_call x1, Pallas kernels, inner_call(): pl.pallas_call(inner_kernel, out_shape=(near((slots + 1,) + turned.shape[...  4.4 us
    pallas_call x1, Pallas kernels, ready_call(): pl.pallas_call(ready_kernel, out_shape=(pltpu.SMEM((5 * slots + 2,), jnp....  2.92 us
    ppermute x4, starting transfers between devices, far_swap(): return lax.ppermute(value, axis, pairs + [(j, i) for i, j in pairs])  2.65 us
    pallas_call x1, Pallas kernels, object_call(): pl.pallas_call(object_kernel, out_shape=(near(grad.shape), row, row, near...  1.67 us
  transfers between devices with their start and end apart: 14, of which 5 were waited for; matrix products, arithmetic and copies ran while one was open for 0% of the time, Pallas kernels for 22%

profile of v10, /device:TPU:0, one launch (start us, length us, event | category | flops | bytes accessed | tf_op | source)
XLA Modules:
  0.0 50.1 jit_solution(9755532241826807252)
XLA Ops:
  0.6 1.0 %edge_rows.1 = (f32[2,64,256]{2,1,0:T(8,128)S(1)}, f32[2,64,256]{2,1,0:T(8,128)S(1)}) custom-call(f32[2,256,256]{2,1,0:T(8,128)} %centre_ref.3), custom_call_target="tpu_custom_call" | custom-call | tf_op jit(solution)/shard_map/edge_rows/pallas_call | solution.py:97
  1.6 0.5 %collective-permute-start = (f32[2,64,256]{2,1,0:T(8,128)S(1)}, f32[2,64,256]{2,1,0:T(8,128)S(1)}, u32[]{:S(2)}, u32[]{:S(2)}) collective-permute-start(f32[2,64,256]{2,1,0:T(8,128)S(1)} %get-tuple-element.36), channel_id=1, source_target_pairs={{0,8},{8,0},{16,24},{24,16},{1,9},{9,1},{17,25},{25,17},{2,10},{10... | collective-permute-start | bytes 393224 | tf_op jit(solution)/shard_map/ppermute | solution.py:508
  2.2 0.7 %collective-permute-start.1 = (f32[2,64,256]{2,1,0:T(8,128)S(1)}, f32[2,64,256]{2,1,0:T(8,128)S(1)}, u32[]{:S(2)}, u32[]{:S(2)}) collective-permute-start(f32[2,64,256]{2,1,0:T(8,128)S(1)} %get-tuple-element.37), channel_id=1, source_target_pairs={{8,16},{16,8},{9,17},{17,9},{10,18},{18,10},{11,19},{19,11},{12,20... | collective-permute-start | bytes 393224 | tf_op jit(solution)/shard_map/ppermute | solution.py:513
  3.5 2.9 %ready.1 = (s32[242]{0:T(256)S(4)}, f32[48,2,128,128]{3,2,1,0:T(8,128)S(1)}, bf16[48,128,128]{2,1,0:T(8,128)(2,1)S(1)}, bf16[4,256,256]{2,1,0:T(8,128)(2,1)S(1)}, f32[8,384,128]{2,1,0:T(8,128)S(1)}) custom-call(s32[48]{0:T(128)} %bitcast.10, s32[48]{0:T(128)} %bitcast.11, s32[8,128]{1,0:T(8,128)S(1)} %broadcast_in_dim.2.count_ref, f32[2,128,128]{2,1,0:T(8,128)} %probe_ref.1, ...), custom_call_target="tpu_custom_call" | custom-call | tf_op jit(solution)/shard_map/ready/pallas_call | solution.py:158
  6.4 0.0 collective-permute-done.near_ref
  6.4 0.0 collective-permute-done.1.far_ref
  6.4 0.2 side_columns.1
  6.7 2.6 %collective-permute-start.2 = (f32[2,192,128]{2,1,0:T(8,128)S(1)}, f32[2,192,128]{2,1,0:T(8,128)S(1)}, u32[]{:S(2)}, u32[]{:S(2)}) collective-permute-start(f32[2,192,128]{2,1,0:T(8,128)S(1)} %get-tuple-element.39), channel_id=1, source_target_pairs={{0,1},{1,0},{2,3},{3,2},{4,5},{5,4},{6,7},{7,6},{8,9},{9,8},{10,11... | collective-permute-start | bytes 589832 | tf_op jit(solution)/shard_map/ppermute | solution.py:508
  9.2 0.7 %collective-permute-start.3 = (f32[2,192,128]{2,1,0:T(8,128)S(1)}, f32[2,192,128]{2,1,0:T(8,128)S(1)}, u32[]{:S(2)}, u32[]{:S(2)}) collective-permute-start(f32[2,192,128]{2,1,0:T(8,128)S(1)} %get-tuple-element.40), channel_id=1, source_target_pairs={{1,2},{3,4},{5,6},{2,1},{4,3},{6,5},{9,10},{11,12},{13,14},{10,9},... | collective-permute-start | bytes 589832 | tf_op jit(solution)/shard_map/ppermute | solution.py:513
  9.9 4.4 %slots_inside.1 = (f32[49,2,128,128]{3,2,1,0:T(8,128)S(1)}, f32[2,128,128]{2,1,0:T(8,128)S(1)}) custom-call(s32[242]{0:T(256)S(4)} %get-tuple-element.33.plan, f32[8,384,128]{2,1,0:T(8,128)S(1)} %get-tuple-element.38.window.window_ref, f32[48,2,128,128]{3,2,1,0:T(8,128)S(1)} %get-tuple-element.34.turned, ...), custom_call_target="tpu_custom_call" | custom-call | flops 10000000000 | bytes 20000000 | tf_op jit(solution)/shard_map/slots_inside/pallas_call | solution.py:305
  14.3 0.0 collective-permute-done.2.near_col_ref
  14.3 0.0 collective-permute-done.3.far_col_ref
  14.3 8.4 %slots_across.1 = (f32[49,2,128,128]{3,2,1,0:T(8,128)S(1)}, f32[128,128]{1,0:T(8,128)S(1)}, f32[128,128]{1,0:T(8,128)S(1)}) custom-call(s32[242]{0:T(256)S(4)} %get-tuple-element.33.plan, f32[8,384,128]{2,1,0:T(8,128)S(1)} %get-tuple-element.38.window.window_ref, f32[2,192,128]{2,1,0:T(8,128)S(1)} %collective-permute-done.2.near_col_ref, ...), custom_call_target="tpu_custom_call" | custom-call | flops 10000000000 | bytes 20000000 | tf_op jit(solution)/shard_map/slots_across/pallas_call | solution.py:349
  22.8 2.9 %collective-permute-start.4 = (f32[128,128]{1,0:T(8,128)S(1)}, f32[128,128]{1,0:T(8,128)S(1)}, u32[]{:S(2)}, u32[]{:S(2)}) collective-permute-start(f32[128,128]{1,0:T(8,128)S(1)} %get-tuple-element.47), channel_id=1, source_target_pairs={{0,8},{8,0},{16,24},{24,16},{1,9},{9,1},{17,25},{25,17},{2,10},{10... | collective-permute-start | bytes 196616 | tf_op jit(solution)/shard_map/ppermute | solution.py:508
  25.7 0.8 %object_inside.1.grad_ref = f32[8,384,128]{2,1,0:T(8,128)S(1)} custom-call(s32[242]{0:T(256)S(4)} %get-tuple-element.33.plan, f32[48,2,128,128]{3,2,1,0:T(8,128)S(1)} %get-tuple-element.34.turned, f32[49,2,128,128]{3,2,1,0:T(8,128)S(1)} %get-tuple-element.50.exits), custom_call_target="tpu_custom_call" | custom-call | flops 1000000000 | bytes 100000 | tf_op jit(solution)/shard_map/object_inside/pallas_call | solution.py:390
  26.6 0.1 collective-permute-done.4
  26.6 2.3 %collective-permute-start.7 = (f32[128,128]{1,0:T(8,128)S(1)}, f32[128,128]{1,0:T(8,128)S(1)}, u32[]{:S(2)}, u32[]{:S(2)}) collective-permute-start(f32[128,128]{1,0:T(8,128)S(1)} %add.17), channel_id=1, source_target_pairs={{0,1},{1,0},{2,3},{3,2},{4,5},{5,4},{6,7},{7,6},{8,9},{9,8},{10,11... | collective-permute-start | bytes 196616 | tf_op jit(solution)/shard_map/ppermute | solution.py:541
  28.9 1.7 %object_across.1 = (f32[8,384,128]{2,1,0:T(8,128)S(1)}, f32[2,64,384]{2,1,0:T(8,128)S(1)}, f32[2,64,384]{2,1,0:T(8,128)S(1)}, f32[2,256,128]{2,1,0:T(8,128)S(1)}) custom-call(s32[242]{0:T(256)S(4)} %get-tuple-element.33.plan, f32[48,2,128,128]{3,2,1,0:T(8,128)S(1)} %get-tuple-element.34.turned, f32[49,2,128,128]{3,2,1,0:T(8,128)S(1)} %get-tuple-element.49.exits, ...), custom_call_target="tpu_custom_call" | custom-call | flops 1000000000 | bytes 100000 | tf_op jit(solution)/shard_map/object_across/pallas_call | solution.py:430
  30.6 0.1 collective-permute-start.5
  30.7 0.7 %collective-permute-start.6 = (f32[2,64,384]{2,1,0:T(8,128)S(1)}, f32[2,64,384]{2,1,0:T(8,128)S(1)}, u32[]{:S(2)}, u32[]{:S(2)}) collective-permute-start(f32[2,64,384]{2,1,0:T(8,128)S(1)} %get-tuple-element.53), channel_id=1, source_target_pairs={{8,16},{16,8},{9,17},{17,9},{10,18},{18,10},{11,19},{19,11},{12,20... | collective-permute-start | bytes 589832 | tf_op jit(solution)/shard_map/ppermute | solution.py:513
  31.4 0.0 collective-permute-done.7
  31.4 2.6 %collective-permute-start.8 = (f32[128,128]{1,0:T(8,128)S(1)}, f32[128,128]{1,0:T(8,128)S(1)}, u32[]{:S(2)}, u32[]{:S(2)}) collective-permute-start(f32[128,128]{1,0:T(8,128)S(1)} %add.18.a_ref), channel_id=1, source_target_pairs={{0,4},{1,5},{2,6},{3,7},{4,0},{5,1},{6,2},{7,3},{8,12},{9,13},{10,... | collective-permute-start | bytes 196616 | tf_op jit(solution)/shard_map/ppermute | solution.py:541
  34.0 2.7 %collective-permute-done.8.b_ref = f32[128,128]{1,0:T(8,128)S(1)} collective-permute-done((f32[128,128]{1,0:T(8,128)S(1)}, f32[128,128]{1,0:T(8,128)S(1)}, u32[]{:S(2)}, u32[]{:S(2)}) %collective-permute-start.8) | collective-permute-done | bytes 65568 | tf_op jit(solution)/shard_map/ppermute | solution.py:541
  36.6 0.0 collective-permute-done.5.near_ref.near_row_ref
  36.7 0.0 collective-permute-done.6.far_ref.far_row_ref
  36.7 0.1 side_sums.1
  36.8 1.8 %collective-permute-start.9 = (f32[128,128]{1,0:T(8,128)S(1)}, f32[128,128]{1,0:T(8,128)S(1)}, u32[]{:S(2)}, u32[]{:S(2)}) collective-permute-start(f32[128,128]{1,0:T(8,128)S(1)} %add.22), channel_id=1, source_target_pairs={{0,2},{1,3},{2,0},{3,1},{4,6},{5,7},{6,4},{7,5},{8,10},{9,11},{10,... | collective-permute-start | bytes 196616 | tf_op jit(solution)/shard_map/ppermute | solution.py:541
  38.6 0.5 %collective-permute-start.11 = (f32[2,128,128]{2,1,0:T(8,128)S(1)}, f32[2,128,128]{2,1,0:T(8,128)S(1)}, u32[]{:S(2)}, u32[]{:S(2)}) collective-permute-start(f32[2,128,128]{2,1,0:T(8,128)S(1)} %get-tuple-element.59), channel_id=1, source_target_pairs={{0,1},{1,0},{2,3},{3,2},{4,5},{5,4},{6,7},{7,6},{8,9},{9,8},{10,11... | collective-permute-start | bytes 393224 | tf_op jit(solution)/shard_map/ppermute | solution.py:508
  39.1 0.7 %collective-permute-start.12 = (f32[2,128,128]{2,1,0:T(8,128)S(1)}, f32[2,128,128]{2,1,0:T(8,128)S(1)}, u32[]{:S(2)}, u32[]{:S(2)}) collective-permute-start(f32[2,128,128]{2,1,0:T(8,128)S(1)} %get-tuple-element.60), channel_id=1, source_target_pairs={{1,2},{3,4},{5,6},{2,1},{4,3},{6,5},{9,10},{11,12},{13,14},{10,9},... | collective-permute-start | bytes 393224 | tf_op jit(solution)/shard_map/ppermute | solution.py:513
  39.8 1.6 %collective-permute-done.9 = f32[128,128]{1,0:T(8,128)S(1)} collective-permute-done((f32[128,128]{1,0:T(8,128)S(1)}, f32[128,128]{1,0:T(8,128)S(1)}, u32[]{:S(2)}, u32[]{:S(2)}) %collective-permute-start.9) | collective-permute-done | bytes 65568 | tf_op jit(solution)/shard_map/ppermute | solution.py:541
  41.3 4.5 %collective-permute-start.10 = (f32[128,128]{1,0:T(8,128)S(1)}, f32[128,128]{1,0:T(8,128)S(1)}, u32[]{:S(2)}, u32[]{:S(2)}) collective-permute-start(f32[128,128]{1,0:T(8,128)S(1)} %add.19), channel_id=1, source_target_pairs={{0,16},{1,17},{2,18},{3,19},{4,20},{5,21},{6,22},{7,23},{8,24},{9,... | collective-permute-start | bytes 196616 | tf_op jit(solution)/shard_map/ppermute | solution.py:541
  45.8 2.2 %collective-permute-done.10 = f32[128,128]{1,0:T(8,128)S(1)} collective-permute-done((f32[128,128]{1,0:T(8,128)S(1)}, f32[128,128]{1,0:T(8,128)S(1)}, u32[]{:S(2)}, u32[]{:S(2)}) %collective-permute-start.10) | collective-permute-done | bytes 65568 | tf_op jit(solution)/shard_map/ppermute | solution.py:541
  48.1 0.0 collective-permute-done.11.near_col_ref
  48.1 0.0 collective-permute-done.12.far_col_ref
  48.1 0.1 collective-permute-start.13
  48.2 1.0 %final_sums.1 = f32[2,256,256]{2,1,0:T(8,128)} custom-call(f32[8,384,128]{2,1,0:T(8,128)S(1)} %get-tuple-element.51.grad, f32[2,64,384]{2,1,0:T(8,128)S(1)} %collective-permute-done.5.near_ref.near_row_ref, f32[2,64,384]{2,1,0:T(8,128)S(1)} %collective-permute-done.6.far_ref.far_row_ref, f32[2,128,128]{2,1,0:T(8,128)S(1)} %collective-permute-done.11.near_col_ref, ...), custom_call_target="tpu_custom_call" | custom-call | tf_op jit(solution)/shard_map/final_sums/pallas_call | solution.py:497
  49.2 0.2 collective-permute-done.13
  49.4 0.7 %maximum_select_fusion = f32[2,128,128]{2,1,0:T(8,128)} fusion(f32[1,128,128]{2,1,0:T(8,128)S(1)} %bitcast.9, f32[1,128,128]{2,1,0:T(8,128)S(1)} %bitcast.8, pred[]{:T(512)S(6)} %eq.5), kind=kLoop, calls=%fused_computation | loop fusion | flops 98304 | bytes 262145 | tf_op jit(solution)/shard_map/jit(_where)/select_n | solution.py:578
  (6 shorter events, 0.1 us)
Async XLA Ops:
  1.6 4.8 %collective-permute-start = (f32[2,64,256]{2,1,0:T(8,128)S(1)}, f32[2,64,256]{2,1,0:T(8,128)S(1)}, u32[]{:S(2)}, u32[]{:S(2)}) collective-permute-start(f32[2,64,256]{2,1,0:T(8,128)S(1)} %get-tuple-element.36), channel_id=1, source_target_pairs={{0,8},{8,0},{16,24},{24,16},{1,9},{9,1},{17,25},{25,17},{2,10},{10... | collective-permute-start | bytes 393224 | tf_op jit(solution)/shard_map/ppermute | solution.py:508
  2.2 4.3 %collective-permute-start.1 = (f32[2,64,256]{2,1,0:T(8,128)S(1)}, f32[2,64,256]{2,1,0:T(8,128)S(1)}, u32[]{:S(2)}, u32[]{:S(2)}) collective-permute-start(f32[2,64,256]{2,1,0:T(8,128)S(1)} %get-tuple-element.37), channel_id=1, source_target_pairs={{8,16},{16,8},{9,17},{17,9},{10,18},{18,10},{11,19},{19,11},{12,20... | collective-permute-start | bytes 393224 | tf_op jit(solution)/shard_map/ppermute | solution.py:513
  6.7 7.7 %collective-permute-start.2 = (f32[2,192,128]{2,1,0:T(8,128)S(1)}, f32[2,192,128]{2,1,0:T(8,128)S(1)}, u32[]{:S(2)}, u32[]{:S(2)}) collective-permute-start(f32[2,192,128]{2,1,0:T(8,128)S(1)} %get-tuple-element.39), channel_id=1, source_target_pairs={{0,1},{1,0},{2,3},{3,2},{4,5},{5,4},{6,7},{7,6},{8,9},{9,8},{10,11... | collective-permute-start | bytes 589832 | tf_op jit(solution)/shard_map/ppermute | solution.py:508
  9.2 5.1 %collective-permute-start.3 = (f32[2,192,128]{2,1,0:T(8,128)S(1)}, f32[2,192,128]{2,1,0:T(8,128)S(1)}, u32[]{:S(2)}, u32[]{:S(2)}) collective-permute-start(f32[2,192,128]{2,1,0:T(8,128)S(1)} %get-tuple-element.40), channel_id=1, source_target_pairs={{1,2},{3,4},{5,6},{2,1},{4,3},{6,5},{9,10},{11,12},{13,14},{10,9},... | collective-permute-start | bytes 589832 | tf_op jit(solution)/shard_map/ppermute | solution.py:513
  22.8 3.8 %collective-permute-start.4 = (f32[128,128]{1,0:T(8,128)S(1)}, f32[128,128]{1,0:T(8,128)S(1)}, u32[]{:S(2)}, u32[]{:S(2)}) collective-permute-start(f32[128,128]{1,0:T(8,128)S(1)} %get-tuple-element.47), channel_id=1, source_target_pairs={{0,8},{8,0},{16,24},{24,16},{1,9},{9,1},{17,25},{25,17},{2,10},{10... | collective-permute-start | bytes 196616 | tf_op jit(solution)/shard_map/ppermute | solution.py:508
  26.6 4.7 %collective-permute-start.7 = (f32[128,128]{1,0:T(8,128)S(1)}, f32[128,128]{1,0:T(8,128)S(1)}, u32[]{:S(2)}, u32[]{:S(2)}) collective-permute-start(f32[128,128]{1,0:T(8,128)S(1)} %add.17), channel_id=1, source_target_pairs={{0,1},{1,0},{2,3},{3,2},{4,5},{5,4},{6,7},{7,6},{8,9},{9,8},{10,11... | collective-permute-start | bytes 196616 | tf_op jit(solution)/shard_map/ppermute | solution.py:541
  30.6 6.0 %collective-permute-start.5 = (f32[2,64,384]{2,1,0:T(8,128)S(1)}, f32[2,64,384]{2,1,0:T(8,128)S(1)}, u32[]{:S(2)}, u32[]{:S(2)}) collective-permute-start(f32[2,64,384]{2,1,0:T(8,128)S(1)} %get-tuple-element.52), channel_id=1, source_target_pairs={{0,8},{8,0},{16,24},{24,16},{1,9},{9,1},{17,25},{25,17},{2,10},{10... | collective-permute-start | bytes 589832 | tf_op jit(solution)/shard_map/ppermute | solution.py:508
  30.7 6.0 %collective-permute-start.6 = (f32[2,64,384]{2,1,0:T(8,128)S(1)}, f32[2,64,384]{2,1,0:T(8,128)S(1)}, u32[]{:S(2)}, u32[]{:S(2)}) collective-permute-start(f32[2,64,384]{2,1,0:T(8,128)S(1)} %get-tuple-element.53), channel_id=1, source_target_pairs={{8,16},{16,8},{9,17},{17,9},{10,18},{18,10},{11,19},{19,11},{12,20... | collective-permute-start | bytes 589832 | tf_op jit(solution)/shard_map/ppermute | solution.py:513
  31.4 5.2 %collective-permute-start.8 = (f32[128,128]{1,0:T(8,128)S(1)}, f32[128,128]{1,0:T(8,128)S(1)}, u32[]{:S(2)}, u32[]{:S(2)}) collective-permute-start(f32[128,128]{1,0:T(8,128)S(1)} %add.18.a_ref), channel_id=1, source_target_pairs={{0,4},{1,5},{2,6},{3,7},{4,0},{5,1},{6,2},{7,3},{8,12},{9,13},{10,... | collective-permute-start | bytes 196616 | tf_op jit(solution)/shard_map/ppermute | solution.py:541
  36.8 4.5 %collective-permute-start.9 = (f32[128,128]{1,0:T(8,128)S(1)}, f32[128,128]{1,0:T(8,128)S(1)}, u32[]{:S(2)}, u32[]{:S(2)}) collective-permute-start(f32[128,128]{1,0:T(8,128)S(1)} %add.22), channel_id=1, source_target_pairs={{0,2},{1,3},{2,0},{3,1},{4,6},{5,7},{6,4},{7,5},{8,10},{9,11},{10,... | collective-permute-start | bytes 196616 | tf_op jit(solution)/shard_map/ppermute | solution.py:541
  38.6 9.5 %collective-permute-start.11 = (f32[2,128,128]{2,1,0:T(8,128)S(1)}, f32[2,128,128]{2,1,0:T(8,128)S(1)}, u32[]{:S(2)}, u32[]{:S(2)}) collective-permute-start(f32[2,128,128]{2,1,0:T(8,128)S(1)} %get-tuple-element.59), channel_id=1, source_target_pairs={{0,1},{1,0},{2,3},{3,2},{4,5},{5,4},{6,7},{7,6},{8,9},{9,8},{10,11... | collective-permute-start | bytes 393224 | tf_op jit(solution)/shard_map/ppermute | solution.py:508
  39.1 9.0 %collective-permute-start.12 = (f32[2,128,128]{2,1,0:T(8,128)S(1)}, f32[2,128,128]{2,1,0:T(8,128)S(1)}, u32[]{:S(2)}, u32[]{:S(2)}) collective-permute-start(f32[2,128,128]{2,1,0:T(8,128)S(1)} %get-tuple-element.60), channel_id=1, source_target_pairs={{1,2},{3,4},{5,6},{2,1},{4,3},{6,5},{9,10},{11,12},{13,14},{10,9},... | collective-permute-start | bytes 393224 | tf_op jit(solution)/shard_map/ppermute | solution.py:513
  41.3 6.7 %collective-permute-start.10 = (f32[128,128]{1,0:T(8,128)S(1)}, f32[128,128]{1,0:T(8,128)S(1)}, u32[]{:S(2)}, u32[]{:S(2)}) collective-permute-start(f32[128,128]{1,0:T(8,128)S(1)} %add.19), channel_id=1, source_target_pairs={{0,16},{1,17},{2,18},{3,19},{4,20},{5,21},{6,22},{7,23},{8,24},{9,... | collective-permute-start | bytes 196616 | tf_op jit(solution)/shard_map/ppermute | solution.py:541
  48.1 1.3 %collective-permute-start.13 = (f32[128,128]{1,0:T(8,128)S(1)}, f32[128,128]{1,0:T(8,128)S(1)}, u32[]{:S(2)}, u32[]{:S(2)}) collective-permute-start(f32[128,128]{1,0:T(8,128)S(1)} %add.20), channel_id=1, source_target_pairs={{0,8},{8,0},{16,24},{24,16},{1,9},{9,1},{17,25},{25,17},{2,10},{10... | collective-permute-start | bytes 196616 | tf_op jit(solution)/shard_map/ppermute | solution.py:508

commit v11 on v10

--- a/solution.py
+++ b/solution.py
@@ -337,7 +337,11 @@
     large = live // (2 * GROUP)
     run_slots(large, 2 * GROUP, 0, find, window, turned, measured, table, exits, probe_sum)
     first = large * 2 * GROUP
-    run_slots((live - first + GROUP - 1) // GROUP, GROUP, first, find, window, turned, measured, table, exits, probe_sum)
+    groups = (live - first + GROUP // 2 - 1) // GROUP
+    run_slots(groups, GROUP, first, find, window, turned, measured, table, exits, probe_sum)
+    first = first + groups * GROUP
+    few = (live > first).astype(jnp.int32)
+    run_slots(few, GROUP // 2, first, find, window, turned, measured, table, exits, probe_sum)
     factor = 1.0 / np.sqrt(np.float32(lax.axis_size("trow") * lax.axis_size("tcol") * slots))
     mine_out[...] = probe_sum[odd_row] * factor
     other_out[...] = probe_sum[1 - odd_row] * factor

time: 50.9 us -> 50.2 us (0.986)
  Pallas kernels: 20.6 us -> 15.1 us
  starting transfers between devices: 20.4 us -> 23.1 us
  waiting for transfers between devices: 6.8 us -> 9.26 us
    ppermute x6, starting transfers between devices: 6.68 us -> 10.2 us  [near_swap(): lax.ppermute(value, axis, [(i, i ^ 1) for i in range(lax.axis_size(axis))])]
    pallas_call x1, Pallas kernels: 8.44 us -> 5.98 us  [outer_call(): pl.pallas_call(outer_kernel, out_shape=(near((slots + 1,) + turned.shape[...]
    pallas_call x1, Pallas kernels: 4.4 us -> 2.23 us  [inner_call(): pl.pallas_call(inner_kernel, out_shape=(near((slots + 1,) + turned.shape[...]
    ppermute x4, waiting for transfers between devices: 6.47 us -> 7.83 us  [add_partner(): return add(mine, lax.ppermute(mine, ('trow', 'tcol'), pairs))]
    ppermute x6, waiting for transfers between devices: 0.32 us -> 1.41 us  [near_swap(): lax.ppermute(value, axis, [(i, i ^ 1) for i in range(lax.axis_size(axis))])]
    ppermute x4, starting transfers between devices: 11.1 us -> 10.3 us  [add_partner(): return add(mine, lax.ppermute(mine, ('trow', 'tcol'), pairs))]
    pallas_call x1, Pallas kernels: 1.67 us -> 1.1 us  [object_call(): pl.pallas_call(object_kernel, out_shape=(near(grad.shape), row, row, near...]
  transfers between devices with their start and end apart: 14 -> 14, of which waited for: 5 -> 7; matrix products, arithmetic and copies ran while one was open for 0% -> 0% of each run, Pallas kernels for 22% -> 16%
where the time goes in v11:
time: 50.2 us; the launch traced here: 49.6 us
  starting transfers between devices  23.1 us (46%)
  Pallas kernels  15.1 us (30%)
  waiting for transfers between devices  9.26 us (18%)
  between operations  1.46 us (3%)
  other arithmetic  0.7 us (1%)
    ppermute x4, starting transfers between devices, add_partner(): return add(mine, lax.ppermute(mine, ('trow', 'tcol'), pairs))  10.3 us
    ppermute x6, starting transfers between devices, near_swap(): lax.ppermute(value, axis, [(i, i ^ 1) for i in range(lax.axis_size(axis))])  10.2 us
    ppermute x4, waiting for transfers between devices, add_partner(): return add(mine, lax.ppermute(mine, ('trow', 'tcol'), pairs))  7.83 us
    pallas_call x1, Pallas kernels, outer_call(): pl.pallas_call(outer_kernel, out_shape=(near((slots + 1,) + turned.shape[...  5.98 us
    pallas_call x1, Pallas kernels, ready_call(): pl.pallas_call(ready_kernel, out_shape=(pltpu.SMEM((5 * slots + 2,), jnp....  2.92 us
    ppermute x4, starting transfers between devices, far_swap(): return lax.ppermute(value, axis, pairs + [(j, i) for i, j in pairs])  2.64 us
    pallas_call x1, Pallas kernels, inner_call(): pl.pallas_call(inner_kernel, out_shape=(near((slots + 1,) + turned.shape[...  2.23 us
    ppermute x6, waiting for transfers between devices, near_swap(): lax.ppermute(value, axis, [(i, i ^ 1) for i in range(lax.axis_size(axis))])  1.41 us
  transfers between devices with their start and end apart: 14, of which 7 were waited for; matrix products, arithmetic and copies ran while one was open for 0% of the time, Pallas kernels for 16%

profile of v11, /device:TPU:0, one launch (start us, length us, event | category | flops | bytes accessed | tf_op | source)
XLA Modules:
  0.0 49.6 jit_solution(11413917643057493729)
XLA Ops:
  0.6 1.0 %edge_rows.1 = (f32[2,64,256]{2,1,0:T(8,128)S(1)}, f32[2,64,256]{2,1,0:T(8,128)S(1)}) custom-call(f32[2,256,256]{2,1,0:T(8,128)} %centre_ref.3), custom_call_target="tpu_custom_call" | custom-call | tf_op jit(solution)/shard_map/edge_rows/pallas_call | solution.py:97
  1.6 0.5 %collective-permute-start = (f32[2,64,256]{2,1,0:T(8,128)S(1)}, f32[2,64,256]{2,1,0:T(8,128)S(1)}, u32[]{:S(2)}, u32[]{:S(2)}) collective-permute-start(f32[2,64,256]{2,1,0:T(8,128)S(1)} %get-tuple-element.36), channel_id=1, source_target_pairs={{0,8},{8,0},{16,24},{24,16},{1,9},{9,1},{17,25},{25,17},{2,10},{10... | collective-permute-start | bytes 393224 | tf_op jit(solution)/shard_map/ppermute | solution.py:512
  2.2 0.7 %collective-permute-start.1 = (f32[2,64,256]{2,1,0:T(8,128)S(1)}, f32[2,64,256]{2,1,0:T(8,128)S(1)}, u32[]{:S(2)}, u32[]{:S(2)}) collective-permute-start(f32[2,64,256]{2,1,0:T(8,128)S(1)} %get-tuple-element.37), channel_id=1, source_target_pairs={{8,16},{16,8},{9,17},{17,9},{10,18},{18,10},{11,19},{19,11},{12,20... | collective-permute-start | bytes 393224 | tf_op jit(solution)/shard_map/ppermute | solution.py:517
  3.5 2.9 %ready.1 = (s32[242]{0:T(256)S(4)}, f32[48,2,128,128]{3,2,1,0:T(8,128)S(1)}, bf16[48,128,128]{2,1,0:T(8,128)(2,1)S(1)}, bf16[4,256,256]{2,1,0:T(8,128)(2,1)S(1)}, f32[8,384,128]{2,1,0:T(8,128)S(1)}) custom-call(s32[48]{0:T(128)} %bitcast.10, s32[48]{0:T(128)} %bitcast.11, s32[8,128]{1,0:T(8,128)S(1)} %broadcast_in_dim.2.count_ref, f32[2,128,128]{2,1,0:T(8,128)} %probe_ref.1, ...), custom_call_target="tpu_custom_call" | custom-call | tf_op jit(solution)/shard_map/ready/pallas_call | solution.py:158
  6.4 0.0 collective-permute-done.near_ref
  6.4 0.0 collective-permute-done.1.far_ref
  6.4 0.2 side_columns.1
  6.7 2.6 %collective-permute-start.2 = (f32[2,192,128]{2,1,0:T(8,128)S(1)}, f32[2,192,128]{2,1,0:T(8,128)S(1)}, u32[]{:S(2)}, u32[]{:S(2)}) collective-permute-start(f32[2,192,128]{2,1,0:T(8,128)S(1)} %get-tuple-element.39), channel_id=1, source_target_pairs={{0,1},{1,0},{2,3},{3,2},{4,5},{5,4},{6,7},{7,6},{8,9},{9,8},{10,11... | collective-permute-start | bytes 589832 | tf_op jit(solution)/shard_map/ppermute | solution.py:512
  9.2 0.7 %collective-permute-start.3 = (f32[2,192,128]{2,1,0:T(8,128)S(1)}, f32[2,192,128]{2,1,0:T(8,128)S(1)}, u32[]{:S(2)}, u32[]{:S(2)}) collective-permute-start(f32[2,192,128]{2,1,0:T(8,128)S(1)} %get-tuple-element.40), channel_id=1, source_target_pairs={{1,2},{3,4},{5,6},{2,1},{4,3},{6,5},{9,10},{11,12},{13,14},{10,9},... | collective-permute-start | bytes 589832 | tf_op jit(solution)/shard_map/ppermute | solution.py:517
  9.9 2.2 %slots_inside.1 = (f32[49,2,128,128]{3,2,1,0:T(8,128)S(1)}, f32[2,128,128]{2,1,0:T(8,128)S(1)}) custom-call(s32[242]{0:T(256)S(4)} %get-tuple-element.33.plan, f32[8,384,128]{2,1,0:T(8,128)S(1)} %get-tuple-element.38.window.window_ref, f32[48,2,128,128]{3,2,1,0:T(8,128)S(1)} %get-tuple-element.34.turned, ...), custom_call_target="tpu_custom_call" | custom-call | flops 10000000000 | bytes 20000000 | tf_op jit(solution)/shard_map/slots_inside/pallas_call | solution.py:305
  12.2 0.7 %collective-permute-done.2.near_col_ref = f32[2,192,128]{2,1,0:T(8,128)S(1)} collective-permute-done((f32[2,192,128]{2,1,0:T(8,128)S(1)}, f32[2,192,128]{2,1,0:T(8,128)S(1)}, u32[]{:S(2)}, u32[]{:S(2)}) %collective-permute-start.2) | collective-permute-done | bytes 196640 | tf_op jit(solution)/shard_map/ppermute | solution.py:512
  12.9 0.0 collective-permute-done.3.far_col_ref
  12.9 6.0 %slots_across.1 = (f32[49,2,128,128]{3,2,1,0:T(8,128)S(1)}, f32[128,128]{1,0:T(8,128)S(1)}, f32[128,128]{1,0:T(8,128)S(1)}) custom-call(s32[242]{0:T(256)S(4)} %get-tuple-element.33.plan, f32[8,384,128]{2,1,0:T(8,128)S(1)} %get-tuple-element.38.window.window_ref, f32[2,192,128]{2,1,0:T(8,128)S(1)} %collective-permute-done.2.near_col_ref, ...), custom_call_target="tpu_custom_call" | custom-call | flops 10000000000 | bytes 20000000 | tf_op jit(solution)/shard_map/slots_across/pallas_call | solution.py:353
  18.9 6.6 %collective-permute-start.4 = (f32[128,128]{1,0:T(8,128)S(1)}, f32[128,128]{1,0:T(8,128)S(1)}, u32[]{:S(2)}, u32[]{:S(2)}) collective-permute-start(f32[128,128]{1,0:T(8,128)S(1)} %get-tuple-element.47), channel_id=1, source_target_pairs={{0,8},{8,0},{16,24},{24,16},{1,9},{9,1},{17,25},{25,17},{2,10},{10... | collective-permute-start | bytes 196616 | tf_op jit(solution)/shard_map/ppermute | solution.py:512
  25.5 0.5 object_inside.1.grad_ref
  25.9 0.4 collective-permute-done.4
  26.4 2.1 %collective-permute-start.7 = (f32[128,128]{1,0:T(8,128)S(1)}, f32[128,128]{1,0:T(8,128)S(1)}, u32[]{:S(2)}, u32[]{:S(2)}) collective-permute-start(f32[128,128]{1,0:T(8,128)S(1)} %add.17), channel_id=1, source_target_pairs={{0,1},{1,0},{2,3},{3,2},{4,5},{5,4},{6,7},{7,6},{8,9},{9,8},{10,11... | collective-permute-start | bytes 196616 | tf_op jit(solution)/shard_map/ppermute | solution.py:545
  28.5 1.1 %object_across.1 = (f32[8,384,128]{2,1,0:T(8,128)S(1)}, f32[2,64,384]{2,1,0:T(8,128)S(1)}, f32[2,64,384]{2,1,0:T(8,128)S(1)}, f32[2,256,128]{2,1,0:T(8,128)S(1)}) custom-call(s32[242]{0:T(256)S(4)} %get-tuple-element.33.plan, f32[48,2,128,128]{3,2,1,0:T(8,128)S(1)} %get-tuple-element.34.turned, f32[49,2,128,128]{3,2,1,0:T(8,128)S(1)} %get-tuple-element.49.exits, ...), custom_call_target="tpu_custom_call" | custom-call | flops 1000000000 | bytes 100000 | tf_op jit(solution)/shard_map/object_across/pallas_call | solution.py:434
  29.6 0.1 collective-permute-start.5
  29.7 0.7 %collective-permute-start.6 = (f32[2,64,384]{2,1,0:T(8,128)S(1)}, f32[2,64,384]{2,1,0:T(8,128)S(1)}, u32[]{:S(2)}, u32[]{:S(2)}) collective-permute-start(f32[2,64,384]{2,1,0:T(8,128)S(1)} %get-tuple-element.53), channel_id=1, source_target_pairs={{8,16},{16,8},{9,17},{17,9},{10,18},{18,10},{11,19},{19,11},{12,20... | collective-permute-start | bytes 589832 | tf_op jit(solution)/shard_map/ppermute | solution.py:517
  30.4 0.5 %collective-permute-done.7 = f32[128,128]{1,0:T(8,128)S(1)} collective-permute-done((f32[128,128]{1,0:T(8,128)S(1)}, f32[128,128]{1,0:T(8,128)S(1)}, u32[]{:S(2)}, u32[]{:S(2)}) %collective-permute-start.7) | collective-permute-done | bytes 65568 | tf_op jit(solution)/shard_map/ppermute | solution.py:545
  30.9 4.2 %collective-permute-start.8 = (f32[128,128]{1,0:T(8,128)S(1)}, f32[128,128]{1,0:T(8,128)S(1)}, u32[]{:S(2)}, u32[]{:S(2)}) collective-permute-start(f32[128,128]{1,0:T(8,128)S(1)} %add.18.a_ref), channel_id=1, source_target_pairs={{0,4},{1,5},{2,6},{3,7},{4,0},{5,1},{6,2},{7,3},{8,12},{9,13},{10,... | collective-permute-start | bytes 196616 | tf_op jit(solution)/shard_map/ppermute | solution.py:545
  35.1 2.9 %collective-permute-done.8.b_ref = f32[128,128]{1,0:T(8,128)S(1)} collective-permute-done((f32[128,128]{1,0:T(8,128)S(1)}, f32[128,128]{1,0:T(8,128)S(1)}, u32[]{:S(2)}, u32[]{:S(2)}) %collective-permute-start.8) | collective-permute-done | bytes 65568 | tf_op jit(solution)/shard_map/ppermute | solution.py:545
  38.1 0.0 collective-permute-done.5.near_ref.near_row_ref
  38.1 0.0 collective-permute-done.6.far_ref.far_row_ref
  38.1 0.1 side_sums.1
  38.3 1.3 %collective-permute-start.9 = (f32[128,128]{1,0:T(8,128)S(1)}, f32[128,128]{1,0:T(8,128)S(1)}, u32[]{:S(2)}, u32[]{:S(2)}) collective-permute-start(f32[128,128]{1,0:T(8,128)S(1)} %add.22), channel_id=1, source_target_pairs={{0,2},{1,3},{2,0},{3,1},{4,6},{5,7},{6,4},{7,5},{8,10},{9,11},{10,... | collective-permute-start | bytes 196616 | tf_op jit(solution)/shard_map/ppermute | solution.py:545
  39.6 0.3 collective-permute-start.11
  39.9 0.7 %collective-permute-start.12 = (f32[2,128,128]{2,1,0:T(8,128)S(1)}, f32[2,128,128]{2,1,0:T(8,128)S(1)}, u32[]{:S(2)}, u32[]{:S(2)}) collective-permute-start(f32[2,128,128]{2,1,0:T(8,128)S(1)} %get-tuple-element.60), channel_id=1, source_target_pairs={{1,2},{3,4},{5,6},{2,1},{4,3},{6,5},{9,10},{11,12},{13,14},{10,9},... | collective-permute-start | bytes 393224 | tf_op jit(solution)/shard_map/ppermute | solution.py:517
  40.6 2.0 %collective-permute-done.9 = f32[128,128]{1,0:T(8,128)S(1)} collective-permute-done((f32[128,128]{1,0:T(8,128)S(1)}, f32[128,128]{1,0:T(8,128)S(1)}, u32[]{:S(2)}, u32[]{:S(2)}) %collective-permute-start.9) | collective-permute-done | bytes 65568 | tf_op jit(solution)/shard_map/ppermute | solution.py:545
  42.6 2.6 %collective-permute-start.10 = (f32[128,128]{1,0:T(8,128)S(1)}, f32[128,128]{1,0:T(8,128)S(1)}, u32[]{:S(2)}, u32[]{:S(2)}) collective-permute-start(f32[128,128]{1,0:T(8,128)S(1)} %add.19), channel_id=1, source_target_pairs={{0,16},{1,17},{2,18},{3,19},{4,20},{5,21},{6,22},{7,23},{8,24},{9,... | collective-permute-start | bytes 196616 | tf_op jit(solution)/shard_map/ppermute | solution.py:545
  45.2 2.4 %collective-permute-done.10 = f32[128,128]{1,0:T(8,128)S(1)} collective-permute-done((f32[128,128]{1,0:T(8,128)S(1)}, f32[128,128]{1,0:T(8,128)S(1)}, u32[]{:S(2)}, u32[]{:S(2)}) %collective-permute-start.10) | collective-permute-done | bytes 65568 | tf_op jit(solution)/shard_map/ppermute | solution.py:545
  47.6 0.0 collective-permute-done.11.near_col_ref
  47.6 0.0 collective-permute-done.12.far_col_ref
  47.7 0.1 collective-permute-start.13
  47.7 1.0 %final_sums.1 = f32[2,256,256]{2,1,0:T(8,128)} custom-call(f32[8,384,128]{2,1,0:T(8,128)S(1)} %get-tuple-element.51.grad, f32[2,64,384]{2,1,0:T(8,128)S(1)} %collective-permute-done.5.near_ref.near_row_ref, f32[2,64,384]{2,1,0:T(8,128)S(1)} %collective-permute-done.6.far_ref.far_row_ref, f32[2,128,128]{2,1,0:T(8,128)S(1)} %collective-permute-done.11.near_col_ref, ...), custom_call_target="tpu_custom_call" | custom-call | tf_op jit(solution)/shard_map/final_sums/pallas_call | solution.py:501
  48.7 0.2 collective-permute-done.13
  49.0 0.7 %maximum_select_fusion = f32[2,128,128]{2,1,0:T(8,128)} fusion(f32[1,128,128]{2,1,0:T(8,128)S(1)} %bitcast.9, f32[1,128,128]{2,1,0:T(8,128)S(1)} %bitcast.8, pred[]{:T(512)S(6)} %eq.5), kind=kLoop, calls=%fused_computation | loop fusion | flops 98304 | bytes 262145 | tf_op jit(solution)/shard_map/jit(_where)/select_n | solution.py:582
  (6 shorter events, 0.0 us)
Async XLA Ops:
  1.6 4.8 %collective-permute-start = (f32[2,64,256]{2,1,0:T(8,128)S(1)}, f32[2,64,256]{2,1,0:T(8,128)S(1)}, u32[]{:S(2)}, u32[]{:S(2)}) collective-permute-start(f32[2,64,256]{2,1,0:T(8,128)S(1)} %get-tuple-element.36), channel_id=1, source_target_pairs={{0,8},{8,0},{16,24},{24,16},{1,9},{9,1},{17,25},{25,17},{2,10},{10... | collective-permute-start | bytes 393224 | tf_op jit(solution)/shard_map/ppermute | solution.py:512
  2.2 4.3 %collective-permute-start.1 = (f32[2,64,256]{2,1,0:T(8,128)S(1)}, f32[2,64,256]{2,1,0:T(8,128)S(1)}, u32[]{:S(2)}, u32[]{:S(2)}) collective-permute-start(f32[2,64,256]{2,1,0:T(8,128)S(1)} %get-tuple-element.37), channel_id=1, source_target_pairs={{8,16},{16,8},{9,17},{17,9},{10,18},{18,10},{11,19},{19,11},{12,20... | collective-permute-start | bytes 393224 | tf_op jit(solution)/shard_map/ppermute | solution.py:517
  6.7 6.2 %collective-permute-start.2 = (f32[2,192,128]{2,1,0:T(8,128)S(1)}, f32[2,192,128]{2,1,0:T(8,128)S(1)}, u32[]{:S(2)}, u32[]{:S(2)}) collective-permute-start(f32[2,192,128]{2,1,0:T(8,128)S(1)} %get-tuple-element.39), channel_id=1, source_target_pairs={{0,1},{1,0},{2,3},{3,2},{4,5},{5,4},{6,7},{7,6},{8,9},{9,8},{10,11... | collective-permute-start | bytes 589832 | tf_op jit(solution)/shard_map/ppermute | solution.py:512
  9.2 3.7 %collective-permute-start.3 = (f32[2,192,128]{2,1,0:T(8,128)S(1)}, f32[2,192,128]{2,1,0:T(8,128)S(1)}, u32[]{:S(2)}, u32[]{:S(2)}) collective-permute-start(f32[2,192,128]{2,1,0:T(8,128)S(1)} %get-tuple-element.40), channel_id=1, source_target_pairs={{1,2},{3,4},{5,6},{2,1},{4,3},{6,5},{9,10},{11,12},{13,14},{10,9},... | collective-permute-start | bytes 589832 | tf_op jit(solution)/shard_map/ppermute | solution.py:517
  18.9 7.5 %collective-permute-start.4 = (f32[128,128]{1,0:T(8,128)S(1)}, f32[128,128]{1,0:T(8,128)S(1)}, u32[]{:S(2)}, u32[]{:S(2)}) collective-permute-start(f32[128,128]{1,0:T(8,128)S(1)} %get-tuple-element.47), channel_id=1, source_target_pairs={{0,8},{8,0},{16,24},{24,16},{1,9},{9,1},{17,25},{25,17},{2,10},{10... | collective-permute-start | bytes 196616 | tf_op jit(solution)/shard_map/ppermute | solution.py:512
  26.4 4.5 %collective-permute-start.7 = (f32[128,128]{1,0:T(8,128)S(1)}, f32[128,128]{1,0:T(8,128)S(1)}, u32[]{:S(2)}, u32[]{:S(2)}) collective-permute-start(f32[128,128]{1,0:T(8,128)S(1)} %add.17), channel_id=1, source_target_pairs={{0,1},{1,0},{2,3},{3,2},{4,5},{5,4},{6,7},{7,6},{8,9},{9,8},{10,11... | collective-permute-start | bytes 196616 | tf_op jit(solution)/shard_map/ppermute | solution.py:545
  29.6 8.5 %collective-permute-start.5 = (f32[2,64,384]{2,1,0:T(8,128)S(1)}, f32[2,64,384]{2,1,0:T(8,128)S(1)}, u32[]{:S(2)}, u32[]{:S(2)}) collective-permute-start(f32[2,64,384]{2,1,0:T(8,128)S(1)} %get-tuple-element.52), channel_id=1, source_target_pairs={{0,8},{8,0},{16,24},{24,16},{1,9},{9,1},{17,25},{25,17},{2,10},{10... | collective-permute-start | bytes 589832 | tf_op jit(solution)/shard_map/ppermute | solution.py:512
  29.7 8.4 %collective-permute-start.6 = (f32[2,64,384]{2,1,0:T(8,128)S(1)}, f32[2,64,384]{2,1,0:T(8,128)S(1)}, u32[]{:S(2)}, u32[]{:S(2)}) collective-permute-start(f32[2,64,384]{2,1,0:T(8,128)S(1)} %get-tuple-element.53), channel_id=1, source_target_pairs={{8,16},{16,8},{9,17},{17,9},{10,18},{18,10},{11,19},{19,11},{12,20... | collective-permute-start | bytes 589832 | tf_op jit(solution)/shard_map/ppermute | solution.py:517
  30.9 7.2 %collective-permute-start.8 = (f32[128,128]{1,0:T(8,128)S(1)}, f32[128,128]{1,0:T(8,128)S(1)}, u32[]{:S(2)}, u32[]{:S(2)}) collective-permute-start(f32[128,128]{1,0:T(8,128)S(1)} %add.18.a_ref), channel_id=1, source_target_pairs={{0,4},{1,5},{2,6},{3,7},{4,0},{5,1},{6,2},{7,3},{8,12},{9,13},{10,... | collective-permute-start | bytes 196616 | tf_op jit(solution)/shard_map/ppermute | solution.py:545
  38.3 4.3 %collective-permute-start.9 = (f32[128,128]{1,0:T(8,128)S(1)}, f32[128,128]{1,0:T(8,128)S(1)}, u32[]{:S(2)}, u32[]{:S(2)}) collective-permute-start(f32[128,128]{1,0:T(8,128)S(1)} %add.22), channel_id=1, source_target_pairs={{0,2},{1,3},{2,0},{3,1},{4,6},{5,7},{6,4},{7,5},{8,10},{9,11},{10,... | collective-permute-start | bytes 196616 | tf_op jit(solution)/shard_map/ppermute | solution.py:545
  39.6 8.0 %collective-permute-start.11 = (f32[2,128,128]{2,1,0:T(8,128)S(1)}, f32[2,128,128]{2,1,0:T(8,128)S(1)}, u32[]{:S(2)}, u32[]{:S(2)}) collective-permute-start(f32[2,128,128]{2,1,0:T(8,128)S(1)} %get-tuple-element.59), channel_id=1, source_target_pairs={{0,1},{1,0},{2,3},{3,2},{4,5},{5,4},{6,7},{7,6},{8,9},{9,8},{10,11... | collective-permute-start | bytes 393224 | tf_op jit(solution)/shard_map/ppermute | solution.py:512
  39.9 7.7 %collective-permute-start.12 = (f32[2,128,128]{2,1,0:T(8,128)S(1)}, f32[2,128,128]{2,1,0:T(8,128)S(1)}, u32[]{:S(2)}, u32[]{:S(2)}) collective-permute-start(f32[2,128,128]{2,1,0:T(8,128)S(1)} %get-tuple-element.60), channel_id=1, source_target_pairs={{1,2},{3,4},{5,6},{2,1},{4,3},{6,5},{9,10},{11,12},{13,14},{10,9},... | collective-permute-start | bytes 393224 | tf_op jit(solution)/shard_map/ppermute | solution.py:517
  42.6 5.0 %collective-permute-start.10 = (f32[128,128]{1,0:T(8,128)S(1)}, f32[128,128]{1,0:T(8,128)S(1)}, u32[]{:S(2)}, u32[]{:S(2)}) collective-permute-start(f32[128,128]{1,0:T(8,128)S(1)} %add.19), channel_id=1, source_target_pairs={{0,16},{1,17},{2,18},{3,19},{4,20},{5,21},{6,22},{7,23},{8,24},{9,... | collective-permute-start | bytes 196616 | tf_op jit(solution)/shard_map/ppermute | solution.py:545
  47.7 1.3 %collective-permute-start.13 = (f32[128,128]{1,0:T(8,128)S(1)}, f32[128,128]{1,0:T(8,128)S(1)}, u32[]{:S(2)}, u32[]{:S(2)}) collective-permute-start(f32[128,128]{1,0:T(8,128)S(1)} %add.20), channel_id=1, source_target_pairs={{0,8},{8,0},{16,24},{24,16},{1,9},{9,1},{17,25},{25,17},{2,10},{10... | collective-permute-start | bytes 196616 | tf_op jit(solution)/shard_map/ppermute | solution.py:512

commit v12 on v10

--- a/solution.py
+++ b/solution.py
@@ -53,7 +53,9 @@
 
 def times_table(value, high, low):
     big, small = split(value)
-    return dot(jnp.concatenate([big, small, big], axis=1), jnp.concatenate([high, high, low], axis=0))
+    rows = value.shape[0]
+    both = dot(jnp.concatenate([big, small], axis=0), high)
+    return both[:rows] + (both[rows:] + dot(big, low))
 
 
 def table_times(high, low, value):

time: 50.9 us -> 51.4 us (level)
  Pallas kernels: 20.6 us -> 10.9 us
  starting transfers between devices: 20.4 us -> 26.5 us
  waiting for transfers between devices: 6.8 us -> 11.5 us
    ppermute x6, starting transfers between devices: 6.68 us -> 14.6 us  [near_swap(): lax.ppermute(value, axis, [(i, i ^ 1) for i in range(lax.axis_size(axis))])]
    pallas_call x1, Pallas kernels: 4.4 us -> 0.02 us  [inner_call(): pl.pallas_call(inner_kernel, out_shape=(near((slots + 1,) + turned.shape[...]
    pallas_call x1, Pallas kernels: 8.44 us -> 4.61 us  [outer_call(): pl.pallas_call(outer_kernel, out_shape=(near((slots + 1,) + turned.shape[...]
    ppermute x6, waiting for transfers between devices: 0.32 us -> 4 us  [near_swap(): lax.ppermute(value, axis, [(i, i ^ 1) for i in range(lax.axis_size(axis))])]
    ppermute x4, starting transfers between devices: 11.1 us -> 9.24 us  [add_partner(): return add(mine, lax.ppermute(mine, ('trow', 'tcol'), pairs))]
    ppermute x4, waiting for transfers between devices: 6.47 us -> 7.51 us  [add_partner(): return add(mine, lax.ppermute(mine, ('trow', 'tcol'), pairs))]
    pallas_call x1, Pallas kernels: 1.67 us -> 0.92 us  [object_call(): pl.pallas_call(object_kernel, out_shape=(near(grad.shape), row, row, near...]
    pallas_call x1, Pallas kernels: 0.84 us -> 0.1 us  [first_object_call(): pl.pallas_call(first_object_kernel, out_shape=near(window.shape), in_spec...]
  transfers between devices with their start and end apart: 14 -> 14, of which waited for: 5 -> 7; matrix products, arithmetic and copies ran while one was open for 0% -> 0% of each run, Pallas kernels for 22% -> 10%
where the time goes in v12:
time: 51.4 us; the launch traced here: 51.1 us
  starting transfers between devices  26.5 us (52%)
  waiting for transfers between devices  11.5 us (22%)
  Pallas kernels  10.9 us (21%)
  between operations  1.46 us (3%)
  other arithmetic  0.7 us (1%)
    ppermute x6, starting transfers between devices, near_swap(): lax.ppermute(value, axis, [(i, i ^ 1) for i in range(lax.axis_size(axis))])  14.6 us
    ppermute x4, starting transfers between devices, add_partner(): return add(mine, lax.ppermute(mine, ('trow', 'tcol'), pairs))  9.24 us
    ppermute x4, waiting for transfers between devices, add_partner(): return add(mine, lax.ppermute(mine, ('trow', 'tcol'), pairs))  7.51 us
    pallas_call x1, Pallas kernels, outer_call(): pl.pallas_call(outer_kernel, out_shape=(near((slots + 1,) + turned.shape[...  4.61 us
    ppermute x6, waiting for transfers between devices, near_swap(): lax.ppermute(value, axis, [(i, i ^ 1) for i in range(lax.axis_size(axis))])  4 us
    pallas_call x1, Pallas kernels, ready_call(): pl.pallas_call(ready_kernel, out_shape=(pltpu.SMEM((5 * slots + 2,), jnp....  2.92 us
    ppermute x4, starting transfers between devices, far_swap(): return lax.ppermute(value, axis, pairs + [(j, i) for i, j in pairs])  2.64 us
  transfers between devices with their start and end apart: 14, of which 7 were waited for; matrix products, arithmetic and copies ran while one was open for 0% of the time, Pallas kernels for 10%

profile of v12, /device:TPU:0, one launch (start us, length us, event | category | flops | bytes accessed | tf_op | source)
XLA Modules:
  0.0 51.1 jit_solution(10518602244703373604)
XLA Ops:
  0.6 1.0 %edge_rows.1 = (f32[2,64,256]{2,1,0:T(8,128)S(1)}, f32[2,64,256]{2,1,0:T(8,128)S(1)}) custom-call(f32[2,256,256]{2,1,0:T(8,128)} %centre_ref.3), custom_call_target="tpu_custom_call" | custom-call | tf_op jit(solution)/shard_map/edge_rows/pallas_call | solution.py:99
  1.6 0.5 %collective-permute-start = (f32[2,64,256]{2,1,0:T(8,128)S(1)}, f32[2,64,256]{2,1,0:T(8,128)S(1)}, u32[]{:S(2)}, u32[]{:S(2)}) collective-permute-start(f32[2,64,256]{2,1,0:T(8,128)S(1)} %get-tuple-element.36), channel_id=1, source_target_pairs={{0,8},{8,0},{16,24},{24,16},{1,9},{9,1},{17,25},{25,17},{2,10},{10... | collective-permute-start | bytes 393224 | tf_op jit(solution)/shard_map/ppermute | solution.py:510
  2.2 0.7 %collective-permute-start.1 = (f32[2,64,256]{2,1,0:T(8,128)S(1)}, f32[2,64,256]{2,1,0:T(8,128)S(1)}, u32[]{:S(2)}, u32[]{:S(2)}) collective-permute-start(f32[2,64,256]{2,1,0:T(8,128)S(1)} %get-tuple-element.37), channel_id=1, source_target_pairs={{8,16},{16,8},{9,17},{17,9},{10,18},{18,10},{11,19},{19,11},{12,20... | collective-permute-start | bytes 393224 | tf_op jit(solution)/shard_map/ppermute | solution.py:515
  3.5 2.9 %ready.1 = (s32[242]{0:T(256)S(4)}, f32[48,2,128,128]{3,2,1,0:T(8,128)S(1)}, bf16[48,128,128]{2,1,0:T(8,128)(2,1)S(1)}, bf16[4,256,256]{2,1,0:T(8,128)(2,1)S(1)}, f32[8,384,128]{2,1,0:T(8,128)S(1)}) custom-call(s32[48]{0:T(128)} %bitcast.10, s32[48]{0:T(128)} %bitcast.11, s32[8,128]{1,0:T(8,128)S(1)} %broadcast_in_dim.2.count_ref, f32[2,128,128]{2,1,0:T(8,128)} %probe_ref.1, ...), custom_call_target="tpu_custom_call" | custom-call | tf_op jit(solution)/shard_map/ready/pallas_call | solution.py:160
  6.4 0.0 collective-permute-done.near_ref
  6.4 0.0 collective-permute-done.1.far_ref
  6.4 0.2 side_columns.1
  6.7 2.6 %collective-permute-start.2 = (f32[2,192,128]{2,1,0:T(8,128)S(1)}, f32[2,192,128]{2,1,0:T(8,128)S(1)}, u32[]{:S(2)}, u32[]{:S(2)}) collective-permute-start(f32[2,192,128]{2,1,0:T(8,128)S(1)} %get-tuple-element.39), channel_id=1, source_target_pairs={{0,1},{1,0},{2,3},{3,2},{4,5},{5,4},{6,7},{7,6},{8,9},{9,8},{10,11... | collective-permute-start | bytes 589832 | tf_op jit(solution)/shard_map/ppermute | solution.py:510
  9.2 0.7 %collective-permute-start.3 = (f32[2,192,128]{2,1,0:T(8,128)S(1)}, f32[2,192,128]{2,1,0:T(8,128)S(1)}, u32[]{:S(2)}, u32[]{:S(2)}) collective-permute-start(f32[2,192,128]{2,1,0:T(8,128)S(1)} %get-tuple-element.40), channel_id=1, source_target_pairs={{1,2},{3,4},{5,6},{2,1},{4,3},{6,5},{9,10},{11,12},{13,14},{10,9},... | collective-permute-start | bytes 589832 | tf_op jit(solution)/shard_map/ppermute | solution.py:515
  9.9 3.0 %collective-permute-done.2.near_col_ref = f32[2,192,128]{2,1,0:T(8,128)S(1)} collective-permute-done((f32[2,192,128]{2,1,0:T(8,128)S(1)}, f32[2,192,128]{2,1,0:T(8,128)S(1)}, u32[]{:S(2)}, u32[]{:S(2)}) %collective-permute-start.2) | collective-permute-done | bytes 196640 | tf_op jit(solution)/shard_map/ppermute | solution.py:510
  12.9 0.0 collective-permute-done.3.far_col_ref
  12.9 4.6 %slots_across.1 = (f32[49,2,128,128]{3,2,1,0:T(8,128)S(1)}, f32[128,128]{1,0:T(8,128)S(1)}, f32[128,128]{1,0:T(8,128)S(1)}) custom-call(s32[242]{0:T(256)S(4)} %get-tuple-element.33.plan, f32[8,384,128]{2,1,0:T(8,128)S(1)} %get-tuple-element.38.window.window_ref, f32[2,192,128]{2,1,0:T(8,128)S(1)} %collective-permute-done.2.near_col_ref, ...), custom_call_target="tpu_custom_call" | custom-call | flops 10000000000 | bytes 20000000 | tf_op jit(solution)/shard_map/slots_across/pallas_call | solution.py:351
  17.5 9.8 %collective-permute-start.4 = (f32[128,128]{1,0:T(8,128)S(1)}, f32[128,128]{1,0:T(8,128)S(1)}, u32[]{:S(2)}, u32[]{:S(2)}) collective-permute-start(f32[128,128]{1,0:T(8,128)S(1)} %get-tuple-element.47), channel_id=1, source_target_pairs={{0,8},{8,0},{16,24},{24,16},{1,9},{9,1},{17,25},{25,17},{2,10},{10... | collective-permute-start | bytes 196616 | tf_op jit(solution)/shard_map/ppermute | solution.py:510
  27.3 0.1 object_inside.1.grad_ref
  27.4 0.8 %collective-permute-done.4 = f32[128,128]{1,0:T(8,128)S(1)} collective-permute-done((f32[128,128]{1,0:T(8,128)S(1)}, f32[128,128]{1,0:T(8,128)S(1)}, u32[]{:S(2)}, u32[]{:S(2)}) %collective-permute-start.4) | collective-permute-done | bytes 65568 | tf_op jit(solution)/shard_map/ppermute | solution.py:510
  28.2 0.4 collective-permute-start.7
  28.6 0.9 %object_across.1 = (f32[8,384,128]{2,1,0:T(8,128)S(1)}, f32[2,64,384]{2,1,0:T(8,128)S(1)}, f32[2,64,384]{2,1,0:T(8,128)S(1)}, f32[2,256,128]{2,1,0:T(8,128)S(1)}) custom-call(s32[242]{0:T(256)S(4)} %get-tuple-element.33.plan, f32[48,2,128,128]{3,2,1,0:T(8,128)S(1)} %get-tuple-element.34.turned, f32[49,2,128,128]{3,2,1,0:T(8,128)S(1)} %get-tuple-element.49.exits, ...), custom_call_target="tpu_custom_call" | custom-call | flops 1000000000 | bytes 100000 | tf_op jit(solution)/shard_map/object_across/pallas_call | solution.py:432
  29.5 0.9 %collective-permute-start.5 = (f32[2,64,384]{2,1,0:T(8,128)S(1)}, f32[2,64,384]{2,1,0:T(8,128)S(1)}, u32[]{:S(2)}, u32[]{:S(2)}) collective-permute-start(f32[2,64,384]{2,1,0:T(8,128)S(1)} %get-tuple-element.52), channel_id=1, source_target_pairs={{0,8},{8,0},{16,24},{24,16},{1,9},{9,1},{17,25},{25,17},{2,10},{10... | collective-permute-start | bytes 589832 | tf_op jit(solution)/shard_map/ppermute | solution.py:510
  30.4 0.7 %collective-permute-start.6 = (f32[2,64,384]{2,1,0:T(8,128)S(1)}, f32[2,64,384]{2,1,0:T(8,128)S(1)}, u32[]{:S(2)}, u32[]{:S(2)}) collective-permute-start(f32[2,64,384]{2,1,0:T(8,128)S(1)} %get-tuple-element.53), channel_id=1, source_target_pairs={{8,16},{16,8},{9,17},{17,9},{10,18},{18,10},{11,19},{19,11},{12,20... | collective-permute-start | bytes 589832 | tf_op jit(solution)/shard_map/ppermute | solution.py:515
  31.1 1.5 %collective-permute-done.7 = f32[128,128]{1,0:T(8,128)S(1)} collective-permute-done((f32[128,128]{1,0:T(8,128)S(1)}, f32[128,128]{1,0:T(8,128)S(1)}, u32[]{:S(2)}, u32[]{:S(2)}) %collective-permute-start.7) | collective-permute-done | bytes 65568 | tf_op jit(solution)/shard_map/ppermute | solution.py:543
  32.6 3.3 %collective-permute-start.8 = (f32[128,128]{1,0:T(8,128)S(1)}, f32[128,128]{1,0:T(8,128)S(1)}, u32[]{:S(2)}, u32[]{:S(2)}) collective-permute-start(f32[128,128]{1,0:T(8,128)S(1)} %add.18.a_ref), channel_id=1, source_target_pairs={{0,4},{1,5},{2,6},{3,7},{4,0},{5,1},{6,2},{7,3},{8,12},{9,13},{10,... | collective-permute-start | bytes 196616 | tf_op jit(solution)/shard_map/ppermute | solution.py:543
  35.9 2.2 %collective-permute-done.8.b_ref = f32[128,128]{1,0:T(8,128)S(1)} collective-permute-done((f32[128,128]{1,0:T(8,128)S(1)}, f32[128,128]{1,0:T(8,128)S(1)}, u32[]{:S(2)}, u32[]{:S(2)}) %collective-permute-start.8) | collective-permute-done | bytes 65568 | tf_op jit(solution)/shard_map/ppermute | solution.py:543
  38.2 0.0 collective-permute-done.5.near_ref.near_row_ref
  38.2 0.0 collective-permute-done.6.far_ref.far_row_ref
  38.2 0.1 side_sums.1
  38.4 1.4 %collective-permute-start.9 = (f32[128,128]{1,0:T(8,128)S(1)}, f32[128,128]{1,0:T(8,128)S(1)}, u32[]{:S(2)}, u32[]{:S(2)}) collective-permute-start(f32[128,128]{1,0:T(8,128)S(1)} %add.22), channel_id=1, source_target_pairs={{0,2},{1,3},{2,0},{3,1},{4,6},{5,7},{6,4},{7,5},{8,10},{9,11},{10,... | collective-permute-start | bytes 196616 | tf_op jit(solution)/shard_map/ppermute | solution.py:543
  39.8 0.8 %collective-permute-start.11 = (f32[2,128,128]{2,1,0:T(8,128)S(1)}, f32[2,128,128]{2,1,0:T(8,128)S(1)}, u32[]{:S(2)}, u32[]{:S(2)}) collective-permute-start(f32[2,128,128]{2,1,0:T(8,128)S(1)} %get-tuple-element.59), channel_id=1, source_target_pairs={{0,1},{1,0},{2,3},{3,2},{4,5},{5,4},{6,7},{7,6},{8,9},{9,8},{10,11... | collective-permute-start | bytes 393224 | tf_op jit(solution)/shard_map/ppermute | solution.py:510
  40.5 0.7 %collective-permute-start.12 = (f32[2,128,128]{2,1,0:T(8,128)S(1)}, f32[2,128,128]{2,1,0:T(8,128)S(1)}, u32[]{:S(2)}, u32[]{:S(2)}) collective-permute-start(f32[2,128,128]{2,1,0:T(8,128)S(1)} %get-tuple-element.60), channel_id=1, source_target_pairs={{1,2},{3,4},{5,6},{2,1},{4,3},{6,5},{9,10},{11,12},{13,14},{10,9},... | collective-permute-start | bytes 393224 | tf_op jit(solution)/shard_map/ppermute | solution.py:515
  41.2 1.5 %collective-permute-done.9 = f32[128,128]{1,0:T(8,128)S(1)} collective-permute-done((f32[128,128]{1,0:T(8,128)S(1)}, f32[128,128]{1,0:T(8,128)S(1)}, u32[]{:S(2)}, u32[]{:S(2)}) %collective-permute-start.9) | collective-permute-done | bytes 65568 | tf_op jit(solution)/shard_map/ppermute | solution.py:543
  42.7 4.1 %collective-permute-start.10 = (f32[128,128]{1,0:T(8,128)S(1)}, f32[128,128]{1,0:T(8,128)S(1)}, u32[]{:S(2)}, u32[]{:S(2)}) collective-permute-start(f32[128,128]{1,0:T(8,128)S(1)} %add.19), channel_id=1, source_target_pairs={{0,16},{1,17},{2,18},{3,19},{4,20},{5,21},{6,22},{7,23},{8,24},{9,... | collective-permute-start | bytes 196616 | tf_op jit(solution)/shard_map/ppermute | solution.py:543
  46.8 2.2 %collective-permute-done.10 = f32[128,128]{1,0:T(8,128)S(1)} collective-permute-done((f32[128,128]{1,0:T(8,128)S(1)}, f32[128,128]{1,0:T(8,128)S(1)}, u32[]{:S(2)}, u32[]{:S(2)}) %collective-permute-start.10) | collective-permute-done | bytes 65568 | tf_op jit(solution)/shard_map/ppermute | solution.py:543
  49.1 0.0 collective-permute-done.11.near_col_ref
  49.1 0.0 collective-permute-done.12.far_col_ref
  49.1 0.1 collective-permute-start.13
  49.2 1.0 %final_sums.1 = f32[2,256,256]{2,1,0:T(8,128)} custom-call(f32[8,384,128]{2,1,0:T(8,128)S(1)} %get-tuple-element.51.grad, f32[2,64,384]{2,1,0:T(8,128)S(1)} %collective-permute-done.5.near_ref.near_row_ref, f32[2,64,384]{2,1,0:T(8,128)S(1)} %collective-permute-done.6.far_ref.far_row_ref, f32[2,128,128]{2,1,0:T(8,128)S(1)} %collective-permute-done.11.near_col_ref, ...), custom_call_target="tpu_custom_call" | custom-call | tf_op jit(solution)/shard_map/final_sums/pallas_call | solution.py:499
  50.2 0.2 collective-permute-done.13
  50.4 0.7 %maximum_select_fusion = f32[2,128,128]{2,1,0:T(8,128)} fusion(f32[1,128,128]{2,1,0:T(8,128)S(1)} %bitcast.9, f32[1,128,128]{2,1,0:T(8,128)S(1)} %bitcast.8, pred[]{:T(512)S(6)} %eq.5), kind=kLoop, calls=%fused_computation | loop fusion | flops 98304 | bytes 262145 | tf_op jit(solution)/shard_map/jit(_where)/select_n | solution.py:580
  (7 shorter events, 0.1 us)
Async XLA Ops:
  1.6 4.8 %collective-permute-start = (f32[2,64,256]{2,1,0:T(8,128)S(1)}, f32[2,64,256]{2,1,0:T(8,128)S(1)}, u32[]{:S(2)}, u32[]{:S(2)}) collective-permute-start(f32[2,64,256]{2,1,0:T(8,128)S(1)} %get-tuple-element.36), channel_id=1, source_target_pairs={{0,8},{8,0},{16,24},{24,16},{1,9},{9,1},{17,25},{25,17},{2,10},{10... | collective-permute-start | bytes 393224 | tf_op jit(solution)/shard_map/ppermute | solution.py:510
  2.2 4.3 %collective-permute-start.1 = (f32[2,64,256]{2,1,0:T(8,128)S(1)}, f32[2,64,256]{2,1,0:T(8,128)S(1)}, u32[]{:S(2)}, u32[]{:S(2)}) collective-permute-start(f32[2,64,256]{2,1,0:T(8,128)S(1)} %get-tuple-element.37), channel_id=1, source_target_pairs={{8,16},{16,8},{9,17},{17,9},{10,18},{18,10},{11,19},{19,11},{12,20... | collective-permute-start | bytes 393224 | tf_op jit(solution)/shard_map/ppermute | solution.py:515
  6.7 6.2 %collective-permute-start.2 = (f32[2,192,128]{2,1,0:T(8,128)S(1)}, f32[2,192,128]{2,1,0:T(8,128)S(1)}, u32[]{:S(2)}, u32[]{:S(2)}) collective-permute-start(f32[2,192,128]{2,1,0:T(8,128)S(1)} %get-tuple-element.39), channel_id=1, source_target_pairs={{0,1},{1,0},{2,3},{3,2},{4,5},{5,4},{6,7},{7,6},{8,9},{9,8},{10,11... | collective-permute-start | bytes 589832 | tf_op jit(solution)/shard_map/ppermute | solution.py:510
  9.2 3.7 %collective-permute-start.3 = (f32[2,192,128]{2,1,0:T(8,128)S(1)}, f32[2,192,128]{2,1,0:T(8,128)S(1)}, u32[]{:S(2)}, u32[]{:S(2)}) collective-permute-start(f32[2,192,128]{2,1,0:T(8,128)S(1)} %get-tuple-element.40), channel_id=1, source_target_pairs={{1,2},{3,4},{5,6},{2,1},{4,3},{6,5},{9,10},{11,12},{13,14},{10,9},... | collective-permute-start | bytes 589832 | tf_op jit(solution)/shard_map/ppermute | solution.py:515
  17.5 10.7 %collective-permute-start.4 = (f32[128,128]{1,0:T(8,128)S(1)}, f32[128,128]{1,0:T(8,128)S(1)}, u32[]{:S(2)}, u32[]{:S(2)}) collective-permute-start(f32[128,128]{1,0:T(8,128)S(1)} %get-tuple-element.47), channel_id=1, source_target_pairs={{0,8},{8,0},{16,24},{24,16},{1,9},{9,1},{17,25},{25,17},{2,10},{10... | collective-permute-start | bytes 196616 | tf_op jit(solution)/shard_map/ppermute | solution.py:510
  28.2 4.4 %collective-permute-start.7 = (f32[128,128]{1,0:T(8,128)S(1)}, f32[128,128]{1,0:T(8,128)S(1)}, u32[]{:S(2)}, u32[]{:S(2)}) collective-permute-start(f32[128,128]{1,0:T(8,128)S(1)} %add.17), channel_id=1, source_target_pairs={{0,1},{1,0},{2,3},{3,2},{4,5},{5,4},{6,7},{7,6},{8,9},{9,8},{10,11... | collective-permute-start | bytes 196616 | tf_op jit(solution)/shard_map/ppermute | solution.py:543
  29.5 8.7 %collective-permute-start.5 = (f32[2,64,384]{2,1,0:T(8,128)S(1)}, f32[2,64,384]{2,1,0:T(8,128)S(1)}, u32[]{:S(2)}, u32[]{:S(2)}) collective-permute-start(f32[2,64,384]{2,1,0:T(8,128)S(1)} %get-tuple-element.52), channel_id=1, source_target_pairs={{0,8},{8,0},{16,24},{24,16},{1,9},{9,1},{17,25},{25,17},{2,10},{10... | collective-permute-start | bytes 589832 | tf_op jit(solution)/shard_map/ppermute | solution.py:510
  30.4 7.8 %collective-permute-start.6 = (f32[2,64,384]{2,1,0:T(8,128)S(1)}, f32[2,64,384]{2,1,0:T(8,128)S(1)}, u32[]{:S(2)}, u32[]{:S(2)}) collective-permute-start(f32[2,64,384]{2,1,0:T(8,128)S(1)} %get-tuple-element.53), channel_id=1, source_target_pairs={{8,16},{16,8},{9,17},{17,9},{10,18},{18,10},{11,19},{19,11},{12,20... | collective-permute-start | bytes 589832 | tf_op jit(solution)/shard_map/ppermute | solution.py:515
  32.6 5.5 %collective-permute-start.8 = (f32[128,128]{1,0:T(8,128)S(1)}, f32[128,128]{1,0:T(8,128)S(1)}, u32[]{:S(2)}, u32[]{:S(2)}) collective-permute-start(f32[128,128]{1,0:T(8,128)S(1)} %add.18.a_ref), channel_id=1, source_target_pairs={{0,4},{1,5},{2,6},{3,7},{4,0},{5,1},{6,2},{7,3},{8,12},{9,13},{10,... | collective-permute-start | bytes 196616 | tf_op jit(solution)/shard_map/ppermute | solution.py:543
  38.4 4.3 %collective-permute-start.9 = (f32[128,128]{1,0:T(8,128)S(1)}, f32[128,128]{1,0:T(8,128)S(1)}, u32[]{:S(2)}, u32[]{:S(2)}) collective-permute-start(f32[128,128]{1,0:T(8,128)S(1)} %add.22), channel_id=1, source_target_pairs={{0,2},{1,3},{2,0},{3,1},{4,6},{5,7},{6,4},{7,5},{8,10},{9,11},{10,... | collective-permute-start | bytes 196616 | tf_op jit(solution)/shard_map/ppermute | solution.py:543
  39.8 9.3 %collective-permute-start.11 = (f32[2,128,128]{2,1,0:T(8,128)S(1)}, f32[2,128,128]{2,1,0:T(8,128)S(1)}, u32[]{:S(2)}, u32[]{:S(2)}) collective-permute-start(f32[2,128,128]{2,1,0:T(8,128)S(1)} %get-tuple-element.59), channel_id=1, source_target_pairs={{0,1},{1,0},{2,3},{3,2},{4,5},{5,4},{6,7},{7,6},{8,9},{9,8},{10,11... | collective-permute-start | bytes 393224 | tf_op jit(solution)/shard_map/ppermute | solution.py:510
  40.5 8.6 %collective-permute-start.12 = (f32[2,128,128]{2,1,0:T(8,128)S(1)}, f32[2,128,128]{2,1,0:T(8,128)S(1)}, u32[]{:S(2)}, u32[]{:S(2)}) collective-permute-start(f32[2,128,128]{2,1,0:T(8,128)S(1)} %get-tuple-element.60), channel_id=1, source_target_pairs={{1,2},{3,4},{5,6},{2,1},{4,3},{6,5},{9,10},{11,12},{13,14},{10,9},... | collective-permute-start | bytes 393224 | tf_op jit(solution)/shard_map/ppermute | solution.py:515
  42.7 6.4 %collective-permute-start.10 = (f32[128,128]{1,0:T(8,128)S(1)}, f32[128,128]{1,0:T(8,128)S(1)}, u32[]{:S(2)}, u32[]{:S(2)}) collective-permute-start(f32[128,128]{1,0:T(8,128)S(1)} %add.19), channel_id=1, source_target_pairs={{0,16},{1,17},{2,18},{3,19},{4,20},{5,21},{6,22},{7,23},{8,24},{9,... | collective-permute-start | bytes 196616 | tf_op jit(solution)/shard_map/ppermute | solution.py:543
  49.1 1.3 %collective-permute-start.13 = (f32[128,128]{1,0:T(8,128)S(1)}, f32[128,128]{1,0:T(8,128)S(1)}, u32[]{:S(2)}, u32[]{:S(2)}) collective-permute-start(f32[128,128]{1,0:T(8,128)S(1)} %add.20), channel_id=1, source_target_pairs={{0,8},{8,0},{16,24},{24,16},{1,9},{9,1},{17,25},{25,17},{2,10},{10... | collective-permute-start | bytes 196616 | tf_op jit(solution)/shard_map/ppermute | solution.py:510
